TPU v7x, 32 devices: a whole 2x2x4 slice. The times are simulated.
32 devices in a mesh: dp: 2 (over x), expert: 4 (over z), tensor: 4 (over y, core).
Axes of the slice: x: 2, y: 2, z: 4, core: 2. Of those that a mesh axis runs over, the one named last changes fastest.
Arguments:
- grad_out: bfloat16 [1024, 4096], P(('dp', 'expert')), may hold values from -6 to 6
- expert_ids: int32 [1024, 8], P(('dp', 'expert')), may hold values from 0 to 127, all different within a row
- gate_values: bfloat16 [1024, 8], P(('dp', 'expert')), may hold values from 0.019897461 to 0.5
- saved_hidden: bfloat16 [2, 4, 16, 1536], P('dp', 'expert', None, 'tensor'), may hold values from -0.59765625 to 0.59765625
- down_weight: bfloat16 [4, 1536, 4096], P('expert', 'tensor'), may hold values from -0.15625 to 0.15625
Outputs:
- gate_grad: float32 [1024, 8], P(('dp', 'expert'))
- hidden_grad: bfloat16 [2, 4, 16, 1536], P('dp', 'expert', None, 'tensor')
- down_grad: float32 [4, 1536, 4096], P('expert', 'tensor', 'dp')
Inputs may be any that keep to these rules, and one draw needn't show every extreme that they name: `expert_ids`: the 8 experts of a row differ.
All inputs are finite; a program needn't handle non-finite values.
Results may differ from a plain program's by a relative error of at most 0.0085.
Values may be sent and summed in bfloat16 or wider, within the bound.
No kernel may reach another device: no remote copies, remote signals or barrier semaphores. Data moves between devices by JAX's collectives and lax.ppermute only.
A program may use at most 64 MiB of HBM per device.

v0:
```python
import jax
import jax.numpy as jnp
from jax import lax
from jax.sharding import PartitionSpec as P

CAP = 4


def slot_table(route_ids, gate_rows, count):
    experts = jnp.arange(count, dtype=jnp.int32)
    hits = (route_ids[:, :, None] == experts[None, None, :]).astype(jnp.int32)
    member = jnp.sum(hits, axis=1)
    gate_expert = jnp.sum(
        jnp.where(hits > 0, gate_rows.astype(jnp.float32)[:, :, None], 0.0), axis=1
    )
    before = jnp.cumsum(member, axis=0) - member
    kept = member * (before < CAP).astype(jnp.int32)
    places = jnp.arange(CAP, dtype=jnp.int32)
    match = kept.T[:, None, :] * (before.T[:, None, :] == places[None, :, None]).astype(jnp.int32)
    positions = jnp.arange(route_ids.shape[0], dtype=jnp.int32)
    source_row = jnp.sum(match * positions[None, None, :], axis=2)
    filled = jnp.sum(match, axis=2)
    slot_gate = jnp.sum(match.astype(jnp.float32) * gate_expert.T[:, None, :], axis=2).astype(
        jnp.bfloat16
    )
    return (source_row, filled, slot_gate, hits, kept, before)


def returned_grad(back, hits, kept, before):
    count = back.shape[0]
    spots = jnp.minimum(before, CAP - 1)
    picked = back[jnp.arange(count, dtype=jnp.int32)[None, :], spots]
    picked = jnp.where(kept > 0, picked, jnp.zeros((), picked.dtype))
    return jnp.sum(hits.astype(picked.dtype) * picked[:, None, :], axis=2)


def on_device(grad_out, expert_ids, gate_values, saved_hidden, down_weight):
    count = lax.axis_size("expert")
    source_row, filled, slot_gate, hits, kept, before = slot_table(expert_ids, gate_values, count)
    outgoing = jnp.where(
        filled[:, :, None] > 0, grad_out[source_row], jnp.zeros((), grad_out.dtype)
    )
    arrived, gate_in = (
        lax.all_to_all(outgoing, "expert", split_axis=0, concat_axis=0, tiled=True),
        lax.all_to_all(slot_gate, "expert", split_axis=0, concat_axis=0, tiled=True),
    )
    slot_count = count * CAP
    arrived = arrived.reshape(slot_count, grad_out.shape[1])
    gate_column = gate_in.reshape(slot_count, 1).astype(jnp.float32)
    weight = down_weight[0]
    hidden = saved_hidden[0, 0]
    upstream = lax.dot_general(
        arrived, weight, (((1,), (1,)), ((), ())), preferred_element_type=jnp.float32
    )
    hidden_grad = (gate_column * upstream).astype(jnp.bfloat16)
    gate_part = jnp.sum(hidden.astype(jnp.float32) * upstream, axis=1)
    gate_total = lax.psum(gate_part, "tensor")
    back = lax.all_to_all(
        gate_total.reshape(count, CAP), "expert", split_axis=0, concat_axis=0, tiled=True
    )
    weighted = (gate_column * arrived.astype(jnp.float32)).astype(jnp.bfloat16)
    summed = lax.psum_scatter(
        lax.dot_general(
            weighted, hidden, (((0,), (0,)), ((), ())), preferred_element_type=jnp.float32
        ).astype(jnp.bfloat16),
        "dp",
        scatter_dimension=0,
        tiled=True,
    ).astype(jnp.float32)
    down_grad = summed.T[None]
    gate_grad = returned_grad(back, hits, kept, before)
    return (gate_grad, hidden_grad[None, None], down_grad)


def solution(mesh):
    return jax.shard_map(
        on_device,
        mesh=mesh,
        in_specs=(
            P(("dp", "expert"), None),
            P(("dp", "expert"), None),
            P(("dp", "expert"), None),
            P("dp", "expert", None, "tensor"),
            P("expert", "tensor", None),
        ),
        out_specs=(
            P(("dp", "expert"), None),
            P("dp", "expert", None, "tensor"),
            P("expert", "tensor", "dp"),
        ),
        check_vma=False,
    )
```

profile of v0, /device:TPU:0, one launch (start us, length us, event | category | flops | bytes accessed | tf_op | source)
XLA Modules:
  0.0 113.0 jit_solution(12452658753684091098)
XLA Ops:
  7.2 0.0 copy-start
  7.2 0.9 convert_reduce_fusion
  8.0 0.1 copy.39
  8.2 0.2 reduce_window_sum.13
  8.3 0.1 copy.43
  8.4 0.1 copy.42
  8.5 0.2 select_reduce_fusion.1
  8.7 0.1 reshape.111
  8.8 2.1 %gather_fusion = bf16[16,4096]{1,0:T(8,128)(2,1)S(1)} fusion(bf16[128,4096]{1,0:T(8,128)(2,1)} %param.5, s32[1024]{0:T(1024)S(1)} %pad_clamp_fusion), kind=kCustom, calls=%fused_computation | custom fusion | bytes 262208 | tf_op jit(solution)/shard_map/gather | solution.py:41
  10.9 0.1 reshape.110
  11.0 0.8 broadcast_select_fusion
  11.8 6.3 %all-to-all-start = ((bf16[4,4,4096]{2,1,0:T(4,128)(2,1)}), bf16[4,4,4096]{2,1,0:T(4,128)(2,1)S(1)}, u32[]{:S(2)}, u32[]{:S(2)}) async-start(bf16[4,4,4096]{2,1,0:T(4,128)(2,1)} %broadcast_select_fusion), calls=%async_computation | async-start | bytes 262144 | tf_op jit(solution)/shard_map/all_to_all | solution.py:44
  18.1 0.1 copy.40
  18.2 0.7 convert_element_type.68
  18.9 0.1 copy.45
  19.0 5.2 %all-to-all-done = bf16[4,4,4096]{2,1,0:T(4,128)(2,1)S(1)} async-done(((bf16[4,4,4096]{2,1,0:T(4,128)(2,1)}), bf16[4,4,4096]{2,1,0:T(4,128)(2,1)S(1)}, u32[]{:S(2)}, u32[]{:S(2)}) %all-to-all-start) | async-done | bytes 131104 | tf_op jit(solution)/shard_map/all_to_all | solution.py:44
  24.2 0.0 copy-done
  24.2 1.7 %multiply_reduce_fusion = (f32[16]{0:T(128)S(1)}, f32[16,384]{1,0:T(8,128)S(1)}) fusion(bf16[1,1,16,384]{3,2,1,0:T(8,128)(2,1)} %param.8, bf16[16,4096]{1,0:T(8,128)(2,1)S(1)} %reshape.105, bf16[1,384,4096]{2,1,0:T(8,128)(2,1)S(1)} %copy-done), kind=kOutput, calls=%fused_computation.14 | convolution fusion | flops 50350064 | bytes 3313728 | tf_op jit(solution)/shard_map/dot_general | solution.py:52
  26.0 0.1 all_to_all.16
  26.1 6.2 %psum.7 = f32[4,1,4]{2,0,1:T(4,128)} all-reduce(f32[4,1,4]{2,0,1:T(4,128)S(1)} %all_to_all.16), channel_id=1, replica_groups=mesh['dp'=2,'expert'=4,'tensor'=4] {'tensor'}, use_global_device_ids=true, to_apply=%region_5.6 | all-reduce | flops 16 | bytes 128 | tf_op jit(solution)/shard_map/psum | solution.py:57
  32.3 3.2 %all-to-all-start.1 = ((f32[4,1,4]{2,1,0:T(1,128)}), f32[4,1,4]{2,1,0:T(1,128)S(1)}, u32[]{:S(2)}, u32[]{:S(2)}) async-start(f32[4,1,4]{2,1,0:T(1,128)} %bitcast.5), calls=%async_computation.1 | async-start | bytes 4096 | tf_op jit(solution)/shard_map/all_to_all | solution.py:58
  35.5 0.0 reduce-scatter.2.cloned.1.call-start
  35.6 0.1 reshape.117
  35.7 5.3 %all-to-all-done.1 = f32[4,1,4]{2,1,0:T(1,128)S(1)} async-done(((f32[4,1,4]{2,1,0:T(1,128)}), f32[4,1,4]{2,1,0:T(1,128)S(1)}, u32[]{:S(2)}, u32[]{:S(2)}) %all-to-all-start.1) | async-done | bytes 96 | tf_op jit(solution)/shard_map/all_to_all | solution.py:58
  40.9 0.0 copy-start.2
  40.9 0.0 copy-start.1
  40.9 4.8 %gather_fusion.1 = f32[512]{0:T(512)S(1)} fusion(f32[4,4]{1,0:T(4,128)S(1)} %bitcast.39, s32[512]{0:T(512)S(1)} %reshape.117), kind=kCustom, calls=%fused_computation.1 | custom fusion | bytes 8192 | tf_op jit(solution)/shard_map/gather | solution.py:32
  45.7 0.1 reshape.120
  45.8 0.1 copy.46
  45.9 0.0 copy-done.2
  45.9 0.6 select_reduce_fusion
  46.5 0.1 fusion.8
  46.6 7.9 %all_to_all.23 = bf16[4,1,4]{2,1,0:T(2,128)(2,1)S(1)} all-to-all(bf16[4,1,4]{2,1,0:T(2,128)(2,1)S(1)} %copy.47), channel_id=1, replica_groups=mesh['dp'=2,'expert'=4,'tensor'=4] {'expert'}, dimensions={0} | all-to-all | bytes 64 | tf_op jit(solution)/shard_map/all_to_all | solution.py:45
  54.5 0.1 multiply_convert_fusion
  54.7 0.0 copy-done.1
  54.7 2.7 %convolution_convert_fusion = bf16[4096,384]{1,0:T(8,128)(2,1)} fusion(bf16[16,4096]{1,0:T(8,128)(2,1)S(1)} %convert_element_type.78, bf16[1,1,16,384]{3,2,1,0:T(8,128)(2,1)S(1)} %copy-done.1), kind=kOutput, calls=%fused_computation.2 | convolution fusion | flops 51904512 | bytes 3289088 | tf_op jit(solution)/shard_map/dot_general | solution.py:63
  57.4 0.0 reduce-scatter.2.cloned.1.call-update
  57.4 0.1 reshape.106
  57.5 0.7 fusion.4
  58.2 41.2 %reduce-scatter.2.cloned.1.call-done = bf16[2048,384]{1,0:T(8,128)(2,1)} async-done(((bf16[4096,384]{1,0:T(8,128)(2,1)}), bf16[2048,384]{1,0:T(8,128)(2,1)}) %reduce-scatter.2.cloned.1.call-update) | async-done | bytes 1572880 | tf_op jit(solution)/shard_map/reduce_scatter | solution.py:62
  99.3 3.3 %convert_bitcast_fusion = f32[1,384,2048]{1,2,0:T(8,128)} fusion(bf16[2048,384]{1,0:T(8,128)(2,1)} %reduce-scatter.2.cloned.1.call-done), kind=kLoop, calls=%fused_computation.5 | loop fusion | flops 786432 | bytes 4718592 | tf_op jit(solution)/shard_map/broadcast_in_dim | solution.py:70
  102.6 3.5 %copy.48 = f32[1,384,2048]{2,1,0:T(8,128)} copy(f32[1,384,2048]{1,2,0:T(8,128)} %convert_bitcast_fusion) | data formatting | bytes 6291456
  (11 shorter events, 0.2 us)
Async XLA Ops:
  7.2 17.1 %copy-start = (bf16[1,384,4096]{2,1,0:T(8,128)(2,1)S(1)}, bf16[1,384,4096]{2,1,0:T(8,128)(2,1)}, u32[]{:S(2)}) copy-start(bf16[1,384,4096]{2,1,0:T(8,128)(2,1)} %param.9) | copy-start | bytes 9437188
  11.8 12.4 %all-to-all-start = ((bf16[4,4,4096]{2,1,0:T(4,128)(2,1)}), bf16[4,4,4096]{2,1,0:T(4,128)(2,1)S(1)}, u32[]{:S(2)}, u32[]{:S(2)}) async-start(bf16[4,4,4096]{2,1,0:T(4,128)(2,1)} %broadcast_select_fusion), calls=%async_computation | async-start | bytes 262144 | tf_op jit(solution)/shard_map/all_to_all | solution.py:44
  32.3 8.7 %all-to-all-start.1 = ((f32[4,1,4]{2,1,0:T(1,128)}), f32[4,1,4]{2,1,0:T(1,128)S(1)}, u32[]{:S(2)}, u32[]{:S(2)}) async-start(f32[4,1,4]{2,1,0:T(1,128)} %bitcast.5), calls=%async_computation.1 | async-start | bytes 4096 | tf_op jit(solution)/shard_map/all_to_all | solution.py:58
  35.5 63.8 %reduce-scatter.2.cloned.1.call-start = ((), (), s32[]{:S(2)}) async-start(), calls=%async_computation.4 | async-start | bytes 4718592 | tf_op jit(solution)/shard_map/reduce_scatter | solution.py:62
  40.9 5.0 %copy-start.2 = (s32[128,8]{0,1:T(8,128)S(1)}, s32[128,8]{0,1:T(8,128)}, u32[]{:S(2)}) copy-start(s32[128,8]{0,1:T(8,128)} %param.6) | copy-start | bytes 12292
  40.9 13.7 %copy-start.1 = (bf16[1,1,16,384]{3,2,1,0:T(8,128)(2,1)S(1)}, bf16[1,1,16,384]{3,2,1,0:T(8,128)(2,1)}, u32[]{:S(2)}) copy-start(bf16[1,1,16,384]{3,2,1,0:T(8,128)(2,1)} %param.8) | copy-start | bytes 36868
Sparse Core Ops, SparseCore 0:
  57.5 41.7 reduce-scatter.1
where the time goes:
time: 113 us
  waiting for transfers between devices  51.6 us (46%)
  blocking collectives  14.1 us (12%)
  between operations  14.1 us (12%)
  local copies, waits for them, and re-layouts  11.5 us (10%)
  starting transfers between devices  9.58 us (8%)
  other arithmetic  7.59 us (7%)
  matrix products  4.43 us (4%)
    reduce_scatter x1, waiting for transfers between devices, on_device(): lax.psum_scatter(lax.dot_general(weighted, hidden, (((0,), (0,)), ((), ()...  41.2 us
    all_to_all x1, blocking collectives, on_device(): lax.all_to_all(slot_gate, 'expert', split_axis=0, concat_axis=0, tiled=True)  7.87 us
    all_to_all x1, starting transfers between devices, on_device(): lax.all_to_all(outgoing, 'expert', split_axis=0, concat_axis=0, tiled=True)  6.32 us
    psum x1, blocking collectives, on_device(): gate_total = lax.psum(gate_part, 'tensor')  6.21 us
    all_to_all x1, waiting for transfers between devices, on_device(): lax.all_to_all(gate_total.reshape(count, CAP), 'expert', split_axis=0, co...  5.28 us
    all_to_all x1, waiting for transfers between devices, on_device(): lax.all_to_all(outgoing, 'expert', split_axis=0, concat_axis=0, tiled=True)  5.18 us
    gather x3, local copies, waits for them, and re-layouts, returned_grad(): picked = back[jnp.arange(count, dtype=jnp.int32)[None, :], spots]  4.92 us
    unnamed x7, local copies, waits for them, and re-layouts  3.57 us
  transfers between devices with their start and end apart: 3, of which 3 were waited for; matrix products, arithmetic and copies ran while one was open for 2% of the time, Pallas kernels for 0%

commit v1 on v0

v1 whole, which is shorter than its diff:
```python
import functools

import jax
import jax.numpy as jnp
from jax import lax
from jax.experimental import pallas as pl
from jax.experimental.pallas import tpu as pltpu
from jax.sharding import PartitionSpec as P

CAP = 4
LANES = 128
PAD = 8
VMEM = pl.BlockSpec(memory_space=pltpu.VMEM)


def dot(a, b, dims):
    return lax.dot_general(a, b, (dims, ((), ())), preferred_element_type=jnp.float32)


def route_kernel(count, ids_ref, gates_ref, grad_ref, match_ref, *sends):
    me = lax.axis_index("expert")
    top, tokens = ids_ref.shape
    width = grad_ref.shape[1]
    rows = count * PAD
    row = lax.broadcasted_iota(jnp.int32, (rows, tokens), 0)
    expert = me + row // PAD
    expert = jnp.where(expert >= count, expert - count, expert)
    place = row % PAD
    ids = ids_ref[...]
    gates = gates_ref[...].astype(jnp.float32)
    member = jnp.zeros((rows, tokens), jnp.float32)
    gate = jnp.zeros((rows, tokens), jnp.float32)
    for k in range(top):
        hit = ids[k : k + 1, :] == expert
        member = jnp.where(hit, 1.0, member)
        gate = jnp.where(hit, gates[k : k + 1, :], gate)
    earlier = lax.broadcasted_iota(jnp.int32, (tokens, tokens), 0)
    later = lax.broadcasted_iota(jnp.int32, (tokens, tokens), 1)
    before = dot(
        member.astype(jnp.bfloat16), (earlier < later).astype(jnp.bfloat16), ((1,), (0,))
    )
    taken = (member > 0) & (before == place.astype(jnp.float32)) & (place < CAP)
    match = taken.astype(jnp.float32)
    match_ref[...] = match
    slot_gate = jnp.sum(match * gate, axis=1, keepdims=True)
    picked = dot(match.astype(jnp.bfloat16), grad_ref[...], ((1,), (0,)))
    for r in range(count):
        part = slice(r * PAD, r * PAD + CAP)
        sends[r][:, :width] = picked[part].astype(jnp.bfloat16)
        sends[r][:, width:] = jnp.broadcast_to(slot_gate[part], (CAP, LANES)).astype(jnp.bfloat16)


def slot_order(count):
    me = lax.axis_index("expert")
    slots = count * CAP
    here = lax.broadcasted_iota(jnp.int32, (slots, slots), 0)
    saved = lax.broadcasted_iota(jnp.int32, (slots, slots), 1)
    block = me - here // CAP
    block = jnp.where(block < 0, block + count, block)
    return (saved == block * CAP + here % CAP).astype(jnp.bfloat16)


def expert_kernel(count, groups, hidden_ref, weight_ref, *refs):
    received = refs[:count]
    hidden_grad_ref, back_ref = refs[count : count + 2]
    pays = refs[count + 2 : count + 2 + groups]
    rows_ref, weighted_ref = refs[count + 2 + groups :]
    width = weight_ref.shape[2]
    units = weight_ref.shape[1]
    for r in range(count):
        rows_ref[r * CAP : (r + 1) * CAP, :] = received[r][...].astype(jnp.float32)
    rows = rows_ref[:, :width]
    gate = rows_ref[:, width : width + 1]
    order = slot_order(count)
    hidden = dot(order, hidden_ref[0, 0], ((1,), (0,)))
    upstream = dot(rows.astype(jnp.bfloat16), weight_ref[0], ((1,), (1,)))
    back = jnp.sum(hidden * upstream, axis=1, keepdims=True)
    back_ref[...] = jnp.broadcast_to(back, back_ref.shape)
    scaled = (gate * upstream).astype(jnp.bfloat16)
    hidden_grad_ref[0, 0] = dot(order, scaled, ((0,), (0,))).astype(jnp.bfloat16)
    weighted_ref[...] = (gate * rows).astype(jnp.bfloat16)
    share = width // groups
    me = lax.axis_index("dp")
    for r in range(groups):
        group = me + r
        group = jnp.where(group >= groups, group - groups, group)
        pays[r][:, :share] = weighted_ref[:, pl.ds(pl.multiple_of(group * share, share), share)]
        pays[r][:, share:] = hidden.astype(jnp.bfloat16)


def down_kernel(groups, *refs):
    out_ref = refs[groups]
    step = pl.program_id(0)
    block, share = out_ref.shape[1:]
    total = None
    for r in range(groups):
        start = pl.multiple_of(share + step * block, LANES)
        hidden = refs[r][:, pl.ds(start, block)]
        term = dot(hidden, refs[r][:, :share], ((0,), (0,)))
        term = term.astype(jnp.bfloat16).astype(jnp.float32)
        total = term if total is None else total + term
    out_ref[0] = total


def gate_kernel(count, parts, ids_ref, match_ref, *refs):
    out_ref = refs[-1]
    me = lax.axis_index("expert")
    ids = ids_ref[...]
    total = jnp.zeros(out_ref.shape, jnp.float32)
    for r in range(count):
        expert = me + r
        expert = jnp.where(expert >= count, expert - count, expert)
        value = refs[0][r * CAP : (r + 1) * CAP, :]
        for part in range(1, parts):
            value = value + refs[part][r * CAP : (r + 1) * CAP, :]
        match = match_ref[r * PAD : r * PAD + CAP, :]
        chosen = jnp.sum(jnp.where(match > 0, value, 0.0), axis=0, keepdims=True)
        total = total + jnp.where(ids == expert, chosen, 0.0)
    out_ref[...] = total


def rotate(value, axis, by):
    size = lax.axis_size(axis)
    return lax.ppermute(value, axis, [(i, (i + by) % size) for i in range(size)])


def on_device(grad_out, expert_ids, gate_values, saved_hidden, down_weight):
    count = lax.axis_size("expert")
    groups = lax.axis_size("dp")
    tensors = lax.axis_size("tensor")
    tokens, width = grad_out.shape
    units = down_weight.shape[1]
    slots = count * CAP
    share = width // groups
    ids = expert_ids.T
    params = pltpu.CompilerParams(vmem_limit_bytes=24 * 2**20)

    match, *sends = pl.pallas_call(
        functools.partial(route_kernel, count),
        out_shape=[jax.ShapeDtypeStruct((count * PAD, tokens), jnp.float32)]
        + [jax.ShapeDtypeStruct((CAP, width + LANES), jnp.bfloat16)] * count,
        in_specs=[VMEM] * 3,
        out_specs=[VMEM] * (1 + count),
        compiler_params=params,
        name="route",
    )(ids, gate_values.T, grad_out)

    received = [sends[0]] + [rotate(sends[r], "expert", r) for r in range(1, count)]

    hidden_grad, back, *pays = pl.pallas_call(
        functools.partial(expert_kernel, count, groups),
        out_shape=[
            jax.ShapeDtypeStruct(saved_hidden.shape, jnp.bfloat16),
            jax.ShapeDtypeStruct((slots, LANES), jnp.float32),
        ]
        + [jax.ShapeDtypeStruct((slots, share + units), jnp.bfloat16)] * groups,
        in_specs=[VMEM] * (2 + count),
        out_specs=[VMEM] * (2 + groups),
        scratch_shapes=[
            pltpu.VMEM((slots, width + LANES), jnp.float32),
            pltpu.VMEM((slots, width), jnp.bfloat16),
        ],
        compiler_params=params,
        name="expert",
    )(saved_hidden, down_weight, *received)

    pays = [pays[0]] + [rotate(pays[r], "dp", r) for r in range(1, groups)]
    chunks = [back[r * CAP : (r + 1) * CAP] for r in range(count)]
    chunks = [chunks[0]] + [rotate(chunks[r], "expert", -r) for r in range(1, count)]
    back = jnp.concatenate(chunks, axis=0)
    backs = [back] + [rotate(back, "tensor", r) for r in range(1, tensors)]

    block = LANES
    down_grad = pl.pallas_call(
        functools.partial(down_kernel, groups),
        grid=(units // block,),
        out_shape=jax.ShapeDtypeStruct((1, units, share), jnp.float32),
        in_specs=[VMEM] * groups,
        out_specs=pl.BlockSpec((1, block, share), lambda i: (0, i, 0)),
        compiler_params=params,
        name="down",
    )(*pays)

    gate_grad = pl.pallas_call(
        functools.partial(gate_kernel, count, tensors),
        out_shape=jax.ShapeDtypeStruct(ids.shape, jnp.float32),
        in_specs=[VMEM] * (2 + tensors),
        out_specs=VMEM,
        compiler_params=params,
        name="gates",
    )(ids, match, *backs)
    return (gate_grad.T, hidden_grad, down_grad)


def solution(mesh):
    return jax.shard_map(
        on_device,
        mesh=mesh,
        in_specs=(
            P(("dp", "expert"), None),
            P(("dp", "expert"), None),
            P(("dp", "expert"), None),
            P("dp", "expert", None, "tensor"),
            P("expert", "tensor", None),
        ),
        out_specs=(
            P(("dp", "expert"), None),
            P("dp", "expert", None, "tensor"),
            P("expert", "tensor", "dp"),
        ),
        check_vma=False,
    )
```

time: 113 us -> 33.3 us (0.29)
  waiting for transfers between devices: 51.6 us -> 7.45 us
  blocking collectives: 14.1 us -> 0 us
  between operations: 14.1 us -> 0.67 us
  other arithmetic: 7.59 us -> 0.01 us
  local copies, waits for them, and re-layouts: 11.5 us -> 5.19 us
  Pallas kernels: 0 us -> 5.54 us
  starting transfers between devices: 9.58 us -> 14.2 us
  matrix products: 4.43 us -> 0 us
    reduce_scatter x1 -> x0, waiting for transfers between devices: 41.2 us -> none  [on_device(): lax.psum_scatter(lax.dot_general(weighted, hidden, (((0,), (0,)), ((), ()...]
    ppermute x0 -> x10, starting transfers between devices: none -> 14.2 us  [rotate(): lax.ppermute(value, axis, [(i, (i + by) % size) for i in range(size)])]
    all_to_all x2 -> x0, waiting for transfers between devices: 10.5 us -> none  [the longest x1 5.28 us: on_device(): lax.all_to_all(gate_total.reshape(count, CAP), 'expert', split_axis=0, co...]
    all_to_all x2 -> x0, starting transfers between devices: 9.54 us -> none  [the longest x1 6.32 us: on_device(): lax.all_to_all(outgoing, 'expert', split_axis=0, concat_axis=0, tiled=True)]
    all_to_all x1 -> x0, blocking collectives: 7.87 us -> none  [on_device(): lax.all_to_all(slot_gate, 'expert', split_axis=0, concat_axis=0, tiled=True)]
    ppermute x0 -> x10, waiting for transfers between devices: none -> 7.45 us  [rotate(): lax.ppermute(value, axis, [(i, (i + by) % size) for i in range(size)])]
    gather x5 -> x0, local copies, waits for them, and re-layouts: 7.09 us -> none  [the longest x3 4.92 us: returned_grad(): picked = back[jnp.arange(count, dtype=jnp.int32)[None, :], spots]]
    psum x1 -> x0, blocking collectives: 6.21 us -> none  [on_device(): gate_total = lax.psum(gate_part, 'tensor')]
  transfers between devices with their start and end apart: 3 -> 10, of which waited for: 3 -> 5; matrix products, arithmetic and copies ran while one was open for 2% -> 0% of each run, Pallas kernels for 0% -> 2%
where the time goes in v1:
time: 33.3 us; the launch traced here: 33 us
  starting transfers between devices  14.2 us (43%)
  waiting for transfers between devices  7.45 us (22%)
  Pallas kernels  5.54 us (17%)
  local copies, waits for them, and re-layouts  5.19 us (16%)
  between operations  0.67 us (2%)
    ppermute x10, starting transfers between devices, rotate(): lax.ppermute(value, axis, [(i, (i + by) % size) for i in range(size)])  14.2 us
    ppermute x10, waiting for transfers between devices, rotate(): lax.ppermute(value, axis, [(i, (i + by) % size) for i in range(size)])  7.45 us
    unnamed x12, local copies, waits for them, and re-layouts  5.18 us
    pallas_call x1, Pallas kernels, on_device(): pl.pallas_call(functools.partial(down_kernel, groups), grid=(units // blo...  2.87 us
    pallas_call x1, Pallas kernels, on_device(): pl.pallas_call(functools.partial(expert_kernel, count, groups), out_shape...  1.66 us
  transfers between devices with their start and end apart: 10, of which 5 were waited for; matrix products, arithmetic and copies ran while one was open for 0% of the time, Pallas kernels for 2%

profile of v1, /device:TPU:0, one launch (start us, length us, event | category | flops | bytes accessed | tf_op | source)
XLA Modules:
  0.0 33.0 jit_solution(17230026081731132544)
XLA Ops:
  0.6 0.0 copy-start.1
  0.6 1.2 %copy-done.1 = bf16[128,4096]{1,0:T(8,128)(2,1)S(1)} copy-done((bf16[128,4096]{1,0:T(8,128)(2,1)S(1)}, bf16[128,4096]{1,0:T(8,128)(2,1)}, u32[]{:S(2)}) %copy-start.1) | copy-done | bytes 1048600
  1.9 0.0 copy-start.2
  1.9 0.7 %copy-done.2 = s32[128,8]{0,1:T(8,128)S(1)} copy-done((s32[128,8]{0,1:T(8,128)S(1)}, s32[128,8]{0,1:T(8,128)}, u32[]{:S(2)}) %copy-start.2) | copy-done | bytes 4120
  2.5 0.0 copy-start.5
  2.5 0.7 %copy-done.5 = bf16[128,8]{0,1:T(8,128)(2,1)S(1)} copy-done((bf16[128,8]{0,1:T(8,128)(2,1)S(1)}, bf16[128,8]{0,1:T(8,128)(2,1)}, u32[]{:S(2)}) %copy-start.5) | copy-done | bytes 2072
  3.2 0.0 copy-start.3
  3.2 0.4 %route.1 = (f32[32,128]{1,0:T(8,128)S(1)}, bf16[4,4224]{1,0:T(4,128)(2,1)S(1)}, bf16[4,4224]{1,0:T(4,128)(2,1)S(1)}, bf16[4,4224]{1,0:T(4,128)(2,1)S(1)}, bf16[4,4224]{1,0:T(4,128)(2,1)S(1)}) custom-call(s32[8,128]{1,0:T(8,128)S(1)} %bitcast.3, bf16[8,128]{1,0:T(8,128)(2,1)S(1)} %bitcast.5, bf16[128,4096]{1,0:T(8,128)(2,1)S(1)} %copy-done.1), custom_call_target="tpu_custom_call" | custom-call | tf_op jit(solution)/shard_map/route/pallas_call | solution.py:138
  3.6 3.1 %collective-permute-start = (bf16[4,4224]{1,0:T(4,128)(2,1)S(1)}, bf16[4,4224]{1,0:T(4,128)(2,1)S(1)}, u32[]{:S(2)}, u32[]{:S(2)}) collective-permute-start(bf16[4,4224]{1,0:T(4,128)(2,1)S(1)} %get-tuple-element.14), channel_id=1, source_target_pairs={{0,4},{4,8},{8,12},{12,0},{1,5},{5,9},{9,13},{13,1},{2,6},{6,10},{... | collective-permute-start | bytes 101384 | tf_op jit(solution)/shard_map/ppermute | solution.py:124
  6.7 2.6 %collective-permute-start.1 = (bf16[4,4224]{1,0:T(4,128)(2,1)S(1)}, bf16[4,4224]{1,0:T(4,128)(2,1)S(1)}, u32[]{:S(2)}, u32[]{:S(2)}) collective-permute-start(bf16[4,4224]{1,0:T(4,128)(2,1)S(1)} %get-tuple-element.15), channel_id=1, source_target_pairs={{0,8},{4,12},{8,0},{12,4},{1,9},{5,13},{9,1},{13,5},{2,10},{6,14},... | collective-permute-start | bytes 101384 | tf_op jit(solution)/shard_map/ppermute | solution.py:124
  9.3 1.3 %collective-permute-start.2 = (bf16[4,4224]{1,0:T(4,128)(2,1)S(1)}, bf16[4,4224]{1,0:T(4,128)(2,1)S(1)}, u32[]{:S(2)}, u32[]{:S(2)}) collective-permute-start(bf16[4,4224]{1,0:T(4,128)(2,1)S(1)} %get-tuple-element.16), channel_id=1, source_target_pairs={{0,12},{4,0},{8,4},{12,8},{1,13},{5,1},{9,5},{13,9},{2,14},{6,2},{... | collective-permute-start | bytes 101384 | tf_op jit(solution)/shard_map/ppermute | solution.py:124
  10.7 0.0 collective-permute-done.refs_1_
  10.7 1.2 %collective-permute-done.1.refs_2_ = bf16[4,4224]{1,0:T(4,128)(2,1)S(1)} collective-permute-done((bf16[4,4224]{1,0:T(4,128)(2,1)S(1)}, bf16[4,4224]{1,0:T(4,128)(2,1)S(1)}, u32[]{:S(2)}, u32[]{:S(2)}) %collective-permute-start.1) | collective-permute-done | bytes 33824 | tf_op jit(solution)/shard_map/ppermute | solution.py:124
  11.9 1.3 %collective-permute-done.2.refs_3_ = bf16[4,4224]{1,0:T(4,128)(2,1)S(1)} collective-permute-done((bf16[4,4224]{1,0:T(4,128)(2,1)S(1)}, bf16[4,4224]{1,0:T(4,128)(2,1)S(1)}, u32[]{:S(2)}, u32[]{:S(2)}) %collective-permute-start.2) | collective-permute-done | bytes 33824 | tf_op jit(solution)/shard_map/ppermute | solution.py:124
  13.2 0.0 copy-start
  13.2 1.9 %copy-done = bf16[1,384,4096]{2,1,0:T(8,128)(2,1)S(1)} copy-done((bf16[1,384,4096]{2,1,0:T(8,128)(2,1)S(1)}, bf16[1,384,4096]{2,1,0:T(8,128)(2,1)}, u32[]{:S(2)}) %copy-start) | copy-done | bytes 3145752
  15.1 0.0 copy-start.4
  15.1 0.7 %copy-done.4 = bf16[1,1,16,384]{3,2,1,0:T(8,128)(2,1)S(1)} copy-done((bf16[1,1,16,384]{3,2,1,0:T(8,128)(2,1)S(1)}, bf16[1,1,16,384]{3,2,1,0:T(8,128)(2,1)}, u32[]{:S(2)}) %copy-start.4) | copy-done | bytes 12312
  15.8 1.7 %expert.1 = (bf16[1,1,16,384]{3,2,1,0:T(8,128)(2,1)}, f32[16,128]{1,0:T(8,128)S(1)}, bf16[16,2432]{1,0:T(8,128)(2,1)S(1)}, bf16[16,2432]{1,0:T(8,128)(2,1)S(1)}) custom-call(bf16[1,1,16,384]{3,2,1,0:T(8,128)(2,1)S(1)} %copy-done.4, bf16[1,384,4096]{2,1,0:T(8,128)(2,1)S(1)} %copy-done, bf16[4,4224]{1,0:T(4,128)(2,1)S(1)} %get-tuple-element.13.refs_0_, ...), custom_call_target="tpu_custom_call" | custom-call | tf_op jit(solution)/shard_map/expert/pallas_call | solution.py:150
  17.5 0.2 collective-permute-start.5
  17.7 3.5 %collective-permute-start.4 = (f32[4,128]{1,0:T(4,128)S(1)}, f32[4,128]{1,0:T(4,128)S(1)}, u32[]{:S(2)}, u32[]{:S(2)}) collective-permute-start(f32[4,128]{1,0:T(4,128)S(1)} %get-tuple-element.23), channel_id=1, source_target_pairs={{0,8},{4,12},{8,0},{12,4},{1,9},{5,13},{9,1},{13,5},{2,10},{6,14},... | collective-permute-start | bytes 6152 | tf_op jit(solution)/shard_map/ppermute | solution.py:124
  21.2 0.1 collective-permute-start.3
  21.3 1.5 %collective-permute-start.9 = (bf16[16,2432]{1,0:T(8,128)(2,1)S(1)}, bf16[16,2432]{1,0:T(8,128)(2,1)S(1)}, u32[]{:S(2)}, u32[]{:S(2)}) collective-permute-start(bf16[16,2432]{1,0:T(8,128)(2,1)S(1)} %get-tuple-element.20), channel_id=1, source_target_pairs={{0,16},{16,0},{1,17},{17,1},{2,18},{18,2},{3,19},{19,3},{4,20},{20... | collective-permute-start | bytes 233480 | tf_op jit(solution)/shard_map/ppermute | solution.py:124
  22.8 0.0 collective-permute-done.5
  22.9 0.0 collective-permute-done.4
  22.9 1.9 %collective-permute-done.3 = f32[4,128]{1,0:T(4,128)S(1)} collective-permute-done((f32[4,128]{1,0:T(4,128)S(1)}, f32[4,128]{1,0:T(4,128)S(1)}, u32[]{:S(2)}, u32[]{:S(2)}) %collective-permute-start.3) | collective-permute-done | bytes 2080 | tf_op jit(solution)/shard_map/ppermute | solution.py:124
  24.8 0.1 collective-permute-start.8
  24.9 1.6 %collective-permute-start.7 = (f32[16,128]{1,0:T(8,128)S(1)}, f32[16,128]{1,0:T(8,128)S(1)}, u32[]{:S(2)}, u32[]{:S(2)}) collective-permute-start(f32[16,128]{1,0:T(8,128)S(1)} %pad_maximum_fusion.refs_0_), channel_id=1, source_target_pairs={{0,2},{1,3},{2,0},{3,1},{4,6},{5,7},{6,4},{7,5},{8,10},{9,11},{10,... | collective-permute-start | bytes 24584 | tf_op jit(solution)/shard_map/ppermute | solution.py:124
  26.5 0.2 collective-permute-start.6
  26.6 0.0 collective-permute-done.8.refs_3_
  26.6 2.0 %collective-permute-done.7.refs_2_ = f32[16,128]{1,0:T(8,128)S(1)} collective-permute-done((f32[16,128]{1,0:T(8,128)S(1)}, f32[16,128]{1,0:T(8,128)S(1)}, u32[]{:S(2)}, u32[]{:S(2)}) %collective-permute-start.7) | collective-permute-done | bytes 8224 | tf_op jit(solution)/shard_map/ppermute | solution.py:124
  28.6 0.9 %collective-permute-done.6.refs_1_ = f32[16,128]{1,0:T(8,128)S(1)} collective-permute-done((f32[16,128]{1,0:T(8,128)S(1)}, f32[16,128]{1,0:T(8,128)S(1)}, u32[]{:S(2)}, u32[]{:S(2)}) %collective-permute-start.6) | collective-permute-done | bytes 8224 | tf_op jit(solution)/shard_map/ppermute | solution.py:124
  29.5 0.0 copy-done.3
  29.5 0.6 %gates.1 = f32[8,128]{1,0:T(8,128)} custom-call(s32[8,128]{1,0:T(8,128)S(1)} %bitcast.4, f32[32,128]{1,0:T(8,128)S(1)} %get-tuple-element.12.match_ref, f32[16,128]{1,0:T(8,128)S(1)} %pad_maximum_fusion.refs_0_, f32[16,128]{1,0:T(8,128)S(1)} %collective-permute-done.6.refs_1_, f32[16,128]{1,0:T(8,128)S(1)} %collective-permute-done.7.refs_2_, ...), custom_call_target="tpu_custom_call" | custom-call | tf_op jit(solution)/shard_map/gates/pallas_call | solution.py:184
  30.1 0.0 collective-permute-done.9.refs_1_
  30.1 2.9 %down.1 = f32[1,384,2048]{2,1,0:T(8,128)} custom-call(bf16[16,2432]{1,0:T(8,128)(2,1)S(1)} %get-tuple-element.19.refs_0_, bf16[16,2432]{1,0:T(8,128)(2,1)S(1)} %collective-permute-done.9.refs_1_), custom_call_target="tpu_custom_call" | custom-call | tf_op jit(solution)/shard_map/down/pallas_call | solution.py:174
  (2 shorter events, 0.0 us)
Async XLA Ops:
  0.6 1.2 %copy-start.1 = (bf16[128,4096]{1,0:T(8,128)(2,1)S(1)}, bf16[128,4096]{1,0:T(8,128)(2,1)}, u32[]{:S(2)}) copy-start(bf16[128,4096]{1,0:T(8,128)(2,1)} %grad_ref.1) | copy-start | bytes 3145732
  1.9 0.7 %copy-start.2 = (s32[128,8]{0,1:T(8,128)S(1)}, s32[128,8]{0,1:T(8,128)}, u32[]{:S(2)}) copy-start(s32[128,8]{0,1:T(8,128)} %param.6) | copy-start | bytes 12292
  2.5 0.7 %copy-start.5 = (bf16[128,8]{0,1:T(8,128)(2,1)S(1)}, bf16[128,8]{0,1:T(8,128)(2,1)}, u32[]{:S(2)}) copy-start(bf16[128,8]{0,1:T(8,128)(2,1)} %param.7) | copy-start | bytes 6148
  3.2 26.3 %copy-start.3 = (s32[128,8]{0,1:T(8,128)S(1)}, s32[128,8]{0,1:T(8,128)}, u32[]{:S(2)}) copy-start(s32[128,8]{0,1:T(8,128)} %param.6) | copy-start | bytes 12292
  3.6 7.0 %collective-permute-start = (bf16[4,4224]{1,0:T(4,128)(2,1)S(1)}, bf16[4,4224]{1,0:T(4,128)(2,1)S(1)}, u32[]{:S(2)}, u32[]{:S(2)}) collective-permute-start(bf16[4,4224]{1,0:T(4,128)(2,1)S(1)} %get-tuple-element.14), channel_id=1, source_target_pairs={{0,4},{4,8},{8,12},{12,0},{1,5},{5,9},{9,13},{13,1},{2,6},{6,10},{... | collective-permute-start | bytes 101384 | tf_op jit(solution)/shard_map/ppermute | solution.py:124
  6.7 5.2 %collective-permute-start.1 = (bf16[4,4224]{1,0:T(4,128)(2,1)S(1)}, bf16[4,4224]{1,0:T(4,128)(2,1)S(1)}, u32[]{:S(2)}, u32[]{:S(2)}) collective-permute-start(bf16[4,4224]{1,0:T(4,128)(2,1)S(1)} %get-tuple-element.15), channel_id=1, source_target_pairs={{0,8},{4,12},{8,0},{12,4},{1,9},{5,13},{9,1},{13,5},{2,10},{6,14},... | collective-permute-start | bytes 101384 | tf_op jit(solution)/shard_map/ppermute | solution.py:124
  9.3 3.9 %collective-permute-start.2 = (bf16[4,4224]{1,0:T(4,128)(2,1)S(1)}, bf16[4,4224]{1,0:T(4,128)(2,1)S(1)}, u32[]{:S(2)}, u32[]{:S(2)}) collective-permute-start(bf16[4,4224]{1,0:T(4,128)(2,1)S(1)} %get-tuple-element.16), channel_id=1, source_target_pairs={{0,12},{4,0},{8,4},{12,8},{1,13},{5,1},{9,5},{13,9},{2,14},{6,2},{... | collective-permute-start | bytes 101384 | tf_op jit(solution)/shard_map/ppermute | solution.py:124
  13.2 1.9 %copy-start = (bf16[1,384,4096]{2,1,0:T(8,128)(2,1)S(1)}, bf16[1,384,4096]{2,1,0:T(8,128)(2,1)}, u32[]{:S(2)}) copy-start(bf16[1,384,4096]{2,1,0:T(8,128)(2,1)} %weight_ref.1) | copy-start | bytes 9437188
  15.1 0.7 %copy-start.4 = (bf16[1,1,16,384]{3,2,1,0:T(8,128)(2,1)S(1)}, bf16[1,1,16,384]{3,2,1,0:T(8,128)(2,1)}, u32[]{:S(2)}) copy-start(bf16[1,1,16,384]{3,2,1,0:T(8,128)(2,1)} %hidden_ref.1) | copy-start | bytes 36868
  17.5 5.4 %collective-permute-start.5 = (f32[4,128]{1,0:T(4,128)S(1)}, f32[4,128]{1,0:T(4,128)S(1)}, u32[]{:S(2)}, u32[]{:S(2)}) collective-permute-start(f32[4,128]{1,0:T(4,128)S(1)} %get-tuple-element.22), channel_id=1, source_target_pairs={{0,4},{4,8},{8,12},{12,0},{1,5},{5,9},{9,13},{13,1},{2,6},{6,10},{... | collective-permute-start | bytes 6152 | tf_op jit(solution)/shard_map/ppermute | solution.py:124
  17.7 5.1 %collective-permute-start.4 = (f32[4,128]{1,0:T(4,128)S(1)}, f32[4,128]{1,0:T(4,128)S(1)}, u32[]{:S(2)}, u32[]{:S(2)}) collective-permute-start(f32[4,128]{1,0:T(4,128)S(1)} %get-tuple-element.23), channel_id=1, source_target_pairs={{0,8},{4,12},{8,0},{12,4},{1,9},{5,13},{9,1},{13,5},{2,10},{6,14},... | collective-permute-start | bytes 6152 | tf_op jit(solution)/shard_map/ppermute | solution.py:124
  21.2 3.6 %collective-permute-start.3 = (f32[4,128]{1,0:T(4,128)S(1)}, f32[4,128]{1,0:T(4,128)S(1)}, u32[]{:S(2)}, u32[]{:S(2)}) collective-permute-start(f32[4,128]{1,0:T(4,128)S(1)} %get-tuple-element.24), channel_id=1, source_target_pairs={{0,12},{4,0},{8,4},{12,8},{1,13},{5,1},{9,5},{13,9},{2,14},{6,2},{... | collective-permute-start | bytes 6152 | tf_op jit(solution)/shard_map/ppermute | solution.py:124
  21.3 8.8 %collective-permute-start.9 = (bf16[16,2432]{1,0:T(8,128)(2,1)S(1)}, bf16[16,2432]{1,0:T(8,128)(2,1)S(1)}, u32[]{:S(2)}, u32[]{:S(2)}) collective-permute-start(bf16[16,2432]{1,0:T(8,128)(2,1)S(1)} %get-tuple-element.20), channel_id=1, source_target_pairs={{0,16},{16,0},{1,17},{17,1},{2,18},{18,2},{3,19},{19,3},{4,20},{20... | collective-permute-start | bytes 233480 | tf_op jit(solution)/shard_map/ppermute | solution.py:124
  24.8 1.8 %collective-permute-start.8 = (f32[16,128]{1,0:T(8,128)S(1)}, f32[16,128]{1,0:T(8,128)S(1)}, u32[]{:S(2)}, u32[]{:S(2)}) collective-permute-start(f32[16,128]{1,0:T(8,128)S(1)} %pad_maximum_fusion.refs_0_), channel_id=1, source_target_pairs={{0,3},{1,0},{2,1},{3,2},{4,7},{5,4},{6,5},{7,6},{8,11},{9,8},{10,9... | collective-permute-start | bytes 24584 | tf_op jit(solution)/shard_map/ppermute | solution.py:124
  24.9 3.7 %collective-permute-start.7 = (f32[16,128]{1,0:T(8,128)S(1)}, f32[16,128]{1,0:T(8,128)S(1)}, u32[]{:S(2)}, u32[]{:S(2)}) collective-permute-start(f32[16,128]{1,0:T(8,128)S(1)} %pad_maximum_fusion.refs_0_), channel_id=1, source_target_pairs={{0,2},{1,3},{2,0},{3,1},{4,6},{5,7},{6,4},{7,5},{8,10},{9,11},{10,... | collective-permute-start | bytes 24584 | tf_op jit(solution)/shard_map/ppermute | solution.py:124
  26.5 3.1 %collective-permute-start.6 = (f32[16,128]{1,0:T(8,128)S(1)}, f32[16,128]{1,0:T(8,128)S(1)}, u32[]{:S(2)}, u32[]{:S(2)}) collective-permute-start(f32[16,128]{1,0:T(8,128)S(1)} %pad_maximum_fusion.refs_0_), channel_id=1, source_target_pairs={{0,1},{1,2},{2,3},{3,0},{4,5},{5,6},{6,7},{7,4},{8,9},{9,10},{10,1... | collective-permute-start | bytes 24584 | tf_op jit(solution)/shard_map/ppermute | solution.py:124

commit v2 on v1

v2 whole, which is shorter than its diff:
```python
import functools

import jax
import jax.numpy as jnp
from jax import lax
from jax.experimental import pallas as pl
from jax.experimental.pallas import tpu as pltpu
from jax.sharding import PartitionSpec as P

CAP = 4
LANES = 128
PAD = 8
VMEM = pl.BlockSpec(memory_space=pltpu.VMEM)
HBM = pl.BlockSpec(memory_space=pltpu.HBM)
PARAMS = pltpu.CompilerParams(vmem_limit_bytes=32 * 2**20)


def dot(a, b, dims):
    return lax.dot_general(a, b, (dims, ((), ())), preferred_element_type=jnp.float32)


def in_hbm(*arrays):
    return [pltpu.with_memory_space_constraint(x, pltpu.HBM) for x in arrays]


def cost(flops, nbytes):
    return pl.CostEstimate(flops=flops, bytes_accessed=nbytes, transcendentals=0)


def paired(size):
    return size & (size - 1) == 0


def target(me, step, size):
    if paired(size):
        return me ^ step
    after = me + step
    return after % size if isinstance(me, int) else jnp.where(after >= size, after - size, after)


def source(me, step, size):
    if paired(size):
        return me ^ step
    before = me - step
    return before % size if isinstance(me, int) else jnp.where(before < 0, before + size, before)


def send(value, axis, step, give=target):
    size = lax.axis_size(axis)
    return lax.ppermute(value, axis, [(i, give(i, step, size)) for i in range(size)])


def route_kernel(count, ids_hbm, gates_hbm, grad_hbm, ids_out, match_ref, *refs):
    sends = refs[:count]
    ids_ref, gates_ref, grad_ref, sems = refs[count:]
    small = [
        pltpu.make_async_copy(ids_hbm, ids_ref, sems.at[0]),
        pltpu.make_async_copy(gates_hbm, gates_ref, sems.at[1]),
    ]
    large = pltpu.make_async_copy(grad_hbm, grad_ref, sems.at[2])
    for copy in small:
        copy.start()
    large.start()
    me = lax.axis_index("expert")
    top, tokens = ids_ref.shape
    width = grad_ref.shape[1]
    rows = count * PAD
    row = lax.broadcasted_iota(jnp.int32, (rows, tokens), 0)
    expert = target(me, row // PAD, count)
    place = row % PAD
    earlier = lax.broadcasted_iota(jnp.int32, (tokens, tokens), 0)
    later = lax.broadcasted_iota(jnp.int32, (tokens, tokens), 1)
    order = (earlier < later).astype(jnp.bfloat16)
    for copy in small:
        copy.wait()
    ids = ids_ref[...]
    ids_out[...] = ids
    gates = gates_ref[...].astype(jnp.float32)
    member = jnp.zeros((rows, tokens), jnp.float32)
    gate = jnp.zeros((rows, tokens), jnp.float32)
    for k in range(top):
        hit = ids[k : k + 1, :] == expert
        member = jnp.where(hit, 1.0, member)
        gate = jnp.where(hit, gates[k : k + 1, :], gate)
    before = dot(member.astype(jnp.bfloat16), order, ((1,), (0,)))
    taken = (member > 0) & (before == place.astype(jnp.float32)) & (place < CAP)
    match = taken.astype(jnp.float32)
    match_ref[...] = match
    slot_gate = jnp.sum(match * gate, axis=1, keepdims=True)
    match = match.astype(jnp.bfloat16)
    large.wait()
    picked = dot(match, grad_ref[...], ((1,), (0,)))
    for r in range(count):
        part = slice(r * PAD, r * PAD + CAP)
        sends[r][:, :width] = picked[part].astype(jnp.bfloat16)
        sends[r][:, width:] = jnp.broadcast_to(slot_gate[part], (CAP, LANES)).astype(jnp.bfloat16)


def slot_order(count):
    me = lax.axis_index("expert")
    slots = count * CAP
    here = lax.broadcasted_iota(jnp.int32, (slots, slots), 0)
    saved = lax.broadcasted_iota(jnp.int32, (slots, slots), 1)
    return (saved == source(me, here // CAP, count) * CAP + here % CAP).astype(jnp.bfloat16)


def forward_kernel(count, pieces, match_ref, hidden_hbm, weight_hbm, weight_ref, hidden_ref, y_ref, *refs):
    saved_ref, sems = refs
    units = weight_ref.shape[0]
    block = units // pieces
    first = pltpu.make_async_copy(hidden_hbm.at[0, 0], saved_ref, sems.at[pieces])
    first.start()
    loads = []
    for p in range(pieces):
        rows = pl.ds(p * block, block)
        loads.append(pltpu.make_async_copy(weight_hbm.at[0, rows], weight_ref.at[rows], sems.at[p]))
        loads[-1].start()
    first.wait()
    hidden = dot(slot_order(count), saved_ref[...], ((1,), (0,))).astype(jnp.bfloat16)
    hidden_ref[...] = hidden
    for p in range(pieces):
        loads[p].wait()
        rows = slice(p * block, (p + 1) * block)
        term = dot(hidden[:, rows], weight_ref[rows, :], ((1,), (0,)))
        if p == 0:
            y_ref[...] = term
        else:
            y_ref[...] += term


def slot_kernel(count, groups, y_ref, hidden_ref, *refs):
    received = refs[:count]
    rows_ref, gate_ref = refs[count : count + 2]
    backs = refs[count + 2 : 2 * count + 2]
    pays = refs[2 * count + 2 : 2 * count + 2 + groups]
    wide_ref, weighted_ref = refs[2 * count + 2 + groups :]
    width = y_ref.shape[1]
    for r in range(count):
        wide_ref[r * CAP : (r + 1) * CAP, :] = received[r][...].astype(jnp.float32)
    rows = wide_ref[:, :width]
    back = jnp.sum(rows * y_ref[...], axis=1, keepdims=True)
    for r in range(count):
        backs[r][...] = jnp.broadcast_to(back[r * CAP : (r + 1) * CAP], backs[r].shape)
    gate = wide_ref[:, width:]
    gate_ref[...] = gate
    rows_ref[...] = rows.astype(jnp.bfloat16)
    weighted_ref[...] = (gate[:, :1] * rows).astype(jnp.bfloat16)
    share = width // groups
    me = lax.axis_index("dp")
    for r in range(groups):
        group = target(me, r, groups)
        pays[r][:, :share] = weighted_ref[:, pl.ds(pl.multiple_of(group * share, share), share)]
        pays[r][:, share:] = hidden_ref[...]


def down_term(pay_ref, share, start, block):
    hidden = pay_ref[:, pl.ds(start, block)]
    return dot(hidden, pay_ref[:, :share], ((0,), (0,))).astype(jnp.bfloat16)


def upstream_kernel(count, pieces, rows_ref, gate_ref, weight_ref, pay_ref, hidden_grad_ref, own_ref):
    units = weight_ref.shape[0]
    share = own_ref.shape[1]
    upstream = dot(rows_ref[...], weight_ref[...], ((1,), (1,)))
    scaled = (gate_ref[:, :1] * upstream).astype(jnp.bfloat16)
    hidden_grad_ref[0, 0] = dot(slot_order(count), scaled, ((0,), (0,))).astype(jnp.bfloat16)
    block = units // pieces
    for p in range(pieces):
        own_ref[p * block : (p + 1) * block, :] = down_term(pay_ref, share, share + p * block, block)


def down_kernel(others, own_ref, *refs):
    out_ref = refs[others]
    block, share = out_ref.shape[1:]
    step = pl.program_id(0)
    total = own_ref[...].astype(jnp.float32)
    for r in range(others):
        start = pl.multiple_of(share + step * block, LANES)
        total = total + down_term(refs[r], share, start, block).astype(jnp.float32)
    out_ref[0] = total


def gate_kernel(count, parts, ids_ref, match_ref, *refs):
    out_ref = refs[-1]
    me = lax.axis_index("expert")
    ids = ids_ref[...]
    total = jnp.zeros(out_ref.shape, jnp.float32)
    for r in range(count):
        value = refs[0][r * CAP : (r + 1) * CAP, :]
        for part in range(1, parts):
            value = value + refs[part][r * CAP : (r + 1) * CAP, :]
        match = match_ref[r * PAD : r * PAD + CAP, :]
        chosen = jnp.sum(jnp.where(match > 0, value, 0.0), axis=0, keepdims=True)
        total = total + jnp.where(ids == target(me, r, count), chosen, 0.0)
    out_ref[...] = total


def on_device(grad_out, expert_ids, gate_values, saved_hidden, down_weight):
    count = lax.axis_size("expert")
    groups = lax.axis_size("dp")
    tensors = lax.axis_size("tensor")
    tokens, width = grad_out.shape
    top = expert_ids.shape[1]
    units = down_weight.shape[1]
    slots = count * CAP
    share = width // groups
    pieces = units // LANES

    ids, match, *sends = pl.pallas_call(
        functools.partial(route_kernel, count),
        out_shape=[
            jax.ShapeDtypeStruct((top, tokens), jnp.int32),
            jax.ShapeDtypeStruct((count * PAD, tokens), jnp.float32),
        ]
        + [jax.ShapeDtypeStruct((CAP, width + LANES), jnp.bfloat16)] * count,
        in_specs=[HBM] * 3,
        out_specs=[VMEM] * (2 + count),
        scratch_shapes=[
            pltpu.VMEM((top, tokens), jnp.int32),
            pltpu.VMEM((top, tokens), jnp.bfloat16),
            pltpu.VMEM((tokens, width), jnp.bfloat16),
            pltpu.SemaphoreType.DMA((3,)),
        ],
        compiler_params=PARAMS,
        cost_estimate=cost(2 * count * PAD * tokens * width, 2 * tokens * width),
        name="route",
    )(*in_hbm(expert_ids.T, gate_values.T, grad_out))

    received = [sends[0]] + [send(sends[r], "expert", r) for r in range(1, count)]

    weight, hidden, y = pl.pallas_call(
        functools.partial(forward_kernel, count, pieces),
        out_shape=[
            jax.ShapeDtypeStruct((units, width), jnp.bfloat16),
            jax.ShapeDtypeStruct((slots, units), jnp.bfloat16),
            jax.ShapeDtypeStruct((slots, width), jnp.float32),
        ],
        in_specs=[VMEM, HBM, HBM],
        out_specs=[VMEM] * 3,
        scratch_shapes=[
            pltpu.VMEM((slots, units), jnp.bfloat16),
            pltpu.SemaphoreType.DMA((pieces + 1,)),
        ],
        compiler_params=PARAMS,
        cost_estimate=cost(2 * slots * units * width, 2 * units * width),
        name="forward",
    )(match, *in_hbm(saved_hidden, down_weight))

    rows, gate, *rest = pl.pallas_call(
        functools.partial(slot_kernel, count, groups),
        out_shape=[
            jax.ShapeDtypeStruct((slots, width), jnp.bfloat16),
            jax.ShapeDtypeStruct((slots, LANES), jnp.float32),
        ]
        + [jax.ShapeDtypeStruct((CAP, LANES), jnp.float32)] * count
        + [jax.ShapeDtypeStruct((slots, share + units), jnp.bfloat16)] * groups,
        in_specs=[VMEM] * (2 + count),
        out_specs=[VMEM] * (2 + count + groups),
        scratch_shapes=[
            pltpu.VMEM((slots, width + LANES), jnp.float32),
            pltpu.VMEM((slots, width), jnp.bfloat16),
        ],
        compiler_params=PARAMS,
        cost_estimate=cost(4 * slots * width, 16 * slots * width),
        name="slots",
    )(y, hidden, *received)
    backs, pays = rest[:count], rest[count:]

    backs = [backs[0]] + [send(backs[r], "expert", r, source) for r in range(1, count)]
    others = [send(pays[r], "dp", r) for r in range(1, groups)]
    back = jnp.concatenate(backs, axis=0)
    backs = [back] + [send(back, "tensor", r) for r in range(1, tensors)]

    hidden_grad, own = pl.pallas_call(
        functools.partial(upstream_kernel, count, pieces),
        out_shape=[
            jax.ShapeDtypeStruct(saved_hidden.shape, jnp.bfloat16),
            jax.ShapeDtypeStruct((units, share), jnp.bfloat16),
        ],
        in_specs=[VMEM] * 4,
        out_specs=[VMEM] * 2,
        compiler_params=PARAMS,
        cost_estimate=cost(2 * slots * units * (width + share), 2 * units * width),
        name="upstream",
    )(rows, gate, weight, pays[0])

    down_grad = pl.pallas_call(
        functools.partial(down_kernel, groups - 1),
        grid=(pieces,),
        out_shape=jax.ShapeDtypeStruct((1, units, share), jnp.float32),
        in_specs=[pl.BlockSpec((LANES, share), lambda i: (i, 0))] + [VMEM] * (groups - 1),
        out_specs=pl.BlockSpec((1, LANES, share), lambda i: (0, i, 0)),
        compiler_params=PARAMS,
        cost_estimate=cost(2 * slots * units * share, 4 * units * share),
        name="down",
    )(own, *others)

    gate_grad = pl.pallas_call(
        functools.partial(gate_kernel, count, tensors),
        out_shape=jax.ShapeDtypeStruct(ids.shape, jnp.float32),
        in_specs=[VMEM] * (2 + tensors),
        out_specs=VMEM,
        compiler_params=PARAMS,
        cost_estimate=cost(tensors * slots * tokens, 4 * tensors * slots * tokens),
        name="gates",
    )(ids, match, *backs)
    return (gate_grad.T, hidden_grad, down_grad)


def solution(mesh):
    return jax.shard_map(
        on_device,
        mesh=mesh,
        in_specs=(
            P(("dp", "expert"), None),
            P(("dp", "expert"), None),
            P(("dp", "expert"), None),
            P("dp", "expert", None, "tensor"),
            P("expert", "tensor", None),
        ),
        out_specs=(
            P(("dp", "expert"), None),
            P("dp", "expert", None, "tensor"),
            P("expert", "tensor", "dp"),
        ),
        check_vma=False,
    )
```

time: 33.3 us -> 28 us (0.84)
  local copies, waits for them, and re-layouts: 5.19 us -> 0 us
  Pallas kernels: 5.54 us -> 9.02 us
  waiting for transfers between devices: 7.45 us -> 4.49 us
  starting transfers between devices: 14.2 us -> 13.5 us
    unnamed x12 -> x0, local copies, waits for them, and re-layouts: 5.18 us -> none
    ppermute x10, waiting for transfers between devices: 7.45 us -> 4.49 us  [send(): lax.ppermute(value, axis, [(i, give(i, step, size)) for i in range(size)])]
    pallas_call x2 -> x4, Pallas kernels: 4.53 us -> 6.84 us  [the longest x1 2.6 us: on_device(): pl.pallas_call(functools.partial(down_kernel, groups - 1), grid=(pieces,)...]
    pallas_call x1, Pallas kernels: 0.4 us -> 1.57 us  [on_device(): pl.pallas_call(functools.partial(route_kernel, count), out_shape=[jax.Sha...]
    ppermute x10, starting transfers between devices: 14.2 us -> 13.5 us  [send(): lax.ppermute(value, axis, [(i, give(i, step, size)) for i in range(size)])]
  transfers between devices with their start and end apart: 10 -> 10, of which waited for: 5 -> 4; matrix products, arithmetic and copies ran while one was open for 0% -> 0% of each run, Pallas kernels for 2% -> 17%
where the time goes in v2:
time: 28 us; the launch traced here: 27.7 us
  starting transfers between devices  13.5 us (48%)
  Pallas kernels  9.02 us (32%)
  waiting for transfers between devices  4.49 us (16%)
  between operations  0.68 us (2%)
    ppermute x10, starting transfers between devices, send(): lax.ppermute(value, axis, [(i, give(i, step, size)) for i in range(size)])  13.5 us
    ppermute x10, waiting for transfers between devices, send(): lax.ppermute(value, axis, [(i, give(i, step, size)) for i in range(size)])  4.49 us
    pallas_call x1, Pallas kernels, on_device(): pl.pallas_call(functools.partial(down_kernel, groups - 1), grid=(pieces,)...  2.6 us
    pallas_call x1, Pallas kernels, on_device(): pl.pallas_call(functools.partial(forward_kernel, count, pieces), out_shap...  2.16 us
    pallas_call x1, Pallas kernels, on_device(): pl.pallas_call(functools.partial(upstream_kernel, count, pieces), out_sha...  1.93 us
    pallas_call x1, Pallas kernels, on_device(): pl.pallas_call(functools.partial(route_kernel, count), out_shape=[jax.Sha...  1.57 us
    pallas_call x1, Pallas kernels, on_device(): pl.pallas_call(functools.partial(gate_kernel, count, tensors), out_shape=...  0.61 us
  transfers between devices with their start and end apart: 10, of which 4 were waited for; matrix products, arithmetic and copies ran while one was open for 0% of the time, Pallas kernels for 17%

profile of v2, /device:TPU:0, one launch (start us, length us, event | category | flops | bytes accessed | tf_op | source)
XLA Modules:
  0.0 27.7 jit_solution(5979282284395295226)
XLA Ops:
  0.6 1.6 %route.1 = (s32[8,128]{1,0:T(8,128)S(1)}, f32[32,128]{1,0:T(8,128)S(1)}, bf16[4,4224]{1,0:T(4,128)(2,1)S(1)}, bf16[4,4224]{1,0:T(4,128)(2,1)S(1)}, bf16[4,4224]{...) custom-call(s32[8,128]{1,0:T(8,128)} %bitcast.3, bf16[8,128]{1,0:T(8,128)(2,1)} %bitcast.5, bf16[128,4096]{1,0:T(8,128)(2,1)} %grad_hbm.1), custom_call_target="tpu_custom_call" | custom-call | flops 33554432 | bytes 1048576 | tf_op jit(solution)/shard_map/route/pallas_call | solution.py:209
  2.2 3.1 %collective-permute-start = (bf16[4,4224]{1,0:T(4,128)(2,1)S(1)}, bf16[4,4224]{1,0:T(4,128)(2,1)S(1)}, u32[]{:S(2)}, u32[]{:S(2)}) collective-permute-start(bf16[4,4224]{1,0:T(4,128)(2,1)S(1)} %get-tuple-element.27), channel_id=1, source_target_pairs={{0,4},{4,0},{8,12},{12,8},{1,5},{5,1},{9,13},{13,9},{2,6},{6,2},{1... | collective-permute-start | bytes 101384 | tf_op jit(solution)/shard_map/ppermute | solution.py:50
  5.3 2.6 %collective-permute-start.1 = (bf16[4,4224]{1,0:T(4,128)(2,1)S(1)}, bf16[4,4224]{1,0:T(4,128)(2,1)S(1)}, u32[]{:S(2)}, u32[]{:S(2)}) collective-permute-start(bf16[4,4224]{1,0:T(4,128)(2,1)S(1)} %get-tuple-element.28), channel_id=1, source_target_pairs={{0,8},{4,12},{8,0},{12,4},{1,9},{5,13},{9,1},{13,5},{2,10},{6,14},... | collective-permute-start | bytes 101384 | tf_op jit(solution)/shard_map/ppermute | solution.py:50
  7.9 0.0 collective-permute-start.2
  7.9 2.2 %forward.1 = (bf16[384,4096]{1,0:T(8,128)(2,1)S(1)}, bf16[16,384]{1,0:T(8,128)(2,1)S(1)}, f32[16,4096]{1,0:T(8,128)S(1)}) custom-call(f32[32,128]{1,0:T(8,128)S(1)} %get-tuple-element.23.match_ref, bf16[1,1,16,384]{3,2,1,0:T(8,128)(2,1)} %hidden_hbm.1, bf16[1,384,4096]{2,1,0:T(8,128)(2,1)} %weight_hbm.1), custom_call_target="tpu_custom_call" | custom-call | flops 50331648 | bytes 3145728 | tf_op jit(solution)/shard_map/forward/pallas_call | solution.py:231
  10.1 0.0 collective-permute-done.refs_1_
  10.1 0.7 %collective-permute-done.1.refs_2_ = bf16[4,4224]{1,0:T(4,128)(2,1)S(1)} collective-permute-done((bf16[4,4224]{1,0:T(4,128)(2,1)S(1)}, bf16[4,4224]{1,0:T(4,128)(2,1)S(1)}, u32[]{:S(2)}, u32[]{:S(2)}) %collective-permute-start.1) | collective-permute-done | bytes 33824 | tf_op jit(solution)/shard_map/ppermute | solution.py:50
  10.7 2.9 %collective-permute-done.2.refs_3_ = bf16[4,4224]{1,0:T(4,128)(2,1)S(1)} collective-permute-done((bf16[4,4224]{1,0:T(4,128)(2,1)S(1)}, bf16[4,4224]{1,0:T(4,128)(2,1)S(1)}, u32[]{:S(2)}, u32[]{:S(2)}) %collective-permute-start.2) | collective-permute-done | bytes 33824 | tf_op jit(solution)/shard_map/ppermute | solution.py:50
  13.6 0.2 slots.1
  13.8 0.4 %collective-permute-start.5 = (f32[4,128]{1,0:T(4,128)S(1)}, f32[4,128]{1,0:T(4,128)S(1)}, u32[]{:S(2)}, u32[]{:S(2)}) collective-permute-start(f32[4,128]{1,0:T(4,128)S(1)} %get-tuple-element.33), channel_id=1, source_target_pairs={{0,12},{4,8},{8,4},{12,0},{1,13},{5,9},{9,5},{13,1},{2,14},{6,10},... | collective-permute-start | bytes 6152 | tf_op jit(solution)/shard_map/ppermute | solution.py:50
  14.2 0.1 collective-permute-start.4
  14.3 3.9 %collective-permute-start.3 = (f32[4,128]{1,0:T(4,128)S(1)}, f32[4,128]{1,0:T(4,128)S(1)}, u32[]{:S(2)}, u32[]{:S(2)}) collective-permute-start(f32[4,128]{1,0:T(4,128)S(1)} %get-tuple-element.31), channel_id=1, source_target_pairs={{0,4},{4,0},{8,12},{12,8},{1,5},{5,1},{9,13},{13,9},{2,6},{6,2},{1... | collective-permute-start | bytes 6152 | tf_op jit(solution)/shard_map/ppermute | solution.py:50
  18.2 1.5 %collective-permute-start.9 = (bf16[16,2432]{1,0:T(8,128)(2,1)S(1)}, bf16[16,2432]{1,0:T(8,128)(2,1)S(1)}, u32[]{:S(2)}, u32[]{:S(2)}) collective-permute-start(bf16[16,2432]{1,0:T(8,128)(2,1)S(1)} %get-tuple-element.40), channel_id=1, source_target_pairs={{0,16},{16,0},{1,17},{17,1},{2,18},{18,2},{3,19},{19,3},{4,20},{20... | collective-permute-start | bytes 233480 | tf_op jit(solution)/shard_map/ppermute | solution.py:50
  19.7 0.0 collective-permute-done.5
  19.7 0.0 collective-permute-done.4
  19.7 0.1 collective-permute-done.3
  19.8 0.1 collective-permute-start.6
  19.8 1.6 %collective-permute-start.7 = (f32[16,128]{1,0:T(8,128)S(1)}, f32[16,128]{1,0:T(8,128)S(1)}, u32[]{:S(2)}, u32[]{:S(2)}) collective-permute-start(f32[16,128]{1,0:T(8,128)S(1)} %pad_maximum_fusion.refs_0_), channel_id=1, source_target_pairs={{0,2},{1,3},{2,0},{3,1},{4,6},{5,7},{6,4},{7,5},{8,10},{9,11},{10,... | collective-permute-start | bytes 24584 | tf_op jit(solution)/shard_map/ppermute | solution.py:50
  21.4 0.3 collective-permute-start.8
  21.7 1.9 %upstream.1 = (bf16[1,1,16,384]{3,2,1,0:T(8,128)(2,1)}, bf16[384,2048]{1,0:T(8,128)(2,1)S(1)}) custom-call(bf16[16,4096]{1,0:T(8,128)(2,1)S(1)} %get-tuple-element.34.rows_ref, f32[16,128]{1,0:T(8,128)S(1)} %get-tuple-element.35.gate_ref, bf16[384,4096]{1,0:T(8,128)(2,1)S(1)} %get-tuple-element.36.weight_ref, bf16[16,2432]{1,0:T(8,128)(2,1)S(1)} %get-tuple-element.37.pay_ref), custom_call_target="tpu_custom_call" | custom-call | flops 75497472 | bytes 3145728 | tf_op jit(solution)/shard_map/upstream/pallas_call | solution.py:274
  23.6 0.0 collective-permute-done.6.refs_1_
  23.6 0.0 collective-permute-done.7.refs_2_
  23.6 0.9 %collective-permute-done.8.refs_3_ = f32[16,128]{1,0:T(8,128)S(1)} collective-permute-done((f32[16,128]{1,0:T(8,128)S(1)}, f32[16,128]{1,0:T(8,128)S(1)}, u32[]{:S(2)}, u32[]{:S(2)}) %collective-permute-start.8) | collective-permute-done | bytes 8224 | tf_op jit(solution)/shard_map/ppermute | solution.py:50
  24.5 0.6 %gates.1 = f32[8,128]{1,0:T(8,128)} custom-call(s32[8,128]{1,0:T(8,128)S(1)} %get-tuple-element.22.ids_ref, f32[32,128]{1,0:T(8,128)S(1)} %get-tuple-element.23.match_ref, f32[16,128]{1,0:T(8,128)S(1)} %pad_maximum_fusion.refs_0_, f32[16,128]{1,0:T(8,128)S(1)} %collective-permute-done.6.refs_1_, f32[16,128]{1,0:T(8,128)S(1)} %collective-permute-done.7.refs_2_, ...), custom_call_target="tpu_custom_call" | custom-call | flops 8192 | bytes 32768 | tf_op jit(solution)/shard_map/gates/pallas_call | solution.py:298
  25.1 0.0 collective-permute-done.9.refs_0_
  25.1 2.6 %down.1 = f32[1,384,2048]{2,1,0:T(8,128)} custom-call(bf16[384,2048]{1,0:T(8,128)(2,1)S(1)} %get-tuple-element.39.own_ref, bf16[16,2432]{1,0:T(8,128)(2,1)S(1)} %collective-permute-done.9.refs_0_), custom_call_target="tpu_custom_call" | custom-call | flops 25165824 | bytes 3145728 | tf_op jit(solution)/shard_map/down/pallas_call | solution.py:287
  (1 shorter events, 0.0 us)
Async XLA Ops:
  2.2 7.9 %collective-permute-start = (bf16[4,4224]{1,0:T(4,128)(2,1)S(1)}, bf16[4,4224]{1,0:T(4,128)(2,1)S(1)}, u32[]{:S(2)}, u32[]{:S(2)}) collective-permute-start(bf16[4,4224]{1,0:T(4,128)(2,1)S(1)} %get-tuple-element.27), channel_id=1, source_target_pairs={{0,4},{4,0},{8,12},{12,8},{1,5},{5,1},{9,13},{13,9},{2,6},{6,2},{1... | collective-permute-start | bytes 101384 | tf_op jit(solution)/shard_map/ppermute | solution.py:50
  5.3 5.4 %collective-permute-start.1 = (bf16[4,4224]{1,0:T(4,128)(2,1)S(1)}, bf16[4,4224]{1,0:T(4,128)(2,1)S(1)}, u32[]{:S(2)}, u32[]{:S(2)}) collective-permute-start(bf16[4,4224]{1,0:T(4,128)(2,1)S(1)} %get-tuple-element.28), channel_id=1, source_target_pairs={{0,8},{4,12},{8,0},{12,4},{1,9},{5,13},{9,1},{13,5},{2,10},{6,14},... | collective-permute-start | bytes 101384 | tf_op jit(solution)/shard_map/ppermute | solution.py:50
  7.9 5.7 %collective-permute-start.2 = (bf16[4,4224]{1,0:T(4,128)(2,1)S(1)}, bf16[4,4224]{1,0:T(4,128)(2,1)S(1)}, u32[]{:S(2)}, u32[]{:S(2)}) collective-permute-start(bf16[4,4224]{1,0:T(4,128)(2,1)S(1)} %get-tuple-element.29), channel_id=1, source_target_pairs={{0,12},{4,8},{8,4},{12,0},{1,13},{5,9},{9,5},{13,1},{2,14},{6,10},... | collective-permute-start | bytes 101384 | tf_op jit(solution)/shard_map/ppermute | solution.py:50
  13.8 5.9 %collective-permute-start.5 = (f32[4,128]{1,0:T(4,128)S(1)}, f32[4,128]{1,0:T(4,128)S(1)}, u32[]{:S(2)}, u32[]{:S(2)}) collective-permute-start(f32[4,128]{1,0:T(4,128)S(1)} %get-tuple-element.33), channel_id=1, source_target_pairs={{0,12},{4,8},{8,4},{12,0},{1,13},{5,9},{9,5},{13,1},{2,14},{6,10},... | collective-permute-start | bytes 6152 | tf_op jit(solution)/shard_map/ppermute | solution.py:50
  14.2 5.5 %collective-permute-start.4 = (f32[4,128]{1,0:T(4,128)S(1)}, f32[4,128]{1,0:T(4,128)S(1)}, u32[]{:S(2)}, u32[]{:S(2)}) collective-permute-start(f32[4,128]{1,0:T(4,128)S(1)} %get-tuple-element.32), channel_id=1, source_target_pairs={{0,8},{4,12},{8,0},{12,4},{1,9},{5,13},{9,1},{13,5},{2,10},{6,14},... | collective-permute-start | bytes 6152 | tf_op jit(solution)/shard_map/ppermute | solution.py:50
  14.3 5.5 %collective-permute-start.3 = (f32[4,128]{1,0:T(4,128)S(1)}, f32[4,128]{1,0:T(4,128)S(1)}, u32[]{:S(2)}, u32[]{:S(2)}) collective-permute-start(f32[4,128]{1,0:T(4,128)S(1)} %get-tuple-element.31), channel_id=1, source_target_pairs={{0,4},{4,0},{8,12},{12,8},{1,5},{5,1},{9,13},{13,9},{2,6},{6,2},{1... | collective-permute-start | bytes 6152 | tf_op jit(solution)/shard_map/ppermute | solution.py:50
  18.2 6.9 %collective-permute-start.9 = (bf16[16,2432]{1,0:T(8,128)(2,1)S(1)}, bf16[16,2432]{1,0:T(8,128)(2,1)S(1)}, u32[]{:S(2)}, u32[]{:S(2)}) collective-permute-start(bf16[16,2432]{1,0:T(8,128)(2,1)S(1)} %get-tuple-element.40), channel_id=1, source_target_pairs={{0,16},{16,0},{1,17},{17,1},{2,18},{18,2},{3,19},{19,3},{4,20},{20... | collective-permute-start | bytes 233480 | tf_op jit(solution)/shard_map/ppermute | solution.py:50
  19.8 3.9 %collective-permute-start.6 = (f32[16,128]{1,0:T(8,128)S(1)}, f32[16,128]{1,0:T(8,128)S(1)}, u32[]{:S(2)}, u32[]{:S(2)}) collective-permute-start(f32[16,128]{1,0:T(8,128)S(1)} %pad_maximum_fusion.refs_0_), channel_id=1, source_target_pairs={{0,1},{1,0},{2,3},{3,2},{4,5},{5,4},{6,7},{7,6},{8,9},{9,8},{10,11... | collective-permute-start | bytes 24584 | tf_op jit(solution)/shard_map/ppermute | solution.py:50
  19.8 3.8 %collective-permute-start.7 = (f32[16,128]{1,0:T(8,128)S(1)}, f32[16,128]{1,0:T(8,128)S(1)}, u32[]{:S(2)}, u32[]{:S(2)}) collective-permute-start(f32[16,128]{1,0:T(8,128)S(1)} %pad_maximum_fusion.refs_0_), channel_id=1, source_target_pairs={{0,2},{1,3},{2,0},{3,1},{4,6},{5,7},{6,4},{7,5},{8,10},{9,11},{10,... | collective-permute-start | bytes 24584 | tf_op jit(solution)/shard_map/ppermute | solution.py:50
  21.4 3.1 %collective-permute-start.8 = (f32[16,128]{1,0:T(8,128)S(1)}, f32[16,128]{1,0:T(8,128)S(1)}, u32[]{:S(2)}, u32[]{:S(2)}) collective-permute-start(f32[16,128]{1,0:T(8,128)S(1)} %pad_maximum_fusion.refs_0_), channel_id=1, source_target_pairs={{0,3},{1,2},{2,1},{3,0},{4,7},{5,6},{6,5},{7,4},{8,11},{9,10},{10,... | collective-permute-start | bytes 24584 | tf_op jit(solution)/shard_map/ppermute | solution.py:50

commit v3 on v2

v3 whole, which is shorter than its diff:
```python
import functools

import jax
import jax.numpy as jnp
from jax import lax
from jax.experimental import pallas as pl
from jax.experimental.pallas import tpu as pltpu
from jax.sharding import PartitionSpec as P

CAP = 4
LANES = 128
PAD = 8
VMEM = pl.BlockSpec(memory_space=pltpu.VMEM)
HBM = pl.BlockSpec(memory_space=pltpu.HBM)
PARAMS = pltpu.CompilerParams(vmem_limit_bytes=32 * 2**20)


def dot(a, b, dims):
    return lax.dot_general(a, b, (dims, ((), ())), preferred_element_type=jnp.float32)


def in_hbm(*arrays):
    return [pltpu.with_memory_space_constraint(x, pltpu.HBM) for x in arrays]


def cost(flops, nbytes):
    return pl.CostEstimate(flops=flops, bytes_accessed=nbytes, transcendentals=0)


def paired(size):
    return size & (size - 1) == 0


def target(me, step, size):
    if paired(size):
        return me ^ step
    after = me + step
    return after % size if isinstance(me, int) else jnp.where(after >= size, after - size, after)


def source(me, step, size):
    if paired(size):
        return me ^ step
    before = me - step
    return before % size if isinstance(me, int) else jnp.where(before < 0, before + size, before)


def reply(step, size):
    return step if paired(size) else -step % size


def send(value, axis, step, give=target):
    size = lax.axis_size(axis)
    return lax.ppermute(value, axis, [(i, give(i, step, size)) for i in range(size)])


def front_kernel(count, pieces, *refs):
    ids_hbm, gates_hbm, grad_hbm, hidden_hbm, weight_hbm = refs[:5]
    ids_ref, match_ref, weight_ref, hidden_ref = refs[5:9]
    sends = refs[9 : 9 + count]
    gates_ref, grad_ref, saved_ref, both_ref, sems = refs[9 + count :]
    units, width = weight_ref.shape
    block = units // pieces
    top, tokens = ids_ref.shape
    pairs = [(ids_hbm, ids_ref), (gates_hbm, gates_ref), (hidden_hbm.at[0, 0], saved_ref), (grad_hbm, grad_ref)]
    for p in range(pieces):
        part = pl.ds(p * block, block)
        pairs.append((weight_hbm.at[0, part], weight_ref.at[part]))
    copies = [pltpu.make_async_copy(*pair, sems.at[n]) for n, pair in enumerate(pairs)]
    for copy in copies:
        copy.start()
    me = lax.axis_index("expert")
    rows = count * PAD
    row = lax.broadcasted_iota(jnp.int32, (rows, tokens), 0)
    expert = target(me, row // PAD, count)
    place = row % PAD
    earlier = lax.broadcasted_iota(jnp.int32, (tokens, tokens), 0)
    later = lax.broadcasted_iota(jnp.int32, (tokens, tokens), 1)
    order = (earlier < later).astype(jnp.bfloat16)
    for copy in copies[:3]:
        copy.wait()
    ids = ids_ref[...]
    gates = gates_ref[...].astype(jnp.float32)
    member = jnp.zeros((rows, tokens), jnp.float32)
    gate = jnp.zeros((rows, tokens), jnp.float32)
    for k in range(top):
        hit = ids[k : k + 1, :] == expert
        member = jnp.where(hit, 1.0, member)
        gate = jnp.where(hit, gates[k : k + 1, :], gate)
    before = dot(member.astype(jnp.bfloat16), order, ((1,), (0,)))
    taken = (member > 0) & (before == place.astype(jnp.float32)) & (place < CAP)
    match = taken.astype(jnp.float32)
    match_ref[...] = match
    slot_gate = jnp.sum(match * gate, axis=1, keepdims=True)
    match = match.astype(jnp.bfloat16)

    slots = count * CAP
    saved = saved_ref[...]
    hidden_ref[...] = dot(slot_order(count), saved, ((1,), (0,))).astype(jnp.bfloat16)
    here = lax.broadcasted_iota(jnp.int32, (rows, slots), 0)
    there = lax.broadcasted_iota(jnp.int32, (rows, slots), 1)
    chosen = (here % PAD >= CAP) & (there == target(me, here // PAD, count) * CAP + here % PAD - CAP)
    hidden = dot(chosen.astype(jnp.bfloat16), saved, ((1,), (0,))).astype(jnp.bfloat16)

    copies[3].wait()
    both_ref[...] = dot(match, grad_ref[...], ((1,), (0,)))
    for p in range(pieces):
        copies[4 + p].wait()
        part = slice(p * block, (p + 1) * block)
        both_ref[...] += dot(hidden[:, part], weight_ref[part, :], ((1,), (0,)))
    for r in range(count):
        part = slice(r * PAD, (r + 1) * PAD)
        sends[r][:, :width] = both_ref[part, :].astype(jnp.bfloat16)
        sends[r][:, width:] = jnp.broadcast_to(slot_gate[part], (PAD, LANES)).astype(jnp.bfloat16)


def slot_order(count):
    me = lax.axis_index("expert")
    slots = count * CAP
    here = lax.broadcasted_iota(jnp.int32, (slots, slots), 0)
    saved = lax.broadcasted_iota(jnp.int32, (slots, slots), 1)
    return (saved == source(me, here // CAP, count) * CAP + here % CAP).astype(jnp.bfloat16)


def slot_kernel(count, groups, hidden_ref, *refs):
    sent = refs[:count]
    received = refs[count : 2 * count]
    back_ref, rows_ref, gate_ref = refs[2 * count : 2 * count + 3]
    pays = refs[2 * count + 3 : 2 * count + 3 + groups]
    wide_ref, weighted_ref = refs[2 * count + 3 + groups :]
    width = rows_ref.shape[1]
    for r in range(count):
        mine = sent[r][...].astype(jnp.float32)[:CAP, :width]
        theirs = received[reply(r, count)][...].astype(jnp.float32)[CAP:, :width]
        back = jnp.sum(mine * theirs, axis=1, keepdims=True)
        back_ref[r * CAP : (r + 1) * CAP, :] = jnp.broadcast_to(back, (CAP, LANES))
        wide_ref[r * CAP : (r + 1) * CAP, :] = received[r][...].astype(jnp.float32)[:CAP]
    rows = wide_ref[:, :width]
    gate = wide_ref[:, width:]
    gate_ref[...] = gate
    rows_ref[...] = rows.astype(jnp.bfloat16)
    weighted_ref[...] = (gate[:, :1] * rows).astype(jnp.bfloat16)
    share = width // groups
    me = lax.axis_index("dp")
    for r in range(groups):
        group = target(me, r, groups)
        pays[r][:, :share] = weighted_ref[:, pl.ds(pl.multiple_of(group * share, share), share)]
        pays[r][:, share:] = hidden_ref[...]


def down_term(pay_ref, share, start, block):
    hidden = pay_ref[:, pl.ds(start, block)]
    return dot(hidden, pay_ref[:, :share], ((0,), (0,))).astype(jnp.bfloat16)


def upstream_kernel(count, pieces, rows_ref, gate_ref, weight_ref, pay_ref, hidden_grad_ref, own_ref):
    units = weight_ref.shape[0]
    share = own_ref.shape[1]
    upstream = dot(weight_ref[...], rows_ref[...], ((1,), (1,))).T
    scaled = (gate_ref[:, :1] * upstream).astype(jnp.bfloat16)
    hidden_grad_ref[0, 0] = dot(slot_order(count), scaled, ((0,), (0,))).astype(jnp.bfloat16)
    block = units // pieces
    for p in range(pieces):
        own_ref[p * block : (p + 1) * block, :] = down_term(pay_ref, share, share + p * block, block)


def down_kernel(others, pieces, own_ref, *refs):
    out_hbm, total_ref, sems = refs[others:]
    units, share = own_ref.shape
    block = units // pieces
    copies = []
    for p in range(pieces):
        part = slice(p * block, (p + 1) * block)
        total = own_ref[part, :].astype(jnp.float32)
        for r in range(others):
            total = total + down_term(refs[r], share, share + p * block, block).astype(jnp.float32)
        total_ref[part, :] = total
        part = pl.ds(p * block, block)
        copies.append(pltpu.make_async_copy(total_ref.at[part], out_hbm.at[0, part], sems.at[p]))
        copies[-1].start()
    for copy in copies:
        copy.wait()


def gate_kernel(count, ids_ref, match_ref, back_ref, out_ref):
    me = lax.axis_index("expert")
    ids = ids_ref[...]
    total = jnp.zeros(out_ref.shape, jnp.float32)
    for r in range(count):
        value = back_ref[r * CAP : (r + 1) * CAP, :]
        match = match_ref[r * PAD : r * PAD + CAP, :]
        chosen = jnp.sum(jnp.where(match > 0, value, 0.0), axis=0, keepdims=True)
        total = total + jnp.where(ids == target(me, r, count), chosen, 0.0)
    out_ref[...] = total


def total_over(value, axis):
    size = lax.axis_size(axis)
    if not paired(size):
        return sum([send(value, axis, r) for r in range(1, size)], value)
    step = 1
    while step < size:
        value = value + send(value, axis, step)
        step *= 2
    return value


def on_device(grad_out, expert_ids, gate_values, saved_hidden, down_weight):
    count = lax.axis_size("expert")
    groups = lax.axis_size("dp")
    tokens, width = grad_out.shape
    top = expert_ids.shape[1]
    units = down_weight.shape[1]
    slots = count * CAP
    share = width // groups
    pieces = units // LANES

    payload = jax.ShapeDtypeStruct((PAD, width + LANES), jnp.bfloat16)
    ids, match, weight, hidden, *sends = pl.pallas_call(
        functools.partial(front_kernel, count, pieces),
        out_shape=[
            jax.ShapeDtypeStruct((top, tokens), jnp.int32),
            jax.ShapeDtypeStruct((count * PAD, tokens), jnp.float32),
            jax.ShapeDtypeStruct((units, width), jnp.bfloat16),
            jax.ShapeDtypeStruct((slots, units), jnp.bfloat16),
        ]
        + [payload] * count,
        in_specs=[HBM] * 5,
        out_specs=[VMEM] * (4 + count),
        scratch_shapes=[
            pltpu.VMEM((top, tokens), jnp.bfloat16),
            pltpu.VMEM((tokens, width), jnp.bfloat16),
            pltpu.VMEM((slots, units), jnp.bfloat16),
            pltpu.VMEM((count * PAD, width), jnp.float32),
            pltpu.SemaphoreType.DMA((4 + pieces,)),
        ],
        compiler_params=PARAMS,
        cost_estimate=cost(2 * count * PAD * (tokens + units) * width, 2 * (tokens + units) * width),
        name="front",
    )(*in_hbm(expert_ids.T, gate_values.T, grad_out, saved_hidden, down_weight))

    received = [sends[0]] + [send(sends[r], "expert", r) for r in range(1, count)]

    back, rows, gate, *pays = pl.pallas_call(
        functools.partial(slot_kernel, count, groups),
        out_shape=[
            jax.ShapeDtypeStruct((slots, LANES), jnp.float32),
            jax.ShapeDtypeStruct((slots, width), jnp.bfloat16),
            jax.ShapeDtypeStruct((slots, LANES), jnp.float32),
        ]
        + [jax.ShapeDtypeStruct((slots, share + units), jnp.bfloat16)] * groups,
        in_specs=[VMEM] * (1 + 2 * count),
        out_specs=[VMEM] * (3 + groups),
        scratch_shapes=[
            pltpu.VMEM((slots, width + LANES), jnp.float32),
            pltpu.VMEM((slots, width), jnp.bfloat16),
        ],
        compiler_params=PARAMS,
        cost_estimate=cost(4 * slots * width, 16 * slots * width),
        name="slots",
    )(hidden, *sends, *received)

    others = [send(pays[r], "dp", r) for r in range(1, groups)]
    back = total_over(back, "tensor")

    hidden_grad, own = pl.pallas_call(
        functools.partial(upstream_kernel, count, pieces),
        out_shape=[
            jax.ShapeDtypeStruct(saved_hidden.shape, jnp.bfloat16),
            jax.ShapeDtypeStruct((units, share), jnp.bfloat16),
        ],
        in_specs=[VMEM] * 4,
        out_specs=[VMEM] * 2,
        compiler_params=PARAMS,
        cost_estimate=cost(2 * slots * units * (width + share), 2 * units * width),
        name="upstream",
    )(rows, gate, weight, pays[0])

    down_grad = pl.pallas_call(
        functools.partial(down_kernel, groups - 1, pieces),
        out_shape=jax.ShapeDtypeStruct((1, units, share), jnp.float32),
        in_specs=[VMEM] * groups,
        out_specs=HBM,
        scratch_shapes=[
            pltpu.VMEM((units, share), jnp.float32),
            pltpu.SemaphoreType.DMA((pieces,)),
        ],
        compiler_params=PARAMS,
        cost_estimate=cost(2 * slots * units * share, 4 * units * share),
        name="down",
    )(own, *others)

    gate_grad = pl.pallas_call(
        functools.partial(gate_kernel, count),
        out_shape=jax.ShapeDtypeStruct(ids.shape, jnp.float32),
        in_specs=[VMEM] * 3,
        out_specs=VMEM,
        compiler_params=PARAMS,
        cost_estimate=cost(slots * tokens, 4 * slots * tokens),
        name="gates",
    )(ids, match, back)
    return (gate_grad.T, hidden_grad, down_grad)


def solution(mesh):
    return jax.shard_map(
        on_device,
        mesh=mesh,
        in_specs=(
            P(("dp", "expert"), None),
            P(("dp", "expert"), None),
            P(("dp", "expert"), None),
            P("dp", "expert", None, "tensor"),
            P("expert", "tensor", None),
        ),
        out_specs=(
            P(("dp", "expert"), None),
            P("dp", "expert", None, "tensor"),
            P("expert", "tensor", "dp"),
        ),
        check_vma=False,
    )
```

time: 28 us -> 24.7 us (0.88)
  starting transfers between devices: 13.5 us -> 8.74 us
  waiting for transfers between devices: 4.49 us -> 7.36 us
  Pallas kernels: 9.02 us -> 7.7 us
    ppermute x10 -> x6, starting transfers between devices: 13.5 us -> 8.74 us  [send(): lax.ppermute(value, axis, [(i, give(i, step, size)) for i in range(size)])]
    ppermute x10 -> x6, waiting for transfers between devices: 4.49 us -> 7.36 us  [send(): lax.ppermute(value, axis, [(i, give(i, step, size)) for i in range(size)])]
    pallas_call x4 -> x3, Pallas kernels: 6.94 us -> 5.18 us  [the longest x1 2.56 us: on_device(): pl.pallas_call(functools.partial(front_kernel, count, pieces), out_shape=...]
    pallas_call x1, Pallas kernels: 1.93 us -> 2.31 us  [on_device(): pl.pallas_call(functools.partial(upstream_kernel, count, pieces), out_sha...]
  transfers between devices with their start and end apart: 10 -> 6, of which waited for: 4 -> 3; matrix products, arithmetic and copies ran while one was open for 0% -> 0% of each run, Pallas kernels for 17% -> 12%
where the time goes in v3:
time: 24.7 us; the launch traced here: 24.5 us
  starting transfers between devices  8.74 us (35%)
  Pallas kernels  7.7 us (31%)
  waiting for transfers between devices  7.36 us (30%)
  between operations  0.67 us (3%)
    ppermute x6, starting transfers between devices, send(): lax.ppermute(value, axis, [(i, give(i, step, size)) for i in range(size)])  8.74 us
    ppermute x6, waiting for transfers between devices, send(): lax.ppermute(value, axis, [(i, give(i, step, size)) for i in range(size)])  7.36 us
    pallas_call x1, Pallas kernels, on_device(): pl.pallas_call(functools.partial(front_kernel, count, pieces), out_shape=...  2.56 us
    pallas_call x1, Pallas kernels, on_device(): pl.pallas_call(functools.partial(upstream_kernel, count, pieces), out_sha...  2.31 us
    pallas_call x1, Pallas kernels, on_device(): pl.pallas_call(functools.partial(down_kernel, groups - 1, pieces), out_sh...  2.01 us
    pallas_call x1, Pallas kernels, on_device(): pl.pallas_call(functools.partial(gate_kernel, count), out_shape=jax.Shape...  0.61 us
  transfers between devices with their start and end apart: 6, of which 3 were waited for; matrix products, arithmetic and copies ran while one was open for 0% of the time, Pallas kernels for 12%

profile of v3, /device:TPU:0, one launch (start us, length us, event | category | flops | bytes accessed | tf_op | source)
XLA Modules:
  0.0 24.5 jit_solution(12109862119217458727)
XLA Ops:
  0.6 2.6 %front.1 = (s32[8,128]{1,0:T(8,128)S(1)}, f32[32,128]{1,0:T(8,128)S(1)}, bf16[384,4096]{1,0:T(8,128)(2,1)S(1)}, bf16[16,384]{1,0:T(8,128)(2,1)S(1)}, bf16[8,4224...) custom-call(s32[8,128]{1,0:T(8,128)} %bitcast.4, ...), custom_call_target="tpu_custom_call" | custom-call | flops 134217728 | bytes 4194304 | tf_op jit(solution)/shard_map/front/pallas_call | solution.py:219
  3.2 3.1 %collective-permute-start = (bf16[8,4224]{1,0:T(8,128)(2,1)S(1)}, bf16[8,4224]{1,0:T(8,128)(2,1)S(1)}, u32[]{:S(2)}, u32[]{:S(2)}) collective-permute-start(bf16[8,4224]{1,0:T(8,128)(2,1)S(1)} %get-tuple-element.22.refs_1_), channel_id=1, source_target_pairs={{0,4},{4,0},{8,12},{12,8},{1,5},{5,1},{9,13},{13,9},{2,6},{6,2},{1... | collective-permute-start | bytes 202760 | tf_op jit(solution)/shard_map/ppermute | solution.py:54
  6.3 2.6 %collective-permute-start.1 = (bf16[8,4224]{1,0:T(8,128)(2,1)S(1)}, bf16[8,4224]{1,0:T(8,128)(2,1)S(1)}, u32[]{:S(2)}, u32[]{:S(2)}) collective-permute-start(bf16[8,4224]{1,0:T(8,128)(2,1)S(1)} %get-tuple-element.23.refs_2_), channel_id=1, source_target_pairs={{0,8},{4,12},{8,0},{12,4},{1,9},{5,13},{9,1},{13,5},{2,10},{6,14},... | collective-permute-start | bytes 202760 | tf_op jit(solution)/shard_map/ppermute | solution.py:54
  8.9 0.0 collective-permute-start.2
  8.9 0.0 collective-permute-done.refs_5_
  8.9 4.8 %collective-permute-done.1.refs_6_ = bf16[8,4224]{1,0:T(8,128)(2,1)S(1)} collective-permute-done((bf16[8,4224]{1,0:T(8,128)(2,1)S(1)}, bf16[8,4224]{1,0:T(8,128)(2,1)S(1)}, u32[]{:S(2)}, u32[]{:S(2)}) %collective-permute-start.1) | collective-permute-done | bytes 67616 | tf_op jit(solution)/shard_map/ppermute | solution.py:54
  13.7 1.4 %collective-permute-done.2.refs_7_ = bf16[8,4224]{1,0:T(8,128)(2,1)S(1)} collective-permute-done((bf16[8,4224]{1,0:T(8,128)(2,1)S(1)}, bf16[8,4224]{1,0:T(8,128)(2,1)S(1)}, u32[]{:S(2)}, u32[]{:S(2)}) %collective-permute-start.2) | collective-permute-done | bytes 67616 | tf_op jit(solution)/shard_map/ppermute | solution.py:54
  15.1 0.2 slots.1
  15.3 1.5 %collective-permute-start.5 = (bf16[16,2432]{1,0:T(8,128)(2,1)S(1)}, bf16[16,2432]{1,0:T(8,128)(2,1)S(1)}, u32[]{:S(2)}, u32[]{:S(2)}) collective-permute-start(bf16[16,2432]{1,0:T(8,128)(2,1)S(1)} %get-tuple-element.32), channel_id=1, source_target_pairs={{0,16},{16,0},{1,17},{17,1},{2,18},{18,2},{3,19},{19,3},{4,20},{20... | collective-permute-start | bytes 233480 | tf_op jit(solution)/shard_map/ppermute | solution.py:54
  16.8 0.0 collective-permute-start.3
  16.8 1.2 %collective-permute-done.3 = f32[16,128]{1,0:T(8,128)S(1)} collective-permute-done((f32[16,128]{1,0:T(8,128)S(1)}, f32[16,128]{1,0:T(8,128)S(1)}, u32[]{:S(2)}, u32[]{:S(2)}) %collective-permute-start.3) | collective-permute-done | bytes 8224 | tf_op jit(solution)/shard_map/ppermute | solution.py:54
  18.0 1.5 %collective-permute-start.4 = (f32[16,128]{1,0:T(8,128)S(1)}, f32[16,128]{1,0:T(8,128)S(1)}, u32[]{:S(2)}, u32[]{:S(2)}) collective-permute-start(f32[16,128]{1,0:T(8,128)S(1)} %add.6), channel_id=1, source_target_pairs={{0,2},{1,3},{2,0},{3,1},{4,6},{5,7},{6,4},{7,5},{8,10},{9,11},{10,... | collective-permute-start | bytes 24584 | tf_op jit(solution)/shard_map/ppermute | solution.py:54
  19.5 2.3 %upstream.1 = (bf16[1,1,16,384]{3,2,1,0:T(8,128)(2,1)}, bf16[384,2048]{1,0:T(8,128)(2,1)S(1)}) custom-call(bf16[16,4096]{1,0:T(8,128)(2,1)S(1)} %get-tuple-element.26.rows_ref, f32[16,128]{1,0:T(8,128)S(1)} %get-tuple-element.27.gate_ref, bf16[384,4096]{1,0:T(8,128)(2,1)S(1)} %get-tuple-element.28.weight_ref, bf16[16,2432]{1,0:T(8,128)(2,1)S(1)} %get-tuple-element.29.pay_ref), custom_call_target="tpu_custom_call" | custom-call | flops 75497472 | bytes 3145728 | tf_op jit(solution)/shard_map/upstream/pallas_call | solution.py:266
  21.8 0.0 collective-permute-done.4
  21.9 0.6 %gates.1 = f32[8,128]{1,0:T(8,128)} custom-call(s32[8,128]{1,0:T(8,128)S(1)} %get-tuple-element.18.ids_ref, f32[32,128]{1,0:T(8,128)S(1)} %get-tuple-element.19.match_ref, f32[16,128]{1,0:T(8,128)S(1)} %add.7.back_ref), custom_call_target="tpu_custom_call" | custom-call | flops 2048 | bytes 8192 | tf_op jit(solution)/shard_map/gates/pallas_call | solution.py:293
  22.5 0.0 collective-permute-done.5.refs_0_
  22.5 2.0 %down.1 = f32[1,384,2048]{2,1,0:T(8,128)} custom-call(bf16[384,2048]{1,0:T(8,128)(2,1)S(1)} %get-tuple-element.31.own_ref, bf16[16,2432]{1,0:T(8,128)(2,1)S(1)} %collective-permute-done.5.refs_0_), custom_call_target="tpu_custom_call" | custom-call | flops 25165824 | bytes 3145728 | tf_op jit(solution)/shard_map/down/pallas_call | solution.py:279
  (2 shorter events, 0.0 us)
Async XLA Ops:
  3.2 5.7 %collective-permute-start = (bf16[8,4224]{1,0:T(8,128)(2,1)S(1)}, bf16[8,4224]{1,0:T(8,128)(2,1)S(1)}, u32[]{:S(2)}, u32[]{:S(2)}) collective-permute-start(bf16[8,4224]{1,0:T(8,128)(2,1)S(1)} %get-tuple-element.22.refs_1_), channel_id=1, source_target_pairs={{0,4},{4,0},{8,12},{12,8},{1,5},{5,1},{9,13},{13,9},{2,6},{6,2},{1... | collective-permute-start | bytes 202760 | tf_op jit(solution)/shard_map/ppermute | solution.py:54
  6.3 7.4 %collective-permute-start.1 = (bf16[8,4224]{1,0:T(8,128)(2,1)S(1)}, bf16[8,4224]{1,0:T(8,128)(2,1)S(1)}, u32[]{:S(2)}, u32[]{:S(2)}) collective-permute-start(bf16[8,4224]{1,0:T(8,128)(2,1)S(1)} %get-tuple-element.23.refs_2_), channel_id=1, source_target_pairs={{0,8},{4,12},{8,0},{12,4},{1,9},{5,13},{9,1},{13,5},{2,10},{6,14},... | collective-permute-start | bytes 202760 | tf_op jit(solution)/shard_map/ppermute | solution.py:54
  8.9 6.2 %collective-permute-start.2 = (bf16[8,4224]{1,0:T(8,128)(2,1)S(1)}, bf16[8,4224]{1,0:T(8,128)(2,1)S(1)}, u32[]{:S(2)}, u32[]{:S(2)}) collective-permute-start(bf16[8,4224]{1,0:T(8,128)(2,1)S(1)} %get-tuple-element.24.refs_3_), channel_id=1, source_target_pairs={{0,12},{4,8},{8,4},{12,0},{1,13},{5,9},{9,5},{13,1},{2,14},{6,10},... | collective-permute-start | bytes 202760 | tf_op jit(solution)/shard_map/ppermute | solution.py:54
  15.3 7.2 %collective-permute-start.5 = (bf16[16,2432]{1,0:T(8,128)(2,1)S(1)}, bf16[16,2432]{1,0:T(8,128)(2,1)S(1)}, u32[]{:S(2)}, u32[]{:S(2)}) collective-permute-start(bf16[16,2432]{1,0:T(8,128)(2,1)S(1)} %get-tuple-element.32), channel_id=1, source_target_pairs={{0,16},{16,0},{1,17},{17,1},{2,18},{18,2},{3,19},{19,3},{4,20},{20... | collective-permute-start | bytes 233480 | tf_op jit(solution)/shard_map/ppermute | solution.py:54
  16.8 1.2 %collective-permute-start.3 = (f32[16,128]{1,0:T(8,128)S(1)}, f32[16,128]{1,0:T(8,128)S(1)}, u32[]{:S(2)}, u32[]{:S(2)}) collective-permute-start(f32[16,128]{1,0:T(8,128)S(1)} %get-tuple-element.25), channel_id=1, source_target_pairs={{0,1},{1,0},{2,3},{3,2},{4,5},{5,4},{6,7},{7,6},{8,9},{9,8},{10,11... | collective-permute-start | bytes 24584 | tf_op jit(solution)/shard_map/ppermute | solution.py:54
  18.0 3.8 %collective-permute-start.4 = (f32[16,128]{1,0:T(8,128)S(1)}, f32[16,128]{1,0:T(8,128)S(1)}, u32[]{:S(2)}, u32[]{:S(2)}) collective-permute-start(f32[16,128]{1,0:T(8,128)S(1)} %add.6), channel_id=1, source_target_pairs={{0,2},{1,3},{2,0},{3,1},{4,6},{5,7},{6,4},{7,5},{8,10},{9,11},{10,... | collective-permute-start | bytes 24584 | tf_op jit(solution)/shard_map/ppermute | solution.py:54

commit v4 on v3

--- a/solution.py
+++ b/solution.py
@@ -58,14 +58,15 @@
     ids_hbm, gates_hbm, grad_hbm, hidden_hbm, weight_hbm = refs[:5]
     ids_ref, match_ref, weight_ref, hidden_ref = refs[5:9]
     sends = refs[9 : 9 + count]
-    gates_ref, grad_ref, saved_ref, both_ref, sems = refs[9 + count :]
+    gates_ref, grad_ref, saved_ref, sems = refs[9 + count :]
     units, width = weight_ref.shape
-    block = units // pieces
+    block = width // pieces
     top, tokens = ids_ref.shape
-    pairs = [(ids_hbm, ids_ref), (gates_hbm, gates_ref), (hidden_hbm.at[0, 0], saved_ref), (grad_hbm, grad_ref)]
+    pairs = [(ids_hbm, ids_ref), (gates_hbm, gates_ref), (hidden_hbm.at[0, 0], saved_ref)]
     for p in range(pieces):
         part = pl.ds(p * block, block)
-        pairs.append((weight_hbm.at[0, part], weight_ref.at[part]))
+        pairs.append((grad_hbm.at[:, part], grad_ref.at[:, part]))
+        pairs.append((weight_hbm.at[0, :, part], weight_ref.at[:, part]))
     copies = [pltpu.make_async_copy(*pair, sems.at[n]) for n, pair in enumerate(pairs)]
     for copy in copies:
         copy.start()
@@ -102,16 +103,17 @@
     chosen = (here % PAD >= CAP) & (there == target(me, here // PAD, count) * CAP + here % PAD - CAP)
     hidden = dot(chosen.astype(jnp.bfloat16), saved, ((1,), (0,))).astype(jnp.bfloat16)
 
-    copies[3].wait()
-    both_ref[...] = dot(match, grad_ref[...], ((1,), (0,)))
-    for p in range(pieces):
-        copies[4 + p].wait()
-        part = slice(p * block, (p + 1) * block)
-        both_ref[...] += dot(hidden[:, part], weight_ref[part, :], ((1,), (0,)))
     for r in range(count):
         part = slice(r * PAD, (r + 1) * PAD)
-        sends[r][:, :width] = both_ref[part, :].astype(jnp.bfloat16)
         sends[r][:, width:] = jnp.broadcast_to(slot_gate[part], (PAD, LANES)).astype(jnp.bfloat16)
+    for p in range(pieces):
+        part = slice(p * block, (p + 1) * block)
+        copies[3 + 2 * p].wait()
+        both = dot(match, grad_ref[:, part], ((1,), (0,)))
+        copies[4 + 2 * p].wait()
+        both = both + dot(hidden, weight_ref[:, part], ((1,), (0,)))
+        for r in range(count):
+            sends[r][:, part] = both[r * PAD : (r + 1) * PAD].astype(jnp.bfloat16)
 
 
 def slot_order(count):
@@ -153,71 +155,73 @@
     return dot(hidden, pay_ref[:, :share], ((0,), (0,))).astype(jnp.bfloat16)
 
 
-def upstream_kernel(count, pieces, rows_ref, gate_ref, weight_ref, pay_ref, hidden_grad_ref, own_ref):
-    units = weight_ref.shape[0]
-    share = own_ref.shape[1]
-    upstream = dot(weight_ref[...], rows_ref[...], ((1,), (1,))).T
-    scaled = (gate_ref[:, :1] * upstream).astype(jnp.bfloat16)
-    hidden_grad_ref[0, 0] = dot(slot_order(count), scaled, ((0,), (0,))).astype(jnp.bfloat16)
+def own_kernel(pieces, pay_ref, own_ref):
+    units, share = own_ref.shape
     block = units // pieces
     for p in range(pieces):
         own_ref[p * block : (p + 1) * block, :] = down_term(pay_ref, share, share + p * block, block)
 
 
-def down_kernel(others, pieces, own_ref, *refs):
-    out_hbm, total_ref, sems = refs[others:]
+def last_kernel(count, others, parts, pieces, *refs):
+    own_ref = refs[0]
+    pays = refs[1 : 1 + others]
+    backs = refs[1 + others : 1 + others + parts]
+    ids_ref, match_ref, rows_ref, gate_ref, weight_ref = refs[1 + others + parts : 6 + others + parts]
+    gate_hbm, hidden_hbm, down_hbm, gate_out, hidden_out, down_out, sems = refs[6 + others + parts :]
     units, share = own_ref.shape
     block = units // pieces
     copies = []
+
+    def write(n, values, destination):
+        copies.append(pltpu.make_async_copy(values, destination, sems.at[n]))
+        copies[-1].start()
+
     for p in range(pieces):
         part = slice(p * block, (p + 1) * block)
         total = own_ref[part, :].astype(jnp.float32)
-        for r in range(others):
-            total = total + down_term(refs[r], share, share + p * block, block).astype(jnp.float32)
-        total_ref[part, :] = total
+        for pay_ref in pays:
+            total = total + down_term(pay_ref, share, share + p * block, block).astype(jnp.float32)
+        down_out[part, :] = total
         part = pl.ds(p * block, block)
-        copies.append(pltpu.make_async_copy(total_ref.at[part], out_hbm.at[0, part], sems.at[p]))
-        copies[-1].start()
-    for copy in copies:
-        copy.wait()
-
-
-def gate_kernel(count, ids_ref, match_ref, back_ref, out_ref):
+        write(p, down_out.at[part], down_hbm.at[0, part])
+
     me = lax.axis_index("expert")
     ids = ids_ref[...]
-    total = jnp.zeros(out_ref.shape, jnp.float32)
+    back = backs[0][...]
+    for ref in backs[1:]:
+        back = back + ref[...]
+    total = jnp.zeros(gate_out.shape, jnp.float32)
     for r in range(count):
-        value = back_ref[r * CAP : (r + 1) * CAP, :]
+        value = back[r * CAP : (r + 1) * CAP, :]
         match = match_ref[r * PAD : r * PAD + CAP, :]
         chosen = jnp.sum(jnp.where(match > 0, value, 0.0), axis=0, keepdims=True)
         total = total + jnp.where(ids == target(me, r, count), chosen, 0.0)
-    out_ref[...] = total
-
-
-def total_over(value, axis):
-    size = lax.axis_size(axis)
-    if not paired(size):
-        return sum([send(value, axis, r) for r in range(1, size)], value)
-    step = 1
-    while step < size:
-        value = value + send(value, axis, step)
-        step *= 2
-    return value
+    gate_out[...] = total
+    write(pieces, gate_out, gate_hbm)
+
+    upstream = dot(rows_ref[...], weight_ref[...], ((1,), (1,)))
+    scaled = (gate_ref[:, :1] * upstream).astype(jnp.bfloat16)
+    hidden_out[...] = dot(slot_order(count), scaled, ((0,), (0,))).astype(jnp.bfloat16)
+    write(pieces + 1, hidden_out, hidden_hbm.at[0, 0])
+    for copy in copies:
+        copy.wait()
 
 
 def on_device(grad_out, expert_ids, gate_values, saved_hidden, down_weight):
     count = lax.axis_size("expert")
     groups = lax.axis_size("dp")
+    tensors = lax.axis_size("tensor")
     tokens, width = grad_out.shape
     top = expert_ids.shape[1]
     units = down_weight.shape[1]
     slots = count * CAP
     share = width // groups
     pieces = units // LANES
+    columns = width // 512
 
     payload = jax.ShapeDtypeStruct((PAD, width + LANES), jnp.bfloat16)
     ids, match, weight, hidden, *sends = pl.pallas_call(
-        functools.partial(front_kernel, count, pieces),
+        functools.partial(front_kernel, count, columns),
         out_shape=[
             jax.ShapeDtypeStruct((top, tokens), jnp.int32),
             jax.ShapeDtypeStruct((count * PAD, tokens), jnp.float32),
@@ -231,15 +235,14 @@
             pltpu.VMEM((top, tokens), jnp.bfloat16),
             pltpu.VMEM((tokens, width), jnp.bfloat16),
             pltpu.VMEM((slots, units), jnp.bfloat16),
-            pltpu.VMEM((count * PAD, width), jnp.float32),
-            pltpu.SemaphoreType.DMA((4 + pieces,)),
+            pltpu.SemaphoreType.DMA((3 + 2 * columns,)),
         ],
         compiler_params=PARAMS,
         cost_estimate=cost(2 * count * PAD * (tokens + units) * width, 2 * (tokens + units) * width),
         name="front",
     )(*in_hbm(expert_ids.T, gate_values.T, grad_out, saved_hidden, down_weight))
 
-    received = [sends[0]] + [send(sends[r], "expert", r) for r in range(1, count)]
+    received = [sends[0]] + [send(sends[r], "expert", r) for r in reversed(range(1, count))][::-1]
 
     back, rows, gate, *pays = pl.pallas_call(
         functools.partial(slot_kernel, count, groups),
@@ -261,44 +264,37 @@
     )(hidden, *sends, *received)
 
     others = [send(pays[r], "dp", r) for r in range(1, groups)]
-    back = total_over(back, "tensor")
-
-    hidden_grad, own = pl.pallas_call(
-        functools.partial(upstream_kernel, count, pieces),
+    backs = [back] + [send(back, "tensor", r) for r in range(1, tensors)]
+
+    own = pl.pallas_call(
+        functools.partial(own_kernel, pieces),
+        out_shape=jax.ShapeDtypeStruct((units, share), jnp.bfloat16),
+        in_specs=[VMEM],
+        out_specs=VMEM,
+        compiler_params=PARAMS,
+        cost_estimate=cost(2 * slots * units * share, 2 * units * share),
+        name="own",
+    )(pays[0])
+
+    gate_grad, hidden_grad, down_grad = pl.pallas_call(
+        functools.partial(last_kernel, count, groups - 1, tensors, pieces),
         out_shape=[
+            jax.ShapeDtypeStruct(ids.shape, jnp.float32),
             jax.ShapeDtypeStruct(saved_hidden.shape, jnp.bfloat16),
-            jax.ShapeDtypeStruct((units, share), jnp.bfloat16),
+            jax.ShapeDtypeStruct((1, units, share), jnp.float32),
         ],
-        in_specs=[VMEM] * 4,
-        out_specs=[VMEM] * 2,
-        compiler_params=PARAMS,
-        cost_estimate=cost(2 * slots * units * (width + share), 2 * units * width),
-        name="upstream",
-    )(rows, gate, weight, pays[0])
-
-    down_grad = pl.pallas_call(
-        functools.partial(down_kernel, groups - 1, pieces),
-        out_shape=jax.ShapeDtypeStruct((1, units, share), jnp.float32),
-        in_specs=[VMEM] * groups,
-        out_specs=HBM,
+        in_specs=[VMEM] * (5 + groups + tensors),
+        out_specs=[HBM] * 3,
         scratch_shapes=[
+            pltpu.VMEM(ids.shape, jnp.float32),
+            pltpu.VMEM((slots, units), jnp.bfloat16),
             pltpu.VMEM((units, share), jnp.float32),
-            pltpu.SemaphoreType.DMA((pieces,)),
+            pltpu.SemaphoreType.DMA((pieces + 2,)),
         ],
         compiler_params=PARAMS,
-        cost_estimate=cost(2 * slots * units * share, 4 * units * share),
-        name="down",
-    )(own, *others)
-
-    gate_grad = pl.pallas_call(
-        functools.partial(gate_kernel, count),
-        out_shape=jax.ShapeDtypeStruct(ids.shape, jnp.float32),
-        in_specs=[VMEM] * 3,
-        out_specs=VMEM,
-        compiler_params=PARAMS,
-        cost_estimate=cost(slots * tokens, 4 * slots * tokens),
-        name="gates",
-    )(ids, match, back)
+        cost_estimate=cost(2 * slots * units * (width + share), 4 * units * share),
+        name="last",
+    )(own, *others, *backs, ids, match, rows, gate, weight)
     return (gate_grad.T, hidden_grad, down_grad)
 
 

time: 24.7 us -> 23.4 us (0.947)
  Pallas kernels: 7.7 us -> 6.04 us
  starting transfers between devices: 8.74 us -> 9.08 us
    pallas_call x4 -> x3, Pallas kernels: 7.49 us -> 5.83 us  [the longest x1 3.01 us: on_device(): pl.pallas_call(functools.partial(front_kernel, count, columns), out_shape...]
    ppermute x6 -> x7, starting transfers between devices: 8.74 us -> 9.08 us  [send(): lax.ppermute(value, axis, [(i, give(i, step, size)) for i in range(size)])]
    ppermute x6 -> x7, waiting for transfers between devices: 7.36 us -> 7.42 us  [send(): lax.ppermute(value, axis, [(i, give(i, step, size)) for i in range(size)])]
  transfers between devices with their start and end apart: 6 -> 7, of which waited for: 3 -> 4; matrix products, arithmetic and copies ran while one was open for 0% -> 0% of each run, Pallas kernels for 12% -> 3%
where the time goes in v4:
time: 23.4 us; the launch traced here: 23.2 us
  starting transfers between devices  9.08 us (39%)
  waiting for transfers between devices  7.42 us (32%)
  Pallas kernels  6.04 us (26%)
  between operations  0.65 us (3%)
    ppermute x7, starting transfers between devices, send(): lax.ppermute(value, axis, [(i, give(i, step, size)) for i in range(size)])  9.08 us
    ppermute x7, waiting for transfers between devices, send(): lax.ppermute(value, axis, [(i, give(i, step, size)) for i in range(size)])  7.42 us
    pallas_call x1, Pallas kernels, on_device(): pl.pallas_call(functools.partial(front_kernel, count, columns), out_shape...  3.01 us
    pallas_call x1, Pallas kernels, on_device(): pl.pallas_call(functools.partial(last_kernel, count, groups - 1, tensors,...  2.23 us
    pallas_call x1, Pallas kernels, on_device(): pl.pallas_call(functools.partial(own_kernel, pieces), out_shape=jax.Shape...  0.59 us
  transfers between devices with their start and end apart: 7, of which 4 were waited for; matrix products, arithmetic and copies ran while one was open for 0% of the time, Pallas kernels for 3%

profile of v4, /device:TPU:0, one launch (start us, length us, event | category | flops | bytes accessed | tf_op | source)
XLA Modules:
  0.0 23.2 jit_solution(9140857627997480979)
XLA Ops:
  0.6 3.0 %front.1 = (s32[8,128]{1,0:T(8,128)S(1)}, f32[32,128]{1,0:T(8,128)S(1)}, bf16[384,4096]{1,0:T(8,128)(2,1)S(1)}, bf16[16,384]{1,0:T(8,128)(2,1)S(1)}, bf16[8,4224...) custom-call(s32[8,128]{1,0:T(8,128)} %bitcast.3, ...), custom_call_target="tpu_custom_call" | custom-call | flops 134217728 | bytes 4194304 | tf_op jit(solution)/shard_map/front/pallas_call | solution.py:223
  3.7 3.1 %collective-permute-start = (bf16[8,4224]{1,0:T(8,128)(2,1)S(1)}, bf16[8,4224]{1,0:T(8,128)(2,1)S(1)}, u32[]{:S(2)}, u32[]{:S(2)}) collective-permute-start(bf16[8,4224]{1,0:T(8,128)(2,1)S(1)} %get-tuple-element.21.refs_1_), channel_id=1, source_target_pairs={{0,4},{4,0},{8,12},{12,8},{1,5},{5,1},{9,13},{13,9},{2,6},{6,2},{1... | collective-permute-start | bytes 202760 | tf_op jit(solution)/shard_map/ppermute | solution.py:54
  6.7 2.6 %collective-permute-start.1 = (bf16[8,4224]{1,0:T(8,128)(2,1)S(1)}, bf16[8,4224]{1,0:T(8,128)(2,1)S(1)}, u32[]{:S(2)}, u32[]{:S(2)}) collective-permute-start(bf16[8,4224]{1,0:T(8,128)(2,1)S(1)} %get-tuple-element.22.refs_2_), channel_id=1, source_target_pairs={{0,8},{4,12},{8,0},{12,4},{1,9},{5,13},{9,1},{13,5},{2,10},{6,14},... | collective-permute-start | bytes 202760 | tf_op jit(solution)/shard_map/ppermute | solution.py:54
  9.3 0.0 collective-permute-start.2
  9.3 0.0 collective-permute-done.refs_5_
  9.3 4.8 %collective-permute-done.1.refs_6_ = bf16[8,4224]{1,0:T(8,128)(2,1)S(1)} collective-permute-done((bf16[8,4224]{1,0:T(8,128)(2,1)S(1)}, bf16[8,4224]{1,0:T(8,128)(2,1)S(1)}, u32[]{:S(2)}, u32[]{:S(2)}) %collective-permute-start.1) | collective-permute-done | bytes 67616 | tf_op jit(solution)/shard_map/ppermute | solution.py:54
  14.1 1.4 %collective-permute-done.2.refs_7_ = bf16[8,4224]{1,0:T(8,128)(2,1)S(1)} collective-permute-done((bf16[8,4224]{1,0:T(8,128)(2,1)S(1)}, bf16[8,4224]{1,0:T(8,128)(2,1)S(1)}, u32[]{:S(2)}, u32[]{:S(2)}) %collective-permute-start.2) | collective-permute-done | bytes 67616 | tf_op jit(solution)/shard_map/ppermute | solution.py:54
  15.5 0.2 slots.1
  15.7 1.5 %collective-permute-start.3 = (bf16[16,2432]{1,0:T(8,128)(2,1)S(1)}, bf16[16,2432]{1,0:T(8,128)(2,1)S(1)}, u32[]{:S(2)}, u32[]{:S(2)}) collective-permute-start(bf16[16,2432]{1,0:T(8,128)(2,1)S(1)} %get-tuple-element.25), channel_id=1, source_target_pairs={{0,16},{16,0},{1,17},{17,1},{2,18},{18,2},{3,19},{19,3},{4,20},{20... | collective-permute-start | bytes 233480 | tf_op jit(solution)/shard_map/ppermute | solution.py:54
  17.3 0.0 collective-permute-start.6
  17.3 1.5 %collective-permute-start.5 = (f32[16,128]{1,0:T(8,128)S(1)}, f32[16,128]{1,0:T(8,128)S(1)}, u32[]{:S(2)}, u32[]{:S(2)}) collective-permute-start(f32[16,128]{1,0:T(8,128)S(1)} %get-tuple-element.26.refs_2_), channel_id=1, source_target_pairs={{0,2},{1,3},{2,0},{3,1},{4,6},{5,7},{6,4},{7,5},{8,10},{9,11},{10,... | collective-permute-start | bytes 24584 | tf_op jit(solution)/shard_map/ppermute | solution.py:54
  18.8 0.3 %collective-permute-start.4 = (f32[16,128]{1,0:T(8,128)S(1)}, f32[16,128]{1,0:T(8,128)S(1)}, u32[]{:S(2)}, u32[]{:S(2)}) collective-permute-start(f32[16,128]{1,0:T(8,128)S(1)} %get-tuple-element.26.refs_2_), channel_id=1, source_target_pairs={{0,1},{1,0},{2,3},{3,2},{4,5},{5,4},{6,7},{7,6},{8,9},{9,8},{10,11... | collective-permute-start | bytes 24584 | tf_op jit(solution)/shard_map/ppermute | solution.py:54
  19.1 0.6 %own.1.refs_0_ = bf16[384,2048]{1,0:T(8,128)(2,1)S(1)} custom-call(bf16[16,2432]{1,0:T(8,128)(2,1)S(1)} %get-tuple-element.24.pay_ref), custom_call_target="tpu_custom_call" | custom-call | flops 25165824 | bytes 1572864 | tf_op jit(solution)/shard_map/own/pallas_call | solution.py:269
  19.7 0.6 %collective-permute-done.6.refs_5_ = f32[16,128]{1,0:T(8,128)S(1)} collective-permute-done((f32[16,128]{1,0:T(8,128)S(1)}, f32[16,128]{1,0:T(8,128)S(1)}, u32[]{:S(2)}, u32[]{:S(2)}) %collective-permute-start.6) | collective-permute-done | bytes 8224 | tf_op jit(solution)/shard_map/ppermute | solution.py:54
  20.4 0.6 %collective-permute-done.5.refs_4_ = f32[16,128]{1,0:T(8,128)S(1)} collective-permute-done((f32[16,128]{1,0:T(8,128)S(1)}, f32[16,128]{1,0:T(8,128)S(1)}, u32[]{:S(2)}, u32[]{:S(2)}) %collective-permute-start.5) | collective-permute-done | bytes 8224 | tf_op jit(solution)/shard_map/ppermute | solution.py:54
  21.0 0.0 collective-permute-done.4.refs_3_
  21.0 0.0 collective-permute-done.3.refs_1_
  21.0 2.2 %last.1 = (f32[8,128]{1,0:T(8,128)}, bf16[1,1,16,384]{3,2,1,0:T(8,128)(2,1)}, f32[1,384,2048]{2,1,0:T(8,128)}) custom-call(bf16[384,2048]{1,0:T(8,128)(2,1)S(1)} %own.1.refs_0_, bf16[16,2432]{1,0:T(8,128)(2,1)S(1)} %collective-permute-done.3.refs_1_, f32[16,128]{1,0:T(8,128)S(1)} %get-tuple-element.26.refs_2_, f32[16,128]{1,0:T(8,128)S(1)} %collective-permute-done.4.refs_3_, ...), custom_call_target="tpu_custom_call" | custom-call | flops 75497472 | bytes 3145728 | tf_op jit(solution)/shard_map/last/pallas_call | solution.py:279
Async XLA Ops:
  3.7 5.7 %collective-permute-start = (bf16[8,4224]{1,0:T(8,128)(2,1)S(1)}, bf16[8,4224]{1,0:T(8,128)(2,1)S(1)}, u32[]{:S(2)}, u32[]{:S(2)}) collective-permute-start(bf16[8,4224]{1,0:T(8,128)(2,1)S(1)} %get-tuple-element.21.refs_1_), channel_id=1, source_target_pairs={{0,4},{4,0},{8,12},{12,8},{1,5},{5,1},{9,13},{13,9},{2,6},{6,2},{1... | collective-permute-start | bytes 202760 | tf_op jit(solution)/shard_map/ppermute | solution.py:54
  6.7 7.4 %collective-permute-start.1 = (bf16[8,4224]{1,0:T(8,128)(2,1)S(1)}, bf16[8,4224]{1,0:T(8,128)(2,1)S(1)}, u32[]{:S(2)}, u32[]{:S(2)}) collective-permute-start(bf16[8,4224]{1,0:T(8,128)(2,1)S(1)} %get-tuple-element.22.refs_2_), channel_id=1, source_target_pairs={{0,8},{4,12},{8,0},{12,4},{1,9},{5,13},{9,1},{13,5},{2,10},{6,14},... | collective-permute-start | bytes 202760 | tf_op jit(solution)/shard_map/ppermute | solution.py:54
  9.3 6.2 %collective-permute-start.2 = (bf16[8,4224]{1,0:T(8,128)(2,1)S(1)}, bf16[8,4224]{1,0:T(8,128)(2,1)S(1)}, u32[]{:S(2)}, u32[]{:S(2)}) collective-permute-start(bf16[8,4224]{1,0:T(8,128)(2,1)S(1)} %get-tuple-element.23.refs_3_), channel_id=1, source_target_pairs={{0,12},{4,8},{8,4},{12,0},{1,13},{5,9},{9,5},{13,1},{2,14},{6,10},... | collective-permute-start | bytes 202760 | tf_op jit(solution)/shard_map/ppermute | solution.py:54
  15.7 5.2 %collective-permute-start.3 = (bf16[16,2432]{1,0:T(8,128)(2,1)S(1)}, bf16[16,2432]{1,0:T(8,128)(2,1)S(1)}, u32[]{:S(2)}, u32[]{:S(2)}) collective-permute-start(bf16[16,2432]{1,0:T(8,128)(2,1)S(1)} %get-tuple-element.25), channel_id=1, source_target_pairs={{0,16},{16,0},{1,17},{17,1},{2,18},{18,2},{3,19},{19,3},{4,20},{20... | collective-permute-start | bytes 233480 | tf_op jit(solution)/shard_map/ppermute | solution.py:54
  17.3 3.1 %collective-permute-start.6 = (f32[16,128]{1,0:T(8,128)S(1)}, f32[16,128]{1,0:T(8,128)S(1)}, u32[]{:S(2)}, u32[]{:S(2)}) collective-permute-start(f32[16,128]{1,0:T(8,128)S(1)} %get-tuple-element.26.refs_2_), channel_id=1, source_target_pairs={{0,3},{1,2},{2,1},{3,0},{4,7},{5,6},{6,5},{7,4},{8,11},{9,10},{10,... | collective-permute-start | bytes 24584 | tf_op jit(solution)/shard_map/ppermute | solution.py:54
  17.3 3.7 %collective-permute-start.5 = (f32[16,128]{1,0:T(8,128)S(1)}, f32[16,128]{1,0:T(8,128)S(1)}, u32[]{:S(2)}, u32[]{:S(2)}) collective-permute-start(f32[16,128]{1,0:T(8,128)S(1)} %get-tuple-element.26.refs_2_), channel_id=1, source_target_pairs={{0,2},{1,3},{2,0},{3,1},{4,6},{5,7},{6,4},{7,5},{8,10},{9,11},{10,... | collective-permute-start | bytes 24584 | tf_op jit(solution)/shard_map/ppermute | solution.py:54
  18.8 2.1 %collective-permute-start.4 = (f32[16,128]{1,0:T(8,128)S(1)}, f32[16,128]{1,0:T(8,128)S(1)}, u32[]{:S(2)}, u32[]{:S(2)}) collective-permute-start(f32[16,128]{1,0:T(8,128)S(1)} %get-tuple-element.26.refs_2_), channel_id=1, source_target_pairs={{0,1},{1,0},{2,3},{3,2},{4,5},{5,4},{6,7},{7,6},{8,9},{9,8},{10,11... | collective-permute-start | bytes 24584 | tf_op jit(solution)/shard_map/ppermute | solution.py:54

commit v5 on v4

--- a/solution.py
+++ b/solution.py
@@ -9,6 +9,8 @@
 
 CAP = 4
 LANES = 128
+JOINT = 1
+AFTER_WAIT = (10**9, 10**7)
 PAD = 8
 VMEM = pl.BlockSpec(memory_space=pltpu.VMEM)
 HBM = pl.BlockSpec(memory_space=pltpu.HBM)
@@ -33,20 +35,24 @@
 
 def target(me, step, size):
     if paired(size):
-        return me ^ step
+        return me ^ ((size - step) % size)
     after = me + step
     return after % size if isinstance(me, int) else jnp.where(after >= size, after - size, after)
 
 
 def source(me, step, size):
     if paired(size):
-        return me ^ step
+        return target(me, step, size)
     before = me - step
     return before % size if isinstance(me, int) else jnp.where(before < 0, before + size, before)
 
 
 def reply(step, size):
     return step if paired(size) else -step % size
+
+
+def apart(size):
+    return [r for r in range(size) if r != JOINT]
 
 
 def send(value, axis, step, give=target):
@@ -58,15 +64,19 @@
     ids_hbm, gates_hbm, grad_hbm, hidden_hbm, weight_hbm = refs[:5]
     ids_ref, match_ref, weight_ref, hidden_ref = refs[5:9]
     sends = refs[9 : 9 + count]
-    gates_ref, grad_ref, saved_ref, sems = refs[9 + count :]
+    products = refs[9 + count : 8 + 2 * count]
+    gates_ref, grad_ref, saved_ref, picked_ref, total_ref, sems = refs[8 + 2 * count :]
     units, width = weight_ref.shape
-    block = width // pieces
     top, tokens = ids_ref.shape
     pairs = [(ids_hbm, ids_ref), (gates_hbm, gates_ref), (hidden_hbm.at[0, 0], saved_ref)]
-    for p in range(pieces):
-        part = pl.ds(p * block, block)
-        pairs.append((grad_hbm.at[:, part], grad_ref.at[:, part]))
-        pairs.append((weight_hbm.at[0, :, part], weight_ref.at[:, part]))
+    half = tokens // 2
+    for p in range(2):
+        part = pl.ds(p * half, half)
+        pairs.append((grad_hbm.at[part], grad_ref.at[part]))
+    half = units // (2 * pieces)
+    for p in range(2 * pieces):
+        part = pl.ds(p * half, half)
+        pairs.append((weight_hbm.at[0, part], weight_ref.at[part]))
     copies = [pltpu.make_async_copy(*pair, sems.at[n]) for n, pair in enumerate(pairs)]
     for copy in copies:
         copy.start()
@@ -100,20 +110,30 @@
     hidden_ref[...] = dot(slot_order(count), saved, ((1,), (0,))).astype(jnp.bfloat16)
     here = lax.broadcasted_iota(jnp.int32, (rows, slots), 0)
     there = lax.broadcasted_iota(jnp.int32, (rows, slots), 1)
-    chosen = (here % PAD >= CAP) & (there == target(me, here // PAD, count) * CAP + here % PAD - CAP)
+    place = here % PAD - jnp.where(here // PAD == JOINT, CAP, 0)
+    chosen = (place >= 0) & (place < CAP) & (there == target(me, here // PAD, count) * CAP + place)
     hidden = dot(chosen.astype(jnp.bfloat16), saved, ((1,), (0,))).astype(jnp.bfloat16)
 
+    for copy in copies[3:5]:
+        copy.wait()
+    picked_ref[...] = dot(match, grad_ref[...], ((1,), (0,)))
     for r in range(count):
-        part = slice(r * PAD, (r + 1) * PAD)
-        sends[r][:, width:] = jnp.broadcast_to(slot_gate[part], (PAD, LANES)).astype(jnp.bfloat16)
+        part = slice(r * PAD, r * PAD + sends[r].shape[0])
+        gate = jnp.broadcast_to(slot_gate[part], (sends[r].shape[0], LANES))
+        sends[r][:, width:] = gate.astype(jnp.bfloat16)
+        if r != JOINT:
+            sends[r][:, :width] = picked_ref[part, :].astype(jnp.bfloat16)
+    block = units // pieces
     for p in range(pieces):
+        for copy in copies[5 + 2 * p : 7 + 2 * p]:
+            copy.wait()
         part = slice(p * block, (p + 1) * block)
-        copies[3 + 2 * p].wait()
-        both = dot(match, grad_ref[:, part], ((1,), (0,)))
-        copies[4 + 2 * p].wait()
-        both = both + dot(hidden, weight_ref[:, part], ((1,), (0,)))
-        for r in range(count):
-            sends[r][:, part] = both[r * PAD : (r + 1) * PAD].astype(jnp.bfloat16)
+        term = dot(hidden[:, part], weight_ref[part, :], ((1,), (0,)))
+        total_ref[...] = term if p == 0 else total_ref[...] + term
+    for product, r in zip(products, apart(count)):
+        product[...] = total_ref[r * PAD : r * PAD + CAP, :].astype(jnp.bfloat16)
+    part = slice(JOINT * PAD, (JOINT + 1) * PAD)
+    sends[JOINT][:, :width] = (picked_ref[part, :] + total_ref[part, :]).astype(jnp.bfloat16)
 
 
 def slot_order(count):
@@ -125,17 +145,12 @@
 
 
 def slot_kernel(count, groups, hidden_ref, *refs):
-    sent = refs[:count]
-    received = refs[count : 2 * count]
-    back_ref, rows_ref, gate_ref = refs[2 * count : 2 * count + 3]
-    pays = refs[2 * count + 3 : 2 * count + 3 + groups]
-    wide_ref, weighted_ref = refs[2 * count + 3 + groups :]
+    received = refs[:count]
+    rows_ref, gate_ref = refs[count : count + 2]
+    pays = refs[count + 2 : count + 2 + groups]
+    wide_ref, weighted_ref = refs[count + 2 + groups :]
     width = rows_ref.shape[1]
     for r in range(count):
-        mine = sent[r][...].astype(jnp.float32)[:CAP, :width]
-        theirs = received[reply(r, count)][...].astype(jnp.float32)[CAP:, :width]
-        back = jnp.sum(mine * theirs, axis=1, keepdims=True)
-        back_ref[r * CAP : (r + 1) * CAP, :] = jnp.broadcast_to(back, (CAP, LANES))
         wide_ref[r * CAP : (r + 1) * CAP, :] = received[r][...].astype(jnp.float32)[:CAP]
     rows = wide_ref[:, :width]
     gate = wide_ref[:, width:]
@@ -148,6 +163,23 @@
         group = target(me, r, groups)
         pays[r][:, :share] = weighted_ref[:, pl.ds(pl.multiple_of(group * share, share), share)]
         pays[r][:, share:] = hidden_ref[...]
+
+
+def back_kernel(count, *refs):
+    sent = refs[:count]
+    joint_ref = refs[count]
+    products = dict(zip(apart(count), refs[count + 1 : 2 * count]))
+    back_ref = refs[2 * count]
+    width = products[0].shape[1]
+    for r in range(count):
+        step = reply(r, count)
+        if step != JOINT:
+            theirs = products[step][...].astype(jnp.float32)
+        else:
+            theirs = joint_ref[:, :width].astype(jnp.float32)[CAP:]
+        mine = sent[r][:, :width].astype(jnp.float32)[:CAP]
+        back = jnp.sum(mine * theirs, axis=1, keepdims=True)
+        back_ref[r * CAP : (r + 1) * CAP, :] = jnp.broadcast_to(back, (CAP, LANES))
 
 
 def down_term(pay_ref, share, start, block):
@@ -217,51 +249,66 @@
     slots = count * CAP
     share = width // groups
     pieces = units // LANES
-    columns = width // 512
-
-    payload = jax.ShapeDtypeStruct((PAD, width + LANES), jnp.bfloat16)
-    ids, match, weight, hidden, *sends = pl.pallas_call(
-        functools.partial(front_kernel, count, columns),
+
+    ids, match, weight, hidden, *rest = pl.pallas_call(
+        functools.partial(front_kernel, count, pieces),
         out_shape=[
             jax.ShapeDtypeStruct((top, tokens), jnp.int32),
             jax.ShapeDtypeStruct((count * PAD, tokens), jnp.float32),
             jax.ShapeDtypeStruct((units, width), jnp.bfloat16),
             jax.ShapeDtypeStruct((slots, units), jnp.bfloat16),
         ]
-        + [payload] * count,
+        + [
+            jax.ShapeDtypeStruct((PAD if r == JOINT else CAP, width + LANES), jnp.bfloat16)
+            for r in range(count)
+        ]
+        + [jax.ShapeDtypeStruct((CAP, width), jnp.bfloat16)] * (count - 1),
         in_specs=[HBM] * 5,
-        out_specs=[VMEM] * (4 + count),
+        out_specs=[VMEM] * (3 + 2 * count),
         scratch_shapes=[
             pltpu.VMEM((top, tokens), jnp.bfloat16),
             pltpu.VMEM((tokens, width), jnp.bfloat16),
             pltpu.VMEM((slots, units), jnp.bfloat16),
-            pltpu.SemaphoreType.DMA((3 + 2 * columns,)),
+            pltpu.VMEM((count * PAD, width), jnp.float32),
+            pltpu.VMEM((count * PAD, width), jnp.float32),
+            pltpu.SemaphoreType.DMA((5 + 2 * pieces,)),
         ],
         compiler_params=PARAMS,
         cost_estimate=cost(2 * count * PAD * (tokens + units) * width, 2 * (tokens + units) * width),
         name="front",
     )(*in_hbm(expert_ids.T, gate_values.T, grad_out, saved_hidden, down_weight))
-
-    received = [sends[0]] + [send(sends[r], "expert", r) for r in reversed(range(1, count))][::-1]
-
-    back, rows, gate, *pays = pl.pallas_call(
+    sends, products = rest[:count], rest[count:]
+
+    received = [sends[0]] + [send(sends[r], "expert", r) for r in range(1, count)]
+    theirs = [products[0]] + [send(products[r - 1], "expert", r) for r in range(JOINT + 1, count)]
+
+    rows, gate, *pays = pl.pallas_call(
         functools.partial(slot_kernel, count, groups),
         out_shape=[
-            jax.ShapeDtypeStruct((slots, LANES), jnp.float32),
             jax.ShapeDtypeStruct((slots, width), jnp.bfloat16),
             jax.ShapeDtypeStruct((slots, LANES), jnp.float32),
         ]
         + [jax.ShapeDtypeStruct((slots, share + units), jnp.bfloat16)] * groups,
-        in_specs=[VMEM] * (1 + 2 * count),
-        out_specs=[VMEM] * (3 + groups),
+        in_specs=[VMEM] * (1 + count),
+        out_specs=[VMEM] * (2 + groups),
         scratch_shapes=[
             pltpu.VMEM((slots, width + LANES), jnp.float32),
             pltpu.VMEM((slots, width), jnp.bfloat16),
         ],
         compiler_params=PARAMS,
-        cost_estimate=cost(4 * slots * width, 16 * slots * width),
+        cost_estimate=cost(4 * slots * width, 8 * slots * width),
         name="slots",
-    )(hidden, *sends, *received)
+    )(hidden, *received)
+
+    back = pl.pallas_call(
+        functools.partial(back_kernel, count),
+        out_shape=jax.ShapeDtypeStruct((slots, LANES), jnp.float32),
+        in_specs=[VMEM] * (2 * count),
+        out_specs=VMEM,
+        compiler_params=PARAMS,
+        cost_estimate=cost(*AFTER_WAIT),
+        name="backs",
+    )(*sends, received[JOINT], *theirs)
 
     others = [send(pays[r], "dp", r) for r in range(1, groups)]
     backs = [back] + [send(back, "tensor", r) for r in range(1, tensors)]

time: 23.4 us -> 22.5 us (0.962)
  waiting for transfers between devices: 7.42 us -> 2.44 us
  starting transfers between devices: 9.08 us -> 13.5 us
  Pallas kernels: 6.04 us -> 5.69 us
    ppermute x7 -> x9, waiting for transfers between devices: 7.42 us -> 2.44 us  [send(): lax.ppermute(value, axis, [(i, give(i, step, size)) for i in range(size)])]
    ppermute x7 -> x9, starting transfers between devices: 9.08 us -> 13.5 us  [send(): lax.ppermute(value, axis, [(i, give(i, step, size)) for i in range(size)])]
    pallas_call x1 -> x2, Pallas kernels: 3.01 us -> 2.75 us  [the longest x1 2.59 us: on_device(): pl.pallas_call(functools.partial(front_kernel, count, pieces), out_shape=...]
  transfers between devices with their start and end apart: 7 -> 9, of which waited for: 4 -> 3; matrix products, arithmetic and copies ran while one was open for 0% -> 0% of each run, Pallas kernels for 3% -> 4%
where the time goes in v5:
time: 22.5 us; the launch traced here: 22.3 us
  starting transfers between devices  13.5 us (60%)
  Pallas kernels  5.69 us (25%)
  waiting for transfers between devices  2.44 us (11%)
  between operations  0.67 us (3%)
    ppermute x9, starting transfers between devices, send(): lax.ppermute(value, axis, [(i, give(i, step, size)) for i in range(size)])  13.5 us
    pallas_call x1, Pallas kernels, on_device(): pl.pallas_call(functools.partial(front_kernel, count, pieces), out_shape=...  2.59 us
    ppermute x9, waiting for transfers between devices, send(): lax.ppermute(value, axis, [(i, give(i, step, size)) for i in range(size)])  2.44 us
    pallas_call x1, Pallas kernels, on_device(): pl.pallas_call(functools.partial(last_kernel, count, groups - 1, tensors,...  2.24 us
    pallas_call x1, Pallas kernels, on_device(): pl.pallas_call(functools.partial(own_kernel, pieces), out_shape=jax.Shape...  0.59 us
  transfers between devices with their start and end apart: 9, of which 3 were waited for; matrix products, arithmetic and copies ran while one was open for 0% of the time, Pallas kernels for 4%

profile of v5, /device:TPU:0, one launch (start us, length us, event | category | flops | bytes accessed | tf_op | source)
XLA Modules:
  0.0 22.3 jit_solution(7450812099678314666)
XLA Ops:
  0.6 2.6 %front.1 = (s32[8,128]{1,0:T(8,128)S(1)}, f32[32,128]{1,0:T(8,128)S(1)}, bf16[384,4096]{1,0:T(8,128)(2,1)S(1)}, bf16[16,384]{1,0:T(8,128)(2,1)S(1)}, bf16[4,4224...) custom-call(s32[8,128]{1,0:T(8,128)} %bitcast.3, ...), custom_call_target="tpu_custom_call" | custom-call | flops 134217728 | bytes 4194304 | tf_op jit(solution)/shard_map/front/pallas_call | solution.py:253
  3.2 5.1 %collective-permute-start = (bf16[8,4224]{1,0:T(8,128)(2,1)S(1)}, bf16[8,4224]{1,0:T(8,128)(2,1)S(1)}, u32[]{:S(2)}, u32[]{:S(2)}) collective-permute-start(bf16[8,4224]{1,0:T(8,128)(2,1)S(1)} %get-tuple-element.23.refs_1_), channel_id=1, source_target_pairs={{0,12},{4,8},{8,4},{12,0},{1,13},{5,9},{9,5},{13,1},{2,14},{6,10},... | collective-permute-start | bytes 202760 | tf_op jit(solution)/shard_map/ppermute | solution.py:60
  8.3 0.0 collective-permute-start.1
  8.3 0.6 %collective-permute-start.2 = (bf16[4,4224]{1,0:T(4,128)(2,1)S(1)}, bf16[4,4224]{1,0:T(4,128)(2,1)S(1)}, u32[]{:S(2)}, u32[]{:S(2)}) collective-permute-start(bf16[4,4224]{1,0:T(4,128)(2,1)S(1)} %get-tuple-element.25.refs_3_), channel_id=1, source_target_pairs={{0,4},{4,0},{8,12},{12,8},{1,5},{5,1},{9,13},{13,9},{2,6},{6,2},{1... | collective-permute-start | bytes 101384 | tf_op jit(solution)/shard_map/ppermute | solution.py:60
  9.0 2.3 %collective-permute-start.4 = (bf16[4,4096]{1,0:T(4,128)(2,1)S(1)}, bf16[4,4096]{1,0:T(4,128)(2,1)S(1)}, u32[]{:S(2)}, u32[]{:S(2)}) collective-permute-start(bf16[4,4096]{1,0:T(4,128)(2,1)S(1)} %get-tuple-element.29), channel_id=1, source_target_pairs={{0,8},{4,12},{8,0},{12,4},{1,9},{5,13},{9,1},{13,5},{2,10},{6,14},... | collective-permute-start | bytes 98312 | tf_op jit(solution)/shard_map/ppermute | solution.py:60
  11.3 2.0 %collective-permute-start.5 = (bf16[4,4096]{1,0:T(4,128)(2,1)S(1)}, bf16[4,4096]{1,0:T(4,128)(2,1)S(1)}, u32[]{:S(2)}, u32[]{:S(2)}) collective-permute-start(bf16[4,4096]{1,0:T(4,128)(2,1)S(1)} %get-tuple-element.30), channel_id=1, source_target_pairs={{0,4},{4,0},{8,12},{12,8},{1,5},{5,1},{9,13},{13,9},{2,6},{6,2},{1... | collective-permute-start | bytes 98312 | tf_op jit(solution)/shard_map/ppermute | solution.py:60
  13.3 0.2 %collective-permute-done.1.refs_2_ = bf16[4,4224]{1,0:T(4,128)(2,1)S(1)} collective-permute-done((bf16[4,4224]{1,0:T(4,128)(2,1)S(1)}, bf16[4,4224]{1,0:T(4,128)(2,1)S(1)}, u32[]{:S(2)}, u32[]{:S(2)}) %collective-permute-start.1) | collective-permute-done | bytes 33824 | tf_op jit(solution)/shard_map/ppermute | solution.py:60
  13.5 0.0 collective-permute-done.2.refs_3_
  13.5 0.0 collective-permute-done.refs_1_.refs_4_
  13.5 0.1 slots.1
  13.6 1.6 %collective-permute-start.3 = (bf16[16,2432]{1,0:T(8,128)(2,1)S(1)}, bf16[16,2432]{1,0:T(8,128)(2,1)S(1)}, u32[]{:S(2)}, u32[]{:S(2)}) collective-permute-start(bf16[16,2432]{1,0:T(8,128)(2,1)S(1)} %get-tuple-element.27), channel_id=1, source_target_pairs={{0,16},{16,0},{1,17},{17,1},{2,18},{18,2},{3,19},{19,3},{4,20},{20... | collective-permute-start | bytes 233480 | tf_op jit(solution)/shard_map/ppermute | solution.py:60
  15.2 0.0 collective-permute-done.4.refs_6_
  15.2 0.0 collective-permute-done.5.refs_7_
  15.2 0.2 backs.1.refs_2_
  15.4 0.0 collective-permute-start.8
  15.4 1.6 %collective-permute-start.7 = (f32[16,128]{1,0:T(8,128)S(1)}, f32[16,128]{1,0:T(8,128)S(1)}, u32[]{:S(2)}, u32[]{:S(2)}) collective-permute-start(f32[16,128]{1,0:T(8,128)S(1)} %backs.1.refs_2_), channel_id=1, source_target_pairs={{0,2},{1,3},{2,0},{3,1},{4,6},{5,7},{6,4},{7,5},{8,10},{9,11},{10,... | collective-permute-start | bytes 24584 | tf_op jit(solution)/shard_map/ppermute | solution.py:60
  17.0 0.3 %collective-permute-start.6 = (f32[16,128]{1,0:T(8,128)S(1)}, f32[16,128]{1,0:T(8,128)S(1)}, u32[]{:S(2)}, u32[]{:S(2)}) collective-permute-start(f32[16,128]{1,0:T(8,128)S(1)} %backs.1.refs_2_), channel_id=1, source_target_pairs={{0,3},{1,2},{2,1},{3,0},{4,7},{5,6},{6,5},{7,4},{8,11},{9,10},{10,... | collective-permute-start | bytes 24584 | tf_op jit(solution)/shard_map/ppermute | solution.py:60
  17.2 0.6 %own.1.refs_0_ = bf16[384,2048]{1,0:T(8,128)(2,1)S(1)} custom-call(bf16[16,2432]{1,0:T(8,128)(2,1)S(1)} %get-tuple-element.26.pay_ref), custom_call_target="tpu_custom_call" | custom-call | flops 25165824 | bytes 1572864 | tf_op jit(solution)/shard_map/own/pallas_call | solution.py:316
  17.8 0.0 collective-permute-done.8.refs_5_
  17.8 1.3 %collective-permute-done.7.refs_4_ = f32[16,128]{1,0:T(8,128)S(1)} collective-permute-done((f32[16,128]{1,0:T(8,128)S(1)}, f32[16,128]{1,0:T(8,128)S(1)}, u32[]{:S(2)}, u32[]{:S(2)}) %collective-permute-start.7) | collective-permute-done | bytes 8224 | tf_op jit(solution)/shard_map/ppermute | solution.py:60
  19.1 0.9 %collective-permute-done.6.refs_3_ = f32[16,128]{1,0:T(8,128)S(1)} collective-permute-done((f32[16,128]{1,0:T(8,128)S(1)}, f32[16,128]{1,0:T(8,128)S(1)}, u32[]{:S(2)}, u32[]{:S(2)}) %collective-permute-start.6) | collective-permute-done | bytes 8224 | tf_op jit(solution)/shard_map/ppermute | solution.py:60
  20.0 0.0 collective-permute-done.3.refs_1_
  20.0 2.2 %last.1 = (f32[8,128]{1,0:T(8,128)}, bf16[1,1,16,384]{3,2,1,0:T(8,128)(2,1)}, f32[1,384,2048]{2,1,0:T(8,128)}) custom-call(bf16[384,2048]{1,0:T(8,128)(2,1)S(1)} %own.1.refs_0_, bf16[16,2432]{1,0:T(8,128)(2,1)S(1)} %collective-permute-done.3.refs_1_, f32[16,128]{1,0:T(8,128)S(1)} %backs.1.refs_2_, f32[16,128]{1,0:T(8,128)S(1)} %collective-permute-done.6.refs_3_, ...), custom_call_target="tpu_custom_call" | custom-call | flops 75497472 | bytes 3145728 | tf_op jit(solution)/shard_map/last/pallas_call | solution.py:326
Async XLA Ops:
  3.2 10.3 %collective-permute-start = (bf16[8,4224]{1,0:T(8,128)(2,1)S(1)}, bf16[8,4224]{1,0:T(8,128)(2,1)S(1)}, u32[]{:S(2)}, u32[]{:S(2)}) collective-permute-start(bf16[8,4224]{1,0:T(8,128)(2,1)S(1)} %get-tuple-element.23.refs_1_), channel_id=1, source_target_pairs={{0,12},{4,8},{8,4},{12,0},{1,13},{5,9},{9,5},{13,1},{2,14},{6,10},... | collective-permute-start | bytes 202760 | tf_op jit(solution)/shard_map/ppermute | solution.py:60
  8.3 5.2 %collective-permute-start.1 = (bf16[4,4224]{1,0:T(4,128)(2,1)S(1)}, bf16[4,4224]{1,0:T(4,128)(2,1)S(1)}, u32[]{:S(2)}, u32[]{:S(2)}) collective-permute-start(bf16[4,4224]{1,0:T(4,128)(2,1)S(1)} %get-tuple-element.24.refs_2_), channel_id=1, source_target_pairs={{0,8},{4,12},{8,0},{12,4},{1,9},{5,13},{9,1},{13,5},{2,10},{6,14},... | collective-permute-start | bytes 101384 | tf_op jit(solution)/shard_map/ppermute | solution.py:60
  8.3 5.2 %collective-permute-start.2 = (bf16[4,4224]{1,0:T(4,128)(2,1)S(1)}, bf16[4,4224]{1,0:T(4,128)(2,1)S(1)}, u32[]{:S(2)}, u32[]{:S(2)}) collective-permute-start(bf16[4,4224]{1,0:T(4,128)(2,1)S(1)} %get-tuple-element.25.refs_3_), channel_id=1, source_target_pairs={{0,4},{4,0},{8,12},{12,8},{1,5},{5,1},{9,13},{13,9},{2,6},{6,2},{1... | collective-permute-start | bytes 101384 | tf_op jit(solution)/shard_map/ppermute | solution.py:60
  9.0 6.2 %collective-permute-start.4 = (bf16[4,4096]{1,0:T(4,128)(2,1)S(1)}, bf16[4,4096]{1,0:T(4,128)(2,1)S(1)}, u32[]{:S(2)}, u32[]{:S(2)}) collective-permute-start(bf16[4,4096]{1,0:T(4,128)(2,1)S(1)} %get-tuple-element.29), channel_id=1, source_target_pairs={{0,8},{4,12},{8,0},{12,4},{1,9},{5,13},{9,1},{13,5},{2,10},{6,14},... | collective-permute-start | bytes 98312 | tf_op jit(solution)/shard_map/ppermute | solution.py:60
  11.3 3.9 %collective-permute-start.5 = (bf16[4,4096]{1,0:T(4,128)(2,1)S(1)}, bf16[4,4096]{1,0:T(4,128)(2,1)S(1)}, u32[]{:S(2)}, u32[]{:S(2)}) collective-permute-start(bf16[4,4096]{1,0:T(4,128)(2,1)S(1)} %get-tuple-element.30), channel_id=1, source_target_pairs={{0,4},{4,0},{8,12},{12,8},{1,5},{5,1},{9,13},{13,9},{2,6},{6,2},{1... | collective-permute-start | bytes 98312 | tf_op jit(solution)/shard_map/ppermute | solution.py:60
  13.6 6.4 %collective-permute-start.3 = (bf16[16,2432]{1,0:T(8,128)(2,1)S(1)}, bf16[16,2432]{1,0:T(8,128)(2,1)S(1)}, u32[]{:S(2)}, u32[]{:S(2)}) collective-permute-start(bf16[16,2432]{1,0:T(8,128)(2,1)S(1)} %get-tuple-element.27), channel_id=1, source_target_pairs={{0,16},{16,0},{1,17},{17,1},{2,18},{18,2},{3,19},{19,3},{4,20},{20... | collective-permute-start | bytes 233480 | tf_op jit(solution)/shard_map/ppermute | solution.py:60
  15.4 2.5 %collective-permute-start.8 = (f32[16,128]{1,0:T(8,128)S(1)}, f32[16,128]{1,0:T(8,128)S(1)}, u32[]{:S(2)}, u32[]{:S(2)}) collective-permute-start(f32[16,128]{1,0:T(8,128)S(1)} %backs.1.refs_2_), channel_id=1, source_target_pairs={{0,1},{1,0},{2,3},{3,2},{4,5},{5,4},{6,7},{7,6},{8,9},{9,8},{10,11... | collective-permute-start | bytes 24584 | tf_op jit(solution)/shard_map/ppermute | solution.py:60
  15.4 3.7 %collective-permute-start.7 = (f32[16,128]{1,0:T(8,128)S(1)}, f32[16,128]{1,0:T(8,128)S(1)}, u32[]{:S(2)}, u32[]{:S(2)}) collective-permute-start(f32[16,128]{1,0:T(8,128)S(1)} %backs.1.refs_2_), channel_id=1, source_target_pairs={{0,2},{1,3},{2,0},{3,1},{4,6},{5,7},{6,4},{7,5},{8,10},{9,11},{10,... | collective-permute-start | bytes 24584 | tf_op jit(solution)/shard_map/ppermute | solution.py:60
  17.0 3.1 %collective-permute-start.6 = (f32[16,128]{1,0:T(8,128)S(1)}, f32[16,128]{1,0:T(8,128)S(1)}, u32[]{:S(2)}, u32[]{:S(2)}) collective-permute-start(f32[16,128]{1,0:T(8,128)S(1)} %backs.1.refs_2_), channel_id=1, source_target_pairs={{0,3},{1,2},{2,1},{3,0},{4,7},{5,6},{6,5},{7,4},{8,11},{9,10},{10,... | collective-permute-start | bytes 24584 | tf_op jit(solution)/shard_map/ppermute | solution.py:60

commit v6 on v5

--- a/solution.py
+++ b/solution.py
@@ -52,7 +52,16 @@
 
 
 def apart(size):
-    return [r for r in range(size) if r != JOINT]
+    return [r for r in range(1, size) if r != JOINT]
+
+
+def halves():
+    return 2 - lax.axis_size("tensor") % 2
+
+
+def half_of(width):
+    size = width // halves()
+    return size, pl.multiple_of(lax.axis_index("tensor") % halves() * size, LANES)
 
 
 def send(value, axis, step, give=target):
@@ -62,10 +71,10 @@
 
 def front_kernel(count, pieces, *refs):
     ids_hbm, gates_hbm, grad_hbm, hidden_hbm, weight_hbm = refs[:5]
-    ids_ref, match_ref, weight_ref, hidden_ref = refs[5:9]
-    sends = refs[9 : 9 + count]
-    products = refs[9 + count : 8 + 2 * count]
-    gates_ref, grad_ref, saved_ref, picked_ref, total_ref, sems = refs[8 + 2 * count :]
+    ids_ref, match_ref, weight_ref, hidden_ref, picked_ref, gate_ref, total_ref = refs[5:12]
+    sends = dict(zip(range(1, count), refs[12 : 11 + count]))
+    products = dict(zip(apart(count), refs[11 + count : 9 + 2 * count]))
+    gates_ref, grad_ref, saved_ref, sems = refs[9 + 2 * count :]
     units, width = weight_ref.shape
     top, tokens = ids_ref.shape
     pairs = [(ids_hbm, ids_ref), (gates_hbm, gates_ref), (hidden_hbm.at[0, 0], saved_ref)]
@@ -110,19 +119,18 @@
     hidden_ref[...] = dot(slot_order(count), saved, ((1,), (0,))).astype(jnp.bfloat16)
     here = lax.broadcasted_iota(jnp.int32, (rows, slots), 0)
     there = lax.broadcasted_iota(jnp.int32, (rows, slots), 1)
-    place = here % PAD - jnp.where(here // PAD == JOINT, CAP, 0)
-    chosen = (place >= 0) & (place < CAP) & (there == target(me, here // PAD, count) * CAP + place)
+    chosen = (here % PAD < CAP) & (there == target(me, here // PAD, count) * CAP + here % PAD)
     hidden = dot(chosen.astype(jnp.bfloat16), saved, ((1,), (0,))).astype(jnp.bfloat16)
 
     for copy in copies[3:5]:
         copy.wait()
+    gate_ref[...] = jnp.broadcast_to(slot_gate, gate_ref.shape)
     picked_ref[...] = dot(match, grad_ref[...], ((1,), (0,)))
-    for r in range(count):
-        part = slice(r * PAD, r * PAD + sends[r].shape[0])
-        gate = jnp.broadcast_to(slot_gate[part], (sends[r].shape[0], LANES))
-        sends[r][:, width:] = gate.astype(jnp.bfloat16)
-        if r != JOINT:
-            sends[r][:, :width] = picked_ref[part, :].astype(jnp.bfloat16)
+    half, begin = half_of(width)
+    for r, ref in sends.items():
+        part = slice(r * PAD, r * PAD + CAP)
+        ref[:, :half] = picked_ref[part, pl.ds(begin, half)].astype(jnp.bfloat16)
+        ref[:, half : half + LANES] = gate_ref[part, :].astype(jnp.bfloat16)
     block = units // pieces
     for p in range(pieces):
         for copy in copies[5 + 2 * p : 7 + 2 * p]:
@@ -130,10 +138,10 @@
         part = slice(p * block, (p + 1) * block)
         term = dot(hidden[:, part], weight_ref[part, :], ((1,), (0,)))
         total_ref[...] = term if p == 0 else total_ref[...] + term
-    for product, r in zip(products, apart(count)):
-        product[...] = total_ref[r * PAD : r * PAD + CAP, :].astype(jnp.bfloat16)
-    part = slice(JOINT * PAD, (JOINT + 1) * PAD)
-    sends[JOINT][:, :width] = (picked_ref[part, :] + total_ref[part, :]).astype(jnp.bfloat16)
+    for r, ref in products.items():
+        ref[...] = total_ref[r * PAD : r * PAD + CAP, :].astype(jnp.bfloat16)
+    product = total_ref[JOINT * PAD : JOINT * PAD + CAP, :].astype(jnp.bfloat16)
+    sends[JOINT][:, half + LANES :] = product
 
 
 def slot_order(count):
@@ -144,19 +152,34 @@
     return (saved == source(me, here // CAP, count) * CAP + here % CAP).astype(jnp.bfloat16)
 
 
-def slot_kernel(count, groups, hidden_ref, *refs):
-    received = refs[:count]
-    rows_ref, gate_ref = refs[count : count + 2]
-    pays = refs[count + 2 : count + 2 + groups]
-    wide_ref, weighted_ref = refs[count + 2 + groups :]
+def pack_kernel(count, *refs):
+    packed_ref, wide_ref = refs[count - 1 :]
+    for r in range(1, count):
+        half = refs[r - 1][:, : packed_ref.shape[1]]
+        wide_ref[(r - 1) * CAP : r * CAP, :] = half.astype(jnp.float32)
+    packed_ref[...] = wide_ref[...].astype(jnp.bfloat16)
+
+
+def slot_kernel(count, groups, hidden_ref, picked_ref, sent_gate_ref, *refs):
+    received = refs[: count - 1]
+    others = refs[count - 1 : -4 - groups]
+    rows_ref, gate_ref = refs[-4 - groups : -2 - groups]
+    pays = refs[-2 - groups : -2]
+    wide_ref, weighted_ref = refs[-2:]
     width = rows_ref.shape[1]
-    for r in range(count):
-        wide_ref[r * CAP : (r + 1) * CAP, :] = received[r][...].astype(jnp.float32)[:CAP]
-    rows = wide_ref[:, :width]
-    gate = wide_ref[:, width:]
-    gate_ref[...] = gate
+    half, begin = half_of(width)
+    wide_ref[:CAP, :] = picked_ref[:CAP, :]
+    gate_ref[:CAP, :] = sent_gate_ref[:CAP, :]
+    for r in range(1, count):
+        part = slice(r * CAP, (r + 1) * CAP)
+        wide_ref[part, pl.ds(begin, half)] = received[r - 1][:, :half].astype(jnp.float32)
+        gate_ref[part, :] = received[r - 1][:, half : half + LANES].astype(jnp.float32)
+    for other in others:
+        begin = pl.multiple_of(width - half - begin, LANES)
+        wide_ref[CAP:, pl.ds(begin, half)] = other[...].astype(jnp.float32)
+    rows = wide_ref[...]
     rows_ref[...] = rows.astype(jnp.bfloat16)
-    weighted_ref[...] = (gate[:, :1] * rows).astype(jnp.bfloat16)
+    weighted_ref[...] = (gate_ref[:, :1] * rows).astype(jnp.bfloat16)
     share = width // groups
     me = lax.axis_index("dp")
     for r in range(groups):
@@ -165,19 +188,19 @@
         pays[r][:, share:] = hidden_ref[...]
 
 
-def back_kernel(count, *refs):
-    sent = refs[:count]
-    joint_ref = refs[count]
-    products = dict(zip(apart(count), refs[count + 1 : 2 * count]))
-    back_ref = refs[2 * count]
-    width = products[0].shape[1]
+def back_kernel(count, picked_ref, total_ref, joint_ref, *refs):
+    products = dict(zip(apart(count), refs[: count - 2]))
+    back_ref = refs[count - 2]
+    width = picked_ref.shape[1]
     for r in range(count):
         step = reply(r, count)
-        if step != JOINT:
+        if step == 0:
+            theirs = total_ref[:CAP, :]
+        elif step == JOINT:
+            theirs = joint_ref[:, joint_ref.shape[1] - width :].astype(jnp.float32)
+        else:
             theirs = products[step][...].astype(jnp.float32)
-        else:
-            theirs = joint_ref[:, :width].astype(jnp.float32)[CAP:]
-        mine = sent[r][:, :width].astype(jnp.float32)[:CAP]
+        mine = picked_ref[r * PAD : r * PAD + CAP, :]
         back = jnp.sum(mine * theirs, axis=1, keepdims=True)
         back_ref[r * CAP : (r + 1) * CAP, :] = jnp.broadcast_to(back, (CAP, LANES))
 
@@ -249,38 +272,54 @@
     slots = count * CAP
     share = width // groups
     pieces = units // LANES
-
-    ids, match, weight, hidden, *rest = pl.pallas_call(
+    half = width // halves()
+
+    ids, match, weight, hidden, picked, sent_gate, total, *rest = pl.pallas_call(
         functools.partial(front_kernel, count, pieces),
         out_shape=[
             jax.ShapeDtypeStruct((top, tokens), jnp.int32),
             jax.ShapeDtypeStruct((count * PAD, tokens), jnp.float32),
             jax.ShapeDtypeStruct((units, width), jnp.bfloat16),
             jax.ShapeDtypeStruct((slots, units), jnp.bfloat16),
+            jax.ShapeDtypeStruct((count * PAD, width), jnp.float32),
+            jax.ShapeDtypeStruct((count * PAD, LANES), jnp.float32),
+            jax.ShapeDtypeStruct((count * PAD, width), jnp.float32),
         ]
         + [
-            jax.ShapeDtypeStruct((PAD if r == JOINT else CAP, width + LANES), jnp.bfloat16)
-            for r in range(count)
+            jax.ShapeDtypeStruct((CAP, half + LANES + width * (r == JOINT)), jnp.bfloat16)
+            for r in range(1, count)
         ]
-        + [jax.ShapeDtypeStruct((CAP, width), jnp.bfloat16)] * (count - 1),
+        + [jax.ShapeDtypeStruct((CAP, width), jnp.bfloat16)] * (count - 2),
         in_specs=[HBM] * 5,
-        out_specs=[VMEM] * (3 + 2 * count),
+        out_specs=[VMEM] * (4 + 2 * count),
         scratch_shapes=[
             pltpu.VMEM((top, tokens), jnp.bfloat16),
             pltpu.VMEM((tokens, width), jnp.bfloat16),
             pltpu.VMEM((slots, units), jnp.bfloat16),
-            pltpu.VMEM((count * PAD, width), jnp.float32),
-            pltpu.VMEM((count * PAD, width), jnp.float32),
             pltpu.SemaphoreType.DMA((5 + 2 * pieces,)),
         ],
         compiler_params=PARAMS,
         cost_estimate=cost(2 * count * PAD * (tokens + units) * width, 2 * (tokens + units) * width),
         name="front",
     )(*in_hbm(expert_ids.T, gate_values.T, grad_out, saved_hidden, down_weight))
-    sends, products = rest[:count], rest[count:]
-
-    received = [sends[0]] + [send(sends[r], "expert", r) for r in range(1, count)]
-    theirs = [products[0]] + [send(products[r - 1], "expert", r) for r in range(JOINT + 1, count)]
+    sends, products = rest[: count - 1], rest[count - 1 :]
+
+    received = [send(x, "expert", r) for r, x in zip(range(1, count), sends)]
+    theirs = [send(x, "expert", r) for r, x in zip(apart(count), products)]
+
+    halved = []
+    if halves() > 1:
+        packed = pl.pallas_call(
+            functools.partial(pack_kernel, count),
+            out_shape=jax.ShapeDtypeStruct((slots - CAP, half), jnp.bfloat16),
+            in_specs=[VMEM] * (count - 1),
+            out_specs=VMEM,
+            scratch_shapes=[pltpu.VMEM((slots - CAP, half), jnp.float32)],
+            compiler_params=PARAMS,
+            cost_estimate=cost(slots * width, 4 * slots * width),
+            name="pack",
+        )(*received)
+        halved = [lax.ppermute(packed, "tensor", [(i, i ^ 1) for i in range(tensors)])]
 
     rows, gate, *pays = pl.pallas_call(
         functools.partial(slot_kernel, count, groups),
@@ -289,29 +328,29 @@
             jax.ShapeDtypeStruct((slots, LANES), jnp.float32),
         ]
         + [jax.ShapeDtypeStruct((slots, share + units), jnp.bfloat16)] * groups,
-        in_specs=[VMEM] * (1 + count),
+        in_specs=[VMEM] * (2 + count + len(halved)),
         out_specs=[VMEM] * (2 + groups),
         scratch_shapes=[
-            pltpu.VMEM((slots, width + LANES), jnp.float32),
+            pltpu.VMEM((slots, width), jnp.float32),
             pltpu.VMEM((slots, width), jnp.bfloat16),
         ],
         compiler_params=PARAMS,
         cost_estimate=cost(4 * slots * width, 8 * slots * width),
         name="slots",
-    )(hidden, *received)
+    )(hidden, picked, sent_gate, *received, *halved)
 
     back = pl.pallas_call(
         functools.partial(back_kernel, count),
         out_shape=jax.ShapeDtypeStruct((slots, LANES), jnp.float32),
-        in_specs=[VMEM] * (2 * count),
+        in_specs=[VMEM] * (1 + count),
         out_specs=VMEM,
         compiler_params=PARAMS,
         cost_estimate=cost(*AFTER_WAIT),
         name="backs",
-    )(*sends, received[JOINT], *theirs)
+    )(picked, total, received[JOINT - 1], *theirs)
 
     others = [send(pays[r], "dp", r) for r in range(1, groups)]
-    backs = [back] + [send(back, "tensor", r) for r in range(1, tensors)]
+    backs = [back] + [send(back, "tensor", r) for r in reversed(range(1, tensors))]
 
     own = pl.pallas_call(
         functools.partial(own_kernel, pieces),

time: 22.5 us -> 25.5 us (1.13)
  waiting for transfers between devices: 2.44 us -> 7.65 us
  starting transfers between devices: 13.5 us -> 11.3 us
    ppermute x9, waiting for transfers between devices: 2.44 us -> 7.64 us  [send(): lax.ppermute(value, axis, [(i, give(i, step, size)) for i in range(size)])]
    ppermute x9, starting transfers between devices: 13.5 us -> 11.3 us  [send(): lax.ppermute(value, axis, [(i, give(i, step, size)) for i in range(size)])]
  transfers between devices with their start and end apart: 9 -> 10, of which waited for: 3 -> 5; matrix products, arithmetic and copies ran while one was open for 0% -> 0% of each run, Pallas kernels for 4% -> 3%
where the time goes in v6:
time: 25.5 us; the launch traced here: 25.4 us
  starting transfers between devices  11.3 us (44%)
  waiting for transfers between devices  7.65 us (30%)
  Pallas kernels  5.7 us (22%)
  between operations  0.67 us (3%)
    ppermute x9, starting transfers between devices, send(): lax.ppermute(value, axis, [(i, give(i, step, size)) for i in range(size)])  11.3 us
    ppermute x9, waiting for transfers between devices, send(): lax.ppermute(value, axis, [(i, give(i, step, size)) for i in range(size)])  7.64 us
    pallas_call x1, Pallas kernels, on_device(): pl.pallas_call(functools.partial(front_kernel, count, pieces), out_shape=...  2.59 us
    pallas_call x1, Pallas kernels, on_device(): pl.pallas_call(functools.partial(last_kernel, count, groups - 1, tensors,...  2.24 us
    pallas_call x1, Pallas kernels, on_device(): pl.pallas_call(functools.partial(own_kernel, pieces), out_shape=jax.Shape...  0.59 us
  transfers between devices with their start and end apart: 10, of which 5 were waited for; matrix products, arithmetic and copies ran while one was open for 0% of the time, Pallas kernels for 3%

profile of v6, /device:TPU:0, one launch (start us, length us, event | category | flops | bytes accessed | tf_op | source)
XLA Modules:
  0.0 25.4 jit_solution(1247281429473642965)
XLA Ops:
  0.6 2.6 %front.1 = (s32[8,128]{1,0:T(8,128)S(1)}, f32[32,128]{1,0:T(8,128)S(1)}, bf16[384,4096]{1,0:T(8,128)(2,1)S(1)}, bf16[16,384]{1,0:T(8,128)(2,1)S(1)}, f32[32,4096...) custom-call(s32[8,128]{1,0:T(8,128)} %bitcast.3, ...), custom_call_target="tpu_custom_call" | custom-call | flops 134217728 | bytes 4194304 | tf_op jit(solution)/shard_map/front/pallas_call | solution.py:277
  3.2 5.1 %collective-permute-start = (bf16[4,6272]{1,0:T(4,128)(2,1)S(1)}, bf16[4,6272]{1,0:T(4,128)(2,1)S(1)}, u32[]{:S(2)}, u32[]{:S(2)}) collective-permute-start(bf16[4,6272]{1,0:T(4,128)(2,1)S(1)} %get-tuple-element.25), channel_id=1, source_target_pairs={{0,12},{4,8},{8,4},{12,0},{1,13},{5,9},{9,5},{13,1},{2,14},{6,10},... | collective-permute-start | bytes 150536 | tf_op jit(solution)/shard_map/ppermute | solution.py:69
  8.3 0.0 collective-permute-start.1
  8.3 0.6 %collective-permute-start.2 = (bf16[4,2176]{1,0:T(4,128)(2,1)S(1)}, bf16[4,2176]{1,0:T(4,128)(2,1)S(1)}, u32[]{:S(2)}, u32[]{:S(2)}) collective-permute-start(bf16[4,2176]{1,0:T(4,128)(2,1)S(1)} %get-tuple-element.27), channel_id=1, source_target_pairs={{0,4},{4,0},{8,12},{12,8},{1,5},{5,1},{9,13},{13,9},{2,6},{6,2},{1... | collective-permute-start | bytes 52232 | tf_op jit(solution)/shard_map/ppermute | solution.py:69
  9.0 4.0 %collective-permute-done.1.refs_1_ = bf16[4,2176]{1,0:T(4,128)(2,1)S(1)} collective-permute-done((bf16[4,2176]{1,0:T(4,128)(2,1)S(1)}, bf16[4,2176]{1,0:T(4,128)(2,1)S(1)}, u32[]{:S(2)}, u32[]{:S(2)}) %collective-permute-start.1) | collective-permute-done | bytes 17440 | tf_op jit(solution)/shard_map/ppermute | solution.py:69
  13.0 0.0 collective-permute-done.2.refs_2_
  13.0 0.0 collective-permute-done.refs_0_.joint_ref
  13.0 0.1 collective-permute-start.3
  13.1 2.1 %collective-permute-start.5 = (bf16[4,4096]{1,0:T(4,128)(2,1)S(1)}, bf16[4,4096]{1,0:T(4,128)(2,1)S(1)}, u32[]{:S(2)}, u32[]{:S(2)}) collective-permute-start(bf16[4,4096]{1,0:T(4,128)(2,1)S(1)} %get-tuple-element.31), channel_id=1, source_target_pairs={{0,8},{4,12},{8,0},{12,4},{1,9},{5,13},{9,1},{13,5},{2,10},{6,14},... | collective-permute-start | bytes 98312 | tf_op jit(solution)/shard_map/ppermute | solution.py:69
  15.2 0.0 collective-permute-start.6
  15.2 0.0 collective-permute-done.3.refs_3_
  15.2 0.1 slots.1
  15.3 1.6 %collective-permute-start.4 = (bf16[16,2432]{1,0:T(8,128)(2,1)S(1)}, bf16[16,2432]{1,0:T(8,128)(2,1)S(1)}, u32[]{:S(2)}, u32[]{:S(2)}) collective-permute-start(bf16[16,2432]{1,0:T(8,128)(2,1)S(1)} %get-tuple-element.29), channel_id=1, source_target_pairs={{0,16},{16,0},{1,17},{17,1},{2,18},{18,2},{3,19},{19,3},{4,20},{20... | collective-permute-start | bytes 233480 | tf_op jit(solution)/shard_map/ppermute | solution.py:69
  16.9 1.1 %collective-permute-done.5.refs_0_ = bf16[4,4096]{1,0:T(4,128)(2,1)S(1)} collective-permute-done((bf16[4,4096]{1,0:T(4,128)(2,1)S(1)}, bf16[4,4096]{1,0:T(4,128)(2,1)S(1)}, u32[]{:S(2)}, u32[]{:S(2)}) %collective-permute-start.5) | collective-permute-done | bytes 32800 | tf_op jit(solution)/shard_map/ppermute | solution.py:69
  18.0 1.1 %collective-permute-done.6.refs_1_ = bf16[4,4096]{1,0:T(4,128)(2,1)S(1)} collective-permute-done((bf16[4,4096]{1,0:T(4,128)(2,1)S(1)}, bf16[4,4096]{1,0:T(4,128)(2,1)S(1)}, u32[]{:S(2)}, u32[]{:S(2)}) %collective-permute-start.6) | collective-permute-done | bytes 32800 | tf_op jit(solution)/shard_map/ppermute | solution.py:69
  19.1 0.2 backs.1.refs_2_
  19.3 0.2 collective-permute-start.9
  19.5 1.4 %collective-permute-start.8 = (f32[16,128]{1,0:T(8,128)S(1)}, f32[16,128]{1,0:T(8,128)S(1)}, u32[]{:S(2)}, u32[]{:S(2)}) collective-permute-start(f32[16,128]{1,0:T(8,128)S(1)} %backs.1.refs_2_), channel_id=1, source_target_pairs={{0,2},{1,3},{2,0},{3,1},{4,6},{5,7},{6,4},{7,5},{8,10},{9,11},{10,... | collective-permute-start | bytes 24584 | tf_op jit(solution)/shard_map/ppermute | solution.py:69
  20.9 0.3 %collective-permute-start.7 = (f32[16,128]{1,0:T(8,128)S(1)}, f32[16,128]{1,0:T(8,128)S(1)}, u32[]{:S(2)}, u32[]{:S(2)}) collective-permute-start(f32[16,128]{1,0:T(8,128)S(1)} %backs.1.refs_2_), channel_id=1, source_target_pairs={{0,1},{1,0},{2,3},{3,2},{4,5},{5,4},{6,7},{7,6},{8,9},{9,8},{10,11... | collective-permute-start | bytes 24584 | tf_op jit(solution)/shard_map/ppermute | solution.py:69
  21.1 0.6 %own.1.refs_0_ = bf16[384,2048]{1,0:T(8,128)(2,1)S(1)} custom-call(bf16[16,2432]{1,0:T(8,128)(2,1)S(1)} %get-tuple-element.28.pay_ref), custom_call_target="tpu_custom_call" | custom-call | flops 25165824 | bytes 1572864 | tf_op jit(solution)/shard_map/own/pallas_call | solution.py:355
  21.7 0.6 %collective-permute-done.9.refs_5_ = f32[16,128]{1,0:T(8,128)S(1)} collective-permute-done((f32[16,128]{1,0:T(8,128)S(1)}, f32[16,128]{1,0:T(8,128)S(1)}, u32[]{:S(2)}, u32[]{:S(2)}) %collective-permute-start.9) | collective-permute-done | bytes 8224 | tf_op jit(solution)/shard_map/ppermute | solution.py:69
  22.4 0.8 %collective-permute-done.8.refs_4_ = f32[16,128]{1,0:T(8,128)S(1)} collective-permute-done((f32[16,128]{1,0:T(8,128)S(1)}, f32[16,128]{1,0:T(8,128)S(1)}, u32[]{:S(2)}, u32[]{:S(2)}) %collective-permute-start.8) | collective-permute-done | bytes 8224 | tf_op jit(solution)/shard_map/ppermute | solution.py:69
  23.1 0.0 collective-permute-done.7.refs_3_
  23.1 0.0 collective-permute-done.4.refs_1_
  23.1 2.2 %last.1 = (f32[8,128]{1,0:T(8,128)}, bf16[1,1,16,384]{3,2,1,0:T(8,128)(2,1)}, f32[1,384,2048]{2,1,0:T(8,128)}) custom-call(bf16[384,2048]{1,0:T(8,128)(2,1)S(1)} %own.1.refs_0_, bf16[16,2432]{1,0:T(8,128)(2,1)S(1)} %collective-permute-done.4.refs_1_, f32[16,128]{1,0:T(8,128)S(1)} %backs.1.refs_2_, f32[16,128]{1,0:T(8,128)S(1)} %collective-permute-done.7.refs_3_, ...), custom_call_target="tpu_custom_call" | custom-call | flops 75497472 | bytes 3145728 | tf_op jit(solution)/shard_map/last/pallas_call | solution.py:365
  (1 shorter events, 0.0 us)
Async XLA Ops:
  3.2 9.8 %collective-permute-start = (bf16[4,6272]{1,0:T(4,128)(2,1)S(1)}, bf16[4,6272]{1,0:T(4,128)(2,1)S(1)}, u32[]{:S(2)}, u32[]{:S(2)}) collective-permute-start(bf16[4,6272]{1,0:T(4,128)(2,1)S(1)} %get-tuple-element.25), channel_id=1, source_target_pairs={{0,12},{4,8},{8,4},{12,0},{1,13},{5,9},{9,5},{13,1},{2,14},{6,10},... | collective-permute-start | bytes 150536 | tf_op jit(solution)/shard_map/ppermute | solution.py:69
  8.3 4.6 %collective-permute-start.1 = (bf16[4,2176]{1,0:T(4,128)(2,1)S(1)}, bf16[4,2176]{1,0:T(4,128)(2,1)S(1)}, u32[]{:S(2)}, u32[]{:S(2)}) collective-permute-start(bf16[4,2176]{1,0:T(4,128)(2,1)S(1)} %get-tuple-element.26), channel_id=1, source_target_pairs={{0,8},{4,12},{8,0},{12,4},{1,9},{5,13},{9,1},{13,5},{2,10},{6,14},... | collective-permute-start | bytes 52232 | tf_op jit(solution)/shard_map/ppermute | solution.py:69
  8.3 4.6 %collective-permute-start.2 = (bf16[4,2176]{1,0:T(4,128)(2,1)S(1)}, bf16[4,2176]{1,0:T(4,128)(2,1)S(1)}, u32[]{:S(2)}, u32[]{:S(2)}) collective-permute-start(bf16[4,2176]{1,0:T(4,128)(2,1)S(1)} %get-tuple-element.27), channel_id=1, source_target_pairs={{0,4},{4,0},{8,12},{12,8},{1,5},{5,1},{9,13},{13,9},{2,6},{6,2},{1... | collective-permute-start | bytes 52232 | tf_op jit(solution)/shard_map/ppermute | solution.py:69
  13.0 2.2 %collective-permute-start.3 = (bf16[12,2048]{1,0:T(8,128)(2,1)S(1)}, bf16[12,2048]{1,0:T(8,128)(2,1)S(1)}, u32[]{:S(2)}, u32[]{:S(2)}) collective-permute-start(bf16[12,2048]{1,0:T(8,128)(2,1)S(1)} %pack.1), channel_id=1, source_target_pairs={{0,1},{1,0},{2,3},{3,2},{4,5},{5,4},{6,7},{7,6},{8,9},{9,8},{10,11... | collective-permute-start | bytes 147464 | tf_op jit(solution)/shard_map/ppermute | solution.py:322
  13.1 4.9 %collective-permute-start.5 = (bf16[4,4096]{1,0:T(4,128)(2,1)S(1)}, bf16[4,4096]{1,0:T(4,128)(2,1)S(1)}, u32[]{:S(2)}, u32[]{:S(2)}) collective-permute-start(bf16[4,4096]{1,0:T(4,128)(2,1)S(1)} %get-tuple-element.31), channel_id=1, source_target_pairs={{0,8},{4,12},{8,0},{12,4},{1,9},{5,13},{9,1},{13,5},{2,10},{6,14},... | collective-permute-start | bytes 98312 | tf_op jit(solution)/shard_map/ppermute | solution.py:69
  15.2 3.9 %collective-permute-start.6 = (bf16[4,4096]{1,0:T(4,128)(2,1)S(1)}, bf16[4,4096]{1,0:T(4,128)(2,1)S(1)}, u32[]{:S(2)}, u32[]{:S(2)}) collective-permute-start(bf16[4,4096]{1,0:T(4,128)(2,1)S(1)} %get-tuple-element.32), channel_id=1, source_target_pairs={{0,4},{4,0},{8,12},{12,8},{1,5},{5,1},{9,13},{13,9},{2,6},{6,2},{1... | collective-permute-start | bytes 98312 | tf_op jit(solution)/shard_map/ppermute | solution.py:69
  15.3 7.8 %collective-permute-start.4 = (bf16[16,2432]{1,0:T(8,128)(2,1)S(1)}, bf16[16,2432]{1,0:T(8,128)(2,1)S(1)}, u32[]{:S(2)}, u32[]{:S(2)}) collective-permute-start(bf16[16,2432]{1,0:T(8,128)(2,1)S(1)} %get-tuple-element.29), channel_id=1, source_target_pairs={{0,16},{16,0},{1,17},{17,1},{2,18},{18,2},{3,19},{19,3},{4,20},{20... | collective-permute-start | bytes 233480 | tf_op jit(solution)/shard_map/ppermute | solution.py:69
  19.3 3.1 %collective-permute-start.9 = (f32[16,128]{1,0:T(8,128)S(1)}, f32[16,128]{1,0:T(8,128)S(1)}, u32[]{:S(2)}, u32[]{:S(2)}) collective-permute-start(f32[16,128]{1,0:T(8,128)S(1)} %backs.1.refs_2_), channel_id=1, source_target_pairs={{0,3},{1,2},{2,1},{3,0},{4,7},{5,6},{6,5},{7,4},{8,11},{9,10},{10,... | collective-permute-start | bytes 24584 | tf_op jit(solution)/shard_map/ppermute | solution.py:69
  19.5 3.7 %collective-permute-start.8 = (f32[16,128]{1,0:T(8,128)S(1)}, f32[16,128]{1,0:T(8,128)S(1)}, u32[]{:S(2)}, u32[]{:S(2)}) collective-permute-start(f32[16,128]{1,0:T(8,128)S(1)} %backs.1.refs_2_), channel_id=1, source_target_pairs={{0,2},{1,3},{2,0},{3,1},{4,6},{5,7},{6,4},{7,5},{8,10},{9,11},{10,... | collective-permute-start | bytes 24584 | tf_op jit(solution)/shard_map/ppermute | solution.py:69
  20.9 2.3 %collective-permute-start.7 = (f32[16,128]{1,0:T(8,128)S(1)}, f32[16,128]{1,0:T(8,128)S(1)}, u32[]{:S(2)}, u32[]{:S(2)}) collective-permute-start(f32[16,128]{1,0:T(8,128)S(1)} %backs.1.refs_2_), channel_id=1, source_target_pairs={{0,1},{1,0},{2,3},{3,2},{4,5},{5,4},{6,7},{7,6},{8,9},{9,8},{10,11... | collective-permute-start | bytes 24584 | tf_op jit(solution)/shard_map/ppermute | solution.py:69

commit v7 on v5

--- a/solution.py
+++ b/solution.py
@@ -194,12 +194,11 @@
         own_ref[p * block : (p + 1) * block, :] = down_term(pay_ref, share, share + p * block, block)
 
 
-def last_kernel(count, others, parts, pieces, *refs):
+def down_kernel(count, others, pieces, *refs):
     own_ref = refs[0]
     pays = refs[1 : 1 + others]
-    backs = refs[1 + others : 1 + others + parts]
-    ids_ref, match_ref, rows_ref, gate_ref, weight_ref = refs[1 + others + parts : 6 + others + parts]
-    gate_hbm, hidden_hbm, down_hbm, gate_out, hidden_out, down_out, sems = refs[6 + others + parts :]
+    rows_ref, gate_ref, weight_ref, match_ref = refs[1 + others : 5 + others]
+    hidden_hbm, down_hbm, match_out, hidden_out, down_out, sems = refs[5 + others :]
     units, share = own_ref.shape
     block = units // pieces
     copies = []
@@ -217,26 +216,29 @@
         part = pl.ds(p * block, block)
         write(p, down_out.at[part], down_hbm.at[0, part])
 
+    match_out[...] = match_ref[...]
+    upstream = dot(rows_ref[...], weight_ref[...], ((1,), (1,)))
+    scaled = (gate_ref[:, :1] * upstream).astype(jnp.bfloat16)
+    hidden_out[...] = dot(slot_order(count), scaled, ((0,), (0,))).astype(jnp.bfloat16)
+    write(pieces, hidden_out, hidden_hbm.at[0, 0])
+    for copy in copies:
+        copy.wait()
+
+
+def gate_kernel(count, ids_ref, match_ref, *refs):
+    backs, out_ref = refs[:-1], refs[-1]
     me = lax.axis_index("expert")
     ids = ids_ref[...]
     back = backs[0][...]
     for ref in backs[1:]:
         back = back + ref[...]
-    total = jnp.zeros(gate_out.shape, jnp.float32)
+    total = jnp.zeros(out_ref.shape, jnp.float32)
     for r in range(count):
         value = back[r * CAP : (r + 1) * CAP, :]
         match = match_ref[r * PAD : r * PAD + CAP, :]
         chosen = jnp.sum(jnp.where(match > 0, value, 0.0), axis=0, keepdims=True)
         total = total + jnp.where(ids == target(me, r, count), chosen, 0.0)
-    gate_out[...] = total
-    write(pieces, gate_out, gate_hbm)
-
-    upstream = dot(rows_ref[...], weight_ref[...], ((1,), (1,)))
-    scaled = (gate_ref[:, :1] * upstream).astype(jnp.bfloat16)
-    hidden_out[...] = dot(slot_order(count), scaled, ((0,), (0,))).astype(jnp.bfloat16)
-    write(pieces + 1, hidden_out, hidden_hbm.at[0, 0])
-    for copy in copies:
-        copy.wait()
+    out_ref[...] = total
 
 
 def on_device(grad_out, expert_ids, gate_values, saved_hidden, down_weight):
@@ -311,7 +313,7 @@
     )(*sends, received[JOINT], *theirs)
 
     others = [send(pays[r], "dp", r) for r in range(1, groups)]
-    backs = [back] + [send(back, "tensor", r) for r in range(1, tensors)]
+    backs = [back] + [send(back, "tensor", r) for r in reversed(range(1, tensors))]
 
     own = pl.pallas_call(
         functools.partial(own_kernel, pieces),
@@ -323,25 +325,34 @@
         name="own",
     )(pays[0])
 
-    gate_grad, hidden_grad, down_grad = pl.pallas_call(
-        functools.partial(last_kernel, count, groups - 1, tensors, pieces),
+    hidden_grad, down_grad, match = pl.pallas_call(
+        functools.partial(down_kernel, count, groups - 1, pieces),
         out_shape=[
-            jax.ShapeDtypeStruct(ids.shape, jnp.float32),
             jax.ShapeDtypeStruct(saved_hidden.shape, jnp.bfloat16),
             jax.ShapeDtypeStruct((1, units, share), jnp.float32),
+            jax.ShapeDtypeStruct(match.shape, jnp.float32),
         ],
-        in_specs=[VMEM] * (5 + groups + tensors),
-        out_specs=[HBM] * 3,
+        in_specs=[VMEM] * (4 + groups),
+        out_specs=[HBM, HBM, VMEM],
         scratch_shapes=[
-            pltpu.VMEM(ids.shape, jnp.float32),
             pltpu.VMEM((slots, units), jnp.bfloat16),
             pltpu.VMEM((units, share), jnp.float32),
-            pltpu.SemaphoreType.DMA((pieces + 2,)),
+            pltpu.SemaphoreType.DMA((pieces + 1,)),
         ],
         compiler_params=PARAMS,
         cost_estimate=cost(2 * slots * units * (width + share), 4 * units * share),
-        name="last",
-    )(own, *others, *backs, ids, match, rows, gate, weight)
+        name="down",
+    )(own, *others, rows, gate, weight, match)
+
+    gate_grad = pl.pallas_call(
+        functools.partial(gate_kernel, count),
+        out_shape=jax.ShapeDtypeStruct(ids.shape, jnp.float32),
+        in_specs=[VMEM] * (2 + tensors),
+        out_specs=VMEM,
+        compiler_params=PARAMS,
+        cost_estimate=cost(slots * tokens, 4 * slots * tokens),
+        name="gates",
+    )(ids, match, *backs)
     return (gate_grad.T, hidden_grad, down_grad)
 
 

time: 22.5 us -> 21.2 us (0.942)
  waiting for transfers between devices: 2.44 us -> 0.52 us
  Pallas kernels: 5.69 us -> 6.29 us
    ppermute x9, waiting for transfers between devices: 2.44 us -> 0.52 us  [send(): lax.ppermute(value, axis, [(i, give(i, step, size)) for i in range(size)])]
    pallas_call x1 -> x2, Pallas kernels: 2.24 us -> 2.83 us  [the longest x1 2.22 us: on_device(): pl.pallas_call(functools.partial(down_kernel, count, groups - 1, pieces),...]
  transfers between devices with their start and end apart: 9 -> 9, of which waited for: 3 -> 2; matrix products, arithmetic and copies ran while one was open for 0% -> 0% of each run, Pallas kernels for 4% -> 15%
where the time goes in v7:
time: 21.2 us; the launch traced here: 21 us
  starting transfers between devices  13.5 us (64%)
  Pallas kernels  6.29 us (30%)
  between operations  0.69 us (3%)
  waiting for transfers between devices  0.52 us (2%)
    ppermute x9, starting transfers between devices, send(): lax.ppermute(value, axis, [(i, give(i, step, size)) for i in range(size)])  13.5 us
    pallas_call x1, Pallas kernels, on_device(): pl.pallas_call(functools.partial(front_kernel, count, pieces), out_shape=...  2.59 us
    pallas_call x1, Pallas kernels, on_device(): pl.pallas_call(functools.partial(down_kernel, count, groups - 1, pieces),...  2.22 us
    pallas_call x1, Pallas kernels, on_device(): pl.pallas_call(functools.partial(gate_kernel, count), out_shape=jax.Shape...  0.61 us
    pallas_call x1, Pallas kernels, on_device(): pl.pallas_call(functools.partial(own_kernel, pieces), out_shape=jax.Shape...  0.59 us
    ppermute x9, waiting for transfers between devices, send(): lax.ppermute(value, axis, [(i, give(i, step, size)) for i in range(size)])  0.52 us
  transfers between devices with their start and end apart: 9, of which 2 were waited for; matrix products, arithmetic and copies ran while one was open for 0% of the time, Pallas kernels for 15%

profile of v7, /device:TPU:0, one launch (start us, length us, event | category | flops | bytes accessed | tf_op | source)
XLA Modules:
  0.0 21.0 jit_solution(4294499398866354725)
XLA Ops:
  0.6 2.6 %front.1 = (s32[8,128]{1,0:T(8,128)S(1)}, f32[32,128]{1,0:T(8,128)S(1)}, bf16[384,4096]{1,0:T(8,128)(2,1)S(1)}, bf16[16,384]{1,0:T(8,128)(2,1)S(1)}, bf16[4,4224...) custom-call(s32[8,128]{1,0:T(8,128)} %bitcast.4, ...), custom_call_target="tpu_custom_call" | custom-call | flops 134217728 | bytes 4194304 | tf_op jit(solution)/shard_map/front/pallas_call | solution.py:255
  3.2 5.1 %collective-permute-start = (bf16[8,4224]{1,0:T(8,128)(2,1)S(1)}, bf16[8,4224]{1,0:T(8,128)(2,1)S(1)}, u32[]{:S(2)}, u32[]{:S(2)}) collective-permute-start(bf16[8,4224]{1,0:T(8,128)(2,1)S(1)} %get-tuple-element.24.refs_1_), channel_id=1, source_target_pairs={{0,12},{4,8},{8,4},{12,0},{1,13},{5,9},{9,5},{13,1},{2,14},{6,10},... | collective-permute-start | bytes 202760 | tf_op jit(solution)/shard_map/ppermute | solution.py:60
  8.3 0.0 collective-permute-start.1
  8.3 0.6 %collective-permute-start.2 = (bf16[4,4224]{1,0:T(4,128)(2,1)S(1)}, bf16[4,4224]{1,0:T(4,128)(2,1)S(1)}, u32[]{:S(2)}, u32[]{:S(2)}) collective-permute-start(bf16[4,4224]{1,0:T(4,128)(2,1)S(1)} %get-tuple-element.26.refs_3_), channel_id=1, source_target_pairs={{0,4},{4,0},{8,12},{12,8},{1,5},{5,1},{9,13},{13,9},{2,6},{6,2},{1... | collective-permute-start | bytes 101384 | tf_op jit(solution)/shard_map/ppermute | solution.py:60
  9.0 2.3 %collective-permute-start.4 = (bf16[4,4096]{1,0:T(4,128)(2,1)S(1)}, bf16[4,4096]{1,0:T(4,128)(2,1)S(1)}, u32[]{:S(2)}, u32[]{:S(2)}) collective-permute-start(bf16[4,4096]{1,0:T(4,128)(2,1)S(1)} %get-tuple-element.35), channel_id=1, source_target_pairs={{0,8},{4,12},{8,0},{12,4},{1,9},{5,13},{9,1},{13,5},{2,10},{6,14},... | collective-permute-start | bytes 98312 | tf_op jit(solution)/shard_map/ppermute | solution.py:60
  11.3 2.0 %collective-permute-start.5 = (bf16[4,4096]{1,0:T(4,128)(2,1)S(1)}, bf16[4,4096]{1,0:T(4,128)(2,1)S(1)}, u32[]{:S(2)}, u32[]{:S(2)}) collective-permute-start(bf16[4,4096]{1,0:T(4,128)(2,1)S(1)} %get-tuple-element.36), channel_id=1, source_target_pairs={{0,4},{4,0},{8,12},{12,8},{1,5},{5,1},{9,13},{13,9},{2,6},{6,2},{1... | collective-permute-start | bytes 98312 | tf_op jit(solution)/shard_map/ppermute | solution.py:60
  13.3 0.2 %collective-permute-done.1.refs_2_ = bf16[4,4224]{1,0:T(4,128)(2,1)S(1)} collective-permute-done((bf16[4,4224]{1,0:T(4,128)(2,1)S(1)}, bf16[4,4224]{1,0:T(4,128)(2,1)S(1)}, u32[]{:S(2)}, u32[]{:S(2)}) %collective-permute-start.1) | collective-permute-done | bytes 33824 | tf_op jit(solution)/shard_map/ppermute | solution.py:60
  13.5 0.0 collective-permute-done.2.refs_3_
  13.5 0.0 collective-permute-done.refs_1_.refs_4_
  13.5 0.1 slots.1
  13.6 1.6 %collective-permute-start.3 = (bf16[16,2432]{1,0:T(8,128)(2,1)S(1)}, bf16[16,2432]{1,0:T(8,128)(2,1)S(1)}, u32[]{:S(2)}, u32[]{:S(2)}) collective-permute-start(bf16[16,2432]{1,0:T(8,128)(2,1)S(1)} %get-tuple-element.28), channel_id=1, source_target_pairs={{0,16},{16,0},{1,17},{17,1},{2,18},{18,2},{3,19},{19,3},{4,20},{20... | collective-permute-start | bytes 233480 | tf_op jit(solution)/shard_map/ppermute | solution.py:60
  15.2 0.0 collective-permute-done.4.refs_6_
  15.2 0.0 collective-permute-done.5.refs_7_
  15.2 0.2 backs.1.refs_0_
  15.4 0.0 collective-permute-start.8
  15.4 1.6 %collective-permute-start.7 = (f32[16,128]{1,0:T(8,128)S(1)}, f32[16,128]{1,0:T(8,128)S(1)}, u32[]{:S(2)}, u32[]{:S(2)}) collective-permute-start(f32[16,128]{1,0:T(8,128)S(1)} %backs.1.refs_0_), channel_id=1, source_target_pairs={{0,2},{1,3},{2,0},{3,1},{4,6},{5,7},{6,4},{7,5},{8,10},{9,11},{10,... | collective-permute-start | bytes 24584 | tf_op jit(solution)/shard_map/ppermute | solution.py:60
  17.0 0.3 %collective-permute-start.6 = (f32[16,128]{1,0:T(8,128)S(1)}, f32[16,128]{1,0:T(8,128)S(1)}, u32[]{:S(2)}, u32[]{:S(2)}) collective-permute-start(f32[16,128]{1,0:T(8,128)S(1)} %backs.1.refs_0_), channel_id=1, source_target_pairs={{0,1},{1,0},{2,3},{3,2},{4,5},{5,4},{6,7},{7,6},{8,9},{9,8},{10,11... | collective-permute-start | bytes 24584 | tf_op jit(solution)/shard_map/ppermute | solution.py:60
  17.2 0.6 %own.1.refs_0_ = bf16[384,2048]{1,0:T(8,128)(2,1)S(1)} custom-call(bf16[16,2432]{1,0:T(8,128)(2,1)S(1)} %get-tuple-element.27.pay_ref), custom_call_target="tpu_custom_call" | custom-call | flops 25165824 | bytes 1572864 | tf_op jit(solution)/shard_map/own/pallas_call | solution.py:318
  17.8 0.3 %collective-permute-done.3.refs_1_ = bf16[16,2432]{1,0:T(8,128)(2,1)S(1)} collective-permute-done((bf16[16,2432]{1,0:T(8,128)(2,1)S(1)}, bf16[16,2432]{1,0:T(8,128)(2,1)S(1)}, u32[]{:S(2)}, u32[]{:S(2)}) %collective-permute-start.3) | collective-permute-done | bytes 77856 | tf_op jit(solution)/shard_map/ppermute | solution.py:60
  18.1 2.2 %down.1 = (bf16[1,1,16,384]{3,2,1,0:T(8,128)(2,1)}, f32[1,384,2048]{2,1,0:T(8,128)}, f32[32,128]{1,0:T(8,128)S(1)}) custom-call(bf16[384,2048]{1,0:T(8,128)(2,1)S(1)} %own.1.refs_0_, bf16[16,2432]{1,0:T(8,128)(2,1)S(1)} %collective-permute-done.3.refs_1_, bf16[16,4096]{1,0:T(8,128)(2,1)S(1)} %get-tuple-element.29.refs_2_, ...), custom_call_target="tpu_custom_call" | custom-call | flops 75497472 | bytes 3145728 | tf_op jit(solution)/shard_map/down/pallas_call | solution.py:328
  20.3 0.0 collective-permute-done.8.refs_3_
  20.3 0.0 collective-permute-done.7.refs_2_
  20.4 0.0 collective-permute-done.6.refs_1_
  20.4 0.6 %gates.1 = f32[8,128]{1,0:T(8,128)} custom-call(s32[8,128]{1,0:T(8,128)S(1)} %get-tuple-element.21.ids_ref, f32[32,128]{1,0:T(8,128)S(1)} %get-tuple-element.33.match_ref, f32[16,128]{1,0:T(8,128)S(1)} %backs.1.refs_0_, f32[16,128]{1,0:T(8,128)S(1)} %collective-permute-done.6.refs_1_, f32[16,128]{1,0:T(8,128)S(1)} %collective-permute-done.7.refs_2_, ...), custom_call_target="tpu_custom_call" | custom-call | flops 2048 | bytes 8192 | tf_op jit(solution)/shard_map/gates/pallas_call | solution.py:347
Async XLA Ops:
  3.2 10.3 %collective-permute-start = (bf16[8,4224]{1,0:T(8,128)(2,1)S(1)}, bf16[8,4224]{1,0:T(8,128)(2,1)S(1)}, u32[]{:S(2)}, u32[]{:S(2)}) collective-permute-start(bf16[8,4224]{1,0:T(8,128)(2,1)S(1)} %get-tuple-element.24.refs_1_), channel_id=1, source_target_pairs={{0,12},{4,8},{8,4},{12,0},{1,13},{5,9},{9,5},{13,1},{2,14},{6,10},... | collective-permute-start | bytes 202760 | tf_op jit(solution)/shard_map/ppermute | solution.py:60
  8.3 5.2 %collective-permute-start.1 = (bf16[4,4224]{1,0:T(4,128)(2,1)S(1)}, bf16[4,4224]{1,0:T(4,128)(2,1)S(1)}, u32[]{:S(2)}, u32[]{:S(2)}) collective-permute-start(bf16[4,4224]{1,0:T(4,128)(2,1)S(1)} %get-tuple-element.25.refs_2_), channel_id=1, source_target_pairs={{0,8},{4,12},{8,0},{12,4},{1,9},{5,13},{9,1},{13,5},{2,10},{6,14},... | collective-permute-start | bytes 101384 | tf_op jit(solution)/shard_map/ppermute | solution.py:60
  8.3 5.2 %collective-permute-start.2 = (bf16[4,4224]{1,0:T(4,128)(2,1)S(1)}, bf16[4,4224]{1,0:T(4,128)(2,1)S(1)}, u32[]{:S(2)}, u32[]{:S(2)}) collective-permute-start(bf16[4,4224]{1,0:T(4,128)(2,1)S(1)} %get-tuple-element.26.refs_3_), channel_id=1, source_target_pairs={{0,4},{4,0},{8,12},{12,8},{1,5},{5,1},{9,13},{13,9},{2,6},{6,2},{1... | collective-permute-start | bytes 101384 | tf_op jit(solution)/shard_map/ppermute | solution.py:60
  9.0 6.2 %collective-permute-start.4 = (bf16[4,4096]{1,0:T(4,128)(2,1)S(1)}, bf16[4,4096]{1,0:T(4,128)(2,1)S(1)}, u32[]{:S(2)}, u32[]{:S(2)}) collective-permute-start(bf16[4,4096]{1,0:T(4,128)(2,1)S(1)} %get-tuple-element.35), channel_id=1, source_target_pairs={{0,8},{4,12},{8,0},{12,4},{1,9},{5,13},{9,1},{13,5},{2,10},{6,14},... | collective-permute-start | bytes 98312 | tf_op jit(solution)/shard_map/ppermute | solution.py:60
  11.3 3.9 %collective-permute-start.5 = (bf16[4,4096]{1,0:T(4,128)(2,1)S(1)}, bf16[4,4096]{1,0:T(4,128)(2,1)S(1)}, u32[]{:S(2)}, u32[]{:S(2)}) collective-permute-start(bf16[4,4096]{1,0:T(4,128)(2,1)S(1)} %get-tuple-element.36), channel_id=1, source_target_pairs={{0,4},{4,0},{8,12},{12,8},{1,5},{5,1},{9,13},{13,9},{2,6},{6,2},{1... | collective-permute-start | bytes 98312 | tf_op jit(solution)/shard_map/ppermute | solution.py:60
  13.6 4.5 %collective-permute-start.3 = (bf16[16,2432]{1,0:T(8,128)(2,1)S(1)}, bf16[16,2432]{1,0:T(8,128)(2,1)S(1)}, u32[]{:S(2)}, u32[]{:S(2)}) collective-permute-start(bf16[16,2432]{1,0:T(8,128)(2,1)S(1)} %get-tuple-element.28), channel_id=1, source_target_pairs={{0,16},{16,0},{1,17},{17,1},{2,18},{18,2},{3,19},{19,3},{4,20},{20... | collective-permute-start | bytes 233480 | tf_op jit(solution)/shard_map/ppermute | solution.py:60
  15.4 5.0 %collective-permute-start.8 = (f32[16,128]{1,0:T(8,128)S(1)}, f32[16,128]{1,0:T(8,128)S(1)}, u32[]{:S(2)}, u32[]{:S(2)}) collective-permute-start(f32[16,128]{1,0:T(8,128)S(1)} %backs.1.refs_0_), channel_id=1, source_target_pairs={{0,3},{1,2},{2,1},{3,0},{4,7},{5,6},{6,5},{7,4},{8,11},{9,10},{10,... | collective-permute-start | bytes 24584 | tf_op jit(solution)/shard_map/ppermute | solution.py:60
  15.4 5.0 %collective-permute-start.7 = (f32[16,128]{1,0:T(8,128)S(1)}, f32[16,128]{1,0:T(8,128)S(1)}, u32[]{:S(2)}, u32[]{:S(2)}) collective-permute-start(f32[16,128]{1,0:T(8,128)S(1)} %backs.1.refs_0_), channel_id=1, source_target_pairs={{0,2},{1,3},{2,0},{3,1},{4,6},{5,7},{6,4},{7,5},{8,10},{9,11},{10,... | collective-permute-start | bytes 24584 | tf_op jit(solution)/shard_map/ppermute | solution.py:60
  17.0 3.4 %collective-permute-start.6 = (f32[16,128]{1,0:T(8,128)S(1)}, f32[16,128]{1,0:T(8,128)S(1)}, u32[]{:S(2)}, u32[]{:S(2)}) collective-permute-start(f32[16,128]{1,0:T(8,128)S(1)} %backs.1.refs_0_), channel_id=1, source_target_pairs={{0,1},{1,0},{2,3},{3,2},{4,5},{5,4},{6,7},{7,6},{8,9},{9,8},{10,11... | collective-permute-start | bytes 24584 | tf_op jit(solution)/shard_map/ppermute | solution.py:60

commit v8 on v7

--- a/solution.py
+++ b/solution.py
@@ -9,7 +9,6 @@
 
 CAP = 4
 LANES = 128
-JOINT = 1
 AFTER_WAIT = (10**9, 10**7)
 PAD = 8
 VMEM = pl.BlockSpec(memory_space=pltpu.VMEM)
@@ -49,10 +48,6 @@
 
 def reply(step, size):
     return step if paired(size) else -step % size
-
-
-def apart(size):
-    return [r for r in range(size) if r != JOINT]
 
 
 def send(value, axis, step, give=target):
@@ -110,7 +105,7 @@
     hidden_ref[...] = dot(slot_order(count), saved, ((1,), (0,))).astype(jnp.bfloat16)
     here = lax.broadcasted_iota(jnp.int32, (rows, slots), 0)
     there = lax.broadcasted_iota(jnp.int32, (rows, slots), 1)
-    place = here % PAD - jnp.where(here // PAD == JOINT, CAP, 0)
+    place = here % PAD - jnp.where(here // PAD == count - 1, CAP, 0)
     chosen = (place >= 0) & (place < CAP) & (there == target(me, here // PAD, count) * CAP + place)
     hidden = dot(chosen.astype(jnp.bfloat16), saved, ((1,), (0,))).astype(jnp.bfloat16)
 
@@ -121,7 +116,7 @@
         part = slice(r * PAD, r * PAD + sends[r].shape[0])
         gate = jnp.broadcast_to(slot_gate[part], (sends[r].shape[0], LANES))
         sends[r][:, width:] = gate.astype(jnp.bfloat16)
-        if r != JOINT:
+        if r != count - 1:
             sends[r][:, :width] = picked_ref[part, :].astype(jnp.bfloat16)
     block = units // pieces
     for p in range(pieces):
@@ -130,10 +125,10 @@
         part = slice(p * block, (p + 1) * block)
         term = dot(hidden[:, part], weight_ref[part, :], ((1,), (0,)))
         total_ref[...] = term if p == 0 else total_ref[...] + term
-    for product, r in zip(products, apart(count)):
+    for r, product in enumerate(products):
         product[...] = total_ref[r * PAD : r * PAD + CAP, :].astype(jnp.bfloat16)
-    part = slice(JOINT * PAD, (JOINT + 1) * PAD)
-    sends[JOINT][:, :width] = (picked_ref[part, :] + total_ref[part, :]).astype(jnp.bfloat16)
+    part = slice((count - 1) * PAD, count * PAD)
+    sends[-1][:, :width] = (picked_ref[part, :] + total_ref[part, :]).astype(jnp.bfloat16)
 
 
 def slot_order(count):
@@ -168,12 +163,12 @@
 def back_kernel(count, *refs):
     sent = refs[:count]
     joint_ref = refs[count]
-    products = dict(zip(apart(count), refs[count + 1 : 2 * count]))
+    products = refs[count + 1 : 2 * count]
     back_ref = refs[2 * count]
     width = products[0].shape[1]
     for r in range(count):
         step = reply(r, count)
-        if step != JOINT:
+        if step != count - 1:
             theirs = products[step][...].astype(jnp.float32)
         else:
             theirs = joint_ref[:, :width].astype(jnp.float32)[CAP:]
@@ -187,26 +182,29 @@
     return dot(hidden, pay_ref[:, :share], ((0,), (0,))).astype(jnp.bfloat16)
 
 
-def own_kernel(pieces, pay_ref, own_ref):
+def upstream_kernel(count, pieces, rows_ref, gate_ref, weight_ref, pay_ref, product_ref, *refs):
+    hidden_hbm, own_ref, product_out, hidden_out, sem = refs
+    product_out[...] = product_ref[...]
+    upstream = dot(rows_ref[...], weight_ref[...], ((1,), (1,)))
+    scaled = (gate_ref[:, :1] * upstream).astype(jnp.bfloat16)
+    hidden_out[...] = dot(slot_order(count), scaled, ((0,), (0,))).astype(jnp.bfloat16)
+    write = pltpu.make_async_copy(hidden_out, hidden_hbm.at[0, 0], sem)
+    write.start()
     units, share = own_ref.shape
     block = units // pieces
     for p in range(pieces):
         own_ref[p * block : (p + 1) * block, :] = down_term(pay_ref, share, share + p * block, block)
-
-
-def down_kernel(count, others, pieces, *refs):
-    own_ref = refs[0]
-    pays = refs[1 : 1 + others]
-    rows_ref, gate_ref, weight_ref, match_ref = refs[1 + others : 5 + others]
-    hidden_hbm, down_hbm, match_out, hidden_out, down_out, sems = refs[5 + others :]
+    write.wait()
+
+
+def down_kernel(others, pieces, *refs):
+    own_ref, match_ref = refs[:2]
+    pays = refs[2 : 2 + others]
+    down_hbm, match_out, down_out, sems = refs[2 + others :]
+    match_out[...] = match_ref[...]
     units, share = own_ref.shape
     block = units // pieces
     copies = []
-
-    def write(n, values, destination):
-        copies.append(pltpu.make_async_copy(values, destination, sems.at[n]))
-        copies[-1].start()
-
     for p in range(pieces):
         part = slice(p * block, (p + 1) * block)
         total = own_ref[part, :].astype(jnp.float32)
@@ -214,13 +212,8 @@
             total = total + down_term(pay_ref, share, share + p * block, block).astype(jnp.float32)
         down_out[part, :] = total
         part = pl.ds(p * block, block)
-        write(p, down_out.at[part], down_hbm.at[0, part])
-
-    match_out[...] = match_ref[...]
-    upstream = dot(rows_ref[...], weight_ref[...], ((1,), (1,)))
-    scaled = (gate_ref[:, :1] * upstream).astype(jnp.bfloat16)
-    hidden_out[...] = dot(slot_order(count), scaled, ((0,), (0,))).astype(jnp.bfloat16)
-    write(pieces, hidden_out, hidden_hbm.at[0, 0])
+        copies.append(pltpu.make_async_copy(down_out.at[part], down_hbm.at[0, part], sems.at[p]))
+        copies[-1].start()
     for copy in copies:
         copy.wait()
 
@@ -261,7 +254,7 @@
             jax.ShapeDtypeStruct((slots, units), jnp.bfloat16),
         ]
         + [
-            jax.ShapeDtypeStruct((PAD if r == JOINT else CAP, width + LANES), jnp.bfloat16)
+            jax.ShapeDtypeStruct((PAD if r == count - 1 else CAP, width + LANES), jnp.bfloat16)
             for r in range(count)
         ]
         + [jax.ShapeDtypeStruct((CAP, width), jnp.bfloat16)] * (count - 1),
@@ -282,7 +275,7 @@
     sends, products = rest[:count], rest[count:]
 
     received = [sends[0]] + [send(sends[r], "expert", r) for r in range(1, count)]
-    theirs = [products[0]] + [send(products[r - 1], "expert", r) for r in range(JOINT + 1, count)]
+    theirs = [products[0]] + [send(products[r], "expert", r) for r in range(1, count - 1)]
 
     rows, gate, *pays = pl.pallas_call(
         functools.partial(slot_kernel, count, groups),
@@ -302,6 +295,23 @@
         name="slots",
     )(hidden, *received)
 
+    others = [send(pays[r], "dp", r) for r in range(1, groups)]
+
+    hidden_grad, own, theirs[0] = pl.pallas_call(
+        functools.partial(upstream_kernel, count, pieces),
+        out_shape=[
+            jax.ShapeDtypeStruct(saved_hidden.shape, jnp.bfloat16),
+            jax.ShapeDtypeStruct((units, share), jnp.bfloat16),
+            jax.ShapeDtypeStruct((CAP, width), jnp.bfloat16),
+        ],
+        in_specs=[VMEM] * 5,
+        out_specs=[HBM, VMEM, VMEM],
+        scratch_shapes=[pltpu.VMEM((slots, units), jnp.bfloat16), pltpu.SemaphoreType.DMA(())],
+        compiler_params=PARAMS,
+        cost_estimate=cost(2 * slots * units * (width + share), 2 * units * width),
+        name="upstream",
+    )(rows, gate, weight, pays[0], theirs[0])
+
     back = pl.pallas_call(
         functools.partial(back_kernel, count),
         out_shape=jax.ShapeDtypeStruct((slots, LANES), jnp.float32),
@@ -310,39 +320,26 @@
         compiler_params=PARAMS,
         cost_estimate=cost(*AFTER_WAIT),
         name="backs",
-    )(*sends, received[JOINT], *theirs)
-
-    others = [send(pays[r], "dp", r) for r in range(1, groups)]
+    )(*sends, received[-1], *theirs)
+
     backs = [back] + [send(back, "tensor", r) for r in reversed(range(1, tensors))]
 
-    own = pl.pallas_call(
-        functools.partial(own_kernel, pieces),
-        out_shape=jax.ShapeDtypeStruct((units, share), jnp.bfloat16),
-        in_specs=[VMEM],
-        out_specs=VMEM,
-        compiler_params=PARAMS,
-        cost_estimate=cost(2 * slots * units * share, 2 * units * share),
-        name="own",
-    )(pays[0])
-
-    hidden_grad, down_grad, match = pl.pallas_call(
-        functools.partial(down_kernel, count, groups - 1, pieces),
+    down_grad, match = pl.pallas_call(
+        functools.partial(down_kernel, groups - 1, pieces),
         out_shape=[
-            jax.ShapeDtypeStruct(saved_hidden.shape, jnp.bfloat16),
             jax.ShapeDtypeStruct((1, units, share), jnp.float32),
             jax.ShapeDtypeStruct(match.shape, jnp.float32),
         ],
-        in_specs=[VMEM] * (4 + groups),
-        out_specs=[HBM, HBM, VMEM],
+        in_specs=[VMEM] * (1 + groups),
+        out_specs=[HBM, VMEM],
         scratch_shapes=[
-            pltpu.VMEM((slots, units), jnp.bfloat16),
             pltpu.VMEM((units, share), jnp.float32),
-            pltpu.SemaphoreType.DMA((pieces + 1,)),
-        ],
-        compiler_params=PARAMS,
-        cost_estimate=cost(2 * slots * units * (width + share), 4 * units * share),
+            pltpu.SemaphoreType.DMA((pieces,)),
+        ],
+        compiler_params=PARAMS,
+        cost_estimate=cost(2 * slots * units * share, 4 * units * share),
         name="down",
-    )(own, *others, rows, gate, weight, match)
+    )(own, match, *others)
 
     gate_grad = pl.pallas_call(
         functools.partial(gate_kernel, count),

time: 21.2 us -> 23.4 us (1.10)
  waiting for transfers between devices: 0.52 us -> 2.77 us
  Pallas kernels: 6.29 us -> 7.41 us
  starting transfers between devices: 13.5 us -> 12.4 us
    ppermute x9, waiting for transfers between devices: 0.52 us -> 2.77 us  [send(): lax.ppermute(value, axis, [(i, give(i, step, size)) for i in range(size)])]
    pallas_call x2, Pallas kernels: 2.81 us -> 3.94 us  [the longest x1 2 us: on_device(): pl.pallas_call(functools.partial(down_kernel, groups - 1, pieces), out_sh...]
    ppermute x9, starting transfers between devices: 13.5 us -> 12.4 us  [send(): lax.ppermute(value, axis, [(i, give(i, step, size)) for i in range(size)])]
  transfers between devices with their start and end apart: 9 -> 9, of which waited for: 2 -> 2; matrix products, arithmetic and copies ran while one was open for 0% -> 0% of each run, Pallas kernels for 15% -> 18%
where the time goes in v8:
time: 23.4 us; the launch traced here: 23.2 us
  starting transfers between devices  12.4 us (53%)
  Pallas kernels  7.41 us (32%)
  waiting for transfers between devices  2.77 us (12%)
  between operations  0.71 us (3%)
    ppermute x9, starting transfers between devices, send(): lax.ppermute(value, axis, [(i, give(i, step, size)) for i in range(size)])  12.4 us
    ppermute x9, waiting for transfers between devices, send(): lax.ppermute(value, axis, [(i, give(i, step, size)) for i in range(size)])  2.77 us
    pallas_call x1, Pallas kernels, on_device(): pl.pallas_call(functools.partial(front_kernel, count, pieces), out_shape=...  2.58 us
    pallas_call x1, Pallas kernels, on_device(): pl.pallas_call(functools.partial(down_kernel, groups - 1, pieces), out_sh...  2 us
    pallas_call x1, Pallas kernels, on_device(): pl.pallas_call(functools.partial(upstream_kernel, count, pieces), out_sha...  1.94 us
    pallas_call x1, Pallas kernels, on_device(): pl.pallas_call(functools.partial(gate_kernel, count), out_shape=jax.Shape...  0.61 us
  transfers between devices with their start and end apart: 9, of which 2 were waited for; matrix products, arithmetic and copies ran while one was open for 0% of the time, Pallas kernels for 18%

profile of v8, /device:TPU:0, one launch (start us, length us, event | category | flops | bytes accessed | tf_op | source)
XLA Modules:
  0.0 23.2 jit_solution(5540154726966644405)
XLA Ops:
  0.6 2.6 %front.1 = (s32[8,128]{1,0:T(8,128)S(1)}, f32[32,128]{1,0:T(8,128)S(1)}, bf16[384,4096]{1,0:T(8,128)(2,1)S(1)}, bf16[16,384]{1,0:T(8,128)(2,1)S(1)}, bf16[4,4224...) custom-call(s32[8,128]{1,0:T(8,128)} %bitcast.4, ...), custom_call_target="tpu_custom_call" | custom-call | flops 134217728 | bytes 4194304 | tf_op jit(solution)/shard_map/front/pallas_call | solution.py:248
  3.2 3.1 %collective-permute-start.2 = (bf16[8,4224]{1,0:T(8,128)(2,1)S(1)}, bf16[8,4224]{1,0:T(8,128)(2,1)S(1)}, u32[]{:S(2)}, u32[]{:S(2)}) collective-permute-start(bf16[8,4224]{1,0:T(8,128)(2,1)S(1)} %get-tuple-element.28.refs_3_), channel_id=1, source_target_pairs={{0,4},{4,0},{8,12},{12,8},{1,5},{5,1},{9,13},{13,9},{2,6},{6,2},{1... | collective-permute-start | bytes 202760 | tf_op jit(solution)/shard_map/ppermute | solution.py:55
  6.3 2.5 %collective-permute-start = (bf16[4,4224]{1,0:T(4,128)(2,1)S(1)}, bf16[4,4224]{1,0:T(4,128)(2,1)S(1)}, u32[]{:S(2)}, u32[]{:S(2)}) collective-permute-start(bf16[4,4224]{1,0:T(4,128)(2,1)S(1)} %get-tuple-element.26.refs_1_), channel_id=1, source_target_pairs={{0,12},{4,8},{8,4},{12,0},{1,13},{5,9},{9,5},{13,1},{2,14},{6,10},... | collective-permute-start | bytes 101384 | tf_op jit(solution)/shard_map/ppermute | solution.py:55
  8.8 0.1 collective-permute-start.1
  8.9 2.9 %collective-permute-start.4 = (bf16[4,4096]{1,0:T(4,128)(2,1)S(1)}, bf16[4,4096]{1,0:T(4,128)(2,1)S(1)}, u32[]{:S(2)}, u32[]{:S(2)}) collective-permute-start(bf16[4,4096]{1,0:T(4,128)(2,1)S(1)} %get-tuple-element.39), channel_id=1, source_target_pairs={{0,12},{4,8},{8,4},{12,0},{1,13},{5,9},{9,5},{13,1},{2,14},{6,10},... | collective-permute-start | bytes 98312 | tf_op jit(solution)/shard_map/ppermute | solution.py:55
  11.8 0.3 %collective-permute-start.5 = (bf16[4,4096]{1,0:T(4,128)(2,1)S(1)}, bf16[4,4096]{1,0:T(4,128)(2,1)S(1)}, u32[]{:S(2)}, u32[]{:S(2)}) collective-permute-start(bf16[4,4096]{1,0:T(4,128)(2,1)S(1)} %get-tuple-element.40), channel_id=1, source_target_pairs={{0,8},{4,12},{8,0},{12,4},{1,9},{5,13},{9,1},{13,5},{2,10},{6,14},... | collective-permute-start | bytes 98312 | tf_op jit(solution)/shard_map/ppermute | solution.py:55
  12.2 0.3 %collective-permute-done.refs_1_ = bf16[4,4224]{1,0:T(4,128)(2,1)S(1)} collective-permute-done((bf16[4,4224]{1,0:T(4,128)(2,1)S(1)}, bf16[4,4224]{1,0:T(4,128)(2,1)S(1)}, u32[]{:S(2)}, u32[]{:S(2)}) %collective-permute-start) | collective-permute-done | bytes 33824 | tf_op jit(solution)/shard_map/ppermute | solution.py:55
  12.5 2.4 %collective-permute-done.1.refs_2_ = bf16[4,4224]{1,0:T(4,128)(2,1)S(1)} collective-permute-done((bf16[4,4224]{1,0:T(4,128)(2,1)S(1)}, bf16[4,4224]{1,0:T(4,128)(2,1)S(1)}, u32[]{:S(2)}, u32[]{:S(2)}) %collective-permute-start.1) | collective-permute-done | bytes 33824 | tf_op jit(solution)/shard_map/ppermute | solution.py:55
  14.9 0.0 collective-permute-done.2.refs_3_.refs_4_
  14.9 0.1 slots.1
  15.0 1.6 %collective-permute-start.3 = (bf16[16,2432]{1,0:T(8,128)(2,1)S(1)}, bf16[16,2432]{1,0:T(8,128)(2,1)S(1)}, u32[]{:S(2)}, u32[]{:S(2)}) collective-permute-start(bf16[16,2432]{1,0:T(8,128)(2,1)S(1)} %get-tuple-element.36), channel_id=1, source_target_pairs={{0,16},{16,0},{1,17},{17,1},{2,18},{18,2},{3,19},{19,3},{4,20},{20... | collective-permute-start | bytes 233480 | tf_op jit(solution)/shard_map/ppermute | solution.py:55
  16.6 1.9 %upstream.1 = (bf16[1,1,16,384]{3,2,1,0:T(8,128)(2,1)}, bf16[384,2048]{1,0:T(8,128)(2,1)S(1)}, bf16[4,4096]{1,0:T(4,128)(2,1)S(1)}) custom-call(bf16[16,4096]{1,0:T(8,128)(2,1)S(1)} %get-tuple-element.29.rows_ref, f32[16,128]{1,0:T(8,128)S(1)} %get-tuple-element.30.gate_ref, bf16[384,4096]{1,0:T(8,128)(2,1)S(1)} %get-tuple-element.31.weight_ref, ...), custom_call_target="tpu_custom_call" | custom-call | flops 75497472 | bytes 3145728 | tf_op jit(solution)/shard_map/upstream/pallas_call | solution.py:300
  18.5 0.0 collective-permute-done.4.refs_6_
  18.5 0.0 collective-permute-done.5.refs_7_
  18.6 0.2 backs.1.refs_0_
  18.7 0.0 collective-permute-start.8
  18.7 1.6 %collective-permute-start.7 = (f32[16,128]{1,0:T(8,128)S(1)}, f32[16,128]{1,0:T(8,128)S(1)}, u32[]{:S(2)}, u32[]{:S(2)}) collective-permute-start(f32[16,128]{1,0:T(8,128)S(1)} %backs.1.refs_0_), channel_id=1, source_target_pairs={{0,2},{1,3},{2,0},{3,1},{4,6},{5,7},{6,4},{7,5},{8,10},{9,11},{10,... | collective-permute-start | bytes 24584 | tf_op jit(solution)/shard_map/ppermute | solution.py:55
  20.3 0.3 %collective-permute-start.6 = (f32[16,128]{1,0:T(8,128)S(1)}, f32[16,128]{1,0:T(8,128)S(1)}, u32[]{:S(2)}, u32[]{:S(2)}) collective-permute-start(f32[16,128]{1,0:T(8,128)S(1)} %backs.1.refs_0_), channel_id=1, source_target_pairs={{0,1},{1,0},{2,3},{3,2},{4,5},{5,4},{6,7},{7,6},{8,9},{9,8},{10,11... | collective-permute-start | bytes 24584 | tf_op jit(solution)/shard_map/ppermute | solution.py:55
  20.6 0.0 collective-permute-done.3.refs_2_
  20.6 2.0 %down.1 = (f32[1,384,2048]{2,1,0:T(8,128)}, f32[32,128]{1,0:T(8,128)S(1)}) custom-call(bf16[384,2048]{1,0:T(8,128)(2,1)S(1)} %get-tuple-element.34.refs_0_, f32[32,128]{1,0:T(8,128)S(1)} %get-tuple-element.35.refs_1_, bf16[16,2432]{1,0:T(8,128)(2,1)S(1)} %collective-permute-done.3.refs_2_), custom_call_target="tpu_custom_call" | custom-call | flops 25165824 | bytes 3145728 | tf_op jit(solution)/shard_map/down/pallas_call | solution.py:327
  22.6 0.0 collective-permute-done.8.refs_3_
  22.6 0.0 collective-permute-done.7.refs_2_
  22.6 0.0 collective-permute-done.6.refs_1_
  22.6 0.6 %gates.1 = f32[8,128]{1,0:T(8,128)} custom-call(s32[8,128]{1,0:T(8,128)S(1)} %get-tuple-element.23.ids_ref, f32[32,128]{1,0:T(8,128)S(1)} %get-tuple-element.37.match_ref, f32[16,128]{1,0:T(8,128)S(1)} %backs.1.refs_0_, f32[16,128]{1,0:T(8,128)S(1)} %collective-permute-done.6.refs_1_, f32[16,128]{1,0:T(8,128)S(1)} %collective-permute-done.7.refs_2_, ...), custom_call_target="tpu_custom_call" | custom-call | flops 2048 | bytes 8192 | tf_op jit(solution)/shard_map/gates/pallas_call | solution.py:344
Async XLA Ops:
  3.2 11.7 %collective-permute-start.2 = (bf16[8,4224]{1,0:T(8,128)(2,1)S(1)}, bf16[8,4224]{1,0:T(8,128)(2,1)S(1)}, u32[]{:S(2)}, u32[]{:S(2)}) collective-permute-start(bf16[8,4224]{1,0:T(8,128)(2,1)S(1)} %get-tuple-element.28.refs_3_), channel_id=1, source_target_pairs={{0,4},{4,0},{8,12},{12,8},{1,5},{5,1},{9,13},{13,9},{2,6},{6,2},{1... | collective-permute-start | bytes 202760 | tf_op jit(solution)/shard_map/ppermute | solution.py:55
  6.3 6.2 %collective-permute-start = (bf16[4,4224]{1,0:T(4,128)(2,1)S(1)}, bf16[4,4224]{1,0:T(4,128)(2,1)S(1)}, u32[]{:S(2)}, u32[]{:S(2)}) collective-permute-start(bf16[4,4224]{1,0:T(4,128)(2,1)S(1)} %get-tuple-element.26.refs_1_), channel_id=1, source_target_pairs={{0,12},{4,8},{8,4},{12,0},{1,13},{5,9},{9,5},{13,1},{2,14},{6,10},... | collective-permute-start | bytes 101384 | tf_op jit(solution)/shard_map/ppermute | solution.py:55
  8.8 6.1 %collective-permute-start.1 = (bf16[4,4224]{1,0:T(4,128)(2,1)S(1)}, bf16[4,4224]{1,0:T(4,128)(2,1)S(1)}, u32[]{:S(2)}, u32[]{:S(2)}) collective-permute-start(bf16[4,4224]{1,0:T(4,128)(2,1)S(1)} %get-tuple-element.27.refs_2_), channel_id=1, source_target_pairs={{0,8},{4,12},{8,0},{12,4},{1,9},{5,13},{9,1},{13,5},{2,10},{6,14},... | collective-permute-start | bytes 101384 | tf_op jit(solution)/shard_map/ppermute | solution.py:55
  8.9 9.6 %collective-permute-start.4 = (bf16[4,4096]{1,0:T(4,128)(2,1)S(1)}, bf16[4,4096]{1,0:T(4,128)(2,1)S(1)}, u32[]{:S(2)}, u32[]{:S(2)}) collective-permute-start(bf16[4,4096]{1,0:T(4,128)(2,1)S(1)} %get-tuple-element.39), channel_id=1, source_target_pairs={{0,12},{4,8},{8,4},{12,0},{1,13},{5,9},{9,5},{13,1},{2,14},{6,10},... | collective-permute-start | bytes 98312 | tf_op jit(solution)/shard_map/ppermute | solution.py:55
  11.8 6.7 %collective-permute-start.5 = (bf16[4,4096]{1,0:T(4,128)(2,1)S(1)}, bf16[4,4096]{1,0:T(4,128)(2,1)S(1)}, u32[]{:S(2)}, u32[]{:S(2)}) collective-permute-start(bf16[4,4096]{1,0:T(4,128)(2,1)S(1)} %get-tuple-element.40), channel_id=1, source_target_pairs={{0,8},{4,12},{8,0},{12,4},{1,9},{5,13},{9,1},{13,5},{2,10},{6,14},... | collective-permute-start | bytes 98312 | tf_op jit(solution)/shard_map/ppermute | solution.py:55
  15.0 5.6 %collective-permute-start.3 = (bf16[16,2432]{1,0:T(8,128)(2,1)S(1)}, bf16[16,2432]{1,0:T(8,128)(2,1)S(1)}, u32[]{:S(2)}, u32[]{:S(2)}) collective-permute-start(bf16[16,2432]{1,0:T(8,128)(2,1)S(1)} %get-tuple-element.36), channel_id=1, source_target_pairs={{0,16},{16,0},{1,17},{17,1},{2,18},{18,2},{3,19},{19,3},{4,20},{20... | collective-permute-start | bytes 233480 | tf_op jit(solution)/shard_map/ppermute | solution.py:55
  18.7 3.9 %collective-permute-start.8 = (f32[16,128]{1,0:T(8,128)S(1)}, f32[16,128]{1,0:T(8,128)S(1)}, u32[]{:S(2)}, u32[]{:S(2)}) collective-permute-start(f32[16,128]{1,0:T(8,128)S(1)} %backs.1.refs_0_), channel_id=1, source_target_pairs={{0,3},{1,2},{2,1},{3,0},{4,7},{5,6},{6,5},{7,4},{8,11},{9,10},{10,... | collective-permute-start | bytes 24584 | tf_op jit(solution)/shard_map/ppermute | solution.py:55
  18.7 3.9 %collective-permute-start.7 = (f32[16,128]{1,0:T(8,128)S(1)}, f32[16,128]{1,0:T(8,128)S(1)}, u32[]{:S(2)}, u32[]{:S(2)}) collective-permute-start(f32[16,128]{1,0:T(8,128)S(1)} %backs.1.refs_0_), channel_id=1, source_target_pairs={{0,2},{1,3},{2,0},{3,1},{4,6},{5,7},{6,4},{7,5},{8,10},{9,11},{10,... | collective-permute-start | bytes 24584 | tf_op jit(solution)/shard_map/ppermute | solution.py:55
  20.3 2.3 %collective-permute-start.6 = (f32[16,128]{1,0:T(8,128)S(1)}, f32[16,128]{1,0:T(8,128)S(1)}, u32[]{:S(2)}, u32[]{:S(2)}) collective-permute-start(f32[16,128]{1,0:T(8,128)S(1)} %backs.1.refs_0_), channel_id=1, source_target_pairs={{0,1},{1,0},{2,3},{3,2},{4,5},{5,4},{6,7},{7,6},{8,9},{9,8},{10,11... | collective-permute-start | bytes 24584 | tf_op jit(solution)/shard_map/ppermute | solution.py:55

commit v9 on v7

--- a/solution.py
+++ b/solution.py
@@ -9,7 +9,6 @@
 
 CAP = 4
 LANES = 128
-JOINT = 1
 AFTER_WAIT = (10**9, 10**7)
 PAD = 8
 VMEM = pl.BlockSpec(memory_space=pltpu.VMEM)
@@ -52,7 +51,7 @@
 
 
 def apart(size):
-    return [r for r in range(size) if r != JOINT]
+    return range(2, size - 1)
 
 
 def send(value, axis, step, give=target):
@@ -62,10 +61,10 @@
 
 def front_kernel(count, pieces, *refs):
     ids_hbm, gates_hbm, grad_hbm, hidden_hbm, weight_hbm = refs[:5]
-    ids_ref, match_ref, weight_ref, hidden_ref = refs[5:9]
-    sends = refs[9 : 9 + count]
-    products = refs[9 + count : 8 + 2 * count]
-    gates_ref, grad_ref, saved_ref, picked_ref, total_ref, sems = refs[8 + 2 * count :]
+    ids_ref, match_ref, weight_ref, hidden_ref, picked_ref, gate_ref, total_ref = refs[5:12]
+    sends = dict(zip(range(1, count), refs[12 : 11 + count]))
+    products = dict(zip(apart(count), refs[11 + count : 11 + count + len(apart(count))]))
+    gates_ref, grad_ref, saved_ref, sems = refs[-4:]
     units, width = weight_ref.shape
     top, tokens = ids_ref.shape
     pairs = [(ids_hbm, ids_ref), (gates_hbm, gates_ref), (hidden_hbm.at[0, 0], saved_ref)]
@@ -110,19 +109,17 @@
     hidden_ref[...] = dot(slot_order(count), saved, ((1,), (0,))).astype(jnp.bfloat16)
     here = lax.broadcasted_iota(jnp.int32, (rows, slots), 0)
     there = lax.broadcasted_iota(jnp.int32, (rows, slots), 1)
-    place = here % PAD - jnp.where(here // PAD == JOINT, CAP, 0)
-    chosen = (place >= 0) & (place < CAP) & (there == target(me, here // PAD, count) * CAP + place)
+    chosen = (here % PAD < CAP) & (there == target(me, here // PAD, count) * CAP + here % PAD)
     hidden = dot(chosen.astype(jnp.bfloat16), saved, ((1,), (0,))).astype(jnp.bfloat16)
 
     for copy in copies[3:5]:
         copy.wait()
+    gate_ref[...] = jnp.broadcast_to(slot_gate, gate_ref.shape)
     picked_ref[...] = dot(match, grad_ref[...], ((1,), (0,)))
-    for r in range(count):
-        part = slice(r * PAD, r * PAD + sends[r].shape[0])
-        gate = jnp.broadcast_to(slot_gate[part], (sends[r].shape[0], LANES))
-        sends[r][:, width:] = gate.astype(jnp.bfloat16)
-        if r != JOINT:
-            sends[r][:, :width] = picked_ref[part, :].astype(jnp.bfloat16)
+    for r, send_ref in sends.items():
+        part = slice(r * PAD, r * PAD + CAP)
+        send_ref[:, :width] = picked_ref[part, :].astype(jnp.bfloat16)
+        send_ref[:, width : width + LANES] = gate_ref[part, :].astype(jnp.bfloat16)
     block = units // pieces
     for p in range(pieces):
         for copy in copies[5 + 2 * p : 7 + 2 * p]:
@@ -130,10 +127,12 @@
         part = slice(p * block, (p + 1) * block)
         term = dot(hidden[:, part], weight_ref[part, :], ((1,), (0,)))
         total_ref[...] = term if p == 0 else total_ref[...] + term
-    for product, r in zip(products, apart(count)):
-        product[...] = total_ref[r * PAD : r * PAD + CAP, :].astype(jnp.bfloat16)
-    part = slice(JOINT * PAD, (JOINT + 1) * PAD)
-    sends[JOINT][:, :width] = (picked_ref[part, :] + total_ref[part, :]).astype(jnp.bfloat16)
+    for r, send_ref in sends.items():
+        product = total_ref[r * PAD : r * PAD + CAP, :].astype(jnp.bfloat16)
+        if r in products:
+            products[r][...] = product
+        else:
+            send_ref[:, width + LANES :] = product
 
 
 def slot_order(count):
@@ -141,65 +140,55 @@
     slots = count * CAP
     here = lax.broadcasted_iota(jnp.int32, (slots, slots), 0)
     saved = lax.broadcasted_iota(jnp.int32, (slots, slots), 1)
-    return (saved == source(me, here // CAP, count) * CAP + here % CAP).astype(jnp.bfloat16)
-
-
-def slot_kernel(count, groups, hidden_ref, *refs):
-    received = refs[:count]
-    rows_ref, gate_ref = refs[count : count + 2]
-    pays = refs[count + 2 : count + 2 + groups]
-    wide_ref, weighted_ref = refs[count + 2 + groups :]
+    return (saved == source(me, (here // CAP + 1) % count, count) * CAP + here % CAP).astype(jnp.bfloat16)
+
+
+def slot_kernel(count, groups, hidden_ref, picked_ref, sent_gate_ref, *refs):
+    received, refs = refs[: count - 1], refs[count - 1 :]
+    rows_ref, gate_ref = refs[:2]
+    pays = refs[2 : 2 + groups]
+    wide_ref, weighted_ref = refs[2 + groups :]
     width = rows_ref.shape[1]
-    for r in range(count):
-        wide_ref[r * CAP : (r + 1) * CAP, :] = received[r][...].astype(jnp.float32)[:CAP]
-    rows = wide_ref[:, :width]
-    gate = wide_ref[:, width:]
-    gate_ref[...] = gate
+    share = width // groups
+    slots = count * CAP
+    wide_ref[slots - CAP : slots, :] = picked_ref[:CAP, :]
+    gates = sent_gate_ref[:CAP, :].astype(jnp.bfloat16).astype(jnp.float32)
+    gate_ref[slots - CAP :, :] = gates
+    for r in range(1, count):
+        part = slice((r - 1) * CAP, r * CAP)
+        wide_ref[part, :] = received[r - 1][:, :width].astype(jnp.float32)
+        gate_ref[part, :] = received[r - 1][:, width : width + LANES].astype(jnp.float32)
+    rows = wide_ref[:slots, :]
     rows_ref[...] = rows.astype(jnp.bfloat16)
-    weighted_ref[...] = (gate[:, :1] * rows).astype(jnp.bfloat16)
-    share = width // groups
+    weighted_ref[...] = (gate_ref[:, :1] * rows).astype(jnp.bfloat16)
     me = lax.axis_index("dp")
     for r in range(groups):
-        group = target(me, r, groups)
-        pays[r][:, :share] = weighted_ref[:, pl.ds(pl.multiple_of(group * share, share), share)]
+        begin = pl.multiple_of(target(me, r, groups) * share, share)
+        pays[r][:, :share] = weighted_ref[:, pl.ds(begin, share)]
         pays[r][:, share:] = hidden_ref[...]
 
 
-def back_kernel(count, *refs):
-    sent = refs[:count]
-    joint_ref = refs[count]
-    products = dict(zip(apart(count), refs[count + 1 : 2 * count]))
-    back_ref = refs[2 * count]
-    width = products[0].shape[1]
+def back_kernel(count, picked_ref, total_ref, *refs):
+    received = refs[: count - 1]
+    products = dict(zip(apart(count), refs[count - 1 : -1]))
+    back_ref = refs[-1]
+    width = picked_ref.shape[1]
     for r in range(count):
         step = reply(r, count)
-        if step != JOINT:
-            theirs = products[step][...].astype(jnp.float32)
+        if step == 0:
+            theirs = total_ref[:CAP, :]
         else:
-            theirs = joint_ref[:, :width].astype(jnp.float32)[CAP:]
-        mine = sent[r][:, :width].astype(jnp.float32)[:CAP]
+            ref = products[step] if step in products else received[step - 1]
+            theirs = ref[:, ref.shape[1] - width :].astype(jnp.float32)
+        mine = picked_ref[r * PAD : r * PAD + CAP, :]
         back = jnp.sum(mine * theirs, axis=1, keepdims=True)
         back_ref[r * CAP : (r + 1) * CAP, :] = jnp.broadcast_to(back, (CAP, LANES))
 
 
-def down_term(pay_ref, share, start, block):
-    hidden = pay_ref[:, pl.ds(start, block)]
-    return dot(hidden, pay_ref[:, :share], ((0,), (0,))).astype(jnp.bfloat16)
-
-
-def own_kernel(pieces, pay_ref, own_ref):
-    units, share = own_ref.shape
-    block = units // pieces
-    for p in range(pieces):
-        own_ref[p * block : (p + 1) * block, :] = down_term(pay_ref, share, share + p * block, block)
-
-
-def down_kernel(count, others, pieces, *refs):
-    own_ref = refs[0]
-    pays = refs[1 : 1 + others]
-    rows_ref, gate_ref, weight_ref, match_ref = refs[1 + others : 5 + others]
-    hidden_hbm, down_hbm, match_out, hidden_out, down_out, sems = refs[5 + others :]
-    units, share = own_ref.shape
+def down_kernel(count, groups, pieces, rows_ref, gate_ref, weight_ref, match_ref, *refs):
+    pays = refs[:groups]
+    hidden_hbm, down_hbm, match_out, hidden_out, down_out, sems = refs[groups:]
+    units, share = down_out.shape
     block = units // pieces
     copies = []
 
@@ -209,9 +198,12 @@
 
     for p in range(pieces):
         part = slice(p * block, (p + 1) * block)
-        total = own_ref[part, :].astype(jnp.float32)
+        total = None
         for pay_ref in pays:
-            total = total + down_term(pay_ref, share, share + p * block, block).astype(jnp.float32)
+            hidden = pay_ref[:, share + p * block : share + (p + 1) * block]
+            term = dot(hidden, pay_ref[:, :share], ((0,), (0,)))
+            term = term.astype(jnp.bfloat16).astype(jnp.float32)
+            total = term if total is None else total + term
         down_out[part, :] = total
         part = pl.ds(p * block, block)
         write(p, down_out.at[part], down_hbm.at[0, part])
@@ -252,37 +244,36 @@
     share = width // groups
     pieces = units // LANES
 
-    ids, match, weight, hidden, *rest = pl.pallas_call(
+    joined = [width + LANES if r in apart(count) else 2 * width + LANES for r in range(1, count)]
+    ids, match, weight, hidden, picked, sent_gate, total, *rest = pl.pallas_call(
         functools.partial(front_kernel, count, pieces),
         out_shape=[
             jax.ShapeDtypeStruct((top, tokens), jnp.int32),
             jax.ShapeDtypeStruct((count * PAD, tokens), jnp.float32),
             jax.ShapeDtypeStruct((units, width), jnp.bfloat16),
             jax.ShapeDtypeStruct((slots, units), jnp.bfloat16),
+            jax.ShapeDtypeStruct((count * PAD, width), jnp.float32),
+            jax.ShapeDtypeStruct((count * PAD, LANES), jnp.float32),
+            jax.ShapeDtypeStruct((count * PAD, width), jnp.float32),
         ]
-        + [
-            jax.ShapeDtypeStruct((PAD if r == JOINT else CAP, width + LANES), jnp.bfloat16)
-            for r in range(count)
-        ]
-        + [jax.ShapeDtypeStruct((CAP, width), jnp.bfloat16)] * (count - 1),
+        + [jax.ShapeDtypeStruct((CAP, size), jnp.bfloat16) for size in joined]
+        + [jax.ShapeDtypeStruct((CAP, width), jnp.bfloat16)] * len(apart(count)),
         in_specs=[HBM] * 5,
-        out_specs=[VMEM] * (3 + 2 * count),
+        out_specs=[VMEM] * (6 + count + len(apart(count))),
         scratch_shapes=[
             pltpu.VMEM((top, tokens), jnp.bfloat16),
             pltpu.VMEM((tokens, width), jnp.bfloat16),
             pltpu.VMEM((slots, units), jnp.bfloat16),
-            pltpu.VMEM((count * PAD, width), jnp.float32),
-            pltpu.VMEM((count * PAD, width), jnp.float32),
             pltpu.SemaphoreType.DMA((5 + 2 * pieces,)),
         ],
         compiler_params=PARAMS,
         cost_estimate=cost(2 * count * PAD * (tokens + units) * width, 2 * (tokens + units) * width),
         name="front",
     )(*in_hbm(expert_ids.T, gate_values.T, grad_out, saved_hidden, down_weight))
-    sends, products = rest[:count], rest[count:]
-
-    received = [sends[0]] + [send(sends[r], "expert", r) for r in range(1, count)]
-    theirs = [products[0]] + [send(products[r - 1], "expert", r) for r in range(JOINT + 1, count)]
+    sends, products = rest[: count - 1], rest[count - 1 :]
+
+    received = [send(x, "expert", r) for r, x in enumerate(sends, 1)]
+    theirs = [send(x, "expert", r) for r, x in zip(apart(count), products)]
 
     rows, gate, *pays = pl.pallas_call(
         functools.partial(slot_kernel, count, groups),
@@ -291,42 +282,32 @@
             jax.ShapeDtypeStruct((slots, LANES), jnp.float32),
         ]
         + [jax.ShapeDtypeStruct((slots, share + units), jnp.bfloat16)] * groups,
-        in_specs=[VMEM] * (1 + count),
+        in_specs=[VMEM] * (2 + count),
         out_specs=[VMEM] * (2 + groups),
         scratch_shapes=[
-            pltpu.VMEM((slots, width + LANES), jnp.float32),
+            pltpu.VMEM((slots + PAD, width), jnp.float32),
             pltpu.VMEM((slots, width), jnp.bfloat16),
         ],
         compiler_params=PARAMS,
         cost_estimate=cost(4 * slots * width, 8 * slots * width),
         name="slots",
-    )(hidden, *received)
+    )(hidden, picked, sent_gate, *received)
 
     back = pl.pallas_call(
         functools.partial(back_kernel, count),
         out_shape=jax.ShapeDtypeStruct((slots, LANES), jnp.float32),
-        in_specs=[VMEM] * (2 * count),
+        in_specs=[VMEM] * (1 + count + len(theirs)),
         out_specs=VMEM,
         compiler_params=PARAMS,
         cost_estimate=cost(*AFTER_WAIT),
         name="backs",
-    )(*sends, received[JOINT], *theirs)
-
-    others = [send(pays[r], "dp", r) for r in range(1, groups)]
+    )(picked, total, *received, *theirs)
+
+    pays = [pays[0]] + [send(pays[r], "dp", r) for r in range(1, groups)]
     backs = [back] + [send(back, "tensor", r) for r in reversed(range(1, tensors))]
 
-    own = pl.pallas_call(
-        functools.partial(own_kernel, pieces),
-        out_shape=jax.ShapeDtypeStruct((units, share), jnp.bfloat16),
-        in_specs=[VMEM],
-        out_specs=VMEM,
-        compiler_params=PARAMS,
-        cost_estimate=cost(2 * slots * units * share, 2 * units * share),
-        name="own",
-    )(pays[0])
-
     hidden_grad, down_grad, match = pl.pallas_call(
-        functools.partial(down_kernel, count, groups - 1, pieces),
+        functools.partial(down_kernel, count, groups, pieces),
         out_shape=[
             jax.ShapeDtypeStruct(saved_hidden.shape, jnp.bfloat16),
             jax.ShapeDtypeStruct((1, units, share), jnp.float32),
@@ -340,9 +321,9 @@
             pltpu.SemaphoreType.DMA((pieces + 1,)),
         ],
         compiler_params=PARAMS,
-        cost_estimate=cost(2 * slots * units * (width + share), 4 * units * share),
+        cost_estimate=cost(2 * slots * units * (width + 2 * share), 4 * units * share),
         name="down",
-    )(own, *others, rows, gate, weight, match)
+    )(rows, gate, weight, match, *pays)
 
     gate_grad = pl.pallas_call(
         functools.partial(gate_kernel, count),

time: 21.2 us -> 21.8 us (1.028)
  waiting for transfers between devices: 0.52 us -> 3.27 us
  starting transfers between devices: 13.5 us -> 11.5 us
    ppermute x9 -> x8, waiting for transfers between devices: 0.52 us -> 3.27 us  [send(): lax.ppermute(value, axis, [(i, give(i, step, size)) for i in range(size)])]
    ppermute x9 -> x8, starting transfers between devices: 13.5 us -> 11.5 us  [send(): lax.ppermute(value, axis, [(i, give(i, step, size)) for i in range(size)])]
    pallas_call x2 -> x1, Pallas kernels: 2.81 us -> 2.68 us  [on_device(): pl.pallas_call(functools.partial(down_kernel, count, groups, pieces), out...]
  transfers between devices with their start and end apart: 9 -> 8, of which waited for: 2 -> 2; matrix products, arithmetic and copies ran while one was open for 0% -> 0% of each run, Pallas kernels for 15% -> 14%
where the time goes in v9:
time: 21.8 us; the launch traced here: 21.6 us
  starting transfers between devices  11.5 us (53%)
  Pallas kernels  6.15 us (28%)
  waiting for transfers between devices  3.27 us (15%)
  between operations  0.69 us (3%)
    ppermute x8, starting transfers between devices, send(): lax.ppermute(value, axis, [(i, give(i, step, size)) for i in range(size)])  11.5 us
    ppermute x8, waiting for transfers between devices, send(): lax.ppermute(value, axis, [(i, give(i, step, size)) for i in range(size)])  3.27 us
    pallas_call x1, Pallas kernels, on_device(): pl.pallas_call(functools.partial(down_kernel, count, groups, pieces), out...  2.68 us
    pallas_call x1, Pallas kernels, on_device(): pl.pallas_call(functools.partial(front_kernel, count, pieces), out_shape=...  2.59 us
    pallas_call x1, Pallas kernels, on_device(): pl.pallas_call(functools.partial(gate_kernel, count), out_shape=jax.Shape...  0.61 us
  transfers between devices with their start and end apart: 8, of which 2 were waited for; matrix products, arithmetic and copies ran while one was open for 0% of the time, Pallas kernels for 14%

profile of v9, /device:TPU:0, one launch (start us, length us, event | category | flops | bytes accessed | tf_op | source)
XLA Modules:
  0.0 21.6 jit_solution(4783166268057968913)
XLA Ops:
  0.6 2.6 %front.1 = (s32[8,128]{1,0:T(8,128)S(1)}, f32[32,128]{1,0:T(8,128)S(1)}, bf16[384,4096]{1,0:T(8,128)(2,1)S(1)}, bf16[16,384]{1,0:T(8,128)(2,1)S(1)}, f32[32,4096...) custom-call(s32[8,128]{1,0:T(8,128)} %bitcast.4, ...), custom_call_target="tpu_custom_call" | custom-call | flops 134217728 | bytes 4194304 | tf_op jit(solution)/shard_map/front/pallas_call | solution.py:248
  3.2 5.1 %collective-permute-start = (bf16[4,8320]{1,0:T(4,128)(2,1)S(1)}, bf16[4,8320]{1,0:T(4,128)(2,1)S(1)}, u32[]{:S(2)}, u32[]{:S(2)}) collective-permute-start(bf16[4,8320]{1,0:T(4,128)(2,1)S(1)} %get-tuple-element.25), channel_id=1, source_target_pairs={{0,12},{4,8},{8,4},{12,0},{1,13},{5,9},{9,5},{13,1},{2,14},{6,10},... | collective-permute-start | bytes 199688 | tf_op jit(solution)/shard_map/ppermute | solution.py:59
  8.3 0.0 collective-permute-start.2
  8.3 0.6 %collective-permute-start.1 = (bf16[4,4224]{1,0:T(4,128)(2,1)S(1)}, bf16[4,4224]{1,0:T(4,128)(2,1)S(1)}, u32[]{:S(2)}, u32[]{:S(2)}) collective-permute-start(bf16[4,4224]{1,0:T(4,128)(2,1)S(1)} %get-tuple-element.26), channel_id=1, source_target_pairs={{0,8},{4,12},{8,0},{12,4},{1,9},{5,13},{9,1},{13,5},{2,10},{6,14},... | collective-permute-start | bytes 101384 | tf_op jit(solution)/shard_map/ppermute | solution.py:59
  9.0 2.3 %collective-permute-start.4 = (bf16[4,4096]{1,0:T(4,128)(2,1)S(1)}, bf16[4,4096]{1,0:T(4,128)(2,1)S(1)}, u32[]{:S(2)}, u32[]{:S(2)}) collective-permute-start(bf16[4,4096]{1,0:T(4,128)(2,1)S(1)} %get-tuple-element.36), channel_id=1, source_target_pairs={{0,8},{4,12},{8,0},{12,4},{1,9},{5,13},{9,1},{13,5},{2,10},{6,14},... | collective-permute-start | bytes 98312 | tf_op jit(solution)/shard_map/ppermute | solution.py:59
  11.3 2.4 %collective-permute-done.1.refs_1_ = bf16[4,4224]{1,0:T(4,128)(2,1)S(1)} collective-permute-done((bf16[4,4224]{1,0:T(4,128)(2,1)S(1)}, bf16[4,4224]{1,0:T(4,128)(2,1)S(1)}, u32[]{:S(2)}, u32[]{:S(2)}) %collective-permute-start.1) | collective-permute-done | bytes 33824 | tf_op jit(solution)/shard_map/ppermute | solution.py:59
  13.6 0.0 collective-permute-done.refs_0_
  13.7 0.0 collective-permute-done.2.refs_2_
  13.7 0.1 slots.1
  13.8 1.6 %collective-permute-start.3 = (bf16[16,2432]{1,0:T(8,128)(2,1)S(1)}, bf16[16,2432]{1,0:T(8,128)(2,1)S(1)}, u32[]{:S(2)}, u32[]{:S(2)}) collective-permute-start(bf16[16,2432]{1,0:T(8,128)(2,1)S(1)} %get-tuple-element.33), channel_id=1, source_target_pairs={{0,16},{16,0},{1,17},{17,1},{2,18},{18,2},{3,19},{19,3},{4,20},{20... | collective-permute-start | bytes 233480 | tf_op jit(solution)/shard_map/ppermute | solution.py:59
  15.3 0.0 collective-permute-done.4.refs_3_
  15.3 0.2 backs.1.refs_0_
  15.5 0.0 collective-permute-start.7
  15.5 1.6 %collective-permute-start.6 = (f32[16,128]{1,0:T(8,128)S(1)}, f32[16,128]{1,0:T(8,128)S(1)}, u32[]{:S(2)}, u32[]{:S(2)}) collective-permute-start(f32[16,128]{1,0:T(8,128)S(1)} %backs.1.refs_0_), channel_id=1, source_target_pairs={{0,2},{1,3},{2,0},{3,1},{4,6},{5,7},{6,4},{7,5},{8,10},{9,11},{10,... | collective-permute-start | bytes 24584 | tf_op jit(solution)/shard_map/ppermute | solution.py:59
  17.1 0.3 %collective-permute-start.5 = (f32[16,128]{1,0:T(8,128)S(1)}, f32[16,128]{1,0:T(8,128)S(1)}, u32[]{:S(2)}, u32[]{:S(2)}) collective-permute-start(f32[16,128]{1,0:T(8,128)S(1)} %backs.1.refs_0_), channel_id=1, source_target_pairs={{0,1},{1,0},{2,3},{3,2},{4,5},{5,4},{6,7},{7,6},{8,9},{9,8},{10,11... | collective-permute-start | bytes 24584 | tf_op jit(solution)/shard_map/ppermute | solution.py:59
  17.4 0.9 %collective-permute-done.3.refs_1_ = bf16[16,2432]{1,0:T(8,128)(2,1)S(1)} collective-permute-done((bf16[16,2432]{1,0:T(8,128)(2,1)S(1)}, bf16[16,2432]{1,0:T(8,128)(2,1)S(1)}, u32[]{:S(2)}, u32[]{:S(2)}) %collective-permute-start.3) | collective-permute-done | bytes 77856 | tf_op jit(solution)/shard_map/ppermute | solution.py:59
  18.2 2.7 %down.1 = (bf16[1,1,16,384]{3,2,1,0:T(8,128)(2,1)}, f32[1,384,2048]{2,1,0:T(8,128)}, f32[32,128]{1,0:T(8,128)S(1)}) custom-call(bf16[16,4096]{1,0:T(8,128)(2,1)S(1)} %get-tuple-element.28.rows_ref, f32[16,128]{1,0:T(8,128)S(1)} %get-tuple-element.29.gate_ref, bf16[384,4096]{1,0:T(8,128)(2,1)S(1)} %get-tuple-element.30.weight_ref, ...), custom_call_target="tpu_custom_call" | custom-call | flops 100663296 | bytes 3145728 | tf_op jit(solution)/shard_map/down/pallas_call | solution.py:309
  20.9 0.0 collective-permute-done.7.refs_3_
  20.9 0.0 collective-permute-done.6.refs_2_
  20.9 0.0 collective-permute-done.5.refs_1_
  21.0 0.6 %gates.1 = f32[8,128]{1,0:T(8,128)} custom-call(s32[8,128]{1,0:T(8,128)S(1)} %get-tuple-element.21.ids_ref, f32[32,128]{1,0:T(8,128)S(1)} %get-tuple-element.34.match_ref, f32[16,128]{1,0:T(8,128)S(1)} %backs.1.refs_0_, f32[16,128]{1,0:T(8,128)S(1)} %collective-permute-done.5.refs_1_, f32[16,128]{1,0:T(8,128)S(1)} %collective-permute-done.6.refs_2_, ...), custom_call_target="tpu_custom_call" | custom-call | flops 2048 | bytes 8192 | tf_op jit(solution)/shard_map/gates/pallas_call | solution.py:328
Async XLA Ops:
  3.2 10.4 %collective-permute-start = (bf16[4,8320]{1,0:T(4,128)(2,1)S(1)}, bf16[4,8320]{1,0:T(4,128)(2,1)S(1)}, u32[]{:S(2)}, u32[]{:S(2)}) collective-permute-start(bf16[4,8320]{1,0:T(4,128)(2,1)S(1)} %get-tuple-element.25), channel_id=1, source_target_pairs={{0,12},{4,8},{8,4},{12,0},{1,13},{5,9},{9,5},{13,1},{2,14},{6,10},... | collective-permute-start | bytes 199688 | tf_op jit(solution)/shard_map/ppermute | solution.py:59
  8.3 5.3 %collective-permute-start.2 = (bf16[4,8320]{1,0:T(4,128)(2,1)S(1)}, bf16[4,8320]{1,0:T(4,128)(2,1)S(1)}, u32[]{:S(2)}, u32[]{:S(2)}) collective-permute-start(bf16[4,8320]{1,0:T(4,128)(2,1)S(1)} %get-tuple-element.27), channel_id=1, source_target_pairs={{0,4},{4,0},{8,12},{12,8},{1,5},{5,1},{9,13},{13,9},{2,6},{6,2},{1... | collective-permute-start | bytes 199688 | tf_op jit(solution)/shard_map/ppermute | solution.py:59
  8.3 5.3 %collective-permute-start.1 = (bf16[4,4224]{1,0:T(4,128)(2,1)S(1)}, bf16[4,4224]{1,0:T(4,128)(2,1)S(1)}, u32[]{:S(2)}, u32[]{:S(2)}) collective-permute-start(bf16[4,4224]{1,0:T(4,128)(2,1)S(1)} %get-tuple-element.26), channel_id=1, source_target_pairs={{0,8},{4,12},{8,0},{12,4},{1,9},{5,13},{9,1},{13,5},{2,10},{6,14},... | collective-permute-start | bytes 101384 | tf_op jit(solution)/shard_map/ppermute | solution.py:59
  9.0 6.3 %collective-permute-start.4 = (bf16[4,4096]{1,0:T(4,128)(2,1)S(1)}, bf16[4,4096]{1,0:T(4,128)(2,1)S(1)}, u32[]{:S(2)}, u32[]{:S(2)}) collective-permute-start(bf16[4,4096]{1,0:T(4,128)(2,1)S(1)} %get-tuple-element.36), channel_id=1, source_target_pairs={{0,8},{4,12},{8,0},{12,4},{1,9},{5,13},{9,1},{13,5},{2,10},{6,14},... | collective-permute-start | bytes 98312 | tf_op jit(solution)/shard_map/ppermute | solution.py:59
  13.8 4.5 %collective-permute-start.3 = (bf16[16,2432]{1,0:T(8,128)(2,1)S(1)}, bf16[16,2432]{1,0:T(8,128)(2,1)S(1)}, u32[]{:S(2)}, u32[]{:S(2)}) collective-permute-start(bf16[16,2432]{1,0:T(8,128)(2,1)S(1)} %get-tuple-element.33), channel_id=1, source_target_pairs={{0,16},{16,0},{1,17},{17,1},{2,18},{18,2},{3,19},{19,3},{4,20},{20... | collective-permute-start | bytes 233480 | tf_op jit(solution)/shard_map/ppermute | solution.py:59
  15.5 5.4 %collective-permute-start.7 = (f32[16,128]{1,0:T(8,128)S(1)}, f32[16,128]{1,0:T(8,128)S(1)}, u32[]{:S(2)}, u32[]{:S(2)}) collective-permute-start(f32[16,128]{1,0:T(8,128)S(1)} %backs.1.refs_0_), channel_id=1, source_target_pairs={{0,3},{1,2},{2,1},{3,0},{4,7},{5,6},{6,5},{7,4},{8,11},{9,10},{10,... | collective-permute-start | bytes 24584 | tf_op jit(solution)/shard_map/ppermute | solution.py:59
  15.5 5.4 %collective-permute-start.6 = (f32[16,128]{1,0:T(8,128)S(1)}, f32[16,128]{1,0:T(8,128)S(1)}, u32[]{:S(2)}, u32[]{:S(2)}) collective-permute-start(f32[16,128]{1,0:T(8,128)S(1)} %backs.1.refs_0_), channel_id=1, source_target_pairs={{0,2},{1,3},{2,0},{3,1},{4,6},{5,7},{6,4},{7,5},{8,10},{9,11},{10,... | collective-permute-start | bytes 24584 | tf_op jit(solution)/shard_map/ppermute | solution.py:59
  17.1 3.9 %collective-permute-start.5 = (f32[16,128]{1,0:T(8,128)S(1)}, f32[16,128]{1,0:T(8,128)S(1)}, u32[]{:S(2)}, u32[]{:S(2)}) collective-permute-start(f32[16,128]{1,0:T(8,128)S(1)} %backs.1.refs_0_), channel_id=1, source_target_pairs={{0,1},{1,0},{2,3},{3,2},{4,5},{5,4},{6,7},{7,6},{8,9},{9,8},{10,11... | collective-permute-start | bytes 24584 | tf_op jit(solution)/shard_map/ppermute | solution.py:59

commit v10 on v9

--- a/solution.py
+++ b/solution.py
@@ -59,11 +59,12 @@
     return lax.ppermute(value, axis, [(i, give(i, step, size)) for i in range(size)])
 
 
-def front_kernel(count, pieces, *refs):
+def front_kernel(count, groups, pieces, *refs):
     ids_hbm, gates_hbm, grad_hbm, hidden_hbm, weight_hbm = refs[:5]
     ids_ref, match_ref, weight_ref, hidden_ref, picked_ref, gate_ref, total_ref = refs[5:12]
     sends = dict(zip(range(1, count), refs[12 : 11 + count]))
     products = dict(zip(apart(count), refs[11 + count : 11 + count + len(apart(count))]))
+    early = refs[-3 - groups : -4]
     gates_ref, grad_ref, saved_ref, sems = refs[-4:]
     units, width = weight_ref.shape
     top, tokens = ids_ref.shape
@@ -107,6 +108,7 @@
     slots = count * CAP
     saved = saved_ref[...]
     hidden_ref[...] = dot(slot_order(count), saved, ((1,), (0,))).astype(jnp.bfloat16)
+    spread = dot(slot_order(count, PAD), saved, ((1,), (0,)))
     here = lax.broadcasted_iota(jnp.int32, (rows, slots), 0)
     there = lax.broadcasted_iota(jnp.int32, (rows, slots), 1)
     chosen = (here % PAD < CAP) & (there == target(me, here // PAD, count) * CAP + here % PAD)
@@ -120,6 +122,15 @@
         part = slice(r * PAD, r * PAD + CAP)
         send_ref[:, :width] = picked_ref[part, :].astype(jnp.bfloat16)
         send_ref[:, width : width + LANES] = gate_ref[part, :].astype(jnp.bfloat16)
+    share = width // groups
+    group = lax.axis_index("dp")
+    for r, early_ref in enumerate(early, 1):
+        begin = pl.multiple_of(target(group, r, groups) * share, share)
+        weighted = gate_ref[:CAP, :1] * picked_ref[:CAP, pl.ds(begin, share)]
+        early_ref[:, :share] = weighted.astype(jnp.bfloat16)
+        for k in range(count):
+            part = slice(share + k * units, share + (k + 1) * units)
+            early_ref[:, part] = spread[k * PAD : k * PAD + CAP].astype(jnp.bfloat16)
     block = units // pieces
     for p in range(pieces):
         for copy in copies[5 + 2 * p : 7 + 2 * p]:
@@ -135,37 +146,51 @@
             send_ref[:, width + LANES :] = product
 
 
-def slot_order(count):
+def slot_order(count, lines=CAP):
     me = lax.axis_index("expert")
-    slots = count * CAP
-    here = lax.broadcasted_iota(jnp.int32, (slots, slots), 0)
-    saved = lax.broadcasted_iota(jnp.int32, (slots, slots), 1)
-    return (saved == source(me, (here // CAP + 1) % count, count) * CAP + here % CAP).astype(jnp.bfloat16)
+    here = lax.broadcasted_iota(jnp.int32, (count * lines, count * CAP), 0)
+    saved = lax.broadcasted_iota(jnp.int32, (count * lines, count * CAP), 1)
+    place = here % lines
+    block = source(me, (here // lines + 1) % count, count)
+    return ((saved == block * CAP + place) & (place < CAP)).astype(jnp.bfloat16)
 
 
 def slot_kernel(count, groups, hidden_ref, picked_ref, sent_gate_ref, *refs):
     received, refs = refs[: count - 1], refs[count - 1 :]
-    rows_ref, gate_ref = refs[:2]
-    pays = refs[2 : 2 + groups]
-    wide_ref, weighted_ref = refs[2 + groups :]
+    early, refs = refs[: groups - 1], refs[groups - 1 :]
+    rows_ref, gate_ref, own_ref = refs[:3]
+    lates, others = refs[3 : 2 + groups], refs[2 + groups : 1 + 2 * groups]
+    wide_ref, spread_ref, units_ref = refs[1 + 2 * groups :]
     width = rows_ref.shape[1]
     share = width // groups
     slots = count * CAP
     wide_ref[slots - CAP : slots, :] = picked_ref[:CAP, :]
-    gates = sent_gate_ref[:CAP, :].astype(jnp.bfloat16).astype(jnp.float32)
-    gate_ref[slots - CAP :, :] = gates
+    gate_ref[slots - CAP :, :] = sent_gate_ref[:CAP, :]
     for r in range(1, count):
         part = slice((r - 1) * CAP, r * CAP)
-        wide_ref[part, :] = received[r - 1][:, :width].astype(jnp.float32)
-        gate_ref[part, :] = received[r - 1][:, width : width + LANES].astype(jnp.float32)
+        rows = received[r - 1][:, :width].astype(jnp.float32)
+        gate = received[r - 1][:, width : width + LANES].astype(jnp.float32)
+        wide_ref[part, :] = rows
+        gate_ref[part, :] = gate
+        spread_ref[r * PAD : r * PAD + CAP, :] = gate[:, :1] * rows
     rows = wide_ref[:slots, :]
     rows_ref[...] = rows.astype(jnp.bfloat16)
-    weighted_ref[...] = (gate_ref[:, :1] * rows).astype(jnp.bfloat16)
     me = lax.axis_index("dp")
-    for r in range(groups):
+    for r, late_ref in enumerate(lates, 1):
         begin = pl.multiple_of(target(me, r, groups) * share, share)
-        pays[r][:, :share] = weighted_ref[:, pl.ds(begin, share)]
-        pays[r][:, share:] = hidden_ref[...]
+        for k in range(1, count):
+            late = spread_ref[k * PAD : k * PAD + CAP, pl.ds(begin, share)]
+            late_ref[:, (k - 1) * share : k * share] = late.astype(jnp.bfloat16)
+    begin = pl.multiple_of(me * share, share)
+    weighted = gate_ref[:, :1] * wide_ref[:slots, pl.ds(begin, share)]
+    own_ref[:, :share] = weighted.astype(jnp.bfloat16)
+    own_ref[:, share:] = hidden_ref[...]
+    units = hidden_ref.shape[1]
+    for early_ref, other_ref in zip(early, others):
+        for k in range(count):
+            part = early_ref[:, share + k * units : share + (k + 1) * units]
+            units_ref[k * CAP : (k + 1) * CAP, :] = part.astype(jnp.float32)
+        other_ref[...] = units_ref[:slots, :].astype(jnp.bfloat16)
 
 
 def back_kernel(count, picked_ref, total_ref, *refs):
@@ -185,10 +210,30 @@
         back_ref[r * CAP : (r + 1) * CAP, :] = jnp.broadcast_to(back, (CAP, LANES))
 
 
-def down_kernel(count, groups, pieces, rows_ref, gate_ref, weight_ref, match_ref, *refs):
-    pays = refs[:groups]
-    hidden_hbm, down_hbm, match_out, hidden_out, down_out, sems = refs[groups:]
+def down_term(hidden, rows):
+    return dot(hidden, rows, ((0,), (0,))).astype(jnp.bfloat16)
+
+
+def own_kernel(pieces, pay_ref, own_ref):
+    units, share = own_ref.shape
+    block = units // pieces
+    for p in range(pieces):
+        hidden = pay_ref[:, share + p * block : share + (p + 1) * block]
+        own_ref[p * block : (p + 1) * block, :] = down_term(hidden, pay_ref[:, :share])
+
+
+def down_kernel(count, others, pieces, own_ref, rows_ref, gate_ref, weight_ref, match_ref, *refs):
+    early, lates, hiddens = refs[:others], refs[others : 2 * others], refs[2 * others : 3 * others]
+    hidden_hbm, down_hbm, match_out, hidden_out, down_out, wide_ref, sems = refs[3 * others :]
     units, share = down_out.shape
+    slots = count * CAP
+    terms = []
+    for early_ref, late_ref, hidden_ref in zip(early, lates, hiddens):
+        for k in range(count - 1):
+            late = late_ref[:, k * share : (k + 1) * share].astype(jnp.float32)
+            wide_ref[k * CAP : (k + 1) * CAP, :] = late
+        wide_ref[slots - CAP : slots, :] = early_ref[:, :share].astype(jnp.float32)
+        terms.append((hidden_ref, wide_ref[:slots, :].astype(jnp.bfloat16)))
     block = units // pieces
     copies = []
 
@@ -198,12 +243,9 @@
 
     for p in range(pieces):
         part = slice(p * block, (p + 1) * block)
-        total = None
-        for pay_ref in pays:
-            hidden = pay_ref[:, share + p * block : share + (p + 1) * block]
-            term = dot(hidden, pay_ref[:, :share], ((0,), (0,)))
-            term = term.astype(jnp.bfloat16).astype(jnp.float32)
-            total = term if total is None else total + term
+        total = own_ref[part, :].astype(jnp.float32)
+        for hidden_ref, rows in terms:
+            total = total + down_term(hidden_ref[:, part], rows).astype(jnp.float32)
         down_out[part, :] = total
         part = pl.ds(p * block, block)
         write(p, down_out.at[part], down_hbm.at[0, part])
@@ -245,8 +287,9 @@
     pieces = units // LANES
 
     joined = [width + LANES if r in apart(count) else 2 * width + LANES for r in range(1, count)]
+    early = jax.ShapeDtypeStruct((CAP, share + count * units), jnp.bfloat16)
     ids, match, weight, hidden, picked, sent_gate, total, *rest = pl.pallas_call(
-        functools.partial(front_kernel, count, pieces),
+        functools.partial(front_kernel, count, groups, pieces),
         out_shape=[
             jax.ShapeDtypeStruct((top, tokens), jnp.int32),
             jax.ShapeDtypeStruct((count * PAD, tokens), jnp.float32),
@@ -257,9 +300,10 @@
             jax.ShapeDtypeStruct((count * PAD, width), jnp.float32),
         ]
         + [jax.ShapeDtypeStruct((CAP, size), jnp.bfloat16) for size in joined]
-        + [jax.ShapeDtypeStruct((CAP, width), jnp.bfloat16)] * len(apart(count)),
+        + [jax.ShapeDtypeStruct((CAP, width), jnp.bfloat16)] * len(apart(count))
+        + [early] * (groups - 1),
         in_specs=[HBM] * 5,
-        out_specs=[VMEM] * (6 + count + len(apart(count))),
+        out_specs=[VMEM] * (5 + count + len(apart(count)) + groups),
         scratch_shapes=[
             pltpu.VMEM((top, tokens), jnp.bfloat16),
             pltpu.VMEM((tokens, width), jnp.bfloat16),
@@ -270,28 +314,34 @@
         cost_estimate=cost(2 * count * PAD * (tokens + units) * width, 2 * (tokens + units) * width),
         name="front",
     )(*in_hbm(expert_ids.T, gate_values.T, grad_out, saved_hidden, down_weight))
-    sends, products = rest[: count - 1], rest[count - 1 :]
+    sends, rest = rest[: count - 1], rest[count - 1 :]
+    products, early = rest[: len(apart(count))], rest[len(apart(count)) :]
 
     received = [send(x, "expert", r) for r, x in enumerate(sends, 1)]
     theirs = [send(x, "expert", r) for r, x in zip(apart(count), products)]
-
-    rows, gate, *pays = pl.pallas_call(
+    early = [send(x, "dp", r) for r, x in enumerate(early, 1)]
+
+    rows, gate, own, *rest = pl.pallas_call(
         functools.partial(slot_kernel, count, groups),
         out_shape=[
             jax.ShapeDtypeStruct((slots, width), jnp.bfloat16),
             jax.ShapeDtypeStruct((slots, LANES), jnp.float32),
+            jax.ShapeDtypeStruct((slots, share + units), jnp.bfloat16),
         ]
-        + [jax.ShapeDtypeStruct((slots, share + units), jnp.bfloat16)] * groups,
-        in_specs=[VMEM] * (2 + count),
-        out_specs=[VMEM] * (2 + groups),
+        + [jax.ShapeDtypeStruct((CAP, (count - 1) * share), jnp.bfloat16)] * (groups - 1)
+        + [jax.ShapeDtypeStruct((slots, units), jnp.bfloat16)] * (groups - 1),
+        in_specs=[VMEM] * (1 + count + groups),
+        out_specs=[VMEM] * (1 + 2 * groups),
         scratch_shapes=[
             pltpu.VMEM((slots + PAD, width), jnp.float32),
-            pltpu.VMEM((slots, width), jnp.bfloat16),
+            pltpu.VMEM((count * PAD, width), jnp.float32),
+            pltpu.VMEM((slots + PAD, units), jnp.float32),
         ],
         compiler_params=PARAMS,
         cost_estimate=cost(4 * slots * width, 8 * slots * width),
         name="slots",
-    )(hidden, picked, sent_gate, *received)
+    )(hidden, picked, sent_gate, *received, *early)
+    lates, others = rest[: groups - 1], rest[groups - 1 :]
 
     back = pl.pallas_call(
         functools.partial(back_kernel, count),
@@ -303,27 +353,38 @@
         name="backs",
     )(picked, total, *received, *theirs)
 
-    pays = [pays[0]] + [send(pays[r], "dp", r) for r in range(1, groups)]
+    lates = [send(x, "dp", r) for r, x in enumerate(lates, 1)]
     backs = [back] + [send(back, "tensor", r) for r in reversed(range(1, tensors))]
 
+    own = pl.pallas_call(
+        functools.partial(own_kernel, pieces),
+        out_shape=jax.ShapeDtypeStruct((units, share), jnp.bfloat16),
+        in_specs=[VMEM],
+        out_specs=VMEM,
+        compiler_params=PARAMS,
+        cost_estimate=cost(2 * slots * units * share, 2 * units * share),
+        name="own",
+    )(own)
+
     hidden_grad, down_grad, match = pl.pallas_call(
-        functools.partial(down_kernel, count, groups, pieces),
+        functools.partial(down_kernel, count, groups - 1, pieces),
         out_shape=[
             jax.ShapeDtypeStruct(saved_hidden.shape, jnp.bfloat16),
             jax.ShapeDtypeStruct((1, units, share), jnp.float32),
             jax.ShapeDtypeStruct(match.shape, jnp.float32),
         ],
-        in_specs=[VMEM] * (4 + groups),
+        in_specs=[VMEM] * (2 + 3 * groups),
         out_specs=[HBM, HBM, VMEM],
         scratch_shapes=[
             pltpu.VMEM((slots, units), jnp.bfloat16),
             pltpu.VMEM((units, share), jnp.float32),
+            pltpu.VMEM((slots + PAD, share), jnp.float32),
             pltpu.SemaphoreType.DMA((pieces + 1,)),
         ],
         compiler_params=PARAMS,
-        cost_estimate=cost(2 * slots * units * (width + 2 * share), 4 * units * share),
+        cost_estimate=cost(2 * slots * units * (width + share), 4 * units * share),
         name="down",
-    )(rows, gate, weight, match, *pays)
+    )(own, rows, gate, weight, match, *early, *lates, *others)
 
     gate_grad = pl.pallas_call(
         functools.partial(gate_kernel, count),

time: 21.8 us -> 22.5 us (1.032)
  starting transfers between devices: 11.5 us -> 12.9 us
  waiting for transfers between devices: 3.27 us -> 2.4 us
    ppermute x8 -> x9, starting transfers between devices: 11.5 us -> 12.9 us  [send(): lax.ppermute(value, axis, [(i, give(i, step, size)) for i in range(size)])]
    ppermute x8 -> x9, waiting for transfers between devices: 3.27 us -> 2.4 us  [send(): lax.ppermute(value, axis, [(i, give(i, step, size)) for i in range(size)])]
    pallas_call x2 -> x3, Pallas kernels: 5.26 us -> 5.4 us  [the longest x1 2.59 us: on_device(): pl.pallas_call(functools.partial(front_kernel, count, groups, pieces), ou...]
  transfers between devices with their start and end apart: 8 -> 9, of which waited for: 2 -> 1; matrix products, arithmetic and copies ran while one was open for 0% -> 0% of each run, Pallas kernels for 14% -> 14%
where the time goes in v10:
time: 22.5 us; the launch traced here: 22.3 us
  starting transfers between devices  12.9 us (57%)
  Pallas kernels  6.29 us (28%)
  waiting for transfers between devices  2.4 us (11%)
  between operations  0.7 us (3%)
    ppermute x9, starting transfers between devices, send(): lax.ppermute(value, axis, [(i, give(i, step, size)) for i in range(size)])  12.9 us
    pallas_call x1, Pallas kernels, on_device(): pl.pallas_call(functools.partial(front_kernel, count, groups, pieces), ou...  2.59 us
    ppermute x9, waiting for transfers between devices, send(): lax.ppermute(value, axis, [(i, give(i, step, size)) for i in range(size)])  2.4 us
    pallas_call x1, Pallas kernels, on_device(): pl.pallas_call(functools.partial(down_kernel, count, groups - 1, pieces),...  2.22 us
    pallas_call x1, Pallas kernels, on_device(): pl.pallas_call(functools.partial(gate_kernel, count), out_shape=jax.Shape...  0.61 us
    pallas_call x1, Pallas kernels, on_device(): pl.pallas_call(functools.partial(own_kernel, pieces), out_shape=jax.Shape...  0.59 us
  transfers between devices with their start and end apart: 9, of which 1 were waited for; matrix products, arithmetic and copies ran while one was open for 0% of the time, Pallas kernels for 14%

profile of v10, /device:TPU:0, one launch (start us, length us, event | category | flops | bytes accessed | tf_op | source)
XLA Modules:
  0.0 22.3 jit_solution(14231215146477779691)
XLA Ops:
  0.6 2.6 %front.1 = (s32[8,128]{1,0:T(8,128)S(1)}, f32[32,128]{1,0:T(8,128)S(1)}, bf16[384,4096]{1,0:T(8,128)(2,1)S(1)}, bf16[16,384]{1,0:T(8,128)(2,1)S(1)}, f32[32,4096...) custom-call(s32[8,128]{1,0:T(8,128)} %bitcast.4, ...), custom_call_target="tpu_custom_call" | custom-call | flops 134217728 | bytes 4194304 | tf_op jit(solution)/shard_map/front/pallas_call | solution.py:291
  3.2 5.1 %collective-permute-start = (bf16[4,8320]{1,0:T(4,128)(2,1)S(1)}, bf16[4,8320]{1,0:T(4,128)(2,1)S(1)}, u32[]{:S(2)}, u32[]{:S(2)}) collective-permute-start(bf16[4,8320]{1,0:T(4,128)(2,1)S(1)} %get-tuple-element.27), channel_id=1, source_target_pairs={{0,12},{4,8},{8,4},{12,0},{1,13},{5,9},{9,5},{13,1},{2,14},{6,10},... | collective-permute-start | bytes 199688 | tf_op jit(solution)/shard_map/ppermute | solution.py:59
  8.3 0.0 collective-permute-start.2
  8.3 0.6 %collective-permute-start.1 = (bf16[4,4224]{1,0:T(4,128)(2,1)S(1)}, bf16[4,4224]{1,0:T(4,128)(2,1)S(1)}, u32[]{:S(2)}, u32[]{:S(2)}) collective-permute-start(bf16[4,4224]{1,0:T(4,128)(2,1)S(1)} %get-tuple-element.28), channel_id=1, source_target_pairs={{0,8},{4,12},{8,0},{12,4},{1,9},{5,13},{9,1},{13,5},{2,10},{6,14},... | collective-permute-start | bytes 101384 | tf_op jit(solution)/shard_map/ppermute | solution.py:59
  9.0 2.3 %collective-permute-start.5 = (bf16[4,4096]{1,0:T(4,128)(2,1)S(1)}, bf16[4,4096]{1,0:T(4,128)(2,1)S(1)}, u32[]{:S(2)}, u32[]{:S(2)}) collective-permute-start(bf16[4,4096]{1,0:T(4,128)(2,1)S(1)} %get-tuple-element.40), channel_id=1, source_target_pairs={{0,8},{4,12},{8,0},{12,4},{1,9},{5,13},{9,1},{13,5},{2,10},{6,14},... | collective-permute-start | bytes 98312 | tf_op jit(solution)/shard_map/ppermute | solution.py:59
  11.3 1.5 %collective-permute-start.3 = (bf16[4,3584]{1,0:T(4,128)(2,1)S(1)}, bf16[4,3584]{1,0:T(4,128)(2,1)S(1)}, u32[]{:S(2)}, u32[]{:S(2)}) collective-permute-start(bf16[4,3584]{1,0:T(4,128)(2,1)S(1)} %get-tuple-element.30), channel_id=1, source_target_pairs={{0,16},{16,0},{1,17},{17,1},{2,18},{18,2},{3,19},{19,3},{4,20},{20... | collective-permute-start | bytes 86024 | tf_op jit(solution)/shard_map/ppermute | solution.py:59
  12.8 2.4 %collective-permute-done.3.refs_3_.refs_0_ = bf16[4,3584]{1,0:T(4,128)(2,1)S(1)} collective-permute-done((bf16[4,3584]{1,0:T(4,128)(2,1)S(1)}, bf16[4,3584]{1,0:T(4,128)(2,1)S(1)}, u32[]{:S(2)}, u32[]{:S(2)}) %collective-permute-start.3) | collective-permute-done | bytes 28704 | tf_op jit(solution)/shard_map/ppermute | solution.py:59
  15.1 0.0 collective-permute-done.1.refs_1_
  15.1 0.0 collective-permute-done.refs_0_
  15.2 0.0 collective-permute-done.2.refs_2_
  15.2 0.1 slots.1
  15.3 1.6 %collective-permute-start.4 = (bf16[4,6144]{1,0:T(4,128)(2,1)S(1)}, bf16[4,6144]{1,0:T(4,128)(2,1)S(1)}, u32[]{:S(2)}, u32[]{:S(2)}) collective-permute-start(bf16[4,6144]{1,0:T(4,128)(2,1)S(1)} %get-tuple-element.36), channel_id=1, source_target_pairs={{0,16},{16,0},{1,17},{17,1},{2,18},{18,2},{3,19},{19,3},{4,20},{20... | collective-permute-start | bytes 147464 | tf_op jit(solution)/shard_map/ppermute | solution.py:59
  16.8 0.0 collective-permute-done.5.refs_3_
  16.8 0.2 backs.1.refs_0_
  17.0 0.0 collective-permute-start.8
  17.0 1.6 %collective-permute-start.7 = (f32[16,128]{1,0:T(8,128)S(1)}, f32[16,128]{1,0:T(8,128)S(1)}, u32[]{:S(2)}, u32[]{:S(2)}) collective-permute-start(f32[16,128]{1,0:T(8,128)S(1)} %backs.1.refs_0_), channel_id=1, source_target_pairs={{0,2},{1,3},{2,0},{3,1},{4,6},{5,7},{6,4},{7,5},{8,10},{9,11},{10,... | collective-permute-start | bytes 24584 | tf_op jit(solution)/shard_map/ppermute | solution.py:59
  18.6 0.3 %collective-permute-start.6 = (f32[16,128]{1,0:T(8,128)S(1)}, f32[16,128]{1,0:T(8,128)S(1)}, u32[]{:S(2)}, u32[]{:S(2)}) collective-permute-start(f32[16,128]{1,0:T(8,128)S(1)} %backs.1.refs_0_), channel_id=1, source_target_pairs={{0,1},{1,0},{2,3},{3,2},{4,5},{5,4},{6,7},{7,6},{8,9},{9,8},{10,11... | collective-permute-start | bytes 24584 | tf_op jit(solution)/shard_map/ppermute | solution.py:59
  18.9 0.6 %own.1.own_ref = bf16[384,2048]{1,0:T(8,128)(2,1)S(1)} custom-call(bf16[16,2432]{1,0:T(8,128)(2,1)S(1)} %get-tuple-element.31.pay_ref), custom_call_target="tpu_custom_call" | custom-call | flops 25165824 | bytes 1572864 | tf_op jit(solution)/shard_map/own/pallas_call | solution.py:359
  19.5 0.0 collective-permute-done.4.refs_1_
  19.5 2.2 %down.1 = (bf16[1,1,16,384]{3,2,1,0:T(8,128)(2,1)}, f32[1,384,2048]{2,1,0:T(8,128)}, f32[32,128]{1,0:T(8,128)S(1)}) custom-call(bf16[384,2048]{1,0:T(8,128)(2,1)S(1)} %own.1.own_ref, bf16[16,4096]{1,0:T(8,128)(2,1)S(1)} %get-tuple-element.32.rows_ref, f32[16,128]{1,0:T(8,128)S(1)} %get-tuple-element.33.gate_ref, ...), custom_call_target="tpu_custom_call" | custom-call | flops 75497472 | bytes 3145728 | tf_op jit(solution)/shard_map/down/pallas_call | solution.py:369
  21.7 0.0 collective-permute-done.8.refs_3_
  21.7 0.0 collective-permute-done.7.refs_2_
  21.7 0.0 collective-permute-done.6.refs_1_
  21.7 0.6 %gates.1 = f32[8,128]{1,0:T(8,128)} custom-call(s32[8,128]{1,0:T(8,128)S(1)} %get-tuple-element.23.ids_ref, f32[32,128]{1,0:T(8,128)S(1)} %get-tuple-element.38.match_ref, f32[16,128]{1,0:T(8,128)S(1)} %backs.1.refs_0_, f32[16,128]{1,0:T(8,128)S(1)} %collective-permute-done.6.refs_1_, f32[16,128]{1,0:T(8,128)S(1)} %collective-permute-done.7.refs_2_, ...), custom_call_target="tpu_custom_call" | custom-call | flops 2048 | bytes 8192 | tf_op jit(solution)/shard_map/gates/pallas_call | solution.py:389
Async XLA Ops:
  3.2 11.9 %collective-permute-start = (bf16[4,8320]{1,0:T(4,128)(2,1)S(1)}, bf16[4,8320]{1,0:T(4,128)(2,1)S(1)}, u32[]{:S(2)}, u32[]{:S(2)}) collective-permute-start(bf16[4,8320]{1,0:T(4,128)(2,1)S(1)} %get-tuple-element.27), channel_id=1, source_target_pairs={{0,12},{4,8},{8,4},{12,0},{1,13},{5,9},{9,5},{13,1},{2,14},{6,10},... | collective-permute-start | bytes 199688 | tf_op jit(solution)/shard_map/ppermute | solution.py:59
  8.3 6.8 %collective-permute-start.2 = (bf16[4,8320]{1,0:T(4,128)(2,1)S(1)}, bf16[4,8320]{1,0:T(4,128)(2,1)S(1)}, u32[]{:S(2)}, u32[]{:S(2)}) collective-permute-start(bf16[4,8320]{1,0:T(4,128)(2,1)S(1)} %get-tuple-element.29), channel_id=1, source_target_pairs={{0,4},{4,0},{8,12},{12,8},{1,5},{5,1},{9,13},{13,9},{2,6},{6,2},{1... | collective-permute-start | bytes 199688 | tf_op jit(solution)/shard_map/ppermute | solution.py:59
  8.3 6.8 %collective-permute-start.1 = (bf16[4,4224]{1,0:T(4,128)(2,1)S(1)}, bf16[4,4224]{1,0:T(4,128)(2,1)S(1)}, u32[]{:S(2)}, u32[]{:S(2)}) collective-permute-start(bf16[4,4224]{1,0:T(4,128)(2,1)S(1)} %get-tuple-element.28), channel_id=1, source_target_pairs={{0,8},{4,12},{8,0},{12,4},{1,9},{5,13},{9,1},{13,5},{2,10},{6,14},... | collective-permute-start | bytes 101384 | tf_op jit(solution)/shard_map/ppermute | solution.py:59
  9.0 7.9 %collective-permute-start.5 = (bf16[4,4096]{1,0:T(4,128)(2,1)S(1)}, bf16[4,4096]{1,0:T(4,128)(2,1)S(1)}, u32[]{:S(2)}, u32[]{:S(2)}) collective-permute-start(bf16[4,4096]{1,0:T(4,128)(2,1)S(1)} %get-tuple-element.40), channel_id=1, source_target_pairs={{0,8},{4,12},{8,0},{12,4},{1,9},{5,13},{9,1},{13,5},{2,10},{6,14},... | collective-permute-start | bytes 98312 | tf_op jit(solution)/shard_map/ppermute | solution.py:59
  11.3 3.9 %collective-permute-start.3 = (bf16[4,3584]{1,0:T(4,128)(2,1)S(1)}, bf16[4,3584]{1,0:T(4,128)(2,1)S(1)}, u32[]{:S(2)}, u32[]{:S(2)}) collective-permute-start(bf16[4,3584]{1,0:T(4,128)(2,1)S(1)} %get-tuple-element.30), channel_id=1, source_target_pairs={{0,16},{16,0},{1,17},{17,1},{2,18},{18,2},{3,19},{19,3},{4,20},{20... | collective-permute-start | bytes 86024 | tf_op jit(solution)/shard_map/ppermute | solution.py:59
  15.3 4.2 %collective-permute-start.4 = (bf16[4,6144]{1,0:T(4,128)(2,1)S(1)}, bf16[4,6144]{1,0:T(4,128)(2,1)S(1)}, u32[]{:S(2)}, u32[]{:S(2)}) collective-permute-start(bf16[4,6144]{1,0:T(4,128)(2,1)S(1)} %get-tuple-element.36), channel_id=1, source_target_pairs={{0,16},{16,0},{1,17},{17,1},{2,18},{18,2},{3,19},{19,3},{4,20},{20... | collective-permute-start | bytes 147464 | tf_op jit(solution)/shard_map/ppermute | solution.py:59
  17.0 4.7 %collective-permute-start.8 = (f32[16,128]{1,0:T(8,128)S(1)}, f32[16,128]{1,0:T(8,128)S(1)}, u32[]{:S(2)}, u32[]{:S(2)}) collective-permute-start(f32[16,128]{1,0:T(8,128)S(1)} %backs.1.refs_0_), channel_id=1, source_target_pairs={{0,3},{1,2},{2,1},{3,0},{4,7},{5,6},{6,5},{7,4},{8,11},{9,10},{10,... | collective-permute-start | bytes 24584 | tf_op jit(solution)/shard_map/ppermute | solution.py:59
  17.0 4.7 %collective-permute-start.7 = (f32[16,128]{1,0:T(8,128)S(1)}, f32[16,128]{1,0:T(8,128)S(1)}, u32[]{:S(2)}, u32[]{:S(2)}) collective-permute-start(f32[16,128]{1,0:T(8,128)S(1)} %backs.1.refs_0_), channel_id=1, source_target_pairs={{0,2},{1,3},{2,0},{3,1},{4,6},{5,7},{6,4},{7,5},{8,10},{9,11},{10,... | collective-permute-start | bytes 24584 | tf_op jit(solution)/shard_map/ppermute | solution.py:59
  18.6 3.1 %collective-permute-start.6 = (f32[16,128]{1,0:T(8,128)S(1)}, f32[16,128]{1,0:T(8,128)S(1)}, u32[]{:S(2)}, u32[]{:S(2)}) collective-permute-start(f32[16,128]{1,0:T(8,128)S(1)} %backs.1.refs_0_), channel_id=1, source_target_pairs={{0,1},{1,0},{2,3},{3,2},{4,5},{5,4},{6,7},{7,6},{8,9},{9,8},{10,11... | collective-permute-start | bytes 24584 | tf_op jit(solution)/shard_map/ppermute | solution.py:59

commit v11 on v7

--- a/solution.py
+++ b/solution.py
@@ -11,6 +11,7 @@
 LANES = 128
 JOINT = 1
 AFTER_WAIT = (10**9, 10**7)
+SPLIT = 4
 PAD = 8
 VMEM = pl.BlockSpec(memory_space=pltpu.VMEM)
 HBM = pl.BlockSpec(memory_space=pltpu.HBM)
@@ -69,13 +70,13 @@
     units, width = weight_ref.shape
     top, tokens = ids_ref.shape
     pairs = [(ids_hbm, ids_ref), (gates_hbm, gates_ref), (hidden_hbm.at[0, 0], saved_ref)]
-    half = tokens // 2
-    for p in range(2):
-        part = pl.ds(p * half, half)
+    lines = tokens // SPLIT
+    for p in range(SPLIT):
+        part = pl.ds(p * lines, lines)
         pairs.append((grad_hbm.at[part], grad_ref.at[part]))
-    half = units // (2 * pieces)
-    for p in range(2 * pieces):
-        part = pl.ds(p * half, half)
+    lines = units // (SPLIT * pieces)
+    for p in range(SPLIT * pieces):
+        part = pl.ds(p * lines, lines)
         pairs.append((weight_hbm.at[0, part], weight_ref.at[part]))
     copies = [pltpu.make_async_copy(*pair, sems.at[n]) for n, pair in enumerate(pairs)]
     for copy in copies:
@@ -114,7 +115,7 @@
     chosen = (place >= 0) & (place < CAP) & (there == target(me, here // PAD, count) * CAP + place)
     hidden = dot(chosen.astype(jnp.bfloat16), saved, ((1,), (0,))).astype(jnp.bfloat16)
 
-    for copy in copies[3:5]:
+    for copy in copies[3 : 3 + SPLIT]:
         copy.wait()
     picked_ref[...] = dot(match, grad_ref[...], ((1,), (0,)))
     for r in range(count):
@@ -125,7 +126,7 @@
             sends[r][:, :width] = picked_ref[part, :].astype(jnp.bfloat16)
     block = units // pieces
     for p in range(pieces):
-        for copy in copies[5 + 2 * p : 7 + 2 * p]:
+        for copy in copies[3 + SPLIT * (p + 1) : 3 + SPLIT * (p + 2)]:
             copy.wait()
         part = slice(p * block, (p + 1) * block)
         term = dot(hidden[:, part], weight_ref[part, :], ((1,), (0,)))
@@ -213,14 +214,16 @@
         for pay_ref in pays:
             total = total + down_term(pay_ref, share, share + p * block, block).astype(jnp.float32)
         down_out[part, :] = total
-        part = pl.ds(p * block, block)
-        write(p, down_out.at[part], down_hbm.at[0, part])
+        lines = block // SPLIT
+        for n in range(SPLIT * p, SPLIT * (p + 1)):
+            part = pl.ds(n * lines, lines)
+            write(n, down_out.at[part], down_hbm.at[0, part])
 
     match_out[...] = match_ref[...]
     upstream = dot(rows_ref[...], weight_ref[...], ((1,), (1,)))
     scaled = (gate_ref[:, :1] * upstream).astype(jnp.bfloat16)
     hidden_out[...] = dot(slot_order(count), scaled, ((0,), (0,))).astype(jnp.bfloat16)
-    write(pieces, hidden_out, hidden_hbm.at[0, 0])
+    write(SPLIT * pieces, hidden_out, hidden_hbm.at[0, 0])
     for copy in copies:
         copy.wait()
 
@@ -273,7 +276,7 @@
             pltpu.VMEM((slots, units), jnp.bfloat16),
             pltpu.VMEM((count * PAD, width), jnp.float32),
             pltpu.VMEM((count * PAD, width), jnp.float32),
-            pltpu.SemaphoreType.DMA((5 + 2 * pieces,)),
+            pltpu.SemaphoreType.DMA((3 + SPLIT * (pieces + 1),)),
         ],
         compiler_params=PARAMS,
         cost_estimate=cost(2 * count * PAD * (tokens + units) * width, 2 * (tokens + units) * width),
@@ -337,7 +340,7 @@
         scratch_shapes=[
             pltpu.VMEM((slots, units), jnp.bfloat16),
             pltpu.VMEM((units, share), jnp.float32),
-            pltpu.SemaphoreType.DMA((pieces + 1,)),
+            pltpu.SemaphoreType.DMA((SPLIT * pieces + 1,)),
         ],
         compiler_params=PARAMS,
         cost_estimate=cost(2 * slots * units * (width + share), 4 * units * share),

time: 21.2 us -> 21.3 us (level)
  no operation moved by 1% of the time
where the time goes in v11:
time: 21.3 us; the launch traced here: 21.1 us
  starting transfers between devices  13.5 us (63%)
  Pallas kernels  6.37 us (30%)
  between operations  0.69 us (3%)
  waiting for transfers between devices  0.52 us (2%)
    ppermute x9, starting transfers between devices, send(): lax.ppermute(value, axis, [(i, give(i, step, size)) for i in range(size)])  13.5 us
    pallas_call x1, Pallas kernels, on_device(): pl.pallas_call(functools.partial(front_kernel, count, pieces), out_shape=...  2.64 us
    pallas_call x1, Pallas kernels, on_device(): pl.pallas_call(functools.partial(down_kernel, count, groups - 1, pieces),...  2.26 us
    pallas_call x1, Pallas kernels, on_device(): pl.pallas_call(functools.partial(gate_kernel, count), out_shape=jax.Shape...  0.61 us
    pallas_call x1, Pallas kernels, on_device(): pl.pallas_call(functools.partial(own_kernel, pieces), out_shape=jax.Shape...  0.58 us
    ppermute x9, waiting for transfers between devices, send(): lax.ppermute(value, axis, [(i, give(i, step, size)) for i in range(size)])  0.52 us
  transfers between devices with their start and end apart: 9, of which 2 were waited for; matrix products, arithmetic and copies ran while one was open for 0% of the time, Pallas kernels for 15%

profile of v11, /device:TPU:0, one launch (start us, length us, event | category | flops | bytes accessed | tf_op | source)
XLA Modules:
  0.0 21.1 jit_solution(14752888804290438246)
XLA Ops:
  0.6 2.6 %front.1 = (s32[8,128]{1,0:T(8,128)S(1)}, f32[32,128]{1,0:T(8,128)S(1)}, bf16[384,4096]{1,0:T(8,128)(2,1)S(1)}, bf16[16,384]{1,0:T(8,128)(2,1)S(1)}, bf16[4,4224...) custom-call(s32[8,128]{1,0:T(8,128)} %bitcast.4, ...), custom_call_target="tpu_custom_call" | custom-call | flops 134217728 | bytes 4194304 | tf_op jit(solution)/shard_map/front/pallas_call | solution.py:258
  3.3 5.1 %collective-permute-start = (bf16[8,4224]{1,0:T(8,128)(2,1)S(1)}, bf16[8,4224]{1,0:T(8,128)(2,1)S(1)}, u32[]{:S(2)}, u32[]{:S(2)}) collective-permute-start(bf16[8,4224]{1,0:T(8,128)(2,1)S(1)} %get-tuple-element.24.refs_1_), channel_id=1, source_target_pairs={{0,12},{4,8},{8,4},{12,0},{1,13},{5,9},{9,5},{13,1},{2,14},{6,10},... | collective-permute-start | bytes 202760 | tf_op jit(solution)/shard_map/ppermute | solution.py:61
  8.4 0.0 collective-permute-start.1
  8.4 0.6 %collective-permute-start.2 = (bf16[4,4224]{1,0:T(4,128)(2,1)S(1)}, bf16[4,4224]{1,0:T(4,128)(2,1)S(1)}, u32[]{:S(2)}, u32[]{:S(2)}) collective-permute-start(bf16[4,4224]{1,0:T(4,128)(2,1)S(1)} %get-tuple-element.26.refs_3_), channel_id=1, source_target_pairs={{0,4},{4,0},{8,12},{12,8},{1,5},{5,1},{9,13},{13,9},{2,6},{6,2},{1... | collective-permute-start | bytes 101384 | tf_op jit(solution)/shard_map/ppermute | solution.py:61
  9.0 2.3 %collective-permute-start.4 = (bf16[4,4096]{1,0:T(4,128)(2,1)S(1)}, bf16[4,4096]{1,0:T(4,128)(2,1)S(1)}, u32[]{:S(2)}, u32[]{:S(2)}) collective-permute-start(bf16[4,4096]{1,0:T(4,128)(2,1)S(1)} %get-tuple-element.35), channel_id=1, source_target_pairs={{0,8},{4,12},{8,0},{12,4},{1,9},{5,13},{9,1},{13,5},{2,10},{6,14},... | collective-permute-start | bytes 98312 | tf_op jit(solution)/shard_map/ppermute | solution.py:61
  11.3 2.0 %collective-permute-start.5 = (bf16[4,4096]{1,0:T(4,128)(2,1)S(1)}, bf16[4,4096]{1,0:T(4,128)(2,1)S(1)}, u32[]{:S(2)}, u32[]{:S(2)}) collective-permute-start(bf16[4,4096]{1,0:T(4,128)(2,1)S(1)} %get-tuple-element.36), channel_id=1, source_target_pairs={{0,4},{4,0},{8,12},{12,8},{1,5},{5,1},{9,13},{13,9},{2,6},{6,2},{1... | collective-permute-start | bytes 98312 | tf_op jit(solution)/shard_map/ppermute | solution.py:61
  13.4 0.2 %collective-permute-done.1.refs_2_ = bf16[4,4224]{1,0:T(4,128)(2,1)S(1)} collective-permute-done((bf16[4,4224]{1,0:T(4,128)(2,1)S(1)}, bf16[4,4224]{1,0:T(4,128)(2,1)S(1)}, u32[]{:S(2)}, u32[]{:S(2)}) %collective-permute-start.1) | collective-permute-done | bytes 33824 | tf_op jit(solution)/shard_map/ppermute | solution.py:61
  13.6 0.0 collective-permute-done.2.refs_3_
  13.6 0.0 collective-permute-done.refs_1_.refs_4_
  13.6 0.1 slots.1
  13.7 1.6 %collective-permute-start.3 = (bf16[16,2432]{1,0:T(8,128)(2,1)S(1)}, bf16[16,2432]{1,0:T(8,128)(2,1)S(1)}, u32[]{:S(2)}, u32[]{:S(2)}) collective-permute-start(bf16[16,2432]{1,0:T(8,128)(2,1)S(1)} %get-tuple-element.28), channel_id=1, source_target_pairs={{0,16},{16,0},{1,17},{17,1},{2,18},{18,2},{3,19},{19,3},{4,20},{20... | collective-permute-start | bytes 233480 | tf_op jit(solution)/shard_map/ppermute | solution.py:61
  15.3 0.0 collective-permute-done.4.refs_6_
  15.3 0.0 collective-permute-done.5.refs_7_
  15.3 0.2 backs.1.refs_0_
  15.4 0.0 collective-permute-start.8
  15.4 1.6 %collective-permute-start.7 = (f32[16,128]{1,0:T(8,128)S(1)}, f32[16,128]{1,0:T(8,128)S(1)}, u32[]{:S(2)}, u32[]{:S(2)}) collective-permute-start(f32[16,128]{1,0:T(8,128)S(1)} %backs.1.refs_0_), channel_id=1, source_target_pairs={{0,2},{1,3},{2,0},{3,1},{4,6},{5,7},{6,4},{7,5},{8,10},{9,11},{10,... | collective-permute-start | bytes 24584 | tf_op jit(solution)/shard_map/ppermute | solution.py:61
  17.0 0.3 %collective-permute-start.6 = (f32[16,128]{1,0:T(8,128)S(1)}, f32[16,128]{1,0:T(8,128)S(1)}, u32[]{:S(2)}, u32[]{:S(2)}) collective-permute-start(f32[16,128]{1,0:T(8,128)S(1)} %backs.1.refs_0_), channel_id=1, source_target_pairs={{0,1},{1,0},{2,3},{3,2},{4,5},{5,4},{6,7},{7,6},{8,9},{9,8},{10,11... | collective-permute-start | bytes 24584 | tf_op jit(solution)/shard_map/ppermute | solution.py:61
  17.3 0.6 %own.1.refs_0_ = bf16[384,2048]{1,0:T(8,128)(2,1)S(1)} custom-call(bf16[16,2432]{1,0:T(8,128)(2,1)S(1)} %get-tuple-element.27.pay_ref), custom_call_target="tpu_custom_call" | custom-call | flops 25165824 | bytes 1572864 | tf_op jit(solution)/shard_map/own/pallas_call | solution.py:321
  17.9 0.3 %collective-permute-done.3.refs_1_ = bf16[16,2432]{1,0:T(8,128)(2,1)S(1)} collective-permute-done((bf16[16,2432]{1,0:T(8,128)(2,1)S(1)}, bf16[16,2432]{1,0:T(8,128)(2,1)S(1)}, u32[]{:S(2)}, u32[]{:S(2)}) %collective-permute-start.3) | collective-permute-done | bytes 77856 | tf_op jit(solution)/shard_map/ppermute | solution.py:61
  18.2 2.3 %down.1 = (bf16[1,1,16,384]{3,2,1,0:T(8,128)(2,1)}, f32[1,384,2048]{2,1,0:T(8,128)}, f32[32,128]{1,0:T(8,128)S(1)}) custom-call(bf16[384,2048]{1,0:T(8,128)(2,1)S(1)} %own.1.refs_0_, bf16[16,2432]{1,0:T(8,128)(2,1)S(1)} %collective-permute-done.3.refs_1_, bf16[16,4096]{1,0:T(8,128)(2,1)S(1)} %get-tuple-element.29.refs_2_, ...), custom_call_target="tpu_custom_call" | custom-call | flops 75497472 | bytes 3145728 | tf_op jit(solution)/shard_map/down/pallas_call | solution.py:331
  20.4 0.0 collective-permute-done.8.refs_3_
  20.4 0.0 collective-permute-done.7.refs_2_
  20.4 0.0 collective-permute-done.6.refs_1_
  20.5 0.6 %gates.1 = f32[8,128]{1,0:T(8,128)} custom-call(s32[8,128]{1,0:T(8,128)S(1)} %get-tuple-element.21.ids_ref, f32[32,128]{1,0:T(8,128)S(1)} %get-tuple-element.33.match_ref, f32[16,128]{1,0:T(8,128)S(1)} %backs.1.refs_0_, f32[16,128]{1,0:T(8,128)S(1)} %collective-permute-done.6.refs_1_, f32[16,128]{1,0:T(8,128)S(1)} %collective-permute-done.7.refs_2_, ...), custom_call_target="tpu_custom_call" | custom-call | flops 2048 | bytes 8192 | tf_op jit(solution)/shard_map/gates/pallas_call | solution.py:350
Async XLA Ops:
  3.3 10.3 %collective-permute-start = (bf16[8,4224]{1,0:T(8,128)(2,1)S(1)}, bf16[8,4224]{1,0:T(8,128)(2,1)S(1)}, u32[]{:S(2)}, u32[]{:S(2)}) collective-permute-start(bf16[8,4224]{1,0:T(8,128)(2,1)S(1)} %get-tuple-element.24.refs_1_), channel_id=1, source_target_pairs={{0,12},{4,8},{8,4},{12,0},{1,13},{5,9},{9,5},{13,1},{2,14},{6,10},... | collective-permute-start | bytes 202760 | tf_op jit(solution)/shard_map/ppermute | solution.py:61
  8.4 5.2 %collective-permute-start.1 = (bf16[4,4224]{1,0:T(4,128)(2,1)S(1)}, bf16[4,4224]{1,0:T(4,128)(2,1)S(1)}, u32[]{:S(2)}, u32[]{:S(2)}) collective-permute-start(bf16[4,4224]{1,0:T(4,128)(2,1)S(1)} %get-tuple-element.25.refs_2_), channel_id=1, source_target_pairs={{0,8},{4,12},{8,0},{12,4},{1,9},{5,13},{9,1},{13,5},{2,10},{6,14},... | collective-permute-start | bytes 101384 | tf_op jit(solution)/shard_map/ppermute | solution.py:61
  8.4 5.2 %collective-permute-start.2 = (bf16[4,4224]{1,0:T(4,128)(2,1)S(1)}, bf16[4,4224]{1,0:T(4,128)(2,1)S(1)}, u32[]{:S(2)}, u32[]{:S(2)}) collective-permute-start(bf16[4,4224]{1,0:T(4,128)(2,1)S(1)} %get-tuple-element.26.refs_3_), channel_id=1, source_target_pairs={{0,4},{4,0},{8,12},{12,8},{1,5},{5,1},{9,13},{13,9},{2,6},{6,2},{1... | collective-permute-start | bytes 101384 | tf_op jit(solution)/shard_map/ppermute | solution.py:61
  9.0 6.2 %collective-permute-start.4 = (bf16[4,4096]{1,0:T(4,128)(2,1)S(1)}, bf16[4,4096]{1,0:T(4,128)(2,1)S(1)}, u32[]{:S(2)}, u32[]{:S(2)}) collective-permute-start(bf16[4,4096]{1,0:T(4,128)(2,1)S(1)} %get-tuple-element.35), channel_id=1, source_target_pairs={{0,8},{4,12},{8,0},{12,4},{1,9},{5,13},{9,1},{13,5},{2,10},{6,14},... | collective-permute-start | bytes 98312 | tf_op jit(solution)/shard_map/ppermute | solution.py:61
  11.3 3.9 %collective-permute-start.5 = (bf16[4,4096]{1,0:T(4,128)(2,1)S(1)}, bf16[4,4096]{1,0:T(4,128)(2,1)S(1)}, u32[]{:S(2)}, u32[]{:S(2)}) collective-permute-start(bf16[4,4096]{1,0:T(4,128)(2,1)S(1)} %get-tuple-element.36), channel_id=1, source_target_pairs={{0,4},{4,0},{8,12},{12,8},{1,5},{5,1},{9,13},{13,9},{2,6},{6,2},{1... | collective-permute-start | bytes 98312 | tf_op jit(solution)/shard_map/ppermute | solution.py:61
  13.7 4.5 %collective-permute-start.3 = (bf16[16,2432]{1,0:T(8,128)(2,1)S(1)}, bf16[16,2432]{1,0:T(8,128)(2,1)S(1)}, u32[]{:S(2)}, u32[]{:S(2)}) collective-permute-start(bf16[16,2432]{1,0:T(8,128)(2,1)S(1)} %get-tuple-element.28), channel_id=1, source_target_pairs={{0,16},{16,0},{1,17},{17,1},{2,18},{18,2},{3,19},{19,3},{4,20},{20... | collective-permute-start | bytes 233480 | tf_op jit(solution)/shard_map/ppermute | solution.py:61
  15.4 5.0 %collective-permute-start.8 = (f32[16,128]{1,0:T(8,128)S(1)}, f32[16,128]{1,0:T(8,128)S(1)}, u32[]{:S(2)}, u32[]{:S(2)}) collective-permute-start(f32[16,128]{1,0:T(8,128)S(1)} %backs.1.refs_0_), channel_id=1, source_target_pairs={{0,3},{1,2},{2,1},{3,0},{4,7},{5,6},{6,5},{7,4},{8,11},{9,10},{10,... | collective-permute-start | bytes 24584 | tf_op jit(solution)/shard_map/ppermute | solution.py:61
  15.4 5.0 %collective-permute-start.7 = (f32[16,128]{1,0:T(8,128)S(1)}, f32[16,128]{1,0:T(8,128)S(1)}, u32[]{:S(2)}, u32[]{:S(2)}) collective-permute-start(f32[16,128]{1,0:T(8,128)S(1)} %backs.1.refs_0_), channel_id=1, source_target_pairs={{0,2},{1,3},{2,0},{3,1},{4,6},{5,7},{6,4},{7,5},{8,10},{9,11},{10,... | collective-permute-start | bytes 24584 | tf_op jit(solution)/shard_map/ppermute | solution.py:61
  17.0 3.4 %collective-permute-start.6 = (f32[16,128]{1,0:T(8,128)S(1)}, f32[16,128]{1,0:T(8,128)S(1)}, u32[]{:S(2)}, u32[]{:S(2)}) collective-permute-start(f32[16,128]{1,0:T(8,128)S(1)} %backs.1.refs_0_), channel_id=1, source_target_pairs={{0,1},{1,0},{2,3},{3,2},{4,5},{5,4},{6,7},{7,6},{8,9},{9,8},{10,11... | collective-permute-start | bytes 24584 | tf_op jit(solution)/shard_map/ppermute | solution.py:61

commit v12 on v7

--- a/solution.py
+++ b/solution.py
@@ -65,7 +65,7 @@
     ids_ref, match_ref, weight_ref, hidden_ref = refs[5:9]
     sends = refs[9 : 9 + count]
     products = refs[9 + count : 8 + 2 * count]
-    gates_ref, grad_ref, saved_ref, picked_ref, total_ref, sems = refs[8 + 2 * count :]
+    gates_ref, grad_ref, saved_ref, picked_ref, total_ref, chosen_ref, sems = refs[8 + 2 * count :]
     units, width = weight_ref.shape
     top, tokens = ids_ref.shape
     pairs = [(ids_hbm, ids_ref), (gates_hbm, gates_ref), (hidden_hbm.at[0, 0], saved_ref)]
@@ -124,12 +124,18 @@
         if r != JOINT:
             sends[r][:, :width] = picked_ref[part, :].astype(jnp.bfloat16)
     block = units // pieces
-    for p in range(pieces):
-        for copy in copies[5 + 2 * p : 7 + 2 * p]:
-            copy.wait()
-        part = slice(p * block, (p + 1) * block)
-        term = dot(hidden[:, part], weight_ref[part, :], ((1,), (0,)))
-        total_ref[...] = term if p == 0 else total_ref[...] + term
+    chosen_ref[...] = hidden
+    total_ref[...] = jnp.zeros(total_ref.shape, jnp.float32)
+
+    @pl.loop(0, pieces)
+    def _(p):
+        for n in range(2):
+            part = pl.ds(pl.multiple_of((2 * p + n) * half, half), half)
+            load = (weight_hbm.at[0, part], weight_ref.at[part])
+            pltpu.make_async_copy(*load, sems.at[5 + 2 * p + n]).wait()
+        part = pl.ds(pl.multiple_of(p * block, block), block)
+        total_ref[...] += dot(chosen_ref[:, part], weight_ref[part, :], ((1,), (0,)))
+
     for product, r in zip(products, apart(count)):
         product[...] = total_ref[r * PAD : r * PAD + CAP, :].astype(jnp.bfloat16)
     part = slice(JOINT * PAD, (JOINT + 1) * PAD)
@@ -190,8 +196,11 @@
 def own_kernel(pieces, pay_ref, own_ref):
     units, share = own_ref.shape
     block = units // pieces
-    for p in range(pieces):
-        own_ref[p * block : (p + 1) * block, :] = down_term(pay_ref, share, share + p * block, block)
+
+    @pl.loop(0, pieces)
+    def _(p):
+        start = pl.multiple_of(p * block, block)
+        own_ref[pl.ds(start, block), :] = down_term(pay_ref, share, share + start, block)
 
 
 def down_kernel(count, others, pieces, *refs):
@@ -201,28 +210,36 @@
     hidden_hbm, down_hbm, match_out, hidden_out, down_out, sems = refs[5 + others :]
     units, share = own_ref.shape
     block = units // pieces
-    copies = []
-
-    def write(n, values, destination):
-        copies.append(pltpu.make_async_copy(values, destination, sems.at[n]))
-        copies[-1].start()
-
-    for p in range(pieces):
-        part = slice(p * block, (p + 1) * block)
+
+    def write(p):
+        part = pl.ds(pl.multiple_of(p * block, block), block)
+        return pltpu.make_async_copy(down_out.at[part], down_hbm.at[0, part], sems.at[p])
+
+    @pl.loop(0, pieces)
+    def _(p):
+        start = pl.multiple_of(p * block, block)
+        part = pl.ds(start, block)
         total = own_ref[part, :].astype(jnp.float32)
         for pay_ref in pays:
-            total = total + down_term(pay_ref, share, share + p * block, block).astype(jnp.float32)
+            total = total + down_term(pay_ref, share, share + start, block).astype(jnp.float32)
         down_out[part, :] = total
-        part = pl.ds(p * block, block)
-        write(p, down_out.at[part], down_hbm.at[0, part])
+        write(p).start()
 
     match_out[...] = match_ref[...]
-    upstream = dot(rows_ref[...], weight_ref[...], ((1,), (1,)))
+    half = weight_ref.shape[1] // 2
+
+    def product(n):
+        part = pl.ds(pl.multiple_of(n * half, half), half)
+        return dot(rows_ref[:, part], weight_ref[:, part], ((1,), (1,)))
+
+    upstream = lax.fori_loop(0, 2, lambda n, total: total + product(n), jnp.zeros((rows_ref.shape[0], units), jnp.float32))
     scaled = (gate_ref[:, :1] * upstream).astype(jnp.bfloat16)
     hidden_out[...] = dot(slot_order(count), scaled, ((0,), (0,))).astype(jnp.bfloat16)
-    write(pieces, hidden_out, hidden_hbm.at[0, 0])
-    for copy in copies:
-        copy.wait()
+    last = pltpu.make_async_copy(hidden_out, hidden_hbm.at[0, 0], sems.at[pieces])
+    last.start()
+    for p in range(pieces):
+        write(p).wait()
+    last.wait()
 
 
 def gate_kernel(count, ids_ref, match_ref, *refs):
@@ -273,6 +290,7 @@
             pltpu.VMEM((slots, units), jnp.bfloat16),
             pltpu.VMEM((count * PAD, width), jnp.float32),
             pltpu.VMEM((count * PAD, width), jnp.float32),
+            pltpu.VMEM((count * PAD, units), jnp.bfloat16),
             pltpu.SemaphoreType.DMA((5 + 2 * pieces,)),
         ],
         compiler_params=PARAMS,

time: 21.2 us -> 21.9 us (1.033)
  Pallas kernels: 6.29 us -> 7.29 us
  waiting for transfers between devices: 0.52 us -> 0.24 us
    pallas_call x1, Pallas kernels: 2.22 us -> 2.85 us  [on_device(): pl.pallas_call(functools.partial(down_kernel, count, groups - 1, pieces),...]
    pallas_call x1, Pallas kernels: 0.59 us -> 0.96 us  [on_device(): pl.pallas_call(functools.partial(own_kernel, pieces), out_shape=jax.Shape...]
    ppermute x9, waiting for transfers between devices: 0.52 us -> 0.24 us  [send(): lax.ppermute(value, axis, [(i, give(i, step, size)) for i in range(size)])]
  transfers between devices with their start and end apart: 9 -> 9, of which waited for: 2 -> 1; matrix products, arithmetic and copies ran while one was open for 0% -> 0% of each run, Pallas kernels for 15% -> 19%
where the time goes in v12:
time: 21.9 us; the launch traced here: 21.7 us
  starting transfers between devices  13.5 us (62%)
  Pallas kernels  7.29 us (33%)
  between operations  0.7 us (3%)
  waiting for transfers between devices  0.24 us (1%)
    ppermute x9, starting transfers between devices, send(): lax.ppermute(value, axis, [(i, give(i, step, size)) for i in range(size)])  13.5 us
    pallas_call x1, Pallas kernels, on_device(): pl.pallas_call(functools.partial(down_kernel, count, groups - 1, pieces),...  2.85 us
    pallas_call x1, Pallas kernels, on_device(): pl.pallas_call(functools.partial(front_kernel, count, pieces), out_shape=...  2.6 us
    pallas_call x1, Pallas kernels, on_device(): pl.pallas_call(functools.partial(own_kernel, pieces), out_shape=jax.Shape...  0.96 us
    pallas_call x1, Pallas kernels, on_device(): pl.pallas_call(functools.partial(gate_kernel, count), out_shape=jax.Shape...  0.61 us
  transfers between devices with their start and end apart: 9, of which 1 were waited for; matrix products, arithmetic and copies ran while one was open for 0% of the time, Pallas kernels for 19%

profile of v12, /device:TPU:0, one launch (start us, length us, event | category | flops | bytes accessed | tf_op | source)
XLA Modules:
  0.0 21.7 jit_solution(2505178009820710403)
XLA Ops:
  0.6 2.6 %front.1 = (s32[8,128]{1,0:T(8,128)S(1)}, f32[32,128]{1,0:T(8,128)S(1)}, bf16[384,4096]{1,0:T(8,128)(2,1)S(1)}, bf16[16,384]{1,0:T(8,128)(2,1)S(1)}, bf16[4,4224...) custom-call(s32[8,128]{1,0:T(8,128)} %bitcast.4, ...), custom_call_target="tpu_custom_call" | custom-call | flops 134217728 | bytes 4194304 | tf_op jit(solution)/shard_map/front/pallas_call | solution.py:272
  3.2 5.1 %collective-permute-start = (bf16[8,4224]{1,0:T(8,128)(2,1)S(1)}, bf16[8,4224]{1,0:T(8,128)(2,1)S(1)}, u32[]{:S(2)}, u32[]{:S(2)}) collective-permute-start(bf16[8,4224]{1,0:T(8,128)(2,1)S(1)} %get-tuple-element.24.refs_1_), channel_id=1, source_target_pairs={{0,12},{4,8},{8,4},{12,0},{1,13},{5,9},{9,5},{13,1},{2,14},{6,10},... | collective-permute-start | bytes 202760 | tf_op jit(solution)/shard_map/ppermute | solution.py:60
  8.4 0.0 collective-permute-start.1
  8.4 0.6 %collective-permute-start.2 = (bf16[4,4224]{1,0:T(4,128)(2,1)S(1)}, bf16[4,4224]{1,0:T(4,128)(2,1)S(1)}, u32[]{:S(2)}, u32[]{:S(2)}) collective-permute-start(bf16[4,4224]{1,0:T(4,128)(2,1)S(1)} %get-tuple-element.26.refs_3_), channel_id=1, source_target_pairs={{0,4},{4,0},{8,12},{12,8},{1,5},{5,1},{9,13},{13,9},{2,6},{6,2},{1... | collective-permute-start | bytes 101384 | tf_op jit(solution)/shard_map/ppermute | solution.py:60
  9.0 2.3 %collective-permute-start.4 = (bf16[4,4096]{1,0:T(4,128)(2,1)S(1)}, bf16[4,4096]{1,0:T(4,128)(2,1)S(1)}, u32[]{:S(2)}, u32[]{:S(2)}) collective-permute-start(bf16[4,4096]{1,0:T(4,128)(2,1)S(1)} %get-tuple-element.35), channel_id=1, source_target_pairs={{0,8},{4,12},{8,0},{12,4},{1,9},{5,13},{9,1},{13,5},{2,10},{6,14},... | collective-permute-start | bytes 98312 | tf_op jit(solution)/shard_map/ppermute | solution.py:60
  11.3 2.0 %collective-permute-start.5 = (bf16[4,4096]{1,0:T(4,128)(2,1)S(1)}, bf16[4,4096]{1,0:T(4,128)(2,1)S(1)}, u32[]{:S(2)}, u32[]{:S(2)}) collective-permute-start(bf16[4,4096]{1,0:T(4,128)(2,1)S(1)} %get-tuple-element.36), channel_id=1, source_target_pairs={{0,4},{4,0},{8,12},{12,8},{1,5},{5,1},{9,13},{13,9},{2,6},{6,2},{1... | collective-permute-start | bytes 98312 | tf_op jit(solution)/shard_map/ppermute | solution.py:60
  13.3 0.2 %collective-permute-done.1.refs_2_ = bf16[4,4224]{1,0:T(4,128)(2,1)S(1)} collective-permute-done((bf16[4,4224]{1,0:T(4,128)(2,1)S(1)}, bf16[4,4224]{1,0:T(4,128)(2,1)S(1)}, u32[]{:S(2)}, u32[]{:S(2)}) %collective-permute-start.1) | collective-permute-done | bytes 33824 | tf_op jit(solution)/shard_map/ppermute | solution.py:60
  13.5 0.0 collective-permute-done.2.refs_3_
  13.5 0.0 collective-permute-done.refs_1_.refs_4_
  13.5 0.1 slots.1
  13.7 1.6 %collective-permute-start.3 = (bf16[16,2432]{1,0:T(8,128)(2,1)S(1)}, bf16[16,2432]{1,0:T(8,128)(2,1)S(1)}, u32[]{:S(2)}, u32[]{:S(2)}) collective-permute-start(bf16[16,2432]{1,0:T(8,128)(2,1)S(1)} %get-tuple-element.28), channel_id=1, source_target_pairs={{0,16},{16,0},{1,17},{17,1},{2,18},{18,2},{3,19},{19,3},{4,20},{20... | collective-permute-start | bytes 233480 | tf_op jit(solution)/shard_map/ppermute | solution.py:60
  15.2 0.0 collective-permute-done.4.refs_6_
  15.2 0.0 collective-permute-done.5.refs_7_
  15.2 0.2 backs.1.refs_0_
  15.4 0.0 collective-permute-start.8
  15.4 1.6 %collective-permute-start.7 = (f32[16,128]{1,0:T(8,128)S(1)}, f32[16,128]{1,0:T(8,128)S(1)}, u32[]{:S(2)}, u32[]{:S(2)}) collective-permute-start(f32[16,128]{1,0:T(8,128)S(1)} %backs.1.refs_0_), channel_id=1, source_target_pairs={{0,2},{1,3},{2,0},{3,1},{4,6},{5,7},{6,4},{7,5},{8,10},{9,11},{10,... | collective-permute-start | bytes 24584 | tf_op jit(solution)/shard_map/ppermute | solution.py:60
  17.0 0.3 %collective-permute-start.6 = (f32[16,128]{1,0:T(8,128)S(1)}, f32[16,128]{1,0:T(8,128)S(1)}, u32[]{:S(2)}, u32[]{:S(2)}) collective-permute-start(f32[16,128]{1,0:T(8,128)S(1)} %backs.1.refs_0_), channel_id=1, source_target_pairs={{0,1},{1,0},{2,3},{3,2},{4,5},{5,4},{6,7},{7,6},{8,9},{9,8},{10,11... | collective-permute-start | bytes 24584 | tf_op jit(solution)/shard_map/ppermute | solution.py:60
  17.2 1.0 %own.1.refs_0_ = bf16[384,2048]{1,0:T(8,128)(2,1)S(1)} custom-call(bf16[16,2432]{1,0:T(8,128)(2,1)S(1)} %get-tuple-element.27.pay_ref), custom_call_target="tpu_custom_call" | custom-call | flops 25165824 | bytes 1572864 | tf_op jit(solution)/shard_map/own/pallas_call | solution.py:336
  18.2 0.0 collective-permute-done.3.refs_1_
  18.2 2.8 %down.1 = (bf16[1,1,16,384]{3,2,1,0:T(8,128)(2,1)}, f32[1,384,2048]{2,1,0:T(8,128)}, f32[32,128]{1,0:T(8,128)S(1)}) custom-call(bf16[384,2048]{1,0:T(8,128)(2,1)S(1)} %own.1.refs_0_, bf16[16,2432]{1,0:T(8,128)(2,1)S(1)} %collective-permute-done.3.refs_1_, bf16[16,4096]{1,0:T(8,128)(2,1)S(1)} %get-tuple-element.29.refs_2_, ...), custom_call_target="tpu_custom_call" | custom-call | flops 75497472 | bytes 3145728 | tf_op jit(solution)/shard_map/down/pallas_call | solution.py:346
  21.1 0.0 collective-permute-done.8.refs_3_
  21.1 0.0 collective-permute-done.7.refs_2_
  21.1 0.0 collective-permute-done.6.refs_1_
  21.1 0.6 %gates.1 = f32[8,128]{1,0:T(8,128)} custom-call(s32[8,128]{1,0:T(8,128)S(1)} %get-tuple-element.21.ids_ref, f32[32,128]{1,0:T(8,128)S(1)} %get-tuple-element.33.match_ref, f32[16,128]{1,0:T(8,128)S(1)} %backs.1.refs_0_, f32[16,128]{1,0:T(8,128)S(1)} %collective-permute-done.6.refs_1_, f32[16,128]{1,0:T(8,128)S(1)} %collective-permute-done.7.refs_2_, ...), custom_call_target="tpu_custom_call" | custom-call | flops 2048 | bytes 8192 | tf_op jit(solution)/shard_map/gates/pallas_call | solution.py:365
Async XLA Ops:
  3.2 10.3 %collective-permute-start = (bf16[8,4224]{1,0:T(8,128)(2,1)S(1)}, bf16[8,4224]{1,0:T(8,128)(2,1)S(1)}, u32[]{:S(2)}, u32[]{:S(2)}) collective-permute-start(bf16[8,4224]{1,0:T(8,128)(2,1)S(1)} %get-tuple-element.24.refs_1_), channel_id=1, source_target_pairs={{0,12},{4,8},{8,4},{12,0},{1,13},{5,9},{9,5},{13,1},{2,14},{6,10},... | collective-permute-start | bytes 202760 | tf_op jit(solution)/shard_map/ppermute | solution.py:60
  8.4 5.2 %collective-permute-start.1 = (bf16[4,4224]{1,0:T(4,128)(2,1)S(1)}, bf16[4,4224]{1,0:T(4,128)(2,1)S(1)}, u32[]{:S(2)}, u32[]{:S(2)}) collective-permute-start(bf16[4,4224]{1,0:T(4,128)(2,1)S(1)} %get-tuple-element.25.refs_2_), channel_id=1, source_target_pairs={{0,8},{4,12},{8,0},{12,4},{1,9},{5,13},{9,1},{13,5},{2,10},{6,14},... | collective-permute-start | bytes 101384 | tf_op jit(solution)/shard_map/ppermute | solution.py:60
  8.4 5.2 %collective-permute-start.2 = (bf16[4,4224]{1,0:T(4,128)(2,1)S(1)}, bf16[4,4224]{1,0:T(4,128)(2,1)S(1)}, u32[]{:S(2)}, u32[]{:S(2)}) collective-permute-start(bf16[4,4224]{1,0:T(4,128)(2,1)S(1)} %get-tuple-element.26.refs_3_), channel_id=1, source_target_pairs={{0,4},{4,0},{8,12},{12,8},{1,5},{5,1},{9,13},{13,9},{2,6},{6,2},{1... | collective-permute-start | bytes 101384 | tf_op jit(solution)/shard_map/ppermute | solution.py:60
  9.0 6.2 %collective-permute-start.4 = (bf16[4,4096]{1,0:T(4,128)(2,1)S(1)}, bf16[4,4096]{1,0:T(4,128)(2,1)S(1)}, u32[]{:S(2)}, u32[]{:S(2)}) collective-permute-start(bf16[4,4096]{1,0:T(4,128)(2,1)S(1)} %get-tuple-element.35), channel_id=1, source_target_pairs={{0,8},{4,12},{8,0},{12,4},{1,9},{5,13},{9,1},{13,5},{2,10},{6,14},... | collective-permute-start | bytes 98312 | tf_op jit(solution)/shard_map/ppermute | solution.py:60
  11.3 3.9 %collective-permute-start.5 = (bf16[4,4096]{1,0:T(4,128)(2,1)S(1)}, bf16[4,4096]{1,0:T(4,128)(2,1)S(1)}, u32[]{:S(2)}, u32[]{:S(2)}) collective-permute-start(bf16[4,4096]{1,0:T(4,128)(2,1)S(1)} %get-tuple-element.36), channel_id=1, source_target_pairs={{0,4},{4,0},{8,12},{12,8},{1,5},{5,1},{9,13},{13,9},{2,6},{6,2},{1... | collective-permute-start | bytes 98312 | tf_op jit(solution)/shard_map/ppermute | solution.py:60
  13.7 4.6 %collective-permute-start.3 = (bf16[16,2432]{1,0:T(8,128)(2,1)S(1)}, bf16[16,2432]{1,0:T(8,128)(2,1)S(1)}, u32[]{:S(2)}, u32[]{:S(2)}) collective-permute-start(bf16[16,2432]{1,0:T(8,128)(2,1)S(1)} %get-tuple-element.28), channel_id=1, source_target_pairs={{0,16},{16,0},{1,17},{17,1},{2,18},{18,2},{3,19},{19,3},{4,20},{20... | collective-permute-start | bytes 233480 | tf_op jit(solution)/shard_map/ppermute | solution.py:60
  15.4 5.7 %collective-permute-start.8 = (f32[16,128]{1,0:T(8,128)S(1)}, f32[16,128]{1,0:T(8,128)S(1)}, u32[]{:S(2)}, u32[]{:S(2)}) collective-permute-start(f32[16,128]{1,0:T(8,128)S(1)} %backs.1.refs_0_), channel_id=1, source_target_pairs={{0,3},{1,2},{2,1},{3,0},{4,7},{5,6},{6,5},{7,4},{8,11},{9,10},{10,... | collective-permute-start | bytes 24584 | tf_op jit(solution)/shard_map/ppermute | solution.py:60
  15.4 5.7 %collective-permute-start.7 = (f32[16,128]{1,0:T(8,128)S(1)}, f32[16,128]{1,0:T(8,128)S(1)}, u32[]{:S(2)}, u32[]{:S(2)}) collective-permute-start(f32[16,128]{1,0:T(8,128)S(1)} %backs.1.refs_0_), channel_id=1, source_target_pairs={{0,2},{1,3},{2,0},{3,1},{4,6},{5,7},{6,4},{7,5},{8,10},{9,11},{10,... | collective-permute-start | bytes 24584 | tf_op jit(solution)/shard_map/ppermute | solution.py:60
  17.0 4.1 %collective-permute-start.6 = (f32[16,128]{1,0:T(8,128)S(1)}, f32[16,128]{1,0:T(8,128)S(1)}, u32[]{:S(2)}, u32[]{:S(2)}) collective-permute-start(f32[16,128]{1,0:T(8,128)S(1)} %backs.1.refs_0_), channel_id=1, source_target_pairs={{0,1},{1,0},{2,3},{3,2},{4,5},{5,4},{6,7},{7,6},{8,9},{9,8},{10,11... | collective-permute-start | bytes 24584 | tf_op jit(solution)/shard_map/ppermute | solution.py:60

commit v13 on v7

--- a/solution.py
+++ b/solution.py
@@ -182,25 +182,12 @@
         back_ref[r * CAP : (r + 1) * CAP, :] = jnp.broadcast_to(back, (CAP, LANES))
 
 
-def down_term(pay_ref, share, start, block):
-    hidden = pay_ref[:, pl.ds(start, block)]
-    return dot(hidden, pay_ref[:, :share], ((0,), (0,))).astype(jnp.bfloat16)
-
-
-def own_kernel(pieces, pay_ref, own_ref):
-    units, share = own_ref.shape
+def down_kernel(count, groups, pieces, rows_ref, gate_ref, weight_ref, match_ref, *refs):
+    pays = refs[:groups]
+    hidden_hbm, down_hbm, match_out, hidden_out, down_out, sems = refs[groups:]
+    units, share = down_out.shape
     block = units // pieces
-    for p in range(pieces):
-        own_ref[p * block : (p + 1) * block, :] = down_term(pay_ref, share, share + p * block, block)
-
-
-def down_kernel(count, others, pieces, *refs):
-    own_ref = refs[0]
-    pays = refs[1 : 1 + others]
-    rows_ref, gate_ref, weight_ref, match_ref = refs[1 + others : 5 + others]
-    hidden_hbm, down_hbm, match_out, hidden_out, down_out, sems = refs[5 + others :]
-    units, share = own_ref.shape
-    block = units // pieces
+    slots = jnp.concatenate([pay_ref[...] for pay_ref in pays], axis=0)
     copies = []
 
     def write(n, values, destination):
@@ -209,10 +196,8 @@
 
     for p in range(pieces):
         part = slice(p * block, (p + 1) * block)
-        total = own_ref[part, :].astype(jnp.float32)
-        for pay_ref in pays:
-            total = total + down_term(pay_ref, share, share + p * block, block).astype(jnp.float32)
-        down_out[part, :] = total
+        hidden = slots[:, share + p * block : share + (p + 1) * block]
+        down_out[part, :] = dot(hidden, slots[:, :share], ((0,), (0,)))
         part = pl.ds(p * block, block)
         write(p, down_out.at[part], down_hbm.at[0, part])
 
@@ -315,18 +300,8 @@
     others = [send(pays[r], "dp", r) for r in range(1, groups)]
     backs = [back] + [send(back, "tensor", r) for r in reversed(range(1, tensors))]
 
-    own = pl.pallas_call(
-        functools.partial(own_kernel, pieces),
-        out_shape=jax.ShapeDtypeStruct((units, share), jnp.bfloat16),
-        in_specs=[VMEM],
-        out_specs=VMEM,
-        compiler_params=PARAMS,
-        cost_estimate=cost(2 * slots * units * share, 2 * units * share),
-        name="own",
-    )(pays[0])
-
     hidden_grad, down_grad, match = pl.pallas_call(
-        functools.partial(down_kernel, count, groups - 1, pieces),
+        functools.partial(down_kernel, count, groups, pieces),
         out_shape=[
             jax.ShapeDtypeStruct(saved_hidden.shape, jnp.bfloat16),
             jax.ShapeDtypeStruct((1, units, share), jnp.float32),
@@ -342,7 +317,7 @@
         compiler_params=PARAMS,
         cost_estimate=cost(2 * slots * units * (width + share), 4 * units * share),
         name="down",
-    )(own, *others, rows, gate, weight, match)
+    )(rows, gate, weight, match, pays[0], *others)
 
     gate_grad = pl.pallas_call(
         functools.partial(gate_kernel, count),

time: 21.2 us -> 21.1 us (level)
  Pallas kernels: 6.29 us -> 5.66 us
  waiting for transfers between devices: 0.52 us -> 1.11 us
    pallas_call x2 -> x1, Pallas kernels: 2.81 us -> 2.18 us  [on_device(): pl.pallas_call(functools.partial(down_kernel, count, groups, pieces), out...]
    ppermute x9, waiting for transfers between devices: 0.52 us -> 1.11 us  [send(): lax.ppermute(value, axis, [(i, give(i, step, size)) for i in range(size)])]
  transfers between devices with their start and end apart: 9 -> 9, of which waited for: 2 -> 2; matrix products, arithmetic and copies ran while one was open for 0% -> 0% of each run, Pallas kernels for 15% -> 12%
where the time goes in v13:
time: 21.1 us; the launch traced here: 20.9 us
  starting transfers between devices  13.5 us (64%)
  Pallas kernels  5.66 us (27%)
  waiting for transfers between devices  1.11 us (5%)
  between operations  0.69 us (3%)
    ppermute x9, starting transfers between devices, send(): lax.ppermute(value, axis, [(i, give(i, step, size)) for i in range(size)])  13.5 us
    pallas_call x1, Pallas kernels, on_device(): pl.pallas_call(functools.partial(front_kernel, count, pieces), out_shape=...  2.59 us
    pallas_call x1, Pallas kernels, on_device(): pl.pallas_call(functools.partial(down_kernel, count, groups, pieces), out...  2.18 us
    ppermute x9, waiting for transfers between devices, send(): lax.ppermute(value, axis, [(i, give(i, step, size)) for i in range(size)])  1.11 us
    pallas_call x1, Pallas kernels, on_device(): pl.pallas_call(functools.partial(gate_kernel, count), out_shape=jax.Shape...  0.61 us
  transfers between devices with their start and end apart: 9, of which 2 were waited for; matrix products, arithmetic and copies ran while one was open for 0% of the time, Pallas kernels for 12%

profile of v13, /device:TPU:0, one launch (start us, length us, event | category | flops | bytes accessed | tf_op | source)
XLA Modules:
  0.0 20.9 jit_solution(5079730479851916507)
XLA Ops:
  0.6 2.6 %front.1 = (s32[8,128]{1,0:T(8,128)S(1)}, f32[32,128]{1,0:T(8,128)S(1)}, bf16[384,4096]{1,0:T(8,128)(2,1)S(1)}, bf16[16,384]{1,0:T(8,128)(2,1)S(1)}, bf16[4,4224...) custom-call(s32[8,128]{1,0:T(8,128)} %bitcast.4, ...), custom_call_target="tpu_custom_call" | custom-call | flops 134217728 | bytes 4194304 | tf_op jit(solution)/shard_map/front/pallas_call | solution.py:240
  3.2 5.1 %collective-permute-start = (bf16[8,4224]{1,0:T(8,128)(2,1)S(1)}, bf16[8,4224]{1,0:T(8,128)(2,1)S(1)}, u32[]{:S(2)}, u32[]{:S(2)}) collective-permute-start(bf16[8,4224]{1,0:T(8,128)(2,1)S(1)} %get-tuple-element.24.refs_1_), channel_id=1, source_target_pairs={{0,12},{4,8},{8,4},{12,0},{1,13},{5,9},{9,5},{13,1},{2,14},{6,10},... | collective-permute-start | bytes 202760 | tf_op jit(solution)/shard_map/ppermute | solution.py:60
  8.3 0.0 collective-permute-start.1
  8.3 0.6 %collective-permute-start.2 = (bf16[4,4224]{1,0:T(4,128)(2,1)S(1)}, bf16[4,4224]{1,0:T(4,128)(2,1)S(1)}, u32[]{:S(2)}, u32[]{:S(2)}) collective-permute-start(bf16[4,4224]{1,0:T(4,128)(2,1)S(1)} %get-tuple-element.26.refs_3_), channel_id=1, source_target_pairs={{0,4},{4,0},{8,12},{12,8},{1,5},{5,1},{9,13},{13,9},{2,6},{6,2},{1... | collective-permute-start | bytes 101384 | tf_op jit(solution)/shard_map/ppermute | solution.py:60
  9.0 2.3 %collective-permute-start.4 = (bf16[4,4096]{1,0:T(4,128)(2,1)S(1)}, bf16[4,4096]{1,0:T(4,128)(2,1)S(1)}, u32[]{:S(2)}, u32[]{:S(2)}) collective-permute-start(bf16[4,4096]{1,0:T(4,128)(2,1)S(1)} %get-tuple-element.35), channel_id=1, source_target_pairs={{0,8},{4,12},{8,0},{12,4},{1,9},{5,13},{9,1},{13,5},{2,10},{6,14},... | collective-permute-start | bytes 98312 | tf_op jit(solution)/shard_map/ppermute | solution.py:60
  11.3 2.0 %collective-permute-start.5 = (bf16[4,4096]{1,0:T(4,128)(2,1)S(1)}, bf16[4,4096]{1,0:T(4,128)(2,1)S(1)}, u32[]{:S(2)}, u32[]{:S(2)}) collective-permute-start(bf16[4,4096]{1,0:T(4,128)(2,1)S(1)} %get-tuple-element.36), channel_id=1, source_target_pairs={{0,4},{4,0},{8,12},{12,8},{1,5},{5,1},{9,13},{13,9},{2,6},{6,2},{1... | collective-permute-start | bytes 98312 | tf_op jit(solution)/shard_map/ppermute | solution.py:60
  13.3 0.2 %collective-permute-done.1.refs_2_ = bf16[4,4224]{1,0:T(4,128)(2,1)S(1)} collective-permute-done((bf16[4,4224]{1,0:T(4,128)(2,1)S(1)}, bf16[4,4224]{1,0:T(4,128)(2,1)S(1)}, u32[]{:S(2)}, u32[]{:S(2)}) %collective-permute-start.1) | collective-permute-done | bytes 33824 | tf_op jit(solution)/shard_map/ppermute | solution.py:60
  13.5 0.0 collective-permute-done.2.refs_3_
  13.5 0.0 collective-permute-done.refs_1_.refs_4_
  13.5 0.1 slots.1
  13.6 1.6 %collective-permute-start.3 = (bf16[16,2432]{1,0:T(8,128)(2,1)S(1)}, bf16[16,2432]{1,0:T(8,128)(2,1)S(1)}, u32[]{:S(2)}, u32[]{:S(2)}) collective-permute-start(bf16[16,2432]{1,0:T(8,128)(2,1)S(1)} %get-tuple-element.32), channel_id=1, source_target_pairs={{0,16},{16,0},{1,17},{17,1},{2,18},{18,2},{3,19},{19,3},{4,20},{20... | collective-permute-start | bytes 233480 | tf_op jit(solution)/shard_map/ppermute | solution.py:60
  15.2 0.0 collective-permute-done.4.refs_6_
  15.2 0.0 collective-permute-done.5.refs_7_
  15.2 0.2 backs.1.refs_0_
  15.4 0.0 collective-permute-start.8
  15.4 1.6 %collective-permute-start.7 = (f32[16,128]{1,0:T(8,128)S(1)}, f32[16,128]{1,0:T(8,128)S(1)}, u32[]{:S(2)}, u32[]{:S(2)}) collective-permute-start(f32[16,128]{1,0:T(8,128)S(1)} %backs.1.refs_0_), channel_id=1, source_target_pairs={{0,2},{1,3},{2,0},{3,1},{4,6},{5,7},{6,4},{7,5},{8,10},{9,11},{10,... | collective-permute-start | bytes 24584 | tf_op jit(solution)/shard_map/ppermute | solution.py:60
  17.0 0.3 %collective-permute-start.6 = (f32[16,128]{1,0:T(8,128)S(1)}, f32[16,128]{1,0:T(8,128)S(1)}, u32[]{:S(2)}, u32[]{:S(2)}) collective-permute-start(f32[16,128]{1,0:T(8,128)S(1)} %backs.1.refs_0_), channel_id=1, source_target_pairs={{0,1},{1,0},{2,3},{3,2},{4,5},{5,4},{6,7},{7,6},{8,9},{9,8},{10,11... | collective-permute-start | bytes 24584 | tf_op jit(solution)/shard_map/ppermute | solution.py:60
  17.2 0.9 %collective-permute-done.3.refs_1_ = bf16[16,2432]{1,0:T(8,128)(2,1)S(1)} collective-permute-done((bf16[16,2432]{1,0:T(8,128)(2,1)S(1)}, bf16[16,2432]{1,0:T(8,128)(2,1)S(1)}, u32[]{:S(2)}, u32[]{:S(2)}) %collective-permute-start.3) | collective-permute-done | bytes 77856 | tf_op jit(solution)/shard_map/ppermute | solution.py:60
  18.1 2.2 %down.1 = (bf16[1,1,16,384]{3,2,1,0:T(8,128)(2,1)}, f32[1,384,2048]{2,1,0:T(8,128)}, f32[32,128]{1,0:T(8,128)S(1)}) custom-call(bf16[16,4096]{1,0:T(8,128)(2,1)S(1)} %get-tuple-element.27.rows_ref, f32[16,128]{1,0:T(8,128)S(1)} %get-tuple-element.28.gate_ref, bf16[384,4096]{1,0:T(8,128)(2,1)S(1)} %get-tuple-element.29.weight_ref, ...), custom_call_target="tpu_custom_call" | custom-call | flops 75497472 | bytes 3145728 | tf_op jit(solution)/shard_map/down/pallas_call | solution.py:303
  20.3 0.0 collective-permute-done.8.refs_3_
  20.3 0.0 collective-permute-done.7.refs_2_
  20.3 0.0 collective-permute-done.6.refs_1_
  20.3 0.6 %gates.1 = f32[8,128]{1,0:T(8,128)} custom-call(s32[8,128]{1,0:T(8,128)S(1)} %get-tuple-element.21.ids_ref, f32[32,128]{1,0:T(8,128)S(1)} %get-tuple-element.33.match_ref, f32[16,128]{1,0:T(8,128)S(1)} %backs.1.refs_0_, f32[16,128]{1,0:T(8,128)S(1)} %collective-permute-done.6.refs_1_, f32[16,128]{1,0:T(8,128)S(1)} %collective-permute-done.7.refs_2_, ...), custom_call_target="tpu_custom_call" | custom-call | flops 2048 | bytes 8192 | tf_op jit(solution)/shard_map/gates/pallas_call | solution.py:322
Async XLA Ops:
  3.2 10.3 %collective-permute-start = (bf16[8,4224]{1,0:T(8,128)(2,1)S(1)}, bf16[8,4224]{1,0:T(8,128)(2,1)S(1)}, u32[]{:S(2)}, u32[]{:S(2)}) collective-permute-start(bf16[8,4224]{1,0:T(8,128)(2,1)S(1)} %get-tuple-element.24.refs_1_), channel_id=1, source_target_pairs={{0,12},{4,8},{8,4},{12,0},{1,13},{5,9},{9,5},{13,1},{2,14},{6,10},... | collective-permute-start | bytes 202760 | tf_op jit(solution)/shard_map/ppermute | solution.py:60
  8.3 5.2 %collective-permute-start.1 = (bf16[4,4224]{1,0:T(4,128)(2,1)S(1)}, bf16[4,4224]{1,0:T(4,128)(2,1)S(1)}, u32[]{:S(2)}, u32[]{:S(2)}) collective-permute-start(bf16[4,4224]{1,0:T(4,128)(2,1)S(1)} %get-tuple-element.25.refs_2_), channel_id=1, source_target_pairs={{0,8},{4,12},{8,0},{12,4},{1,9},{5,13},{9,1},{13,5},{2,10},{6,14},... | collective-permute-start | bytes 101384 | tf_op jit(solution)/shard_map/ppermute | solution.py:60
  8.3 5.2 %collective-permute-start.2 = (bf16[4,4224]{1,0:T(4,128)(2,1)S(1)}, bf16[4,4224]{1,0:T(4,128)(2,1)S(1)}, u32[]{:S(2)}, u32[]{:S(2)}) collective-permute-start(bf16[4,4224]{1,0:T(4,128)(2,1)S(1)} %get-tuple-element.26.refs_3_), channel_id=1, source_target_pairs={{0,4},{4,0},{8,12},{12,8},{1,5},{5,1},{9,13},{13,9},{2,6},{6,2},{1... | collective-permute-start | bytes 101384 | tf_op jit(solution)/shard_map/ppermute | solution.py:60
  9.0 6.2 %collective-permute-start.4 = (bf16[4,4096]{1,0:T(4,128)(2,1)S(1)}, bf16[4,4096]{1,0:T(4,128)(2,1)S(1)}, u32[]{:S(2)}, u32[]{:S(2)}) collective-permute-start(bf16[4,4096]{1,0:T(4,128)(2,1)S(1)} %get-tuple-element.35), channel_id=1, source_target_pairs={{0,8},{4,12},{8,0},{12,4},{1,9},{5,13},{9,1},{13,5},{2,10},{6,14},... | collective-permute-start | bytes 98312 | tf_op jit(solution)/shard_map/ppermute | solution.py:60
  11.3 3.9 %collective-permute-start.5 = (bf16[4,4096]{1,0:T(4,128)(2,1)S(1)}, bf16[4,4096]{1,0:T(4,128)(2,1)S(1)}, u32[]{:S(2)}, u32[]{:S(2)}) collective-permute-start(bf16[4,4096]{1,0:T(4,128)(2,1)S(1)} %get-tuple-element.36), channel_id=1, source_target_pairs={{0,4},{4,0},{8,12},{12,8},{1,5},{5,1},{9,13},{13,9},{2,6},{6,2},{1... | collective-permute-start | bytes 98312 | tf_op jit(solution)/shard_map/ppermute | solution.py:60
  13.6 4.5 %collective-permute-start.3 = (bf16[16,2432]{1,0:T(8,128)(2,1)S(1)}, bf16[16,2432]{1,0:T(8,128)(2,1)S(1)}, u32[]{:S(2)}, u32[]{:S(2)}) collective-permute-start(bf16[16,2432]{1,0:T(8,128)(2,1)S(1)} %get-tuple-element.32), channel_id=1, source_target_pairs={{0,16},{16,0},{1,17},{17,1},{2,18},{18,2},{3,19},{19,3},{4,20},{20... | collective-permute-start | bytes 233480 | tf_op jit(solution)/shard_map/ppermute | solution.py:60
  15.4 4.9 %collective-permute-start.8 = (f32[16,128]{1,0:T(8,128)S(1)}, f32[16,128]{1,0:T(8,128)S(1)}, u32[]{:S(2)}, u32[]{:S(2)}) collective-permute-start(f32[16,128]{1,0:T(8,128)S(1)} %backs.1.refs_0_), channel_id=1, source_target_pairs={{0,3},{1,2},{2,1},{3,0},{4,7},{5,6},{6,5},{7,4},{8,11},{9,10},{10,... | collective-permute-start | bytes 24584 | tf_op jit(solution)/shard_map/ppermute | solution.py:60
  15.4 4.9 %collective-permute-start.7 = (f32[16,128]{1,0:T(8,128)S(1)}, f32[16,128]{1,0:T(8,128)S(1)}, u32[]{:S(2)}, u32[]{:S(2)}) collective-permute-start(f32[16,128]{1,0:T(8,128)S(1)} %backs.1.refs_0_), channel_id=1, source_target_pairs={{0,2},{1,3},{2,0},{3,1},{4,6},{5,7},{6,4},{7,5},{8,10},{9,11},{10,... | collective-permute-start | bytes 24584 | tf_op jit(solution)/shard_map/ppermute | solution.py:60
  17.0 3.4 %collective-permute-start.6 = (f32[16,128]{1,0:T(8,128)S(1)}, f32[16,128]{1,0:T(8,128)S(1)}, u32[]{:S(2)}, u32[]{:S(2)}) collective-permute-start(f32[16,128]{1,0:T(8,128)S(1)} %backs.1.refs_0_), channel_id=1, source_target_pairs={{0,1},{1,0},{2,3},{3,2},{4,5},{5,4},{6,7},{7,6},{8,9},{9,8},{10,11... | collective-permute-start | bytes 24584 | tf_op jit(solution)/shard_map/ppermute | solution.py:60

commit v14 on v13

--- a/solution.py
+++ b/solution.py
@@ -182,7 +182,15 @@
         back_ref[r * CAP : (r + 1) * CAP, :] = jnp.broadcast_to(back, (CAP, LANES))
 
 
-def down_kernel(count, groups, pieces, rows_ref, gate_ref, weight_ref, match_ref, *refs):
+def upstream_part(rows_ref, weight_ref, begin, end):
+    return dot(rows_ref[:, begin:end], weight_ref[:, begin:end], ((1,), (1,)))
+
+
+def upstream_kernel(split, rows_ref, weight_ref, out_ref):
+    out_ref[...] = upstream_part(rows_ref, weight_ref, 0, split)
+
+
+def down_kernel(count, groups, pieces, split, part_ref, rows_ref, gate_ref, weight_ref, match_ref, *refs):
     pays = refs[:groups]
     hidden_hbm, down_hbm, match_out, hidden_out, down_out, sems = refs[groups:]
     units, share = down_out.shape
@@ -202,7 +210,7 @@
         write(p, down_out.at[part], down_hbm.at[0, part])
 
     match_out[...] = match_ref[...]
-    upstream = dot(rows_ref[...], weight_ref[...], ((1,), (1,)))
+    upstream = part_ref[...] + upstream_part(rows_ref, weight_ref, split, weight_ref.shape[1])
     scaled = (gate_ref[:, :1] * upstream).astype(jnp.bfloat16)
     hidden_out[...] = dot(slot_order(count), scaled, ((0,), (0,))).astype(jnp.bfloat16)
     write(pieces, hidden_out, hidden_hbm.at[0, 0])
@@ -300,14 +308,25 @@
     others = [send(pays[r], "dp", r) for r in range(1, groups)]
     backs = [back] + [send(back, "tensor", r) for r in reversed(range(1, tensors))]
 
+    split = width * 5 // 8
+    upstream = pl.pallas_call(
+        functools.partial(upstream_kernel, split),
+        out_shape=jax.ShapeDtypeStruct((slots, units), jnp.float32),
+        in_specs=[VMEM] * 2,
+        out_specs=VMEM,
+        compiler_params=PARAMS,
+        cost_estimate=cost(2 * slots * units * split, 2 * units * split),
+        name="upstream",
+    )(rows, weight)
+
     hidden_grad, down_grad, match = pl.pallas_call(
-        functools.partial(down_kernel, count, groups, pieces),
+        functools.partial(down_kernel, count, groups, pieces, split),
         out_shape=[
             jax.ShapeDtypeStruct(saved_hidden.shape, jnp.bfloat16),
             jax.ShapeDtypeStruct((1, units, share), jnp.float32),
             jax.ShapeDtypeStruct(match.shape, jnp.float32),
         ],
-        in_specs=[VMEM] * (4 + groups),
+        in_specs=[VMEM] * (5 + groups),
         out_specs=[HBM, HBM, VMEM],
         scratch_shapes=[
             pltpu.VMEM((slots, units), jnp.bfloat16),
@@ -317,7 +336,7 @@
         compiler_params=PARAMS,
         cost_estimate=cost(2 * slots * units * (width + share), 4 * units * share),
         name="down",
-    )(rows, gate, weight, match, pays[0], *others)
+    )(upstream, rows, gate, weight, match, pays[0], *others)
 
     gate_grad = pl.pallas_call(
         functools.partial(gate_kernel, count),

time: 21.1 us -> 21 us (level)
  waiting for transfers between devices: 1.11 us -> 0.49 us
  Pallas kernels: 5.66 us -> 6.14 us
    ppermute x9, waiting for transfers between devices: 1.11 us -> 0.49 us  [send(): lax.ppermute(value, axis, [(i, give(i, step, size)) for i in range(size)])]
    pallas_call x1 -> x2, Pallas kernels: 2.18 us -> 2.67 us  [the longest x1 2.05 us: on_device(): pl.pallas_call(functools.partial(down_kernel, count, groups, pieces, spli...]
  transfers between devices with their start and end apart: 9 -> 9, of which waited for: 2 -> 2; matrix products, arithmetic and copies ran while one was open for 0% -> 0% of each run, Pallas kernels for 12% -> 14%
where the time goes in v14:
time: 21 us; the launch traced here: 20.8 us
  starting transfers between devices  13.5 us (64%)
  Pallas kernels  6.14 us (29%)
  between operations  0.69 us (3%)
  waiting for transfers between devices  0.49 us (2%)
    ppermute x9, starting transfers between devices, send(): lax.ppermute(value, axis, [(i, give(i, step, size)) for i in range(size)])  13.5 us
    pallas_call x1, Pallas kernels, on_device(): pl.pallas_call(functools.partial(front_kernel, count, pieces), out_shape=...  2.59 us
    pallas_call x1, Pallas kernels, on_device(): pl.pallas_call(functools.partial(down_kernel, count, groups, pieces, spli...  2.05 us
    pallas_call x1, Pallas kernels, on_device(): pl.pallas_call(functools.partial(upstream_kernel, split), out_shape=jax.S...  0.62 us
    pallas_call x1, Pallas kernels, on_device(): pl.pallas_call(functools.partial(gate_kernel, count), out_shape=jax.Shape...  0.61 us
    ppermute x9, waiting for transfers between devices, send(): lax.ppermute(value, axis, [(i, give(i, step, size)) for i in range(size)])  0.49 us
  transfers between devices with their start and end apart: 9, of which 2 were waited for; matrix products, arithmetic and copies ran while one was open for 0% of the time, Pallas kernels for 14%

profile of v14, /device:TPU:0, one launch (start us, length us, event | category | flops | bytes accessed | tf_op | source)
XLA Modules:
  0.0 20.8 jit_solution(8972452581808715029)
XLA Ops:
  0.6 2.6 %front.1 = (s32[8,128]{1,0:T(8,128)S(1)}, f32[32,128]{1,0:T(8,128)S(1)}, bf16[384,4096]{1,0:T(8,128)(2,1)S(1)}, bf16[16,384]{1,0:T(8,128)(2,1)S(1)}, bf16[4,4224...) custom-call(s32[8,128]{1,0:T(8,128)} %bitcast.4, ...), custom_call_target="tpu_custom_call" | custom-call | flops 134217728 | bytes 4194304 | tf_op jit(solution)/shard_map/front/pallas_call | solution.py:248
  3.2 5.1 %collective-permute-start = (bf16[8,4224]{1,0:T(8,128)(2,1)S(1)}, bf16[8,4224]{1,0:T(8,128)(2,1)S(1)}, u32[]{:S(2)}, u32[]{:S(2)}) collective-permute-start(bf16[8,4224]{1,0:T(8,128)(2,1)S(1)} %get-tuple-element.24.refs_1_), channel_id=1, source_target_pairs={{0,12},{4,8},{8,4},{12,0},{1,13},{5,9},{9,5},{13,1},{2,14},{6,10},... | collective-permute-start | bytes 202760 | tf_op jit(solution)/shard_map/ppermute | solution.py:60
  8.3 0.0 collective-permute-start.1
  8.3 0.6 %collective-permute-start.2 = (bf16[4,4224]{1,0:T(4,128)(2,1)S(1)}, bf16[4,4224]{1,0:T(4,128)(2,1)S(1)}, u32[]{:S(2)}, u32[]{:S(2)}) collective-permute-start(bf16[4,4224]{1,0:T(4,128)(2,1)S(1)} %get-tuple-element.26.refs_3_), channel_id=1, source_target_pairs={{0,4},{4,0},{8,12},{12,8},{1,5},{5,1},{9,13},{13,9},{2,6},{6,2},{1... | collective-permute-start | bytes 101384 | tf_op jit(solution)/shard_map/ppermute | solution.py:60
  9.0 2.3 %collective-permute-start.4 = (bf16[4,4096]{1,0:T(4,128)(2,1)S(1)}, bf16[4,4096]{1,0:T(4,128)(2,1)S(1)}, u32[]{:S(2)}, u32[]{:S(2)}) collective-permute-start(bf16[4,4096]{1,0:T(4,128)(2,1)S(1)} %get-tuple-element.35), channel_id=1, source_target_pairs={{0,8},{4,12},{8,0},{12,4},{1,9},{5,13},{9,1},{13,5},{2,10},{6,14},... | collective-permute-start | bytes 98312 | tf_op jit(solution)/shard_map/ppermute | solution.py:60
  11.3 2.0 %collective-permute-start.5 = (bf16[4,4096]{1,0:T(4,128)(2,1)S(1)}, bf16[4,4096]{1,0:T(4,128)(2,1)S(1)}, u32[]{:S(2)}, u32[]{:S(2)}) collective-permute-start(bf16[4,4096]{1,0:T(4,128)(2,1)S(1)} %get-tuple-element.36), channel_id=1, source_target_pairs={{0,4},{4,0},{8,12},{12,8},{1,5},{5,1},{9,13},{13,9},{2,6},{6,2},{1... | collective-permute-start | bytes 98312 | tf_op jit(solution)/shard_map/ppermute | solution.py:60
  13.3 0.2 %collective-permute-done.1.refs_2_ = bf16[4,4224]{1,0:T(4,128)(2,1)S(1)} collective-permute-done((bf16[4,4224]{1,0:T(4,128)(2,1)S(1)}, bf16[4,4224]{1,0:T(4,128)(2,1)S(1)}, u32[]{:S(2)}, u32[]{:S(2)}) %collective-permute-start.1) | collective-permute-done | bytes 33824 | tf_op jit(solution)/shard_map/ppermute | solution.py:60
  13.5 0.0 collective-permute-done.2.refs_3_
  13.5 0.0 collective-permute-done.refs_1_.refs_4_
  13.5 0.1 slots.1
  13.6 1.6 %collective-permute-start.3 = (bf16[16,2432]{1,0:T(8,128)(2,1)S(1)}, bf16[16,2432]{1,0:T(8,128)(2,1)S(1)}, u32[]{:S(2)}, u32[]{:S(2)}) collective-permute-start(bf16[16,2432]{1,0:T(8,128)(2,1)S(1)} %get-tuple-element.32), channel_id=1, source_target_pairs={{0,16},{16,0},{1,17},{17,1},{2,18},{18,2},{3,19},{19,3},{4,20},{20... | collective-permute-start | bytes 233480 | tf_op jit(solution)/shard_map/ppermute | solution.py:60
  15.2 0.0 collective-permute-done.4.refs_6_
  15.2 0.0 collective-permute-done.5.refs_7_
  15.2 0.2 backs.1.refs_0_
  15.4 0.0 collective-permute-start.8
  15.4 1.6 %collective-permute-start.7 = (f32[16,128]{1,0:T(8,128)S(1)}, f32[16,128]{1,0:T(8,128)S(1)}, u32[]{:S(2)}, u32[]{:S(2)}) collective-permute-start(f32[16,128]{1,0:T(8,128)S(1)} %backs.1.refs_0_), channel_id=1, source_target_pairs={{0,2},{1,3},{2,0},{3,1},{4,6},{5,7},{6,4},{7,5},{8,10},{9,11},{10,... | collective-permute-start | bytes 24584 | tf_op jit(solution)/shard_map/ppermute | solution.py:60
  17.0 0.3 %collective-permute-start.6 = (f32[16,128]{1,0:T(8,128)S(1)}, f32[16,128]{1,0:T(8,128)S(1)}, u32[]{:S(2)}, u32[]{:S(2)}) collective-permute-start(f32[16,128]{1,0:T(8,128)S(1)} %backs.1.refs_0_), channel_id=1, source_target_pairs={{0,1},{1,0},{2,3},{3,2},{4,5},{5,4},{6,7},{7,6},{8,9},{9,8},{10,11... | collective-permute-start | bytes 24584 | tf_op jit(solution)/shard_map/ppermute | solution.py:60
  17.2 0.6 %upstream.1.part_ref = f32[16,384]{1,0:T(8,128)S(1)} custom-call(bf16[16,4096]{1,0:T(8,128)(2,1)S(1)} %get-tuple-element.27.rows_ref, bf16[384,4096]{1,0:T(8,128)(2,1)S(1)} %get-tuple-element.28.weight_ref), custom_call_target="tpu_custom_call" | custom-call | flops 31457280 | bytes 1966080 | tf_op jit(solution)/shard_map/upstream/pallas_call | solution.py:312
  17.9 0.2 %collective-permute-done.3.refs_1_ = bf16[16,2432]{1,0:T(8,128)(2,1)S(1)} collective-permute-done((bf16[16,2432]{1,0:T(8,128)(2,1)S(1)}, bf16[16,2432]{1,0:T(8,128)(2,1)S(1)}, u32[]{:S(2)}, u32[]{:S(2)}) %collective-permute-start.3) | collective-permute-done | bytes 77856 | tf_op jit(solution)/shard_map/ppermute | solution.py:60
  18.1 2.0 %down.1 = (bf16[1,1,16,384]{3,2,1,0:T(8,128)(2,1)}, f32[1,384,2048]{2,1,0:T(8,128)}, f32[32,128]{1,0:T(8,128)S(1)}) custom-call(f32[16,384]{1,0:T(8,128)S(1)} %upstream.1.part_ref, bf16[16,4096]{1,0:T(8,128)(2,1)S(1)} %get-tuple-element.27.rows_ref, f32[16,128]{1,0:T(8,128)S(1)} %get-tuple-element.29.gate_ref, ...), custom_call_target="tpu_custom_call" | custom-call | flops 75497472 | bytes 3145728 | tf_op jit(solution)/shard_map/down/pallas_call | solution.py:322
  20.2 0.0 collective-permute-done.8.refs_3_
  20.2 0.0 collective-permute-done.7.refs_2_
  20.2 0.0 collective-permute-done.6.refs_1_
  20.2 0.6 %gates.1 = f32[8,128]{1,0:T(8,128)} custom-call(s32[8,128]{1,0:T(8,128)S(1)} %get-tuple-element.21.ids_ref, f32[32,128]{1,0:T(8,128)S(1)} %get-tuple-element.33.match_ref, f32[16,128]{1,0:T(8,128)S(1)} %backs.1.refs_0_, f32[16,128]{1,0:T(8,128)S(1)} %collective-permute-done.6.refs_1_, f32[16,128]{1,0:T(8,128)S(1)} %collective-permute-done.7.refs_2_, ...), custom_call_target="tpu_custom_call" | custom-call | flops 2048 | bytes 8192 | tf_op jit(solution)/shard_map/gates/pallas_call | solution.py:341
Async XLA Ops:
  3.2 10.3 %collective-permute-start = (bf16[8,4224]{1,0:T(8,128)(2,1)S(1)}, bf16[8,4224]{1,0:T(8,128)(2,1)S(1)}, u32[]{:S(2)}, u32[]{:S(2)}) collective-permute-start(bf16[8,4224]{1,0:T(8,128)(2,1)S(1)} %get-tuple-element.24.refs_1_), channel_id=1, source_target_pairs={{0,12},{4,8},{8,4},{12,0},{1,13},{5,9},{9,5},{13,1},{2,14},{6,10},... | collective-permute-start | bytes 202760 | tf_op jit(solution)/shard_map/ppermute | solution.py:60
  8.3 5.2 %collective-permute-start.1 = (bf16[4,4224]{1,0:T(4,128)(2,1)S(1)}, bf16[4,4224]{1,0:T(4,128)(2,1)S(1)}, u32[]{:S(2)}, u32[]{:S(2)}) collective-permute-start(bf16[4,4224]{1,0:T(4,128)(2,1)S(1)} %get-tuple-element.25.refs_2_), channel_id=1, source_target_pairs={{0,8},{4,12},{8,0},{12,4},{1,9},{5,13},{9,1},{13,5},{2,10},{6,14},... | collective-permute-start | bytes 101384 | tf_op jit(solution)/shard_map/ppermute | solution.py:60
  8.3 5.2 %collective-permute-start.2 = (bf16[4,4224]{1,0:T(4,128)(2,1)S(1)}, bf16[4,4224]{1,0:T(4,128)(2,1)S(1)}, u32[]{:S(2)}, u32[]{:S(2)}) collective-permute-start(bf16[4,4224]{1,0:T(4,128)(2,1)S(1)} %get-tuple-element.26.refs_3_), channel_id=1, source_target_pairs={{0,4},{4,0},{8,12},{12,8},{1,5},{5,1},{9,13},{13,9},{2,6},{6,2},{1... | collective-permute-start | bytes 101384 | tf_op jit(solution)/shard_map/ppermute | solution.py:60
  9.0 6.2 %collective-permute-start.4 = (bf16[4,4096]{1,0:T(4,128)(2,1)S(1)}, bf16[4,4096]{1,0:T(4,128)(2,1)S(1)}, u32[]{:S(2)}, u32[]{:S(2)}) collective-permute-start(bf16[4,4096]{1,0:T(4,128)(2,1)S(1)} %get-tuple-element.35), channel_id=1, source_target_pairs={{0,8},{4,12},{8,0},{12,4},{1,9},{5,13},{9,1},{13,5},{2,10},{6,14},... | collective-permute-start | bytes 98312 | tf_op jit(solution)/shard_map/ppermute | solution.py:60
  11.3 3.9 %collective-permute-start.5 = (bf16[4,4096]{1,0:T(4,128)(2,1)S(1)}, bf16[4,4096]{1,0:T(4,128)(2,1)S(1)}, u32[]{:S(2)}, u32[]{:S(2)}) collective-permute-start(bf16[4,4096]{1,0:T(4,128)(2,1)S(1)} %get-tuple-element.36), channel_id=1, source_target_pairs={{0,4},{4,0},{8,12},{12,8},{1,5},{5,1},{9,13},{13,9},{2,6},{6,2},{1... | collective-permute-start | bytes 98312 | tf_op jit(solution)/shard_map/ppermute | solution.py:60
  13.6 4.5 %collective-permute-start.3 = (bf16[16,2432]{1,0:T(8,128)(2,1)S(1)}, bf16[16,2432]{1,0:T(8,128)(2,1)S(1)}, u32[]{:S(2)}, u32[]{:S(2)}) collective-permute-start(bf16[16,2432]{1,0:T(8,128)(2,1)S(1)} %get-tuple-element.32), channel_id=1, source_target_pairs={{0,16},{16,0},{1,17},{17,1},{2,18},{18,2},{3,19},{19,3},{4,20},{20... | collective-permute-start | bytes 233480 | tf_op jit(solution)/shard_map/ppermute | solution.py:60
  15.4 4.8 %collective-permute-start.8 = (f32[16,128]{1,0:T(8,128)S(1)}, f32[16,128]{1,0:T(8,128)S(1)}, u32[]{:S(2)}, u32[]{:S(2)}) collective-permute-start(f32[16,128]{1,0:T(8,128)S(1)} %backs.1.refs_0_), channel_id=1, source_target_pairs={{0,3},{1,2},{2,1},{3,0},{4,7},{5,6},{6,5},{7,4},{8,11},{9,10},{10,... | collective-permute-start | bytes 24584 | tf_op jit(solution)/shard_map/ppermute | solution.py:60
  15.4 4.8 %collective-permute-start.7 = (f32[16,128]{1,0:T(8,128)S(1)}, f32[16,128]{1,0:T(8,128)S(1)}, u32[]{:S(2)}, u32[]{:S(2)}) collective-permute-start(f32[16,128]{1,0:T(8,128)S(1)} %backs.1.refs_0_), channel_id=1, source_target_pairs={{0,2},{1,3},{2,0},{3,1},{4,6},{5,7},{6,4},{7,5},{8,10},{9,11},{10,... | collective-permute-start | bytes 24584 | tf_op jit(solution)/shard_map/ppermute | solution.py:60
  17.0 3.2 %collective-permute-start.6 = (f32[16,128]{1,0:T(8,128)S(1)}, f32[16,128]{1,0:T(8,128)S(1)}, u32[]{:S(2)}, u32[]{:S(2)}) collective-permute-start(f32[16,128]{1,0:T(8,128)S(1)} %backs.1.refs_0_), channel_id=1, source_target_pairs={{0,1},{1,0},{2,3},{3,2},{4,5},{5,4},{6,7},{7,6},{8,9},{9,8},{10,11... | collective-permute-start | bytes 24584 | tf_op jit(solution)/shard_map/ppermute | solution.py:60

commit v15 on v5

--- a/solution.py
+++ b/solution.py
@@ -182,40 +182,32 @@
         back_ref[r * CAP : (r + 1) * CAP, :] = jnp.broadcast_to(back, (CAP, LANES))
 
 
-def down_term(pay_ref, share, start, block):
-    hidden = pay_ref[:, pl.ds(start, block)]
-    return dot(hidden, pay_ref[:, :share], ((0,), (0,))).astype(jnp.bfloat16)
-
-
-def own_kernel(pieces, pay_ref, own_ref):
-    units, share = own_ref.shape
+def upstream_kernel(count, rows_ref, gate_ref, weight_ref, out_ref):
+    upstream = dot(rows_ref[...], weight_ref[...], ((1,), (1,)))
+    scaled = (gate_ref[:, :1] * upstream).astype(jnp.bfloat16)
+    out_ref[...] = dot(slot_order(count), scaled, ((0,), (0,))).astype(jnp.bfloat16)
+
+
+def last_kernel(count, groups, parts, pieces, ids_ref, match_ref, hidden_ref, *refs):
+    pays, refs = refs[:groups], refs[groups:]
+    backs, refs = refs[:parts], refs[parts:]
+    gate_hbm, hidden_hbm, down_hbm, gate_out, down_out, sems = refs
+    units, share = down_out.shape
     block = units // pieces
-    for p in range(pieces):
-        own_ref[p * block : (p + 1) * block, :] = down_term(pay_ref, share, share + p * block, block)
-
-
-def last_kernel(count, others, parts, pieces, *refs):
-    own_ref = refs[0]
-    pays = refs[1 : 1 + others]
-    backs = refs[1 + others : 1 + others + parts]
-    ids_ref, match_ref, rows_ref, gate_ref, weight_ref = refs[1 + others + parts : 6 + others + parts]
-    gate_hbm, hidden_hbm, down_hbm, gate_out, hidden_out, down_out, sems = refs[6 + others + parts :]
-    units, share = own_ref.shape
-    block = units // pieces
+    slots = jnp.concatenate([pay_ref[...] for pay_ref in pays], axis=0)
     copies = []
 
-    def write(n, values, destination):
-        copies.append(pltpu.make_async_copy(values, destination, sems.at[n]))
+    def write(values, destination):
+        copies.append(pltpu.make_async_copy(values, destination, sems.at[len(copies)]))
         copies[-1].start()
 
     for p in range(pieces):
         part = slice(p * block, (p + 1) * block)
-        total = own_ref[part, :].astype(jnp.float32)
-        for pay_ref in pays:
-            total = total + down_term(pay_ref, share, share + p * block, block).astype(jnp.float32)
-        down_out[part, :] = total
+        hidden = slots[:, share + p * block : share + (p + 1) * block]
+        down_out[part, :] = dot(hidden, slots[:, :share], ((0,), (0,)))
         part = pl.ds(p * block, block)
-        write(p, down_out.at[part], down_hbm.at[0, part])
+        write(down_out.at[part], down_hbm.at[0, part])
+    write(hidden_ref, hidden_hbm.at[0, 0])
 
     me = lax.axis_index("expert")
     ids = ids_ref[...]
@@ -229,12 +221,7 @@
         chosen = jnp.sum(jnp.where(match > 0, value, 0.0), axis=0, keepdims=True)
         total = total + jnp.where(ids == target(me, r, count), chosen, 0.0)
     gate_out[...] = total
-    write(pieces, gate_out, gate_hbm)
-
-    upstream = dot(rows_ref[...], weight_ref[...], ((1,), (1,)))
-    scaled = (gate_ref[:, :1] * upstream).astype(jnp.bfloat16)
-    hidden_out[...] = dot(slot_order(count), scaled, ((0,), (0,))).astype(jnp.bfloat16)
-    write(pieces + 1, hidden_out, hidden_hbm.at[0, 0])
+    write(gate_out, gate_hbm)
     for copy in copies:
         copy.wait()
 
@@ -311,37 +298,36 @@
     )(*sends, received[JOINT], *theirs)
 
     others = [send(pays[r], "dp", r) for r in range(1, groups)]
-    backs = [back] + [send(back, "tensor", r) for r in range(1, tensors)]
-
-    own = pl.pallas_call(
-        functools.partial(own_kernel, pieces),
-        out_shape=jax.ShapeDtypeStruct((units, share), jnp.bfloat16),
-        in_specs=[VMEM],
+    backs = [back] + [send(back, "tensor", r) for r in reversed(range(1, tensors))]
+
+    hidden_grad = pl.pallas_call(
+        functools.partial(upstream_kernel, count),
+        out_shape=jax.ShapeDtypeStruct((slots, units), jnp.bfloat16),
+        in_specs=[VMEM] * 3,
         out_specs=VMEM,
         compiler_params=PARAMS,
-        cost_estimate=cost(2 * slots * units * share, 2 * units * share),
-        name="own",
-    )(pays[0])
+        cost_estimate=cost(2 * slots * units * width, 2 * units * width),
+        name="upstream",
+    )(rows, gate, weight)
 
     gate_grad, hidden_grad, down_grad = pl.pallas_call(
-        functools.partial(last_kernel, count, groups - 1, tensors, pieces),
+        functools.partial(last_kernel, count, groups, tensors, pieces),
         out_shape=[
             jax.ShapeDtypeStruct(ids.shape, jnp.float32),
             jax.ShapeDtypeStruct(saved_hidden.shape, jnp.bfloat16),
             jax.ShapeDtypeStruct((1, units, share), jnp.float32),
         ],
-        in_specs=[VMEM] * (5 + groups + tensors),
+        in_specs=[VMEM] * (3 + groups + tensors),
         out_specs=[HBM] * 3,
         scratch_shapes=[
             pltpu.VMEM(ids.shape, jnp.float32),
-            pltpu.VMEM((slots, units), jnp.bfloat16),
             pltpu.VMEM((units, share), jnp.float32),
             pltpu.SemaphoreType.DMA((pieces + 2,)),
         ],
         compiler_params=PARAMS,
-        cost_estimate=cost(2 * slots * units * (width + share), 4 * units * share),
+        cost_estimate=cost(2 * slots * units * share, 4 * units * share),
         name="last",
-    )(own, *others, *backs, ids, match, rows, gate, weight)
+    )(ids, match, hidden_grad, pays[0], *others, *backs)
     return (gate_grad.T, hidden_grad, down_grad)
 
 

time: 22.5 us -> 21.3 us (0.947)
  waiting for transfers between devices: 2.44 us -> 1.06 us
  Pallas kernels: 5.69 us -> 5.93 us
    ppermute x9, waiting for transfers between devices: 2.44 us -> 1.06 us  [send(): lax.ppermute(value, axis, [(i, give(i, step, size)) for i in range(size)])]
    pallas_call x2, Pallas kernels: 2.82 us -> 3.06 us  [the longest x1 2.03 us: on_device(): pl.pallas_call(functools.partial(last_kernel, count, groups, tensors, pie...]
  transfers between devices with their start and end apart: 9 -> 9, of which waited for: 3 -> 3; matrix products, arithmetic and copies ran while one was open for 0% -> 0% of each run, Pallas kernels for 4% -> 6%
where the time goes in v15:
time: 21.3 us; the launch traced here: 21.1 us
  starting transfers between devices  13.5 us (63%)
  Pallas kernels  5.93 us (28%)
  waiting for transfers between devices  1.06 us (5%)
  between operations  0.66 us (3%)
    ppermute x9, starting transfers between devices, send(): lax.ppermute(value, axis, [(i, give(i, step, size)) for i in range(size)])  13.5 us
    pallas_call x1, Pallas kernels, on_device(): pl.pallas_call(functools.partial(front_kernel, count, pieces), out_shape=...  2.59 us
    pallas_call x1, Pallas kernels, on_device(): pl.pallas_call(functools.partial(last_kernel, count, groups, tensors, pie...  2.03 us
    ppermute x9, waiting for transfers between devices, send(): lax.ppermute(value, axis, [(i, give(i, step, size)) for i in range(size)])  1.06 us
    pallas_call x1, Pallas kernels, on_device(): pl.pallas_call(functools.partial(upstream_kernel, count), out_shape=jax.S...  1.03 us
  transfers between devices with their start and end apart: 9, of which 3 were waited for; matrix products, arithmetic and copies ran while one was open for 0% of the time, Pallas kernels for 6%

profile of v15, /device:TPU:0, one launch (start us, length us, event | category | flops | bytes accessed | tf_op | source)
XLA Modules:
  0.0 21.1 jit_solution(7642406054813464863)
XLA Ops:
  0.6 2.6 %front.1 = (s32[8,128]{1,0:T(8,128)S(1)}, f32[32,128]{1,0:T(8,128)S(1)}, bf16[384,4096]{1,0:T(8,128)(2,1)S(1)}, bf16[16,384]{1,0:T(8,128)(2,1)S(1)}, bf16[4,4224...) custom-call(s32[8,128]{1,0:T(8,128)} %bitcast.3, ...), custom_call_target="tpu_custom_call" | custom-call | flops 134217728 | bytes 4194304 | tf_op jit(solution)/shard_map/front/pallas_call | solution.py:240
  3.2 5.1 %collective-permute-start = (bf16[8,4224]{1,0:T(8,128)(2,1)S(1)}, bf16[8,4224]{1,0:T(8,128)(2,1)S(1)}, u32[]{:S(2)}, u32[]{:S(2)}) collective-permute-start(bf16[8,4224]{1,0:T(8,128)(2,1)S(1)} %get-tuple-element.25.refs_1_), channel_id=1, source_target_pairs={{0,12},{4,8},{8,4},{12,0},{1,13},{5,9},{9,5},{13,1},{2,14},{6,10},... | collective-permute-start | bytes 202760 | tf_op jit(solution)/shard_map/ppermute | solution.py:60
  8.3 0.0 collective-permute-start.1
  8.3 0.6 %collective-permute-start.2 = (bf16[4,4224]{1,0:T(4,128)(2,1)S(1)}, bf16[4,4224]{1,0:T(4,128)(2,1)S(1)}, u32[]{:S(2)}, u32[]{:S(2)}) collective-permute-start(bf16[4,4224]{1,0:T(4,128)(2,1)S(1)} %get-tuple-element.27.refs_3_), channel_id=1, source_target_pairs={{0,4},{4,0},{8,12},{12,8},{1,5},{5,1},{9,13},{13,9},{2,6},{6,2},{1... | collective-permute-start | bytes 101384 | tf_op jit(solution)/shard_map/ppermute | solution.py:60
  9.0 2.3 %collective-permute-start.4 = (bf16[4,4096]{1,0:T(4,128)(2,1)S(1)}, bf16[4,4096]{1,0:T(4,128)(2,1)S(1)}, u32[]{:S(2)}, u32[]{:S(2)}) collective-permute-start(bf16[4,4096]{1,0:T(4,128)(2,1)S(1)} %get-tuple-element.34), channel_id=1, source_target_pairs={{0,8},{4,12},{8,0},{12,4},{1,9},{5,13},{9,1},{13,5},{2,10},{6,14},... | collective-permute-start | bytes 98312 | tf_op jit(solution)/shard_map/ppermute | solution.py:60
  11.3 2.0 %collective-permute-start.5 = (bf16[4,4096]{1,0:T(4,128)(2,1)S(1)}, bf16[4,4096]{1,0:T(4,128)(2,1)S(1)}, u32[]{:S(2)}, u32[]{:S(2)}) collective-permute-start(bf16[4,4096]{1,0:T(4,128)(2,1)S(1)} %get-tuple-element.35), channel_id=1, source_target_pairs={{0,4},{4,0},{8,12},{12,8},{1,5},{5,1},{9,13},{13,9},{2,6},{6,2},{1... | collective-permute-start | bytes 98312 | tf_op jit(solution)/shard_map/ppermute | solution.py:60
  13.3 0.2 %collective-permute-done.1.refs_2_ = bf16[4,4224]{1,0:T(4,128)(2,1)S(1)} collective-permute-done((bf16[4,4224]{1,0:T(4,128)(2,1)S(1)}, bf16[4,4224]{1,0:T(4,128)(2,1)S(1)}, u32[]{:S(2)}, u32[]{:S(2)}) %collective-permute-start.1) | collective-permute-done | bytes 33824 | tf_op jit(solution)/shard_map/ppermute | solution.py:60
  13.5 0.0 collective-permute-done.2.refs_3_
  13.5 0.0 collective-permute-done.refs_1_.refs_4_
  13.5 0.1 slots.1
  13.6 1.6 %collective-permute-start.3 = (bf16[16,2432]{1,0:T(8,128)(2,1)S(1)}, bf16[16,2432]{1,0:T(8,128)(2,1)S(1)}, u32[]{:S(2)}, u32[]{:S(2)}) collective-permute-start(bf16[16,2432]{1,0:T(8,128)(2,1)S(1)} %get-tuple-element.32), channel_id=1, source_target_pairs={{0,16},{16,0},{1,17},{17,1},{2,18},{18,2},{3,19},{19,3},{4,20},{20... | collective-permute-start | bytes 233480 | tf_op jit(solution)/shard_map/ppermute | solution.py:60
  15.2 0.0 collective-permute-done.4.refs_6_
  15.2 0.0 collective-permute-done.5.refs_7_
  15.2 0.2 backs.1.refs_2_
  15.4 0.0 collective-permute-start.8
  15.4 1.6 %collective-permute-start.7 = (f32[16,128]{1,0:T(8,128)S(1)}, f32[16,128]{1,0:T(8,128)S(1)}, u32[]{:S(2)}, u32[]{:S(2)}) collective-permute-start(f32[16,128]{1,0:T(8,128)S(1)} %backs.1.refs_2_), channel_id=1, source_target_pairs={{0,2},{1,3},{2,0},{3,1},{4,6},{5,7},{6,4},{7,5},{8,10},{9,11},{10,... | collective-permute-start | bytes 24584 | tf_op jit(solution)/shard_map/ppermute | solution.py:60
  17.0 0.3 %collective-permute-start.6 = (f32[16,128]{1,0:T(8,128)S(1)}, f32[16,128]{1,0:T(8,128)S(1)}, u32[]{:S(2)}, u32[]{:S(2)}) collective-permute-start(f32[16,128]{1,0:T(8,128)S(1)} %backs.1.refs_2_), channel_id=1, source_target_pairs={{0,1},{1,0},{2,3},{3,2},{4,5},{5,4},{6,7},{7,6},{8,9},{9,8},{10,11... | collective-permute-start | bytes 24584 | tf_op jit(solution)/shard_map/ppermute | solution.py:60
  17.2 1.0 %upstream.1.hidden_ref = bf16[16,384]{1,0:T(8,128)(2,1)S(1)} custom-call(bf16[16,4096]{1,0:T(8,128)(2,1)S(1)} %get-tuple-element.28.rows_ref, f32[16,128]{1,0:T(8,128)S(1)} %get-tuple-element.29.gate_ref, bf16[384,4096]{1,0:T(8,128)(2,1)S(1)} %get-tuple-element.30.weight_ref), custom_call_target="tpu_custom_call" | custom-call | flops 50331648 | bytes 3145728 | tf_op jit(solution)/shard_map/upstream/pallas_call | solution.py:303
  18.3 0.2 collective-permute-done.8.refs_5_
  18.5 0.6 %collective-permute-done.7.refs_4_ = f32[16,128]{1,0:T(8,128)S(1)} collective-permute-done((f32[16,128]{1,0:T(8,128)S(1)}, f32[16,128]{1,0:T(8,128)S(1)}, u32[]{:S(2)}, u32[]{:S(2)}) %collective-permute-start.7) | collective-permute-done | bytes 8224 | tf_op jit(solution)/shard_map/ppermute | solution.py:60
  19.1 0.0 collective-permute-done.6.refs_3_
  19.1 0.0 collective-permute-done.3.refs_1_
  19.1 2.0 %last.1 = (f32[8,128]{1,0:T(8,128)}, bf16[1,1,16,384]{3,2,1,0:T(8,128)(2,1)}, f32[1,384,2048]{2,1,0:T(8,128)}) custom-call(s32[8,128]{1,0:T(8,128)S(1)} %get-tuple-element.21.ids_ref, f32[32,128]{1,0:T(8,128)S(1)} %get-tuple-element.22.match_ref, bf16[16,384]{1,0:T(8,128)(2,1)S(1)} %upstream.1.hidden_ref, bf16[16,2432]{1,0:T(8,128)(2,1)S(1)} %get-tuple-element.31.refs_0_, ...), custom_call_target="tpu_custom_call" | custom-call | flops 25165824 | bytes 3145728 | tf_op jit(solution)/shard_map/last/pallas_call | solution.py:313
Async XLA Ops:
  3.2 10.3 %collective-permute-start = (bf16[8,4224]{1,0:T(8,128)(2,1)S(1)}, bf16[8,4224]{1,0:T(8,128)(2,1)S(1)}, u32[]{:S(2)}, u32[]{:S(2)}) collective-permute-start(bf16[8,4224]{1,0:T(8,128)(2,1)S(1)} %get-tuple-element.25.refs_1_), channel_id=1, source_target_pairs={{0,12},{4,8},{8,4},{12,0},{1,13},{5,9},{9,5},{13,1},{2,14},{6,10},... | collective-permute-start | bytes 202760 | tf_op jit(solution)/shard_map/ppermute | solution.py:60
  8.3 5.2 %collective-permute-start.1 = (bf16[4,4224]{1,0:T(4,128)(2,1)S(1)}, bf16[4,4224]{1,0:T(4,128)(2,1)S(1)}, u32[]{:S(2)}, u32[]{:S(2)}) collective-permute-start(bf16[4,4224]{1,0:T(4,128)(2,1)S(1)} %get-tuple-element.26.refs_2_), channel_id=1, source_target_pairs={{0,8},{4,12},{8,0},{12,4},{1,9},{5,13},{9,1},{13,5},{2,10},{6,14},... | collective-permute-start | bytes 101384 | tf_op jit(solution)/shard_map/ppermute | solution.py:60
  8.3 5.2 %collective-permute-start.2 = (bf16[4,4224]{1,0:T(4,128)(2,1)S(1)}, bf16[4,4224]{1,0:T(4,128)(2,1)S(1)}, u32[]{:S(2)}, u32[]{:S(2)}) collective-permute-start(bf16[4,4224]{1,0:T(4,128)(2,1)S(1)} %get-tuple-element.27.refs_3_), channel_id=1, source_target_pairs={{0,4},{4,0},{8,12},{12,8},{1,5},{5,1},{9,13},{13,9},{2,6},{6,2},{1... | collective-permute-start | bytes 101384 | tf_op jit(solution)/shard_map/ppermute | solution.py:60
  9.0 6.2 %collective-permute-start.4 = (bf16[4,4096]{1,0:T(4,128)(2,1)S(1)}, bf16[4,4096]{1,0:T(4,128)(2,1)S(1)}, u32[]{:S(2)}, u32[]{:S(2)}) collective-permute-start(bf16[4,4096]{1,0:T(4,128)(2,1)S(1)} %get-tuple-element.34), channel_id=1, source_target_pairs={{0,8},{4,12},{8,0},{12,4},{1,9},{5,13},{9,1},{13,5},{2,10},{6,14},... | collective-permute-start | bytes 98312 | tf_op jit(solution)/shard_map/ppermute | solution.py:60
  11.3 3.9 %collective-permute-start.5 = (bf16[4,4096]{1,0:T(4,128)(2,1)S(1)}, bf16[4,4096]{1,0:T(4,128)(2,1)S(1)}, u32[]{:S(2)}, u32[]{:S(2)}) collective-permute-start(bf16[4,4096]{1,0:T(4,128)(2,1)S(1)} %get-tuple-element.35), channel_id=1, source_target_pairs={{0,4},{4,0},{8,12},{12,8},{1,5},{5,1},{9,13},{13,9},{2,6},{6,2},{1... | collective-permute-start | bytes 98312 | tf_op jit(solution)/shard_map/ppermute | solution.py:60
  13.6 5.5 %collective-permute-start.3 = (bf16[16,2432]{1,0:T(8,128)(2,1)S(1)}, bf16[16,2432]{1,0:T(8,128)(2,1)S(1)}, u32[]{:S(2)}, u32[]{:S(2)}) collective-permute-start(bf16[16,2432]{1,0:T(8,128)(2,1)S(1)} %get-tuple-element.32), channel_id=1, source_target_pairs={{0,16},{16,0},{1,17},{17,1},{2,18},{18,2},{3,19},{19,3},{4,20},{20... | collective-permute-start | bytes 233480 | tf_op jit(solution)/shard_map/ppermute | solution.py:60
  15.4 3.1 %collective-permute-start.8 = (f32[16,128]{1,0:T(8,128)S(1)}, f32[16,128]{1,0:T(8,128)S(1)}, u32[]{:S(2)}, u32[]{:S(2)}) collective-permute-start(f32[16,128]{1,0:T(8,128)S(1)} %backs.1.refs_2_), channel_id=1, source_target_pairs={{0,3},{1,2},{2,1},{3,0},{4,7},{5,6},{6,5},{7,4},{8,11},{9,10},{10,... | collective-permute-start | bytes 24584 | tf_op jit(solution)/shard_map/ppermute | solution.py:60
  15.4 3.7 %collective-permute-start.7 = (f32[16,128]{1,0:T(8,128)S(1)}, f32[16,128]{1,0:T(8,128)S(1)}, u32[]{:S(2)}, u32[]{:S(2)}) collective-permute-start(f32[16,128]{1,0:T(8,128)S(1)} %backs.1.refs_2_), channel_id=1, source_target_pairs={{0,2},{1,3},{2,0},{3,1},{4,6},{5,7},{6,4},{7,5},{8,10},{9,11},{10,... | collective-permute-start | bytes 24584 | tf_op jit(solution)/shard_map/ppermute | solution.py:60
  17.0 2.1 %collective-permute-start.6 = (f32[16,128]{1,0:T(8,128)S(1)}, f32[16,128]{1,0:T(8,128)S(1)}, u32[]{:S(2)}, u32[]{:S(2)}) collective-permute-start(f32[16,128]{1,0:T(8,128)S(1)} %backs.1.refs_2_), channel_id=1, source_target_pairs={{0,1},{1,0},{2,3},{3,2},{4,5},{5,4},{6,7},{7,6},{8,9},{9,8},{10,11... | collective-permute-start | bytes 24584 | tf_op jit(solution)/shard_map/ppermute | solution.py:60

commit v16 on v13

--- a/solution.py
+++ b/solution.py
@@ -11,6 +11,7 @@
 LANES = 128
 JOINT = 1
 AFTER_WAIT = (10**9, 10**7)
+WIDE = 1024
 PAD = 8
 VMEM = pl.BlockSpec(memory_space=pltpu.VMEM)
 HBM = pl.BlockSpec(memory_space=pltpu.HBM)
@@ -65,7 +66,7 @@
     ids_ref, match_ref, weight_ref, hidden_ref = refs[5:9]
     sends = refs[9 : 9 + count]
     products = refs[9 + count : 8 + 2 * count]
-    gates_ref, grad_ref, saved_ref, picked_ref, total_ref, sems = refs[8 + 2 * count :]
+    gates_ref, grad_ref, saved_ref, total_ref, sems = refs[8 + 2 * count :]
     units, width = weight_ref.shape
     top, tokens = ids_ref.shape
     pairs = [(ids_hbm, ids_ref), (gates_hbm, gates_ref), (hidden_hbm.at[0, 0], saved_ref)]
@@ -110,30 +111,39 @@
     hidden_ref[...] = dot(slot_order(count), saved, ((1,), (0,))).astype(jnp.bfloat16)
     here = lax.broadcasted_iota(jnp.int32, (rows, slots), 0)
     there = lax.broadcasted_iota(jnp.int32, (rows, slots), 1)
-    place = here % PAD - jnp.where(here // PAD == JOINT, CAP, 0)
-    chosen = (place >= 0) & (place < CAP) & (there == target(me, here // PAD, count) * CAP + place)
+    chosen = (here % PAD < CAP) & (there == target(me, here // PAD, count) * CAP + here % PAD)
     hidden = dot(chosen.astype(jnp.bfloat16), saved, ((1,), (0,))).astype(jnp.bfloat16)
 
     for copy in copies[3:5]:
         copy.wait()
-    picked_ref[...] = dot(match, grad_ref[...], ((1,), (0,)))
     for r in range(count):
-        part = slice(r * PAD, r * PAD + sends[r].shape[0])
-        gate = jnp.broadcast_to(slot_gate[part], (sends[r].shape[0], LANES))
-        sends[r][:, width:] = gate.astype(jnp.bfloat16)
-        if r != JOINT:
-            sends[r][:, :width] = picked_ref[part, :].astype(jnp.bfloat16)
+        part = slice(r * PAD, r * PAD + CAP)
+        gate = jnp.broadcast_to(slot_gate[part], (CAP, LANES)).astype(jnp.bfloat16)
+        sends[r][:, width : width + LANES] = gate
+    wide = min(width, WIDE)
+    for begin in range(0, width, wide):
+        part = slice(begin, begin + wide)
+        picked = dot(match, grad_ref[:, part], ((1,), (0,)))
+        for r in range(count):
+            sends[r][:, part] = picked[r * PAD : r * PAD + CAP].astype(jnp.bfloat16)
     block = units // pieces
     for p in range(pieces):
         for copy in copies[5 + 2 * p : 7 + 2 * p]:
             copy.wait()
-        part = slice(p * block, (p + 1) * block)
-        term = dot(hidden[:, part], weight_ref[part, :], ((1,), (0,)))
-        total_ref[...] = term if p == 0 else total_ref[...] + term
-    for product, r in zip(products, apart(count)):
-        product[...] = total_ref[r * PAD : r * PAD + CAP, :].astype(jnp.bfloat16)
-    part = slice(JOINT * PAD, (JOINT + 1) * PAD)
-    sends[JOINT][:, :width] = (picked_ref[part, :] + total_ref[part, :]).astype(jnp.bfloat16)
+        rows = slice(p * block, (p + 1) * block)
+        for begin in range(0, width, wide):
+            part = slice(begin, begin + wide)
+            term = dot(hidden[:, rows], weight_ref[rows, part], ((1,), (0,)))
+            if p > 0:
+                term = total_ref[:, part] + term
+            if p < pieces - 1:
+                total_ref[:, part] = term
+                continue
+            for product_ref, r in zip(products, apart(count)):
+                product_ref[:, part] = term[r * PAD : r * PAD + CAP].astype(jnp.bfloat16)
+            begin += width + LANES
+            joint = term[JOINT * PAD : JOINT * PAD + CAP].astype(jnp.bfloat16)
+            sends[JOINT][:, begin : begin + wide] = joint
 
 
 def slot_order(count):
@@ -151,7 +161,8 @@
     wide_ref, weighted_ref = refs[count + 2 + groups :]
     width = rows_ref.shape[1]
     for r in range(count):
-        wide_ref[r * CAP : (r + 1) * CAP, :] = received[r][...].astype(jnp.float32)[:CAP]
+        row = received[r][:, : width + LANES]
+        wide_ref[r * CAP : (r + 1) * CAP, :] = row.astype(jnp.float32)
     rows = wide_ref[:, :width]
     gate = wide_ref[:, width:]
     gate_ref[...] = gate
@@ -176,22 +187,28 @@
         if step != JOINT:
             theirs = products[step][...].astype(jnp.float32)
         else:
-            theirs = joint_ref[:, :width].astype(jnp.float32)[CAP:]
-        mine = sent[r][:, :width].astype(jnp.float32)[:CAP]
+            theirs = joint_ref[:, joint_ref.shape[1] - width :].astype(jnp.float32)
+        mine = sent[r][:, :width].astype(jnp.float32)
         back = jnp.sum(mine * theirs, axis=1, keepdims=True)
         back_ref[r * CAP : (r + 1) * CAP, :] = jnp.broadcast_to(back, (CAP, LANES))
 
 
-def down_kernel(count, groups, pieces, rows_ref, gate_ref, weight_ref, match_ref, *refs):
+def upstream_kernel(count, rows_ref, gate_ref, weight_ref, out_ref):
+    upstream = dot(rows_ref[...], weight_ref[...], ((1,), (1,)))
+    scaled = (gate_ref[:, :1] * upstream).astype(jnp.bfloat16)
+    out_ref[...] = dot(slot_order(count), scaled, ((0,), (0,))).astype(jnp.bfloat16)
+
+
+def down_kernel(groups, pieces, hidden_ref, match_ref, *refs):
     pays = refs[:groups]
-    hidden_hbm, down_hbm, match_out, hidden_out, down_out, sems = refs[groups:]
+    hidden_hbm, down_hbm, match_out, down_out, sems = refs[groups:]
     units, share = down_out.shape
     block = units // pieces
     slots = jnp.concatenate([pay_ref[...] for pay_ref in pays], axis=0)
     copies = []
 
-    def write(n, values, destination):
-        copies.append(pltpu.make_async_copy(values, destination, sems.at[n]))
+    def write(values, destination):
+        copies.append(pltpu.make_async_copy(values, destination, sems.at[len(copies)]))
         copies[-1].start()
 
     for p in range(pieces):
@@ -199,13 +216,9 @@
         hidden = slots[:, share + p * block : share + (p + 1) * block]
         down_out[part, :] = dot(hidden, slots[:, :share], ((0,), (0,)))
         part = pl.ds(p * block, block)
-        write(p, down_out.at[part], down_hbm.at[0, part])
-
+        write(down_out.at[part], down_hbm.at[0, part])
+    write(hidden_ref, hidden_hbm.at[0, 0])
     match_out[...] = match_ref[...]
-    upstream = dot(rows_ref[...], weight_ref[...], ((1,), (1,)))
-    scaled = (gate_ref[:, :1] * upstream).astype(jnp.bfloat16)
-    hidden_out[...] = dot(slot_order(count), scaled, ((0,), (0,))).astype(jnp.bfloat16)
-    write(pieces, hidden_out, hidden_hbm.at[0, 0])
     for copy in copies:
         copy.wait()
 
@@ -246,7 +259,7 @@
             jax.ShapeDtypeStruct((slots, units), jnp.bfloat16),
         ]
         + [
-            jax.ShapeDtypeStruct((PAD if r == JOINT else CAP, width + LANES), jnp.bfloat16)
+            jax.ShapeDtypeStruct((CAP, width + LANES + width * (r == JOINT)), jnp.bfloat16)
             for r in range(count)
         ]
         + [jax.ShapeDtypeStruct((CAP, width), jnp.bfloat16)] * (count - 1),
@@ -256,7 +269,6 @@
             pltpu.VMEM((top, tokens), jnp.bfloat16),
             pltpu.VMEM((tokens, width), jnp.bfloat16),
             pltpu.VMEM((slots, units), jnp.bfloat16),
-            pltpu.VMEM((count * PAD, width), jnp.float32),
             pltpu.VMEM((count * PAD, width), jnp.float32),
             pltpu.SemaphoreType.DMA((5 + 2 * pieces,)),
         ],
@@ -300,24 +312,33 @@
     others = [send(pays[r], "dp", r) for r in range(1, groups)]
     backs = [back] + [send(back, "tensor", r) for r in reversed(range(1, tensors))]
 
+    hidden_grad = pl.pallas_call(
+        functools.partial(upstream_kernel, count),
+        out_shape=jax.ShapeDtypeStruct((slots, units), jnp.bfloat16),
+        in_specs=[VMEM] * 3,
+        out_specs=VMEM,
+        compiler_params=PARAMS,
+        cost_estimate=cost(2 * slots * units * width, 2 * units * width),
+        name="upstream",
+    )(rows, gate, weight)
+
     hidden_grad, down_grad, match = pl.pallas_call(
-        functools.partial(down_kernel, count, groups, pieces),
+        functools.partial(down_kernel, groups, pieces),
         out_shape=[
             jax.ShapeDtypeStruct(saved_hidden.shape, jnp.bfloat16),
             jax.ShapeDtypeStruct((1, units, share), jnp.float32),
             jax.ShapeDtypeStruct(match.shape, jnp.float32),
         ],
-        in_specs=[VMEM] * (4 + groups),
+        in_specs=[VMEM] * (2 + groups),
         out_specs=[HBM, HBM, VMEM],
         scratch_shapes=[
-            pltpu.VMEM((slots, units), jnp.bfloat16),
             pltpu.VMEM((units, share), jnp.float32),
             pltpu.SemaphoreType.DMA((pieces + 1,)),
         ],
         compiler_params=PARAMS,
-        cost_estimate=cost(2 * slots * units * (width + share), 4 * units * share),
+        cost_estimate=cost(2 * slots * units * share, 4 * units * share),
         name="down",
-    )(rows, gate, weight, match, pays[0], *others)
+    )(hidden_grad, match, pays[0], *others)
 
     gate_grad = pl.pallas_call(
         functools.partial(gate_kernel, count),

time: 21.1 us -> 21.1 us (level)
  waiting for transfers between devices: 1.11 us -> 0.24 us
  Pallas kernels: 5.66 us -> 6.51 us
    pallas_call x1 -> x2, Pallas kernels: 2.18 us -> 3.06 us  [the longest x1 2.03 us: on_device(): pl.pallas_call(functools.partial(down_kernel, groups, pieces), out_shape=...]
    ppermute x9, waiting for transfers between devices: 1.11 us -> 0.24 us  [send(): lax.ppermute(value, axis, [(i, give(i, step, size)) for i in range(size)])]
  transfers between devices with their start and end apart: 9 -> 9, of which waited for: 2 -> 1; matrix products, arithmetic and copies ran while one was open for 0% -> 0% of each run, Pallas kernels for 12% -> 16%
where the time goes in v16:
time: 21.1 us; the launch traced here: 20.9 us
  starting transfers between devices  13.5 us (64%)
  Pallas kernels  6.51 us (31%)
  between operations  0.69 us (3%)
  waiting for transfers between devices  0.24 us (1%)
    ppermute x9, starting transfers between devices, send(): lax.ppermute(value, axis, [(i, give(i, step, size)) for i in range(size)])  13.5 us
    pallas_call x1, Pallas kernels, on_device(): pl.pallas_call(functools.partial(front_kernel, count, pieces), out_shape=...  2.57 us
    pallas_call x1, Pallas kernels, on_device(): pl.pallas_call(functools.partial(down_kernel, groups, pieces), out_shape=...  2.03 us
    pallas_call x1, Pallas kernels, on_device(): pl.pallas_call(functools.partial(upstream_kernel, count), out_shape=jax.S...  1.03 us
    pallas_call x1, Pallas kernels, on_device(): pl.pallas_call(functools.partial(gate_kernel, count), out_shape=jax.Shape...  0.61 us
  transfers between devices with their start and end apart: 9, of which 1 were waited for; matrix products, arithmetic and copies ran while one was open for 0% of the time, Pallas kernels for 16%

profile of v16, /device:TPU:0, one launch (start us, length us, event | category | flops | bytes accessed | tf_op | source)
XLA Modules:
  0.0 20.9 jit_solution(2018357645679650333)
XLA Ops:
  0.6 2.6 %front.1 = (s32[8,128]{1,0:T(8,128)S(1)}, f32[32,128]{1,0:T(8,128)S(1)}, bf16[384,4096]{1,0:T(8,128)(2,1)S(1)}, bf16[16,384]{1,0:T(8,128)(2,1)S(1)}, bf16[4,4224...) custom-call(s32[8,128]{1,0:T(8,128)} %bitcast.4, ...), custom_call_target="tpu_custom_call" | custom-call | flops 134217728 | bytes 4194304 | tf_op jit(solution)/shard_map/front/pallas_call | solution.py:253
  3.2 5.1 %collective-permute-start = (bf16[4,8320]{1,0:T(4,128)(2,1)S(1)}, bf16[4,8320]{1,0:T(4,128)(2,1)S(1)}, u32[]{:S(2)}, u32[]{:S(2)}) collective-permute-start(bf16[4,8320]{1,0:T(4,128)(2,1)S(1)} %get-tuple-element.24.refs_1_), channel_id=1, source_target_pairs={{0,12},{4,8},{8,4},{12,0},{1,13},{5,9},{9,5},{13,1},{2,14},{6,10},... | collective-permute-start | bytes 199688 | tf_op jit(solution)/shard_map/ppermute | solution.py:61
  8.3 0.0 collective-permute-start.1
  8.3 0.6 %collective-permute-start.2 = (bf16[4,4224]{1,0:T(4,128)(2,1)S(1)}, bf16[4,4224]{1,0:T(4,128)(2,1)S(1)}, u32[]{:S(2)}, u32[]{:S(2)}) collective-permute-start(bf16[4,4224]{1,0:T(4,128)(2,1)S(1)} %get-tuple-element.26.refs_3_), channel_id=1, source_target_pairs={{0,4},{4,0},{8,12},{12,8},{1,5},{5,1},{9,13},{13,9},{2,6},{6,2},{1... | collective-permute-start | bytes 101384 | tf_op jit(solution)/shard_map/ppermute | solution.py:61
  9.0 2.3 %collective-permute-start.4 = (bf16[4,4096]{1,0:T(4,128)(2,1)S(1)}, bf16[4,4096]{1,0:T(4,128)(2,1)S(1)}, u32[]{:S(2)}, u32[]{:S(2)}) collective-permute-start(bf16[4,4096]{1,0:T(4,128)(2,1)S(1)} %get-tuple-element.35), channel_id=1, source_target_pairs={{0,8},{4,12},{8,0},{12,4},{1,9},{5,13},{9,1},{13,5},{2,10},{6,14},... | collective-permute-start | bytes 98312 | tf_op jit(solution)/shard_map/ppermute | solution.py:61
  11.3 2.0 %collective-permute-start.5 = (bf16[4,4096]{1,0:T(4,128)(2,1)S(1)}, bf16[4,4096]{1,0:T(4,128)(2,1)S(1)}, u32[]{:S(2)}, u32[]{:S(2)}) collective-permute-start(bf16[4,4096]{1,0:T(4,128)(2,1)S(1)} %get-tuple-element.36), channel_id=1, source_target_pairs={{0,4},{4,0},{8,12},{12,8},{1,5},{5,1},{9,13},{13,9},{2,6},{6,2},{1... | collective-permute-start | bytes 98312 | tf_op jit(solution)/shard_map/ppermute | solution.py:61
  13.3 0.2 %collective-permute-done.1.refs_2_ = bf16[4,4224]{1,0:T(4,128)(2,1)S(1)} collective-permute-done((bf16[4,4224]{1,0:T(4,128)(2,1)S(1)}, bf16[4,4224]{1,0:T(4,128)(2,1)S(1)}, u32[]{:S(2)}, u32[]{:S(2)}) %collective-permute-start.1) | collective-permute-done | bytes 33824 | tf_op jit(solution)/shard_map/ppermute | solution.py:61
  13.5 0.0 collective-permute-done.2.refs_3_
  13.5 0.0 collective-permute-done.refs_1_.refs_4_
  13.5 0.1 slots.1
  13.6 1.6 %collective-permute-start.3 = (bf16[16,2432]{1,0:T(8,128)(2,1)S(1)}, bf16[16,2432]{1,0:T(8,128)(2,1)S(1)}, u32[]{:S(2)}, u32[]{:S(2)}) collective-permute-start(bf16[16,2432]{1,0:T(8,128)(2,1)S(1)} %get-tuple-element.32), channel_id=1, source_target_pairs={{0,16},{16,0},{1,17},{17,1},{2,18},{18,2},{3,19},{19,3},{4,20},{20... | collective-permute-start | bytes 233480 | tf_op jit(solution)/shard_map/ppermute | solution.py:61
  15.2 0.0 collective-permute-done.4.refs_6_
  15.2 0.0 collective-permute-done.5.refs_7_
  15.2 0.2 backs.1.refs_0_
  15.3 0.0 collective-permute-start.8
  15.4 1.6 %collective-permute-start.7 = (f32[16,128]{1,0:T(8,128)S(1)}, f32[16,128]{1,0:T(8,128)S(1)}, u32[]{:S(2)}, u32[]{:S(2)}) collective-permute-start(f32[16,128]{1,0:T(8,128)S(1)} %backs.1.refs_0_), channel_id=1, source_target_pairs={{0,2},{1,3},{2,0},{3,1},{4,6},{5,7},{6,4},{7,5},{8,10},{9,11},{10,... | collective-permute-start | bytes 24584 | tf_op jit(solution)/shard_map/ppermute | solution.py:61
  16.9 0.3 %collective-permute-start.6 = (f32[16,128]{1,0:T(8,128)S(1)}, f32[16,128]{1,0:T(8,128)S(1)}, u32[]{:S(2)}, u32[]{:S(2)}) collective-permute-start(f32[16,128]{1,0:T(8,128)S(1)} %backs.1.refs_0_), channel_id=1, source_target_pairs={{0,1},{1,0},{2,3},{3,2},{4,5},{5,4},{6,7},{7,6},{8,9},{9,8},{10,11... | collective-permute-start | bytes 24584 | tf_op jit(solution)/shard_map/ppermute | solution.py:61
  17.2 1.0 %upstream.1.hidden_ref = bf16[16,384]{1,0:T(8,128)(2,1)S(1)} custom-call(bf16[16,4096]{1,0:T(8,128)(2,1)S(1)} %get-tuple-element.27.rows_ref, f32[16,128]{1,0:T(8,128)S(1)} %get-tuple-element.28.gate_ref, bf16[384,4096]{1,0:T(8,128)(2,1)S(1)} %get-tuple-element.29.weight_ref), custom_call_target="tpu_custom_call" | custom-call | flops 50331648 | bytes 3145728 | tf_op jit(solution)/shard_map/upstream/pallas_call | solution.py:315
  18.2 0.0 collective-permute-done.3.refs_1_
  18.2 2.0 %down.1 = (bf16[1,1,16,384]{3,2,1,0:T(8,128)(2,1)}, f32[1,384,2048]{2,1,0:T(8,128)}, f32[32,128]{1,0:T(8,128)S(1)}) custom-call(bf16[16,384]{1,0:T(8,128)(2,1)S(1)} %upstream.1.hidden_ref, f32[32,128]{1,0:T(8,128)S(1)} %get-tuple-element.30.match_ref, bf16[16,2432]{1,0:T(8,128)(2,1)S(1)} %get-tuple-element.31.refs_0_, ...), custom_call_target="tpu_custom_call" | custom-call | flops 25165824 | bytes 3145728 | tf_op jit(solution)/shard_map/down/pallas_call | solution.py:325
  20.3 0.0 collective-permute-done.8.refs_3_
  20.3 0.0 collective-permute-done.7.refs_2_
  20.3 0.0 collective-permute-done.6.refs_1_
  20.3 0.6 %gates.1 = f32[8,128]{1,0:T(8,128)} custom-call(s32[8,128]{1,0:T(8,128)S(1)} %get-tuple-element.21.ids_ref, f32[32,128]{1,0:T(8,128)S(1)} %get-tuple-element.33.match_ref, f32[16,128]{1,0:T(8,128)S(1)} %backs.1.refs_0_, f32[16,128]{1,0:T(8,128)S(1)} %collective-permute-done.6.refs_1_, f32[16,128]{1,0:T(8,128)S(1)} %collective-permute-done.7.refs_2_, ...), custom_call_target="tpu_custom_call" | custom-call | flops 2048 | bytes 8192 | tf_op jit(solution)/shard_map/gates/pallas_call | solution.py:343
Async XLA Ops:
  3.2 10.3 %collective-permute-start = (bf16[4,8320]{1,0:T(4,128)(2,1)S(1)}, bf16[4,8320]{1,0:T(4,128)(2,1)S(1)}, u32[]{:S(2)}, u32[]{:S(2)}) collective-permute-start(bf16[4,8320]{1,0:T(4,128)(2,1)S(1)} %get-tuple-element.24.refs_1_), channel_id=1, source_target_pairs={{0,12},{4,8},{8,4},{12,0},{1,13},{5,9},{9,5},{13,1},{2,14},{6,10},... | collective-permute-start | bytes 199688 | tf_op jit(solution)/shard_map/ppermute | solution.py:61
  8.3 5.2 %collective-permute-start.1 = (bf16[4,4224]{1,0:T(4,128)(2,1)S(1)}, bf16[4,4224]{1,0:T(4,128)(2,1)S(1)}, u32[]{:S(2)}, u32[]{:S(2)}) collective-permute-start(bf16[4,4224]{1,0:T(4,128)(2,1)S(1)} %get-tuple-element.25.refs_2_), channel_id=1, source_target_pairs={{0,8},{4,12},{8,0},{12,4},{1,9},{5,13},{9,1},{13,5},{2,10},{6,14},... | collective-permute-start | bytes 101384 | tf_op jit(solution)/shard_map/ppermute | solution.py:61
  8.3 5.2 %collective-permute-start.2 = (bf16[4,4224]{1,0:T(4,128)(2,1)S(1)}, bf16[4,4224]{1,0:T(4,128)(2,1)S(1)}, u32[]{:S(2)}, u32[]{:S(2)}) collective-permute-start(bf16[4,4224]{1,0:T(4,128)(2,1)S(1)} %get-tuple-element.26.refs_3_), channel_id=1, source_target_pairs={{0,4},{4,0},{8,12},{12,8},{1,5},{5,1},{9,13},{13,9},{2,6},{6,2},{1... | collective-permute-start | bytes 101384 | tf_op jit(solution)/shard_map/ppermute | solution.py:61
  9.0 6.2 %collective-permute-start.4 = (bf16[4,4096]{1,0:T(4,128)(2,1)S(1)}, bf16[4,4096]{1,0:T(4,128)(2,1)S(1)}, u32[]{:S(2)}, u32[]{:S(2)}) collective-permute-start(bf16[4,4096]{1,0:T(4,128)(2,1)S(1)} %get-tuple-element.35), channel_id=1, source_target_pairs={{0,8},{4,12},{8,0},{12,4},{1,9},{5,13},{9,1},{13,5},{2,10},{6,14},... | collective-permute-start | bytes 98312 | tf_op jit(solution)/shard_map/ppermute | solution.py:61
  11.3 3.9 %collective-permute-start.5 = (bf16[4,4096]{1,0:T(4,128)(2,1)S(1)}, bf16[4,4096]{1,0:T(4,128)(2,1)S(1)}, u32[]{:S(2)}, u32[]{:S(2)}) collective-permute-start(bf16[4,4096]{1,0:T(4,128)(2,1)S(1)} %get-tuple-element.36), channel_id=1, source_target_pairs={{0,4},{4,0},{8,12},{12,8},{1,5},{5,1},{9,13},{13,9},{2,6},{6,2},{1... | collective-permute-start | bytes 98312 | tf_op jit(solution)/shard_map/ppermute | solution.py:61
  13.6 4.6 %collective-permute-start.3 = (bf16[16,2432]{1,0:T(8,128)(2,1)S(1)}, bf16[16,2432]{1,0:T(8,128)(2,1)S(1)}, u32[]{:S(2)}, u32[]{:S(2)}) collective-permute-start(bf16[16,2432]{1,0:T(8,128)(2,1)S(1)} %get-tuple-element.32), channel_id=1, source_target_pairs={{0,16},{16,0},{1,17},{17,1},{2,18},{18,2},{3,19},{19,3},{4,20},{20... | collective-permute-start | bytes 233480 | tf_op jit(solution)/shard_map/ppermute | solution.py:61
  15.3 4.9 %collective-permute-start.8 = (f32[16,128]{1,0:T(8,128)S(1)}, f32[16,128]{1,0:T(8,128)S(1)}, u32[]{:S(2)}, u32[]{:S(2)}) collective-permute-start(f32[16,128]{1,0:T(8,128)S(1)} %backs.1.refs_0_), channel_id=1, source_target_pairs={{0,3},{1,2},{2,1},{3,0},{4,7},{5,6},{6,5},{7,4},{8,11},{9,10},{10,... | collective-permute-start | bytes 24584 | tf_op jit(solution)/shard_map/ppermute | solution.py:61
  15.4 4.9 %collective-permute-start.7 = (f32[16,128]{1,0:T(8,128)S(1)}, f32[16,128]{1,0:T(8,128)S(1)}, u32[]{:S(2)}, u32[]{:S(2)}) collective-permute-start(f32[16,128]{1,0:T(8,128)S(1)} %backs.1.refs_0_), channel_id=1, source_target_pairs={{0,2},{1,3},{2,0},{3,1},{4,6},{5,7},{6,4},{7,5},{8,10},{9,11},{10,... | collective-permute-start | bytes 24584 | tf_op jit(solution)/shard_map/ppermute | solution.py:61
  16.9 3.4 %collective-permute-start.6 = (f32[16,128]{1,0:T(8,128)S(1)}, f32[16,128]{1,0:T(8,128)S(1)}, u32[]{:S(2)}, u32[]{:S(2)}) collective-permute-start(f32[16,128]{1,0:T(8,128)S(1)} %backs.1.refs_0_), channel_id=1, source_target_pairs={{0,1},{1,0},{2,3},{3,2},{4,5},{5,4},{6,7},{7,6},{8,9},{9,8},{10,11... | collective-permute-start | bytes 24584 | tf_op jit(solution)/shard_map/ppermute | solution.py:61

commit v17 on v16

--- a/solution.py
+++ b/solution.py
@@ -11,6 +11,7 @@
 LANES = 128
 JOINT = 1
 AFTER_WAIT = (10**9, 10**7)
+DEEP = 256
 WIDE = 1024
 PAD = 8
 VMEM = pl.BlockSpec(memory_space=pltpu.VMEM)
@@ -61,23 +62,19 @@
     return lax.ppermute(value, axis, [(i, give(i, step, size)) for i in range(size)])
 
 
-def front_kernel(count, pieces, *refs):
+def front_kernel(count, *refs):
     ids_hbm, gates_hbm, grad_hbm, hidden_hbm, weight_hbm = refs[:5]
-    ids_ref, match_ref, weight_ref, hidden_ref = refs[5:9]
+    ids_ref, match_ref, stack_ref, hidden_ref = refs[5:9]
     sends = refs[9 : 9 + count]
     products = refs[9 + count : 8 + 2 * count]
-    gates_ref, grad_ref, saved_ref, total_ref, sems = refs[8 + 2 * count :]
-    units, width = weight_ref.shape
+    gates_ref, saved_ref, total_ref, sems = refs[8 + 2 * count :]
+    depth, width = stack_ref.shape
     top, tokens = ids_ref.shape
     pairs = [(ids_hbm, ids_ref), (gates_hbm, gates_ref), (hidden_hbm.at[0, 0], saved_ref)]
-    half = tokens // 2
-    for p in range(2):
-        part = pl.ds(p * half, half)
-        pairs.append((grad_hbm.at[part], grad_ref.at[part]))
-    half = units // (2 * pieces)
-    for p in range(2 * pieces):
-        part = pl.ds(p * half, half)
-        pairs.append((weight_hbm.at[0, part], weight_ref.at[part]))
+    pairs.append((grad_hbm, stack_ref.at[pl.ds(0, tokens)]))
+    for begin in range(0, depth - tokens, LANES):
+        part = stack_ref.at[pl.ds(tokens + begin, LANES)]
+        pairs.append((weight_hbm.at[0, pl.ds(begin, LANES)], part))
     copies = [pltpu.make_async_copy(*pair, sems.at[n]) for n, pair in enumerate(pairs)]
     for copy in copies:
         copy.start()
@@ -114,29 +111,31 @@
     chosen = (here % PAD < CAP) & (there == target(me, here // PAD, count) * CAP + here % PAD)
     hidden = dot(chosen.astype(jnp.bfloat16), saved, ((1,), (0,))).astype(jnp.bfloat16)
 
-    for copy in copies[3:5]:
-        copy.wait()
     for r in range(count):
         part = slice(r * PAD, r * PAD + CAP)
         gate = jnp.broadcast_to(slot_gate[part], (CAP, LANES)).astype(jnp.bfloat16)
         sends[r][:, width : width + LANES] = gate
+    above = jnp.concatenate([match, jnp.zeros(hidden.shape, jnp.bfloat16)], axis=1)
+    below = jnp.concatenate([jnp.zeros(match.shape, jnp.bfloat16), hidden], axis=1)
+    left = jnp.concatenate([above, below], axis=0)
     wide = min(width, WIDE)
-    for begin in range(0, width, wide):
-        part = slice(begin, begin + wide)
-        picked = dot(match, grad_ref[:, part], ((1,), (0,)))
-        for r in range(count):
-            sends[r][:, part] = picked[r * PAD : r * PAD + CAP].astype(jnp.bfloat16)
-    block = units // pieces
-    for p in range(pieces):
-        for copy in copies[5 + 2 * p : 7 + 2 * p]:
-            copy.wait()
-        rows = slice(p * block, (p + 1) * block)
+    arrived = copies[3:]
+    for start in range(0, depth, DEEP):
+        lines = slice(start, start + DEEP)
+        while arrived and (len(copies) - len(arrived) - 3) * LANES < start + DEEP:
+            arrived[0].wait()
+            arrived = arrived[1:]
         for begin in range(0, width, wide):
             part = slice(begin, begin + wide)
-            term = dot(hidden[:, rows], weight_ref[rows, part], ((1,), (0,)))
-            if p > 0:
-                term = total_ref[:, part] + term
-            if p < pieces - 1:
+            if start == 0:
+                term = dot(left[:, lines], stack_ref[lines, part], ((1,), (0,)))
+                for r in range(count):
+                    sends[r][:, part] = term[r * PAD : r * PAD + CAP].astype(jnp.bfloat16)
+                total_ref[:, part] = term[rows:]
+                continue
+            term = dot(below[:, lines], stack_ref[lines, part], ((1,), (0,)))
+            term = total_ref[:, part] + term
+            if start + DEEP < depth:
                 total_ref[:, part] = term
                 continue
             for product_ref, r in zip(products, apart(count)):
@@ -194,7 +193,8 @@
 
 
 def upstream_kernel(count, rows_ref, gate_ref, weight_ref, out_ref):
-    upstream = dot(rows_ref[...], weight_ref[...], ((1,), (1,)))
+    first = weight_ref.shape[0] - out_ref.shape[1]
+    upstream = dot(rows_ref[...], weight_ref[first:, :], ((1,), (1,)))
     scaled = (gate_ref[:, :1] * upstream).astype(jnp.bfloat16)
     out_ref[...] = dot(slot_order(count), scaled, ((0,), (0,))).astype(jnp.bfloat16)
 
@@ -251,11 +251,11 @@
     pieces = units // LANES
 
     ids, match, weight, hidden, *rest = pl.pallas_call(
-        functools.partial(front_kernel, count, pieces),
+        functools.partial(front_kernel, count),
         out_shape=[
             jax.ShapeDtypeStruct((top, tokens), jnp.int32),
             jax.ShapeDtypeStruct((count * PAD, tokens), jnp.float32),
-            jax.ShapeDtypeStruct((units, width), jnp.bfloat16),
+            jax.ShapeDtypeStruct((tokens + units, width), jnp.bfloat16),
             jax.ShapeDtypeStruct((slots, units), jnp.bfloat16),
         ]
         + [
@@ -267,10 +267,9 @@
         out_specs=[VMEM] * (3 + 2 * count),
         scratch_shapes=[
             pltpu.VMEM((top, tokens), jnp.bfloat16),
-            pltpu.VMEM((tokens, width), jnp.bfloat16),
             pltpu.VMEM((slots, units), jnp.bfloat16),
             pltpu.VMEM((count * PAD, width), jnp.float32),
-            pltpu.SemaphoreType.DMA((5 + 2 * pieces,)),
+            pltpu.SemaphoreType.DMA((4 + pieces,)),
         ],
         compiler_params=PARAMS,
         cost_estimate=cost(2 * count * PAD * (tokens + units) * width, 2 * (tokens + units) * width),

time: 21.1 us -> 21.3 us (level)
  no operation moved by 1% of the time
where the time goes in v17:
time: 21.3 us; the launch traced here: 21.1 us
  starting transfers between devices  13.5 us (63%)
  Pallas kernels  6.71 us (32%)
  between operations  0.69 us (3%)
  waiting for transfers between devices  0.24 us (1%)
    ppermute x9, starting transfers between devices, send(): lax.ppermute(value, axis, [(i, give(i, step, size)) for i in range(size)])  13.5 us
    pallas_call x1, Pallas kernels, on_device(): pl.pallas_call(functools.partial(front_kernel, count), out_shape=[jax.Sha...  2.76 us
    pallas_call x1, Pallas kernels, on_device(): pl.pallas_call(functools.partial(down_kernel, groups, pieces), out_shape=...  2.04 us
    pallas_call x1, Pallas kernels, on_device(): pl.pallas_call(functools.partial(upstream_kernel, count), out_shape=jax.S...  1.03 us
    pallas_call x1, Pallas kernels, on_device(): pl.pallas_call(functools.partial(gate_kernel, count), out_shape=jax.Shape...  0.61 us
  transfers between devices with their start and end apart: 9, of which 1 were waited for; matrix products, arithmetic and copies ran while one was open for 0% of the time, Pallas kernels for 16%

profile of v17, /device:TPU:0, one launch (start us, length us, event | category | flops | bytes accessed | tf_op | source)
XLA Modules:
  0.0 21.1 jit_solution(7945158298804144381)
XLA Ops:
  0.6 2.8 %front.1 = (s32[8,128]{1,0:T(8,128)S(1)}, f32[32,128]{1,0:T(8,128)S(1)}, bf16[512,4096]{1,0:T(8,128)(2,1)S(1)}, bf16[16,384]{1,0:T(8,128)(2,1)S(1)}, bf16[4,4224...) custom-call(s32[8,128]{1,0:T(8,128)} %bitcast.4, ...), custom_call_target="tpu_custom_call" | custom-call | flops 134217728 | bytes 4194304 | tf_op jit(solution)/shard_map/front/pallas_call | solution.py:253
  3.4 5.1 %collective-permute-start = (bf16[4,8320]{1,0:T(4,128)(2,1)S(1)}, bf16[4,8320]{1,0:T(4,128)(2,1)S(1)}, u32[]{:S(2)}, u32[]{:S(2)}) collective-permute-start(bf16[4,8320]{1,0:T(4,128)(2,1)S(1)} %get-tuple-element.24.refs_1_), channel_id=1, source_target_pairs={{0,12},{4,8},{8,4},{12,0},{1,13},{5,9},{9,5},{13,1},{2,14},{6,10},... | collective-permute-start | bytes 199688 | tf_op jit(solution)/shard_map/ppermute | solution.py:62
  8.5 0.0 collective-permute-start.1
  8.5 0.6 %collective-permute-start.2 = (bf16[4,4224]{1,0:T(4,128)(2,1)S(1)}, bf16[4,4224]{1,0:T(4,128)(2,1)S(1)}, u32[]{:S(2)}, u32[]{:S(2)}) collective-permute-start(bf16[4,4224]{1,0:T(4,128)(2,1)S(1)} %get-tuple-element.26.refs_3_), channel_id=1, source_target_pairs={{0,4},{4,0},{8,12},{12,8},{1,5},{5,1},{9,13},{13,9},{2,6},{6,2},{1... | collective-permute-start | bytes 101384 | tf_op jit(solution)/shard_map/ppermute | solution.py:62
  9.2 2.3 %collective-permute-start.4 = (bf16[4,4096]{1,0:T(4,128)(2,1)S(1)}, bf16[4,4096]{1,0:T(4,128)(2,1)S(1)}, u32[]{:S(2)}, u32[]{:S(2)}) collective-permute-start(bf16[4,4096]{1,0:T(4,128)(2,1)S(1)} %get-tuple-element.35), channel_id=1, source_target_pairs={{0,8},{4,12},{8,0},{12,4},{1,9},{5,13},{9,1},{13,5},{2,10},{6,14},... | collective-permute-start | bytes 98312 | tf_op jit(solution)/shard_map/ppermute | solution.py:62
  11.4 2.0 %collective-permute-start.5 = (bf16[4,4096]{1,0:T(4,128)(2,1)S(1)}, bf16[4,4096]{1,0:T(4,128)(2,1)S(1)}, u32[]{:S(2)}, u32[]{:S(2)}) collective-permute-start(bf16[4,4096]{1,0:T(4,128)(2,1)S(1)} %get-tuple-element.36), channel_id=1, source_target_pairs={{0,4},{4,0},{8,12},{12,8},{1,5},{5,1},{9,13},{13,9},{2,6},{6,2},{1... | collective-permute-start | bytes 98312 | tf_op jit(solution)/shard_map/ppermute | solution.py:62
  13.5 0.2 %collective-permute-done.1.refs_2_ = bf16[4,4224]{1,0:T(4,128)(2,1)S(1)} collective-permute-done((bf16[4,4224]{1,0:T(4,128)(2,1)S(1)}, bf16[4,4224]{1,0:T(4,128)(2,1)S(1)}, u32[]{:S(2)}, u32[]{:S(2)}) %collective-permute-start.1) | collective-permute-done | bytes 33824 | tf_op jit(solution)/shard_map/ppermute | solution.py:62
  13.7 0.0 collective-permute-done.2.refs_3_
  13.7 0.0 collective-permute-done.refs_1_.refs_4_
  13.7 0.1 slots.1
  13.8 1.6 %collective-permute-start.3 = (bf16[16,2432]{1,0:T(8,128)(2,1)S(1)}, bf16[16,2432]{1,0:T(8,128)(2,1)S(1)}, u32[]{:S(2)}, u32[]{:S(2)}) collective-permute-start(bf16[16,2432]{1,0:T(8,128)(2,1)S(1)} %get-tuple-element.32), channel_id=1, source_target_pairs={{0,16},{16,0},{1,17},{17,1},{2,18},{18,2},{3,19},{19,3},{4,20},{20... | collective-permute-start | bytes 233480 | tf_op jit(solution)/shard_map/ppermute | solution.py:62
  15.4 0.0 collective-permute-done.4.refs_6_
  15.4 0.0 collective-permute-done.5.refs_7_
  15.4 0.2 backs.1.refs_0_
  15.5 0.0 collective-permute-start.8
  15.5 1.6 %collective-permute-start.7 = (f32[16,128]{1,0:T(8,128)S(1)}, f32[16,128]{1,0:T(8,128)S(1)}, u32[]{:S(2)}, u32[]{:S(2)}) collective-permute-start(f32[16,128]{1,0:T(8,128)S(1)} %backs.1.refs_0_), channel_id=1, source_target_pairs={{0,2},{1,3},{2,0},{3,1},{4,6},{5,7},{6,4},{7,5},{8,10},{9,11},{10,... | collective-permute-start | bytes 24584 | tf_op jit(solution)/shard_map/ppermute | solution.py:62
  17.1 0.3 %collective-permute-start.6 = (f32[16,128]{1,0:T(8,128)S(1)}, f32[16,128]{1,0:T(8,128)S(1)}, u32[]{:S(2)}, u32[]{:S(2)}) collective-permute-start(f32[16,128]{1,0:T(8,128)S(1)} %backs.1.refs_0_), channel_id=1, source_target_pairs={{0,1},{1,0},{2,3},{3,2},{4,5},{5,4},{6,7},{7,6},{8,9},{9,8},{10,11... | collective-permute-start | bytes 24584 | tf_op jit(solution)/shard_map/ppermute | solution.py:62
  17.4 1.0 %upstream.1.hidden_ref = bf16[16,384]{1,0:T(8,128)(2,1)S(1)} custom-call(bf16[16,4096]{1,0:T(8,128)(2,1)S(1)} %get-tuple-element.27.rows_ref, f32[16,128]{1,0:T(8,128)S(1)} %get-tuple-element.28.gate_ref, bf16[512,4096]{1,0:T(8,128)(2,1)S(1)} %get-tuple-element.29.weight_ref), custom_call_target="tpu_custom_call" | custom-call | flops 50331648 | bytes 3145728 | tf_op jit(solution)/shard_map/upstream/pallas_call | solution.py:314
  18.4 0.0 collective-permute-done.3.refs_1_
  18.4 2.0 %down.1 = (bf16[1,1,16,384]{3,2,1,0:T(8,128)(2,1)}, f32[1,384,2048]{2,1,0:T(8,128)}, f32[32,128]{1,0:T(8,128)S(1)}) custom-call(bf16[16,384]{1,0:T(8,128)(2,1)S(1)} %upstream.1.hidden_ref, f32[32,128]{1,0:T(8,128)S(1)} %get-tuple-element.30.match_ref, bf16[16,2432]{1,0:T(8,128)(2,1)S(1)} %get-tuple-element.31.refs_0_, ...), custom_call_target="tpu_custom_call" | custom-call | flops 25165824 | bytes 3145728 | tf_op jit(solution)/shard_map/down/pallas_call | solution.py:324
  20.5 0.0 collective-permute-done.8.refs_3_
  20.5 0.0 collective-permute-done.7.refs_2_
  20.5 0.0 collective-permute-done.6.refs_1_
  20.5 0.6 %gates.1 = f32[8,128]{1,0:T(8,128)} custom-call(s32[8,128]{1,0:T(8,128)S(1)} %get-tuple-element.21.ids_ref, f32[32,128]{1,0:T(8,128)S(1)} %get-tuple-element.33.match_ref, f32[16,128]{1,0:T(8,128)S(1)} %backs.1.refs_0_, f32[16,128]{1,0:T(8,128)S(1)} %collective-permute-done.6.refs_1_, f32[16,128]{1,0:T(8,128)S(1)} %collective-permute-done.7.refs_2_, ...), custom_call_target="tpu_custom_call" | custom-call | flops 2048 | bytes 8192 | tf_op jit(solution)/shard_map/gates/pallas_call | solution.py:342
Async XLA Ops:
  3.4 10.3 %collective-permute-start = (bf16[4,8320]{1,0:T(4,128)(2,1)S(1)}, bf16[4,8320]{1,0:T(4,128)(2,1)S(1)}, u32[]{:S(2)}, u32[]{:S(2)}) collective-permute-start(bf16[4,8320]{1,0:T(4,128)(2,1)S(1)} %get-tuple-element.24.refs_1_), channel_id=1, source_target_pairs={{0,12},{4,8},{8,4},{12,0},{1,13},{5,9},{9,5},{13,1},{2,14},{6,10},... | collective-permute-start | bytes 199688 | tf_op jit(solution)/shard_map/ppermute | solution.py:62
  8.5 5.2 %collective-permute-start.1 = (bf16[4,4224]{1,0:T(4,128)(2,1)S(1)}, bf16[4,4224]{1,0:T(4,128)(2,1)S(1)}, u32[]{:S(2)}, u32[]{:S(2)}) collective-permute-start(bf16[4,4224]{1,0:T(4,128)(2,1)S(1)} %get-tuple-element.25.refs_2_), channel_id=1, source_target_pairs={{0,8},{4,12},{8,0},{12,4},{1,9},{5,13},{9,1},{13,5},{2,10},{6,14},... | collective-permute-start | bytes 101384 | tf_op jit(solution)/shard_map/ppermute | solution.py:62
  8.5 5.2 %collective-permute-start.2 = (bf16[4,4224]{1,0:T(4,128)(2,1)S(1)}, bf16[4,4224]{1,0:T(4,128)(2,1)S(1)}, u32[]{:S(2)}, u32[]{:S(2)}) collective-permute-start(bf16[4,4224]{1,0:T(4,128)(2,1)S(1)} %get-tuple-element.26.refs_3_), channel_id=1, source_target_pairs={{0,4},{4,0},{8,12},{12,8},{1,5},{5,1},{9,13},{13,9},{2,6},{6,2},{1... | collective-permute-start | bytes 101384 | tf_op jit(solution)/shard_map/ppermute | solution.py:62
  9.2 6.2 %collective-permute-start.4 = (bf16[4,4096]{1,0:T(4,128)(2,1)S(1)}, bf16[4,4096]{1,0:T(4,128)(2,1)S(1)}, u32[]{:S(2)}, u32[]{:S(2)}) collective-permute-start(bf16[4,4096]{1,0:T(4,128)(2,1)S(1)} %get-tuple-element.35), channel_id=1, source_target_pairs={{0,8},{4,12},{8,0},{12,4},{1,9},{5,13},{9,1},{13,5},{2,10},{6,14},... | collective-permute-start | bytes 98312 | tf_op jit(solution)/shard_map/ppermute | solution.py:62
  11.4 3.9 %collective-permute-start.5 = (bf16[4,4096]{1,0:T(4,128)(2,1)S(1)}, bf16[4,4096]{1,0:T(4,128)(2,1)S(1)}, u32[]{:S(2)}, u32[]{:S(2)}) collective-permute-start(bf16[4,4096]{1,0:T(4,128)(2,1)S(1)} %get-tuple-element.36), channel_id=1, source_target_pairs={{0,4},{4,0},{8,12},{12,8},{1,5},{5,1},{9,13},{13,9},{2,6},{6,2},{1... | collective-permute-start | bytes 98312 | tf_op jit(solution)/shard_map/ppermute | solution.py:62
  13.8 4.6 %collective-permute-start.3 = (bf16[16,2432]{1,0:T(8,128)(2,1)S(1)}, bf16[16,2432]{1,0:T(8,128)(2,1)S(1)}, u32[]{:S(2)}, u32[]{:S(2)}) collective-permute-start(bf16[16,2432]{1,0:T(8,128)(2,1)S(1)} %get-tuple-element.32), channel_id=1, source_target_pairs={{0,16},{16,0},{1,17},{17,1},{2,18},{18,2},{3,19},{19,3},{4,20},{20... | collective-permute-start | bytes 233480 | tf_op jit(solution)/shard_map/ppermute | solution.py:62
  15.5 4.9 %collective-permute-start.8 = (f32[16,128]{1,0:T(8,128)S(1)}, f32[16,128]{1,0:T(8,128)S(1)}, u32[]{:S(2)}, u32[]{:S(2)}) collective-permute-start(f32[16,128]{1,0:T(8,128)S(1)} %backs.1.refs_0_), channel_id=1, source_target_pairs={{0,3},{1,2},{2,1},{3,0},{4,7},{5,6},{6,5},{7,4},{8,11},{9,10},{10,... | collective-permute-start | bytes 24584 | tf_op jit(solution)/shard_map/ppermute | solution.py:62
  15.5 5.0 %collective-permute-start.7 = (f32[16,128]{1,0:T(8,128)S(1)}, f32[16,128]{1,0:T(8,128)S(1)}, u32[]{:S(2)}, u32[]{:S(2)}) collective-permute-start(f32[16,128]{1,0:T(8,128)S(1)} %backs.1.refs_0_), channel_id=1, source_target_pairs={{0,2},{1,3},{2,0},{3,1},{4,6},{5,7},{6,4},{7,5},{8,10},{9,11},{10,... | collective-permute-start | bytes 24584 | tf_op jit(solution)/shard_map/ppermute | solution.py:62
  17.1 3.4 %collective-permute-start.6 = (f32[16,128]{1,0:T(8,128)S(1)}, f32[16,128]{1,0:T(8,128)S(1)}, u32[]{:S(2)}, u32[]{:S(2)}) collective-permute-start(f32[16,128]{1,0:T(8,128)S(1)} %backs.1.refs_0_), channel_id=1, source_target_pairs={{0,1},{1,0},{2,3},{3,2},{4,5},{5,4},{6,7},{7,6},{8,9},{9,8},{10,11... | collective-permute-start | bytes 24584 | tf_op jit(solution)/shard_map/ppermute | solution.py:62

commit v18 on v16

--- a/solution.py
+++ b/solution.py
@@ -61,7 +61,7 @@
     return lax.ppermute(value, axis, [(i, give(i, step, size)) for i in range(size)])
 
 
-def front_kernel(count, pieces, *refs):
+def front_kernel(count, *refs):
     ids_hbm, gates_hbm, grad_hbm, hidden_hbm, weight_hbm = refs[:5]
     ids_ref, match_ref, weight_ref, hidden_ref = refs[5:9]
     sends = refs[9 : 9 + count]
@@ -74,9 +74,9 @@
     for p in range(2):
         part = pl.ds(p * half, half)
         pairs.append((grad_hbm.at[part], grad_ref.at[part]))
-    half = units // (2 * pieces)
-    for p in range(2 * pieces):
-        part = pl.ds(p * half, half)
+    cuts = cuts_of(units)
+    for start, end in zip(cuts, cuts[1:]):
+        part = pl.ds(start, end - start)
         pairs.append((weight_hbm.at[0, part], weight_ref.at[part]))
     copies = [pltpu.make_async_copy(*pair, sems.at[n]) for n, pair in enumerate(pairs)]
     for copy in copies:
@@ -126,17 +126,15 @@
         picked = dot(match, grad_ref[:, part], ((1,), (0,)))
         for r in range(count):
             sends[r][:, part] = picked[r * PAD : r * PAD + CAP].astype(jnp.bfloat16)
-    block = units // pieces
-    for p in range(pieces):
-        for copy in copies[5 + 2 * p : 7 + 2 * p]:
-            copy.wait()
-        rows = slice(p * block, (p + 1) * block)
+    for p, (start, end) in enumerate(zip(cuts, cuts[1:])):
+        copies[5 + p].wait()
+        rows = slice(start, end)
         for begin in range(0, width, wide):
             part = slice(begin, begin + wide)
             term = dot(hidden[:, rows], weight_ref[rows, part], ((1,), (0,)))
             if p > 0:
                 term = total_ref[:, part] + term
-            if p < pieces - 1:
+            if end < units:
                 total_ref[:, part] = term
                 continue
             for product_ref, r in zip(products, apart(count)):
@@ -144,6 +142,10 @@
             begin += width + LANES
             joint = term[JOINT * PAD : JOINT * PAD + CAP].astype(jnp.bfloat16)
             sends[JOINT][:, begin : begin + wide] = joint
+
+
+def cuts_of(units):
+    return [*range(0, units, LANES), units - LANES // 2, units]
 
 
 def slot_order(count):
@@ -199,11 +201,10 @@
     out_ref[...] = dot(slot_order(count), scaled, ((0,), (0,))).astype(jnp.bfloat16)
 
 
-def down_kernel(groups, pieces, hidden_ref, match_ref, *refs):
+def down_kernel(groups, hidden_ref, match_ref, *refs):
     pays = refs[:groups]
     hidden_hbm, down_hbm, match_out, down_out, sems = refs[groups:]
     units, share = down_out.shape
-    block = units // pieces
     slots = jnp.concatenate([pay_ref[...] for pay_ref in pays], axis=0)
     copies = []
 
@@ -211,11 +212,11 @@
         copies.append(pltpu.make_async_copy(values, destination, sems.at[len(copies)]))
         copies[-1].start()
 
-    for p in range(pieces):
-        part = slice(p * block, (p + 1) * block)
-        hidden = slots[:, share + p * block : share + (p + 1) * block]
-        down_out[part, :] = dot(hidden, slots[:, :share], ((0,), (0,)))
-        part = pl.ds(p * block, block)
+    cuts = [units - cut for cut in reversed(cuts_of(units))]
+    for start, end in zip(cuts, cuts[1:]):
+        hidden = slots[:, share + start : share + end]
+        down_out[start:end, :] = dot(hidden, slots[:, :share], ((0,), (0,)))
+        part = pl.ds(start, end - start)
         write(down_out.at[part], down_hbm.at[0, part])
     write(hidden_ref, hidden_hbm.at[0, 0])
     match_out[...] = match_ref[...]
@@ -248,10 +249,9 @@
     units = down_weight.shape[1]
     slots = count * CAP
     share = width // groups
-    pieces = units // LANES
 
     ids, match, weight, hidden, *rest = pl.pallas_call(
-        functools.partial(front_kernel, count, pieces),
+        functools.partial(front_kernel, count),
         out_shape=[
             jax.ShapeDtypeStruct((top, tokens), jnp.int32),
             jax.ShapeDtypeStruct((count * PAD, tokens), jnp.float32),
@@ -270,7 +270,7 @@
             pltpu.VMEM((tokens, width), jnp.bfloat16),
             pltpu.VMEM((slots, units), jnp.bfloat16),
             pltpu.VMEM((count * PAD, width), jnp.float32),
-            pltpu.SemaphoreType.DMA((5 + 2 * pieces,)),
+            pltpu.SemaphoreType.DMA((4 + len(cuts_of(units)),)),
         ],
         compiler_params=PARAMS,
         cost_estimate=cost(2 * count * PAD * (tokens + units) * width, 2 * (tokens + units) * width),
@@ -323,7 +323,7 @@
     )(rows, gate, weight)
 
     hidden_grad, down_grad, match = pl.pallas_call(
-        functools.partial(down_kernel, groups, pieces),
+        functools.partial(down_kernel, groups),
         out_shape=[
             jax.ShapeDtypeStruct(saved_hidden.shape, jnp.bfloat16),
             jax.ShapeDtypeStruct((1, units, share), jnp.float32),
@@ -333,7 +333,7 @@
         out_specs=[HBM, HBM, VMEM],
         scratch_shapes=[
             pltpu.VMEM((units, share), jnp.float32),
-            pltpu.SemaphoreType.DMA((pieces + 1,)),
+            pltpu.SemaphoreType.DMA((len(cuts_of(units)),)),
         ],
         compiler_params=PARAMS,
         cost_estimate=cost(2 * slots * units * share, 4 * units * share),

time: 21.1 us -> 21 us (level)
  no operation moved by 1% of the time
where the time goes in v18:
time: 21 us; the launch traced here: 20.9 us
  starting transfers between devices  13.5 us (64%)
  Pallas kernels  6.44 us (31%)
  between operations  0.69 us (3%)
  waiting for transfers between devices  0.24 us (1%)
    ppermute x9, starting transfers between devices, send(): lax.ppermute(value, axis, [(i, give(i, step, size)) for i in range(size)])  13.5 us
    pallas_call x1, Pallas kernels, on_device(): pl.pallas_call(functools.partial(front_kernel, count), out_shape=[jax.Sha...  2.55 us
    pallas_call x1, Pallas kernels, on_device(): pl.pallas_call(functools.partial(down_kernel, groups), out_shape=[jax.Sha...  1.97 us
    pallas_call x1, Pallas kernels, on_device(): pl.pallas_call(functools.partial(upstream_kernel, count), out_shape=jax.S...  1.03 us
    pallas_call x1, Pallas kernels, on_device(): pl.pallas_call(functools.partial(gate_kernel, count), out_shape=jax.Shape...  0.61 us
  transfers between devices with their start and end apart: 9, of which 1 were waited for; matrix products, arithmetic and copies ran while one was open for 0% of the time, Pallas kernels for 16%

profile of v18, /device:TPU:0, one launch (start us, length us, event | category | flops | bytes accessed | tf_op | source)
XLA Modules:
  0.0 20.9 jit_solution(8583295842883154447)
XLA Ops:
  0.6 2.6 %front.1 = (s32[8,128]{1,0:T(8,128)S(1)}, f32[32,128]{1,0:T(8,128)S(1)}, bf16[384,4096]{1,0:T(8,128)(2,1)S(1)}, bf16[16,384]{1,0:T(8,128)(2,1)S(1)}, bf16[4,4224...) custom-call(s32[8,128]{1,0:T(8,128)} %bitcast.4, ...), custom_call_target="tpu_custom_call" | custom-call | flops 134217728 | bytes 4194304 | tf_op jit(solution)/shard_map/front/pallas_call | solution.py:253
  3.2 5.1 %collective-permute-start = (bf16[4,8320]{1,0:T(4,128)(2,1)S(1)}, bf16[4,8320]{1,0:T(4,128)(2,1)S(1)}, u32[]{:S(2)}, u32[]{:S(2)}) collective-permute-start(bf16[4,8320]{1,0:T(4,128)(2,1)S(1)} %get-tuple-element.24.refs_1_), channel_id=1, source_target_pairs={{0,12},{4,8},{8,4},{12,0},{1,13},{5,9},{9,5},{13,1},{2,14},{6,10},... | collective-permute-start | bytes 199688 | tf_op jit(solution)/shard_map/ppermute | solution.py:61
  8.3 0.0 collective-permute-start.1
  8.3 0.6 %collective-permute-start.2 = (bf16[4,4224]{1,0:T(4,128)(2,1)S(1)}, bf16[4,4224]{1,0:T(4,128)(2,1)S(1)}, u32[]{:S(2)}, u32[]{:S(2)}) collective-permute-start(bf16[4,4224]{1,0:T(4,128)(2,1)S(1)} %get-tuple-element.26.refs_3_), channel_id=1, source_target_pairs={{0,4},{4,0},{8,12},{12,8},{1,5},{5,1},{9,13},{13,9},{2,6},{6,2},{1... | collective-permute-start | bytes 101384 | tf_op jit(solution)/shard_map/ppermute | solution.py:61
  8.9 2.3 %collective-permute-start.4 = (bf16[4,4096]{1,0:T(4,128)(2,1)S(1)}, bf16[4,4096]{1,0:T(4,128)(2,1)S(1)}, u32[]{:S(2)}, u32[]{:S(2)}) collective-permute-start(bf16[4,4096]{1,0:T(4,128)(2,1)S(1)} %get-tuple-element.35), channel_id=1, source_target_pairs={{0,8},{4,12},{8,0},{12,4},{1,9},{5,13},{9,1},{13,5},{2,10},{6,14},... | collective-permute-start | bytes 98312 | tf_op jit(solution)/shard_map/ppermute | solution.py:61
  11.2 2.0 %collective-permute-start.5 = (bf16[4,4096]{1,0:T(4,128)(2,1)S(1)}, bf16[4,4096]{1,0:T(4,128)(2,1)S(1)}, u32[]{:S(2)}, u32[]{:S(2)}) collective-permute-start(bf16[4,4096]{1,0:T(4,128)(2,1)S(1)} %get-tuple-element.36), channel_id=1, source_target_pairs={{0,4},{4,0},{8,12},{12,8},{1,5},{5,1},{9,13},{13,9},{2,6},{6,2},{1... | collective-permute-start | bytes 98312 | tf_op jit(solution)/shard_map/ppermute | solution.py:61
  13.3 0.2 %collective-permute-done.1.refs_2_ = bf16[4,4224]{1,0:T(4,128)(2,1)S(1)} collective-permute-done((bf16[4,4224]{1,0:T(4,128)(2,1)S(1)}, bf16[4,4224]{1,0:T(4,128)(2,1)S(1)}, u32[]{:S(2)}, u32[]{:S(2)}) %collective-permute-start.1) | collective-permute-done | bytes 33824 | tf_op jit(solution)/shard_map/ppermute | solution.py:61
  13.5 0.0 collective-permute-done.2.refs_3_
  13.5 0.0 collective-permute-done.refs_1_.refs_4_
  13.5 0.1 slots.1
  13.6 1.6 %collective-permute-start.3 = (bf16[16,2432]{1,0:T(8,128)(2,1)S(1)}, bf16[16,2432]{1,0:T(8,128)(2,1)S(1)}, u32[]{:S(2)}, u32[]{:S(2)}) collective-permute-start(bf16[16,2432]{1,0:T(8,128)(2,1)S(1)} %get-tuple-element.32), channel_id=1, source_target_pairs={{0,16},{16,0},{1,17},{17,1},{2,18},{18,2},{3,19},{19,3},{4,20},{20... | collective-permute-start | bytes 233480 | tf_op jit(solution)/shard_map/ppermute | solution.py:61
  15.2 0.0 collective-permute-done.4.refs_6_
  15.2 0.0 collective-permute-done.5.refs_7_
  15.2 0.2 backs.1.refs_0_
  15.3 0.0 collective-permute-start.8
  15.3 1.6 %collective-permute-start.7 = (f32[16,128]{1,0:T(8,128)S(1)}, f32[16,128]{1,0:T(8,128)S(1)}, u32[]{:S(2)}, u32[]{:S(2)}) collective-permute-start(f32[16,128]{1,0:T(8,128)S(1)} %backs.1.refs_0_), channel_id=1, source_target_pairs={{0,2},{1,3},{2,0},{3,1},{4,6},{5,7},{6,4},{7,5},{8,10},{9,11},{10,... | collective-permute-start | bytes 24584 | tf_op jit(solution)/shard_map/ppermute | solution.py:61
  16.9 0.3 %collective-permute-start.6 = (f32[16,128]{1,0:T(8,128)S(1)}, f32[16,128]{1,0:T(8,128)S(1)}, u32[]{:S(2)}, u32[]{:S(2)}) collective-permute-start(f32[16,128]{1,0:T(8,128)S(1)} %backs.1.refs_0_), channel_id=1, source_target_pairs={{0,1},{1,0},{2,3},{3,2},{4,5},{5,4},{6,7},{7,6},{8,9},{9,8},{10,11... | collective-permute-start | bytes 24584 | tf_op jit(solution)/shard_map/ppermute | solution.py:61
  17.2 1.0 %upstream.1.hidden_ref = bf16[16,384]{1,0:T(8,128)(2,1)S(1)} custom-call(bf16[16,4096]{1,0:T(8,128)(2,1)S(1)} %get-tuple-element.27.rows_ref, f32[16,128]{1,0:T(8,128)S(1)} %get-tuple-element.28.gate_ref, bf16[384,4096]{1,0:T(8,128)(2,1)S(1)} %get-tuple-element.29.weight_ref), custom_call_target="tpu_custom_call" | custom-call | flops 50331648 | bytes 3145728 | tf_op jit(solution)/shard_map/upstream/pallas_call | solution.py:315
  18.2 0.0 collective-permute-done.3.refs_1_
  18.2 2.0 %down.1 = (bf16[1,1,16,384]{3,2,1,0:T(8,128)(2,1)}, f32[1,384,2048]{2,1,0:T(8,128)}, f32[32,128]{1,0:T(8,128)S(1)}) custom-call(bf16[16,384]{1,0:T(8,128)(2,1)S(1)} %upstream.1.hidden_ref, f32[32,128]{1,0:T(8,128)S(1)} %get-tuple-element.30.match_ref, bf16[16,2432]{1,0:T(8,128)(2,1)S(1)} %get-tuple-element.31.refs_0_, ...), custom_call_target="tpu_custom_call" | custom-call | flops 25165824 | bytes 3145728 | tf_op jit(solution)/shard_map/down/pallas_call | solution.py:325
  20.2 0.0 collective-permute-done.8.refs_3_
  20.2 0.0 collective-permute-done.7.refs_2_
  20.2 0.0 collective-permute-done.6.refs_1_
  20.2 0.6 %gates.1 = f32[8,128]{1,0:T(8,128)} custom-call(s32[8,128]{1,0:T(8,128)S(1)} %get-tuple-element.21.ids_ref, f32[32,128]{1,0:T(8,128)S(1)} %get-tuple-element.33.match_ref, f32[16,128]{1,0:T(8,128)S(1)} %backs.1.refs_0_, f32[16,128]{1,0:T(8,128)S(1)} %collective-permute-done.6.refs_1_, f32[16,128]{1,0:T(8,128)S(1)} %collective-permute-done.7.refs_2_, ...), custom_call_target="tpu_custom_call" | custom-call | flops 2048 | bytes 8192 | tf_op jit(solution)/shard_map/gates/pallas_call | solution.py:343
Async XLA Ops:
  3.2 10.3 %collective-permute-start = (bf16[4,8320]{1,0:T(4,128)(2,1)S(1)}, bf16[4,8320]{1,0:T(4,128)(2,1)S(1)}, u32[]{:S(2)}, u32[]{:S(2)}) collective-permute-start(bf16[4,8320]{1,0:T(4,128)(2,1)S(1)} %get-tuple-element.24.refs_1_), channel_id=1, source_target_pairs={{0,12},{4,8},{8,4},{12,0},{1,13},{5,9},{9,5},{13,1},{2,14},{6,10},... | collective-permute-start | bytes 199688 | tf_op jit(solution)/shard_map/ppermute | solution.py:61
  8.3 5.2 %collective-permute-start.1 = (bf16[4,4224]{1,0:T(4,128)(2,1)S(1)}, bf16[4,4224]{1,0:T(4,128)(2,1)S(1)}, u32[]{:S(2)}, u32[]{:S(2)}) collective-permute-start(bf16[4,4224]{1,0:T(4,128)(2,1)S(1)} %get-tuple-element.25.refs_2_), channel_id=1, source_target_pairs={{0,8},{4,12},{8,0},{12,4},{1,9},{5,13},{9,1},{13,5},{2,10},{6,14},... | collective-permute-start | bytes 101384 | tf_op jit(solution)/shard_map/ppermute | solution.py:61
  8.3 5.2 %collective-permute-start.2 = (bf16[4,4224]{1,0:T(4,128)(2,1)S(1)}, bf16[4,4224]{1,0:T(4,128)(2,1)S(1)}, u32[]{:S(2)}, u32[]{:S(2)}) collective-permute-start(bf16[4,4224]{1,0:T(4,128)(2,1)S(1)} %get-tuple-element.26.refs_3_), channel_id=1, source_target_pairs={{0,4},{4,0},{8,12},{12,8},{1,5},{5,1},{9,13},{13,9},{2,6},{6,2},{1... | collective-permute-start | bytes 101384 | tf_op jit(solution)/shard_map/ppermute | solution.py:61
  8.9 6.2 %collective-permute-start.4 = (bf16[4,4096]{1,0:T(4,128)(2,1)S(1)}, bf16[4,4096]{1,0:T(4,128)(2,1)S(1)}, u32[]{:S(2)}, u32[]{:S(2)}) collective-permute-start(bf16[4,4096]{1,0:T(4,128)(2,1)S(1)} %get-tuple-element.35), channel_id=1, source_target_pairs={{0,8},{4,12},{8,0},{12,4},{1,9},{5,13},{9,1},{13,5},{2,10},{6,14},... | collective-permute-start | bytes 98312 | tf_op jit(solution)/shard_map/ppermute | solution.py:61
  11.2 3.9 %collective-permute-start.5 = (bf16[4,4096]{1,0:T(4,128)(2,1)S(1)}, bf16[4,4096]{1,0:T(4,128)(2,1)S(1)}, u32[]{:S(2)}, u32[]{:S(2)}) collective-permute-start(bf16[4,4096]{1,0:T(4,128)(2,1)S(1)} %get-tuple-element.36), channel_id=1, source_target_pairs={{0,4},{4,0},{8,12},{12,8},{1,5},{5,1},{9,13},{13,9},{2,6},{6,2},{1... | collective-permute-start | bytes 98312 | tf_op jit(solution)/shard_map/ppermute | solution.py:61
  13.6 4.6 %collective-permute-start.3 = (bf16[16,2432]{1,0:T(8,128)(2,1)S(1)}, bf16[16,2432]{1,0:T(8,128)(2,1)S(1)}, u32[]{:S(2)}, u32[]{:S(2)}) collective-permute-start(bf16[16,2432]{1,0:T(8,128)(2,1)S(1)} %get-tuple-element.32), channel_id=1, source_target_pairs={{0,16},{16,0},{1,17},{17,1},{2,18},{18,2},{3,19},{19,3},{4,20},{20... | collective-permute-start | bytes 233480 | tf_op jit(solution)/shard_map/ppermute | solution.py:61
  15.3 4.9 %collective-permute-start.8 = (f32[16,128]{1,0:T(8,128)S(1)}, f32[16,128]{1,0:T(8,128)S(1)}, u32[]{:S(2)}, u32[]{:S(2)}) collective-permute-start(f32[16,128]{1,0:T(8,128)S(1)} %backs.1.refs_0_), channel_id=1, source_target_pairs={{0,3},{1,2},{2,1},{3,0},{4,7},{5,6},{6,5},{7,4},{8,11},{9,10},{10,... | collective-permute-start | bytes 24584 | tf_op jit(solution)/shard_map/ppermute | solution.py:61
  15.3 4.9 %collective-permute-start.7 = (f32[16,128]{1,0:T(8,128)S(1)}, f32[16,128]{1,0:T(8,128)S(1)}, u32[]{:S(2)}, u32[]{:S(2)}) collective-permute-start(f32[16,128]{1,0:T(8,128)S(1)} %backs.1.refs_0_), channel_id=1, source_target_pairs={{0,2},{1,3},{2,0},{3,1},{4,6},{5,7},{6,4},{7,5},{8,10},{9,11},{10,... | collective-permute-start | bytes 24584 | tf_op jit(solution)/shard_map/ppermute | solution.py:61
  16.9 3.3 %collective-permute-start.6 = (f32[16,128]{1,0:T(8,128)S(1)}, f32[16,128]{1,0:T(8,128)S(1)}, u32[]{:S(2)}, u32[]{:S(2)}) collective-permute-start(f32[16,128]{1,0:T(8,128)S(1)} %backs.1.refs_0_), channel_id=1, source_target_pairs={{0,1},{1,0},{2,3},{3,2},{4,5},{5,4},{6,7},{7,6},{8,9},{9,8},{10,11... | collective-permute-start | bytes 24584 | tf_op jit(solution)/shard_map/ppermute | solution.py:61

commit v19 on v16

--- a/solution.py
+++ b/solution.py
@@ -163,8 +163,9 @@
     for r in range(count):
         row = received[r][:, : width + LANES]
         wide_ref[r * CAP : (r + 1) * CAP, :] = row.astype(jnp.float32)
-    rows = wide_ref[:, :width]
-    gate = wide_ref[:, width:]
+    slots = count * CAP
+    rows = wide_ref[:slots, :width]
+    gate = wide_ref[:slots, width:]
     gate_ref[...] = gate
     rows_ref[...] = rows.astype(jnp.bfloat16)
     weighted_ref[...] = (gate[:, :1] * rows).astype(jnp.bfloat16)
@@ -180,7 +181,7 @@
     sent = refs[:count]
     joint_ref = refs[count]
     products = dict(zip(apart(count), refs[count + 1 : 2 * count]))
-    back_ref = refs[2 * count]
+    out_ref, back_ref = refs[2 * count :]
     width = products[0].shape[1]
     for r in range(count):
         step = reply(r, count)
@@ -191,17 +192,20 @@
         mine = sent[r][:, :width].astype(jnp.float32)
         back = jnp.sum(mine * theirs, axis=1, keepdims=True)
         back_ref[r * CAP : (r + 1) * CAP, :] = jnp.broadcast_to(back, (CAP, LANES))
-
-
-def upstream_kernel(count, rows_ref, gate_ref, weight_ref, out_ref):
-    upstream = dot(rows_ref[...], weight_ref[...], ((1,), (1,)))
-    scaled = (gate_ref[:, :1] * upstream).astype(jnp.bfloat16)
-    out_ref[...] = dot(slot_order(count), scaled, ((0,), (0,))).astype(jnp.bfloat16)
-
-
-def down_kernel(groups, pieces, hidden_ref, match_ref, *refs):
+    out_ref[...] = back_ref[: count * CAP, :]
+
+
+def upstream_part(rows_ref, weight_ref, begin, end):
+    return dot(rows_ref[:, begin:end], weight_ref[:, begin:end], ((1,), (1,)))
+
+
+def upstream_kernel(split, rows_ref, weight_ref, out_ref):
+    out_ref[...] = upstream_part(rows_ref, weight_ref, 0, split)
+
+
+def down_kernel(count, groups, pieces, split, part_ref, rows_ref, gate_ref, weight_ref, match_ref, *refs):
     pays = refs[:groups]
-    hidden_hbm, down_hbm, match_out, down_out, sems = refs[groups:]
+    hidden_hbm, down_hbm, match_out, hidden_out, down_out, sems = refs[groups:]
     units, share = down_out.shape
     block = units // pieces
     slots = jnp.concatenate([pay_ref[...] for pay_ref in pays], axis=0)
@@ -217,7 +221,10 @@
         down_out[part, :] = dot(hidden, slots[:, :share], ((0,), (0,)))
         part = pl.ds(p * block, block)
         write(down_out.at[part], down_hbm.at[0, part])
-    write(hidden_ref, hidden_hbm.at[0, 0])
+    upstream = part_ref[...] + upstream_part(rows_ref, weight_ref, split, weight_ref.shape[1])
+    scaled = (gate_ref[:, :1] * upstream).astype(jnp.bfloat16)
+    hidden_out[...] = dot(slot_order(count), scaled, ((0,), (0,))).astype(jnp.bfloat16)
+    write(hidden_out, hidden_hbm.at[0, 0])
     match_out[...] = match_ref[...]
     for copy in copies:
         copy.wait()
@@ -291,7 +298,7 @@
         in_specs=[VMEM] * (1 + count),
         out_specs=[VMEM] * (2 + groups),
         scratch_shapes=[
-            pltpu.VMEM((slots, width + LANES), jnp.float32),
+            pltpu.VMEM((slots + PAD, width + LANES), jnp.float32),
             pltpu.VMEM((slots, width), jnp.bfloat16),
         ],
         compiler_params=PARAMS,
@@ -304,6 +311,7 @@
         out_shape=jax.ShapeDtypeStruct((slots, LANES), jnp.float32),
         in_specs=[VMEM] * (2 * count),
         out_specs=VMEM,
+        scratch_shapes=[pltpu.VMEM((slots + PAD, LANES), jnp.float32)],
         compiler_params=PARAMS,
         cost_estimate=cost(*AFTER_WAIT),
         name="backs",
@@ -312,33 +320,35 @@
     others = [send(pays[r], "dp", r) for r in range(1, groups)]
     backs = [back] + [send(back, "tensor", r) for r in reversed(range(1, tensors))]
 
-    hidden_grad = pl.pallas_call(
-        functools.partial(upstream_kernel, count),
-        out_shape=jax.ShapeDtypeStruct((slots, units), jnp.bfloat16),
-        in_specs=[VMEM] * 3,
+    split = width * 3 // 4
+    upstream = pl.pallas_call(
+        functools.partial(upstream_kernel, split),
+        out_shape=jax.ShapeDtypeStruct((slots, units), jnp.float32),
+        in_specs=[VMEM] * 2,
         out_specs=VMEM,
         compiler_params=PARAMS,
-        cost_estimate=cost(2 * slots * units * width, 2 * units * width),
+        cost_estimate=cost(2 * slots * units * split, 2 * units * split),
         name="upstream",
-    )(rows, gate, weight)
+    )(rows, weight)
 
     hidden_grad, down_grad, match = pl.pallas_call(
-        functools.partial(down_kernel, groups, pieces),
+        functools.partial(down_kernel, count, groups, pieces, split),
         out_shape=[
             jax.ShapeDtypeStruct(saved_hidden.shape, jnp.bfloat16),
             jax.ShapeDtypeStruct((1, units, share), jnp.float32),
             jax.ShapeDtypeStruct(match.shape, jnp.float32),
         ],
-        in_specs=[VMEM] * (2 + groups),
+        in_specs=[VMEM] * (5 + groups),
         out_specs=[HBM, HBM, VMEM],
         scratch_shapes=[
+            pltpu.VMEM((slots, units), jnp.bfloat16),
             pltpu.VMEM((units, share), jnp.float32),
             pltpu.SemaphoreType.DMA((pieces + 1,)),
         ],
         compiler_params=PARAMS,
         cost_estimate=cost(2 * slots * units * share, 4 * units * share),
         name="down",
-    )(hidden_grad, match, pays[0], *others)
+    )(upstream, rows, gate, weight, match, pays[0], *others)
 
     gate_grad = pl.pallas_call(
         functools.partial(gate_kernel, count),

time: 21.1 us -> 20.9 us (level)
  Pallas kernels: 6.51 us -> 6.18 us
    pallas_call x2, Pallas kernels: 3.06 us -> 2.72 us  [the longest x1 2.02 us: on_device(): pl.pallas_call(functools.partial(down_kernel, count, groups, pieces, spli...]
  transfers between devices with their start and end apart: 9 -> 9, of which waited for: 1 -> 2; matrix products, arithmetic and copies ran while one was open for 0% -> 0% of each run, Pallas kernels for 16% -> 14%
where the time goes in v19:
time: 20.9 us; the launch traced here: 20.8 us
  starting transfers between devices  13.5 us (65%)
  Pallas kernels  6.18 us (30%)
  between operations  0.69 us (3%)
  waiting for transfers between devices  0.41 us (2%)
    ppermute x9, starting transfers between devices, send(): lax.ppermute(value, axis, [(i, give(i, step, size)) for i in range(size)])  13.5 us
    pallas_call x1, Pallas kernels, on_device(): pl.pallas_call(functools.partial(front_kernel, count, pieces), out_shape=...  2.57 us
    pallas_call x1, Pallas kernels, on_device(): pl.pallas_call(functools.partial(down_kernel, count, groups, pieces, spli...  2.02 us
    pallas_call x1, Pallas kernels, on_device(): pl.pallas_call(functools.partial(upstream_kernel, split), out_shape=jax.S...  0.71 us
    pallas_call x1, Pallas kernels, on_device(): pl.pallas_call(functools.partial(gate_kernel, count), out_shape=jax.Shape...  0.61 us
  transfers between devices with their start and end apart: 9, of which 2 were waited for; matrix products, arithmetic and copies ran while one was open for 0% of the time, Pallas kernels for 14%

profile of v19, /device:TPU:0, one launch (start us, length us, event | category | flops | bytes accessed | tf_op | source)
XLA Modules:
  0.0 20.8 jit_solution(17268804640746317390)
XLA Ops:
  0.6 2.6 %front.1 = (s32[8,128]{1,0:T(8,128)S(1)}, f32[32,128]{1,0:T(8,128)S(1)}, bf16[384,4096]{1,0:T(8,128)(2,1)S(1)}, bf16[16,384]{1,0:T(8,128)(2,1)S(1)}, bf16[4,4224...) custom-call(s32[8,128]{1,0:T(8,128)} %bitcast.4, ...), custom_call_target="tpu_custom_call" | custom-call | flops 134217728 | bytes 4194304 | tf_op jit(solution)/shard_map/front/pallas_call | solution.py:260
  3.2 5.1 %collective-permute-start = (bf16[4,8320]{1,0:T(4,128)(2,1)S(1)}, bf16[4,8320]{1,0:T(4,128)(2,1)S(1)}, u32[]{:S(2)}, u32[]{:S(2)}) collective-permute-start(bf16[4,8320]{1,0:T(4,128)(2,1)S(1)} %get-tuple-element.24.refs_1_), channel_id=1, source_target_pairs={{0,12},{4,8},{8,4},{12,0},{1,13},{5,9},{9,5},{13,1},{2,14},{6,10},... | collective-permute-start | bytes 199688 | tf_op jit(solution)/shard_map/ppermute | solution.py:61
  8.3 0.0 collective-permute-start.1
  8.3 0.6 %collective-permute-start.2 = (bf16[4,4224]{1,0:T(4,128)(2,1)S(1)}, bf16[4,4224]{1,0:T(4,128)(2,1)S(1)}, u32[]{:S(2)}, u32[]{:S(2)}) collective-permute-start(bf16[4,4224]{1,0:T(4,128)(2,1)S(1)} %get-tuple-element.26.refs_3_), channel_id=1, source_target_pairs={{0,4},{4,0},{8,12},{12,8},{1,5},{5,1},{9,13},{13,9},{2,6},{6,2},{1... | collective-permute-start | bytes 101384 | tf_op jit(solution)/shard_map/ppermute | solution.py:61
  9.0 2.3 %collective-permute-start.4 = (bf16[4,4096]{1,0:T(4,128)(2,1)S(1)}, bf16[4,4096]{1,0:T(4,128)(2,1)S(1)}, u32[]{:S(2)}, u32[]{:S(2)}) collective-permute-start(bf16[4,4096]{1,0:T(4,128)(2,1)S(1)} %get-tuple-element.35), channel_id=1, source_target_pairs={{0,8},{4,12},{8,0},{12,4},{1,9},{5,13},{9,1},{13,5},{2,10},{6,14},... | collective-permute-start | bytes 98312 | tf_op jit(solution)/shard_map/ppermute | solution.py:61
  11.3 2.0 %collective-permute-start.5 = (bf16[4,4096]{1,0:T(4,128)(2,1)S(1)}, bf16[4,4096]{1,0:T(4,128)(2,1)S(1)}, u32[]{:S(2)}, u32[]{:S(2)}) collective-permute-start(bf16[4,4096]{1,0:T(4,128)(2,1)S(1)} %get-tuple-element.36), channel_id=1, source_target_pairs={{0,4},{4,0},{8,12},{12,8},{1,5},{5,1},{9,13},{13,9},{2,6},{6,2},{1... | collective-permute-start | bytes 98312 | tf_op jit(solution)/shard_map/ppermute | solution.py:61
  13.3 0.2 %collective-permute-done.1.refs_2_ = bf16[4,4224]{1,0:T(4,128)(2,1)S(1)} collective-permute-done((bf16[4,4224]{1,0:T(4,128)(2,1)S(1)}, bf16[4,4224]{1,0:T(4,128)(2,1)S(1)}, u32[]{:S(2)}, u32[]{:S(2)}) %collective-permute-start.1) | collective-permute-done | bytes 33824 | tf_op jit(solution)/shard_map/ppermute | solution.py:61
  13.5 0.0 collective-permute-done.2.refs_3_
  13.5 0.0 collective-permute-done.refs_1_.refs_4_
  13.5 0.1 slots.1
  13.6 1.6 %collective-permute-start.3 = (bf16[16,2432]{1,0:T(8,128)(2,1)S(1)}, bf16[16,2432]{1,0:T(8,128)(2,1)S(1)}, u32[]{:S(2)}, u32[]{:S(2)}) collective-permute-start(bf16[16,2432]{1,0:T(8,128)(2,1)S(1)} %get-tuple-element.32), channel_id=1, source_target_pairs={{0,16},{16,0},{1,17},{17,1},{2,18},{18,2},{3,19},{19,3},{4,20},{20... | collective-permute-start | bytes 233480 | tf_op jit(solution)/shard_map/ppermute | solution.py:61
  15.2 0.0 collective-permute-done.4.refs_6_
  15.2 0.0 collective-permute-done.5.refs_7_
  15.2 0.2 backs.1.refs_0_
  15.4 0.0 collective-permute-start.8
  15.4 1.6 %collective-permute-start.7 = (f32[16,128]{1,0:T(8,128)S(1)}, f32[16,128]{1,0:T(8,128)S(1)}, u32[]{:S(2)}, u32[]{:S(2)}) collective-permute-start(f32[16,128]{1,0:T(8,128)S(1)} %backs.1.refs_0_), channel_id=1, source_target_pairs={{0,2},{1,3},{2,0},{3,1},{4,6},{5,7},{6,4},{7,5},{8,10},{9,11},{10,... | collective-permute-start | bytes 24584 | tf_op jit(solution)/shard_map/ppermute | solution.py:61
  16.9 0.3 %collective-permute-start.6 = (f32[16,128]{1,0:T(8,128)S(1)}, f32[16,128]{1,0:T(8,128)S(1)}, u32[]{:S(2)}, u32[]{:S(2)}) collective-permute-start(f32[16,128]{1,0:T(8,128)S(1)} %backs.1.refs_0_), channel_id=1, source_target_pairs={{0,1},{1,0},{2,3},{3,2},{4,5},{5,4},{6,7},{7,6},{8,9},{9,8},{10,11... | collective-permute-start | bytes 24584 | tf_op jit(solution)/shard_map/ppermute | solution.py:61
  17.2 0.7 %upstream.1.part_ref = f32[16,384]{1,0:T(8,128)S(1)} custom-call(bf16[16,4096]{1,0:T(8,128)(2,1)S(1)} %get-tuple-element.27.rows_ref, bf16[384,4096]{1,0:T(8,128)(2,1)S(1)} %get-tuple-element.28.weight_ref), custom_call_target="tpu_custom_call" | custom-call | flops 37748736 | bytes 2359296 | tf_op jit(solution)/shard_map/upstream/pallas_call | solution.py:324
  17.9 0.2 collective-permute-done.3.refs_1_
  18.1 2.0 %down.1 = (bf16[1,1,16,384]{3,2,1,0:T(8,128)(2,1)}, f32[1,384,2048]{2,1,0:T(8,128)}, f32[32,128]{1,0:T(8,128)S(1)}) custom-call(f32[16,384]{1,0:T(8,128)S(1)} %upstream.1.part_ref, bf16[16,4096]{1,0:T(8,128)(2,1)S(1)} %get-tuple-element.27.rows_ref, f32[16,128]{1,0:T(8,128)S(1)} %get-tuple-element.29.gate_ref, ...), custom_call_target="tpu_custom_call" | custom-call | flops 25165824 | bytes 3145728 | tf_op jit(solution)/shard_map/down/pallas_call | solution.py:334
  20.1 0.0 collective-permute-done.8.refs_3_
  20.1 0.0 collective-permute-done.7.refs_2_
  20.1 0.0 collective-permute-done.6.refs_1_
  20.1 0.6 %gates.1 = f32[8,128]{1,0:T(8,128)} custom-call(s32[8,128]{1,0:T(8,128)S(1)} %get-tuple-element.21.ids_ref, f32[32,128]{1,0:T(8,128)S(1)} %get-tuple-element.33.match_ref, f32[16,128]{1,0:T(8,128)S(1)} %backs.1.refs_0_, f32[16,128]{1,0:T(8,128)S(1)} %collective-permute-done.6.refs_1_, f32[16,128]{1,0:T(8,128)S(1)} %collective-permute-done.7.refs_2_, ...), custom_call_target="tpu_custom_call" | custom-call | flops 2048 | bytes 8192 | tf_op jit(solution)/shard_map/gates/pallas_call | solution.py:353
Async XLA Ops:
  3.2 10.3 %collective-permute-start = (bf16[4,8320]{1,0:T(4,128)(2,1)S(1)}, bf16[4,8320]{1,0:T(4,128)(2,1)S(1)}, u32[]{:S(2)}, u32[]{:S(2)}) collective-permute-start(bf16[4,8320]{1,0:T(4,128)(2,1)S(1)} %get-tuple-element.24.refs_1_), channel_id=1, source_target_pairs={{0,12},{4,8},{8,4},{12,0},{1,13},{5,9},{9,5},{13,1},{2,14},{6,10},... | collective-permute-start | bytes 199688 | tf_op jit(solution)/shard_map/ppermute | solution.py:61
  8.3 5.2 %collective-permute-start.1 = (bf16[4,4224]{1,0:T(4,128)(2,1)S(1)}, bf16[4,4224]{1,0:T(4,128)(2,1)S(1)}, u32[]{:S(2)}, u32[]{:S(2)}) collective-permute-start(bf16[4,4224]{1,0:T(4,128)(2,1)S(1)} %get-tuple-element.25.refs_2_), channel_id=1, source_target_pairs={{0,8},{4,12},{8,0},{12,4},{1,9},{5,13},{9,1},{13,5},{2,10},{6,14},... | collective-permute-start | bytes 101384 | tf_op jit(solution)/shard_map/ppermute | solution.py:61
  8.3 5.2 %collective-permute-start.2 = (bf16[4,4224]{1,0:T(4,128)(2,1)S(1)}, bf16[4,4224]{1,0:T(4,128)(2,1)S(1)}, u32[]{:S(2)}, u32[]{:S(2)}) collective-permute-start(bf16[4,4224]{1,0:T(4,128)(2,1)S(1)} %get-tuple-element.26.refs_3_), channel_id=1, source_target_pairs={{0,4},{4,0},{8,12},{12,8},{1,5},{5,1},{9,13},{13,9},{2,6},{6,2},{1... | collective-permute-start | bytes 101384 | tf_op jit(solution)/shard_map/ppermute | solution.py:61
  9.0 6.2 %collective-permute-start.4 = (bf16[4,4096]{1,0:T(4,128)(2,1)S(1)}, bf16[4,4096]{1,0:T(4,128)(2,1)S(1)}, u32[]{:S(2)}, u32[]{:S(2)}) collective-permute-start(bf16[4,4096]{1,0:T(4,128)(2,1)S(1)} %get-tuple-element.35), channel_id=1, source_target_pairs={{0,8},{4,12},{8,0},{12,4},{1,9},{5,13},{9,1},{13,5},{2,10},{6,14},... | collective-permute-start | bytes 98312 | tf_op jit(solution)/shard_map/ppermute | solution.py:61
  11.3 3.9 %collective-permute-start.5 = (bf16[4,4096]{1,0:T(4,128)(2,1)S(1)}, bf16[4,4096]{1,0:T(4,128)(2,1)S(1)}, u32[]{:S(2)}, u32[]{:S(2)}) collective-permute-start(bf16[4,4096]{1,0:T(4,128)(2,1)S(1)} %get-tuple-element.36), channel_id=1, source_target_pairs={{0,4},{4,0},{8,12},{12,8},{1,5},{5,1},{9,13},{13,9},{2,6},{6,2},{1... | collective-permute-start | bytes 98312 | tf_op jit(solution)/shard_map/ppermute | solution.py:61
  13.6 4.5 %collective-permute-start.3 = (bf16[16,2432]{1,0:T(8,128)(2,1)S(1)}, bf16[16,2432]{1,0:T(8,128)(2,1)S(1)}, u32[]{:S(2)}, u32[]{:S(2)}) collective-permute-start(bf16[16,2432]{1,0:T(8,128)(2,1)S(1)} %get-tuple-element.32), channel_id=1, source_target_pairs={{0,16},{16,0},{1,17},{17,1},{2,18},{18,2},{3,19},{19,3},{4,20},{20... | collective-permute-start | bytes 233480 | tf_op jit(solution)/shard_map/ppermute | solution.py:61
  15.4 4.8 %collective-permute-start.8 = (f32[16,128]{1,0:T(8,128)S(1)}, f32[16,128]{1,0:T(8,128)S(1)}, u32[]{:S(2)}, u32[]{:S(2)}) collective-permute-start(f32[16,128]{1,0:T(8,128)S(1)} %backs.1.refs_0_), channel_id=1, source_target_pairs={{0,3},{1,2},{2,1},{3,0},{4,7},{5,6},{6,5},{7,4},{8,11},{9,10},{10,... | collective-permute-start | bytes 24584 | tf_op jit(solution)/shard_map/ppermute | solution.py:61
  15.4 4.8 %collective-permute-start.7 = (f32[16,128]{1,0:T(8,128)S(1)}, f32[16,128]{1,0:T(8,128)S(1)}, u32[]{:S(2)}, u32[]{:S(2)}) collective-permute-start(f32[16,128]{1,0:T(8,128)S(1)} %backs.1.refs_0_), channel_id=1, source_target_pairs={{0,2},{1,3},{2,0},{3,1},{4,6},{5,7},{6,4},{7,5},{8,10},{9,11},{10,... | collective-permute-start | bytes 24584 | tf_op jit(solution)/shard_map/ppermute | solution.py:61
  16.9 3.2 %collective-permute-start.6 = (f32[16,128]{1,0:T(8,128)S(1)}, f32[16,128]{1,0:T(8,128)S(1)}, u32[]{:S(2)}, u32[]{:S(2)}) collective-permute-start(f32[16,128]{1,0:T(8,128)S(1)} %backs.1.refs_0_), channel_id=1, source_target_pairs={{0,1},{1,0},{2,3},{3,2},{4,5},{5,4},{6,7},{7,6},{8,9},{9,8},{10,11... | collective-permute-start | bytes 24584 | tf_op jit(solution)/shard_map/ppermute | solution.py:61

commit v20 on v19

--- a/solution.py
+++ b/solution.py
@@ -9,7 +9,6 @@
 
 CAP = 4
 LANES = 128
-JOINT = 1
 AFTER_WAIT = (10**9, 10**7)
 WIDE = 1024
 PAD = 8
@@ -53,7 +52,7 @@
 
 
 def apart(size):
-    return [r for r in range(size) if r != JOINT]
+    return [r for r in range(size) if r not in (1, size - 1)]
 
 
 def send(value, axis, step, give=target):
@@ -61,12 +60,13 @@
     return lax.ppermute(value, axis, [(i, give(i, step, size)) for i in range(size)])
 
 
-def front_kernel(count, pieces, *refs):
+def front_kernel(count, groups, pieces, *refs):
     ids_hbm, gates_hbm, grad_hbm, hidden_hbm, weight_hbm = refs[:5]
     ids_ref, match_ref, weight_ref, hidden_ref = refs[5:9]
     sends = refs[9 : 9 + count]
-    products = refs[9 + count : 8 + 2 * count]
-    gates_ref, grad_ref, saved_ref, total_ref, sems = refs[8 + 2 * count :]
+    products = dict(zip(apart(count), refs[9 + count :]))
+    early = refs[-4 - groups : -5]
+    gates_ref, grad_ref, saved_ref, total_ref, sems = refs[-5:]
     units, width = weight_ref.shape
     top, tokens = ids_ref.shape
     pairs = [(ids_hbm, ids_ref), (gates_hbm, gates_ref), (hidden_hbm.at[0, 0], saved_ref)]
@@ -109,6 +109,7 @@
     slots = count * CAP
     saved = saved_ref[...]
     hidden_ref[...] = dot(slot_order(count), saved, ((1,), (0,))).astype(jnp.bfloat16)
+    spread = dot(slot_order(count, PAD), saved, ((1,), (0,)))
     here = lax.broadcasted_iota(jnp.int32, (rows, slots), 0)
     there = lax.broadcasted_iota(jnp.int32, (rows, slots), 1)
     chosen = (here % PAD < CAP) & (there == target(me, here // PAD, count) * CAP + here % PAD)
@@ -126,6 +127,16 @@
         picked = dot(match, grad_ref[:, part], ((1,), (0,)))
         for r in range(count):
             sends[r][:, part] = picked[r * PAD : r * PAD + CAP].astype(jnp.bfloat16)
+        total_ref[:PAD, part] = picked[:PAD]
+    share = width // groups
+    group = lax.axis_index("dp")
+    for r, early_ref in enumerate(early, 1):
+        begin = pl.multiple_of(target(group, r, groups) * share, share)
+        weighted = slot_gate[:CAP] * total_ref[:CAP, pl.ds(begin, share)]
+        early_ref[:, :share] = weighted.astype(jnp.bfloat16)
+        for k in range(count):
+            part = slice(share + k * units, share + (k + 1) * units)
+            early_ref[:, part] = spread[k * PAD : k * PAD + CAP].astype(jnp.bfloat16)
     block = units // pieces
     for p in range(pieces):
         for copy in copies[5 + 2 * p : 7 + 2 * p]:
@@ -139,60 +150,74 @@
             if p < pieces - 1:
                 total_ref[:, part] = term
                 continue
-            for product_ref, r in zip(products, apart(count)):
-                product_ref[:, part] = term[r * PAD : r * PAD + CAP].astype(jnp.bfloat16)
-            begin += width + LANES
-            joint = term[JOINT * PAD : JOINT * PAD + CAP].astype(jnp.bfloat16)
-            sends[JOINT][:, begin : begin + wide] = joint
-
-
-def slot_order(count):
+            for r in range(count):
+                product = term[r * PAD : r * PAD + CAP].astype(jnp.bfloat16)
+                if r in products:
+                    products[r][:, part] = product
+                else:
+                    joint = slice(width + LANES + begin, width + LANES + begin + wide)
+                    sends[r][:, joint] = product
+
+
+def slot_order(count, lines=CAP):
     me = lax.axis_index("expert")
-    slots = count * CAP
-    here = lax.broadcasted_iota(jnp.int32, (slots, slots), 0)
-    saved = lax.broadcasted_iota(jnp.int32, (slots, slots), 1)
-    return (saved == source(me, here // CAP, count) * CAP + here % CAP).astype(jnp.bfloat16)
+    here = lax.broadcasted_iota(jnp.int32, (count * lines, count * CAP), 0)
+    saved = lax.broadcasted_iota(jnp.int32, (count * lines, count * CAP), 1)
+    place = here % lines
+    block = source(me, here // lines, count)
+    return ((saved == block * CAP + place) & (place < CAP)).astype(jnp.bfloat16)
 
 
 def slot_kernel(count, groups, hidden_ref, *refs):
     received = refs[:count]
-    rows_ref, gate_ref = refs[count : count + 2]
-    pays = refs[count + 2 : count + 2 + groups]
-    wide_ref, weighted_ref = refs[count + 2 + groups :]
+    rows_ref, gate_ref, own_ref = refs[count : count + 3]
+    lates = refs[count + 3 : count + 2 + groups]
+    wide_ref, spread_ref = refs[count + 2 + groups :]
     width = rows_ref.shape[1]
+    share = width // groups
+    slots = count * CAP
     for r in range(count):
-        row = received[r][:, : width + LANES]
-        wide_ref[r * CAP : (r + 1) * CAP, :] = row.astype(jnp.float32)
-    slots = count * CAP
+        row = received[r][:, : width + LANES].astype(jnp.float32)
+        wide_ref[r * CAP : (r + 1) * CAP, :] = row
+        spread_ref[r * PAD : r * PAD + CAP, :] = row[:, width : width + 1] * row[:, :width]
     rows = wide_ref[:slots, :width]
     gate = wide_ref[:slots, width:]
     gate_ref[...] = gate
     rows_ref[...] = rows.astype(jnp.bfloat16)
-    weighted_ref[...] = (gate[:, :1] * rows).astype(jnp.bfloat16)
-    share = width // groups
     me = lax.axis_index("dp")
-    for r in range(groups):
-        group = target(me, r, groups)
-        pays[r][:, :share] = weighted_ref[:, pl.ds(pl.multiple_of(group * share, share), share)]
-        pays[r][:, share:] = hidden_ref[...]
-
-
-def back_kernel(count, *refs):
-    sent = refs[:count]
-    joint_ref = refs[count]
-    products = dict(zip(apart(count), refs[count + 1 : 2 * count]))
-    out_ref, back_ref = refs[2 * count :]
-    width = products[0].shape[1]
+    for r, late_ref in enumerate(lates, 1):
+        begin = pl.multiple_of(target(me, r, groups) * share, share)
+        for k in range(1, count):
+            late = spread_ref[k * PAD : k * PAD + CAP, pl.ds(begin, share)]
+            late_ref[:, (k - 1) * share : k * share] = late.astype(jnp.bfloat16)
+    weighted = gate[:, :1] * wide_ref[:slots, pl.ds(pl.multiple_of(me * share, share), share)]
+    own_ref[:, :share] = weighted.astype(jnp.bfloat16)
+    own_ref[:, share:] = hidden_ref[...]
+
+
+def back_kernel(count, groups, *refs):
+    sent, refs = refs[:count], refs[count:]
+    received, refs = dict(enumerate(refs[: count - 1], 1)), refs[count - 1 :]
+    received.update(zip(apart(count), refs))
+    refs = refs[len(apart(count)) :]
+    early, refs = refs[: groups - 1], refs[groups - 1 :]
+    out_ref, hiddens = refs[0], refs[1:groups]
+    back_ref, units_ref = refs[groups:]
+    width = received[0].shape[1]
     for r in range(count):
-        step = reply(r, count)
-        if step != JOINT:
-            theirs = products[step][...].astype(jnp.float32)
-        else:
-            theirs = joint_ref[:, joint_ref.shape[1] - width :].astype(jnp.float32)
+        ref = received[reply(r, count)]
+        theirs = ref[:, ref.shape[1] - width :].astype(jnp.float32)
         mine = sent[r][:, :width].astype(jnp.float32)
         back = jnp.sum(mine * theirs, axis=1, keepdims=True)
         back_ref[r * CAP : (r + 1) * CAP, :] = jnp.broadcast_to(back, (CAP, LANES))
-    out_ref[...] = back_ref[: count * CAP, :]
+    slots, units = count * CAP, units_ref.shape[1]
+    out_ref[...] = back_ref[:slots, :]
+    for early_ref, hidden_ref in zip(early, hiddens):
+        share = early_ref.shape[1] - count * units
+        for k in range(count):
+            part = early_ref[:, share + k * units : share + (k + 1) * units]
+            units_ref[k * CAP : (k + 1) * CAP, :] = part.astype(jnp.float32)
+        hidden_ref[...] = units_ref[:slots, :].astype(jnp.bfloat16)
 
 
 def upstream_part(rows_ref, weight_ref, begin, end):
@@ -204,11 +229,21 @@
 
 
 def down_kernel(count, groups, pieces, split, part_ref, rows_ref, gate_ref, weight_ref, match_ref, *refs):
-    pays = refs[:groups]
-    hidden_hbm, down_hbm, match_out, hidden_out, down_out, sems = refs[groups:]
+    others = groups - 1
+    own_ref, early, refs = refs[0], refs[1:groups], refs[groups:]
+    lates, hiddens, refs = refs[:others], refs[others : 2 * others], refs[2 * others :]
+    hidden_hbm, down_hbm, match_out, hidden_out, down_out, wide_ref, sems = refs
     units, share = down_out.shape
     block = units // pieces
-    slots = jnp.concatenate([pay_ref[...] for pay_ref in pays], axis=0)
+    rows, hidden = [own_ref[:, :share]], [own_ref[:, share:]]
+    for early_ref, late_ref, hidden_ref in zip(early, lates, hiddens):
+        wide_ref[:CAP, :] = early_ref[:, :share].astype(jnp.float32)
+        for k in range(1, count):
+            late = late_ref[:, (k - 1) * share : k * share].astype(jnp.float32)
+            wide_ref[k * CAP : (k + 1) * CAP, :] = late
+        rows.append(wide_ref[: count * CAP, :].astype(jnp.bfloat16))
+        hidden.append(hidden_ref[...])
+    rows, hidden = jnp.concatenate(rows, axis=0), jnp.concatenate(hidden, axis=0)
     copies = []
 
     def write(values, destination):
@@ -217,8 +252,7 @@
 
     for p in range(pieces):
         part = slice(p * block, (p + 1) * block)
-        hidden = slots[:, share + p * block : share + (p + 1) * block]
-        down_out[part, :] = dot(hidden, slots[:, :share], ((0,), (0,)))
+        down_out[part, :] = dot(hidden[:, part], rows, ((0,), (0,)))
         part = pl.ds(p * block, block)
         write(down_out.at[part], down_hbm.at[0, part])
     upstream = part_ref[...] + upstream_part(rows_ref, weight_ref, split, weight_ref.shape[1])
@@ -258,7 +292,7 @@
     pieces = units // LANES
 
     ids, match, weight, hidden, *rest = pl.pallas_call(
-        functools.partial(front_kernel, count, pieces),
+        functools.partial(front_kernel, count, groups, pieces),
         out_shape=[
             jax.ShapeDtypeStruct((top, tokens), jnp.int32),
             jax.ShapeDtypeStruct((count * PAD, tokens), jnp.float32),
@@ -266,12 +300,13 @@
             jax.ShapeDtypeStruct((slots, units), jnp.bfloat16),
         ]
         + [
-            jax.ShapeDtypeStruct((CAP, width + LANES + width * (r == JOINT)), jnp.bfloat16)
+            jax.ShapeDtypeStruct((CAP, width + LANES + width * (r not in apart(count))), jnp.bfloat16)
             for r in range(count)
         ]
-        + [jax.ShapeDtypeStruct((CAP, width), jnp.bfloat16)] * (count - 1),
+        + [jax.ShapeDtypeStruct((CAP, width), jnp.bfloat16)] * len(apart(count))
+        + [jax.ShapeDtypeStruct((CAP, share + count * units), jnp.bfloat16)] * (groups - 1),
         in_specs=[HBM] * 5,
-        out_specs=[VMEM] * (3 + 2 * count),
+        out_specs=[VMEM] * (3 + count + len(apart(count)) + groups),
         scratch_shapes=[
             pltpu.VMEM((top, tokens), jnp.bfloat16),
             pltpu.VMEM((tokens, width), jnp.bfloat16),
@@ -283,44 +318,52 @@
         cost_estimate=cost(2 * count * PAD * (tokens + units) * width, 2 * (tokens + units) * width),
         name="front",
     )(*in_hbm(expert_ids.T, gate_values.T, grad_out, saved_hidden, down_weight))
-    sends, products = rest[:count], rest[count:]
+    sends, rest = rest[:count], rest[count:]
+    products, early = rest[: len(apart(count))], rest[len(apart(count)) :]
 
     received = [sends[0]] + [send(sends[r], "expert", r) for r in range(1, count)]
-    theirs = [products[0]] + [send(products[r - 1], "expert", r) for r in range(JOINT + 1, count)]
-
-    rows, gate, *pays = pl.pallas_call(
+    theirs = [products[0]]
+    theirs += [send(x, "expert", r) for r, x in zip(apart(count)[1:], products[1:])]
+    early = [send(x, "dp", r) for r, x in enumerate(early, 1)]
+
+    rows, gate, own, *lates = pl.pallas_call(
         functools.partial(slot_kernel, count, groups),
         out_shape=[
             jax.ShapeDtypeStruct((slots, width), jnp.bfloat16),
             jax.ShapeDtypeStruct((slots, LANES), jnp.float32),
+            jax.ShapeDtypeStruct((slots, share + units), jnp.bfloat16),
         ]
-        + [jax.ShapeDtypeStruct((slots, share + units), jnp.bfloat16)] * groups,
+        + [jax.ShapeDtypeStruct((CAP, (count - 1) * share), jnp.bfloat16)] * (groups - 1),
         in_specs=[VMEM] * (1 + count),
         out_specs=[VMEM] * (2 + groups),
         scratch_shapes=[
             pltpu.VMEM((slots + PAD, width + LANES), jnp.float32),
-            pltpu.VMEM((slots, width), jnp.bfloat16),
+            pltpu.VMEM((count * PAD, width), jnp.float32),
         ],
         compiler_params=PARAMS,
         cost_estimate=cost(4 * slots * width, 8 * slots * width),
         name="slots",
     )(hidden, *received)
 
-    back = pl.pallas_call(
-        functools.partial(back_kernel, count),
-        out_shape=jax.ShapeDtypeStruct((slots, LANES), jnp.float32),
-        in_specs=[VMEM] * (2 * count),
-        out_specs=VMEM,
-        scratch_shapes=[pltpu.VMEM((slots + PAD, LANES), jnp.float32)],
+    back, *hiddens = pl.pallas_call(
+        functools.partial(back_kernel, count, groups),
+        out_shape=[jax.ShapeDtypeStruct((slots, LANES), jnp.float32)]
+        + [jax.ShapeDtypeStruct((slots, units), jnp.bfloat16)] * (groups - 1),
+        in_specs=[VMEM] * (2 * count - 2 + len(apart(count)) + groups),
+        out_specs=[VMEM] * groups,
+        scratch_shapes=[
+            pltpu.VMEM((slots + PAD, LANES), jnp.float32),
+            pltpu.VMEM((slots + PAD, units), jnp.float32),
+        ],
         compiler_params=PARAMS,
         cost_estimate=cost(*AFTER_WAIT),
         name="backs",
-    )(*sends, received[JOINT], *theirs)
-
-    others = [send(pays[r], "dp", r) for r in range(1, groups)]
-    backs = [back] + [send(back, "tensor", r) for r in reversed(range(1, tensors))]
-
-    split = width * 3 // 4
+    )(*sends, *received[1:], *theirs, *early)
+
+    lates = [send(x, "dp", r) for r, x in enumerate(lates, 1)]
+    backs = [back] + [send(back, "tensor", r) for r in range(1, tensors)]
+
+    split = width * 3 // 8
     upstream = pl.pallas_call(
         functools.partial(upstream_kernel, split),
         out_shape=jax.ShapeDtypeStruct((slots, units), jnp.float32),
@@ -338,17 +381,18 @@
             jax.ShapeDtypeStruct((1, units, share), jnp.float32),
             jax.ShapeDtypeStruct(match.shape, jnp.float32),
         ],
-        in_specs=[VMEM] * (5 + groups),
+        in_specs=[VMEM] * (3 + 3 * groups),
         out_specs=[HBM, HBM, VMEM],
         scratch_shapes=[
             pltpu.VMEM((slots, units), jnp.bfloat16),
             pltpu.VMEM((units, share), jnp.float32),
+            pltpu.VMEM((slots + PAD, share), jnp.float32),
             pltpu.SemaphoreType.DMA((pieces + 1,)),
         ],
         compiler_params=PARAMS,
         cost_estimate=cost(2 * slots * units * share, 4 * units * share),
         name="down",
-    )(upstream, rows, gate, weight, match, pays[0], *others)
+    )(upstream, rows, gate, weight, match, own, *early, *lates, *hiddens)
 
     gate_grad = pl.pallas_call(
         functools.partial(gate_kernel, count),

time: 20.9 us -> 20.8 us (level)
  waiting for transfers between devices: 0.41 us -> 1.05 us
  starting transfers between devices: 13.5 us -> 12.9 us
  Pallas kernels: 6.18 us -> 5.95 us
    ppermute x9, waiting for transfers between devices: 0.41 us -> 1.05 us  [send(): lax.ppermute(value, axis, [(i, give(i, step, size)) for i in range(size)])]
    ppermute x9, starting transfers between devices: 13.5 us -> 12.9 us  [send(): lax.ppermute(value, axis, [(i, give(i, step, size)) for i in range(size)])]
    pallas_call x1, Pallas kernels: 0.71 us -> 0.42 us  [on_device(): pl.pallas_call(functools.partial(upstream_kernel, split), out_shape=jax.S...]
  transfers between devices with their start and end apart: 9 -> 9, of which waited for: 2 -> 2; matrix products, arithmetic and copies ran while one was open for 0% -> 0% of each run, Pallas kernels for 14% -> 13%
where the time goes in v20:
time: 20.8 us; the launch traced here: 20.6 us
  starting transfers between devices  12.9 us (62%)
  Pallas kernels  5.95 us (29%)
  waiting for transfers between devices  1.05 us (5%)
  between operations  0.69 us (3%)
    ppermute x9, starting transfers between devices, send(): lax.ppermute(value, axis, [(i, give(i, step, size)) for i in range(size)])  12.9 us
    pallas_call x1, Pallas kernels, on_device(): pl.pallas_call(functools.partial(front_kernel, count, groups, pieces), ou...  2.58 us
    pallas_call x1, Pallas kernels, on_device(): pl.pallas_call(functools.partial(down_kernel, count, groups, pieces, spli...  2.05 us
    ppermute x9, waiting for transfers between devices, send(): lax.ppermute(value, axis, [(i, give(i, step, size)) for i in range(size)])  1.05 us
    pallas_call x1, Pallas kernels, on_device(): pl.pallas_call(functools.partial(gate_kernel, count), out_shape=jax.Shape...  0.61 us
    pallas_call x1, Pallas kernels, on_device(): pl.pallas_call(functools.partial(upstream_kernel, split), out_shape=jax.S...  0.42 us
  transfers between devices with their start and end apart: 9, of which 2 were waited for; matrix products, arithmetic and copies ran while one was open for 0% of the time, Pallas kernels for 13%

profile of v20, /device:TPU:0, one launch (start us, length us, event | category | flops | bytes accessed | tf_op | source)
XLA Modules:
  0.0 20.6 jit_solution(1743306244703342885)
XLA Ops:
  0.6 2.6 %front.1 = (s32[8,128]{1,0:T(8,128)S(1)}, f32[32,128]{1,0:T(8,128)S(1)}, bf16[384,4096]{1,0:T(8,128)(2,1)S(1)}, bf16[16,384]{1,0:T(8,128)(2,1)S(1)}, bf16[4,4224...) custom-call(s32[8,128]{1,0:T(8,128)} %bitcast.4, ...), custom_call_target="tpu_custom_call" | custom-call | flops 134217728 | bytes 4194304 | tf_op jit(solution)/shard_map/front/pallas_call | solution.py:294
  3.2 5.1 %collective-permute-start = (bf16[4,8320]{1,0:T(4,128)(2,1)S(1)}, bf16[4,8320]{1,0:T(4,128)(2,1)S(1)}, u32[]{:S(2)}, u32[]{:S(2)}) collective-permute-start(bf16[4,8320]{1,0:T(4,128)(2,1)S(1)} %get-tuple-element.26.refs_1_), channel_id=1, source_target_pairs={{0,12},{4,8},{8,4},{12,0},{1,13},{5,9},{9,5},{13,1},{2,14},{6,10},... | collective-permute-start | bytes 199688 | tf_op jit(solution)/shard_map/ppermute | solution.py:60
  8.3 0.0 collective-permute-start.2
  8.3 0.6 %collective-permute-start.1 = (bf16[4,4224]{1,0:T(4,128)(2,1)S(1)}, bf16[4,4224]{1,0:T(4,128)(2,1)S(1)}, u32[]{:S(2)}, u32[]{:S(2)}) collective-permute-start(bf16[4,4224]{1,0:T(4,128)(2,1)S(1)} %get-tuple-element.27.refs_2_), channel_id=1, source_target_pairs={{0,8},{4,12},{8,0},{12,4},{1,9},{5,13},{9,1},{13,5},{2,10},{6,14},... | collective-permute-start | bytes 101384 | tf_op jit(solution)/shard_map/ppermute | solution.py:60
  9.0 2.3 %collective-permute-start.5 = (bf16[4,4096]{1,0:T(4,128)(2,1)S(1)}, bf16[4,4096]{1,0:T(4,128)(2,1)S(1)}, u32[]{:S(2)}, u32[]{:S(2)}) collective-permute-start(bf16[4,4096]{1,0:T(4,128)(2,1)S(1)} %get-tuple-element.37), channel_id=1, source_target_pairs={{0,8},{4,12},{8,0},{12,4},{1,9},{5,13},{9,1},{13,5},{2,10},{6,14},... | collective-permute-start | bytes 98312 | tf_op jit(solution)/shard_map/ppermute | solution.py:60
  11.3 1.5 %collective-permute-start.3 = (bf16[4,3584]{1,0:T(4,128)(2,1)S(1)}, bf16[4,3584]{1,0:T(4,128)(2,1)S(1)}, u32[]{:S(2)}, u32[]{:S(2)}) collective-permute-start(bf16[4,3584]{1,0:T(4,128)(2,1)S(1)} %get-tuple-element.34), channel_id=1, source_target_pairs={{0,16},{16,0},{1,17},{17,1},{2,18},{18,2},{3,19},{19,3},{4,20},{20... | collective-permute-start | bytes 86024 | tf_op jit(solution)/shard_map/ppermute | solution.py:60
  12.7 0.9 %collective-permute-done.1.refs_2_.refs_5_ = bf16[4,4224]{1,0:T(4,128)(2,1)S(1)} collective-permute-done((bf16[4,4224]{1,0:T(4,128)(2,1)S(1)}, bf16[4,4224]{1,0:T(4,128)(2,1)S(1)}, u32[]{:S(2)}, u32[]{:S(2)}) %collective-permute-start.1) | collective-permute-done | bytes 33824 | tf_op jit(solution)/shard_map/ppermute | solution.py:60
  13.6 0.0 collective-permute-done.refs_1_.refs_4_
  13.6 0.0 collective-permute-done.2.refs_3_.refs_6_
  13.6 0.1 slots.1
  13.8 1.6 %collective-permute-start.4 = (bf16[4,6144]{1,0:T(4,128)(2,1)S(1)}, bf16[4,6144]{1,0:T(4,128)(2,1)S(1)}, u32[]{:S(2)}, u32[]{:S(2)}) collective-permute-start(bf16[4,6144]{1,0:T(4,128)(2,1)S(1)} %get-tuple-element.35), channel_id=1, source_target_pairs={{0,16},{16,0},{1,17},{17,1},{2,18},{18,2},{3,19},{19,3},{4,20},{20... | collective-permute-start | bytes 147464 | tf_op jit(solution)/shard_map/ppermute | solution.py:60
  15.3 0.0 collective-permute-done.3.refs_9_.refs_1_
  15.3 0.0 collective-permute-done.5.refs_8_
  15.3 0.2 backs.1
  15.5 0.0 collective-permute-start.6
  15.5 1.6 %collective-permute-start.7 = (f32[16,128]{1,0:T(8,128)S(1)}, f32[16,128]{1,0:T(8,128)S(1)}, u32[]{:S(2)}, u32[]{:S(2)}) collective-permute-start(f32[16,128]{1,0:T(8,128)S(1)} %get-tuple-element.40.refs_0_), channel_id=1, source_target_pairs={{0,2},{1,3},{2,0},{3,1},{4,6},{5,7},{6,4},{7,5},{8,10},{9,11},{10,... | collective-permute-start | bytes 24584 | tf_op jit(solution)/shard_map/ppermute | solution.py:60
  17.1 0.3 %collective-permute-start.8 = (f32[16,128]{1,0:T(8,128)S(1)}, f32[16,128]{1,0:T(8,128)S(1)}, u32[]{:S(2)}, u32[]{:S(2)}) collective-permute-start(f32[16,128]{1,0:T(8,128)S(1)} %get-tuple-element.40.refs_0_), channel_id=1, source_target_pairs={{0,1},{1,0},{2,3},{3,2},{4,5},{5,4},{6,7},{7,6},{8,9},{9,8},{10,11... | collective-permute-start | bytes 24584 | tf_op jit(solution)/shard_map/ppermute | solution.py:60
  17.4 0.4 %upstream.1.part_ref = f32[16,384]{1,0:T(8,128)S(1)} custom-call(bf16[16,4096]{1,0:T(8,128)(2,1)S(1)} %get-tuple-element.29.rows_ref, bf16[384,4096]{1,0:T(8,128)(2,1)S(1)} %get-tuple-element.30.weight_ref), custom_call_target="tpu_custom_call" | custom-call | flops 18874368 | bytes 1179648 | tf_op jit(solution)/shard_map/upstream/pallas_call | solution.py:367
  17.8 0.1 collective-permute-done.4.refs_2_
  17.9 2.1 %down.1 = (bf16[1,1,16,384]{3,2,1,0:T(8,128)(2,1)}, f32[1,384,2048]{2,1,0:T(8,128)}, f32[32,128]{1,0:T(8,128)S(1)}) custom-call(f32[16,384]{1,0:T(8,128)S(1)} %upstream.1.part_ref, bf16[16,4096]{1,0:T(8,128)(2,1)S(1)} %get-tuple-element.29.rows_ref, f32[16,128]{1,0:T(8,128)S(1)} %get-tuple-element.31.gate_ref, ...), custom_call_target="tpu_custom_call" | custom-call | flops 25165824 | bytes 3145728 | tf_op jit(solution)/shard_map/down/pallas_call | solution.py:377
  20.0 0.0 collective-permute-done.6.refs_1_
  20.0 0.0 collective-permute-done.7.refs_2_
  20.0 0.0 collective-permute-done.8.refs_3_
  20.0 0.6 %gates.1 = f32[8,128]{1,0:T(8,128)} custom-call(s32[8,128]{1,0:T(8,128)S(1)} %get-tuple-element.23.ids_ref, f32[32,128]{1,0:T(8,128)S(1)} %get-tuple-element.39.match_ref, f32[16,128]{1,0:T(8,128)S(1)} %get-tuple-element.40.refs_0_, f32[16,128]{1,0:T(8,128)S(1)} %collective-permute-done.6.refs_1_, f32[16,128]{1,0:T(8,128)S(1)} %collective-permute-done.7.refs_2_, ...), custom_call_target="tpu_custom_call" | custom-call | flops 2048 | bytes 8192 | tf_op jit(solution)/shard_map/gates/pallas_call | solution.py:397
Async XLA Ops:
  3.2 10.4 %collective-permute-start = (bf16[4,8320]{1,0:T(4,128)(2,1)S(1)}, bf16[4,8320]{1,0:T(4,128)(2,1)S(1)}, u32[]{:S(2)}, u32[]{:S(2)}) collective-permute-start(bf16[4,8320]{1,0:T(4,128)(2,1)S(1)} %get-tuple-element.26.refs_1_), channel_id=1, source_target_pairs={{0,12},{4,8},{8,4},{12,0},{1,13},{5,9},{9,5},{13,1},{2,14},{6,10},... | collective-permute-start | bytes 199688 | tf_op jit(solution)/shard_map/ppermute | solution.py:60
  8.3 5.3 %collective-permute-start.2 = (bf16[4,8320]{1,0:T(4,128)(2,1)S(1)}, bf16[4,8320]{1,0:T(4,128)(2,1)S(1)}, u32[]{:S(2)}, u32[]{:S(2)}) collective-permute-start(bf16[4,8320]{1,0:T(4,128)(2,1)S(1)} %get-tuple-element.28.refs_3_), channel_id=1, source_target_pairs={{0,4},{4,0},{8,12},{12,8},{1,5},{5,1},{9,13},{13,9},{2,6},{6,2},{1... | collective-permute-start | bytes 199688 | tf_op jit(solution)/shard_map/ppermute | solution.py:60
  8.3 5.3 %collective-permute-start.1 = (bf16[4,4224]{1,0:T(4,128)(2,1)S(1)}, bf16[4,4224]{1,0:T(4,128)(2,1)S(1)}, u32[]{:S(2)}, u32[]{:S(2)}) collective-permute-start(bf16[4,4224]{1,0:T(4,128)(2,1)S(1)} %get-tuple-element.27.refs_2_), channel_id=1, source_target_pairs={{0,8},{4,12},{8,0},{12,4},{1,9},{5,13},{9,1},{13,5},{2,10},{6,14},... | collective-permute-start | bytes 101384 | tf_op jit(solution)/shard_map/ppermute | solution.py:60
  9.0 6.4 %collective-permute-start.5 = (bf16[4,4096]{1,0:T(4,128)(2,1)S(1)}, bf16[4,4096]{1,0:T(4,128)(2,1)S(1)}, u32[]{:S(2)}, u32[]{:S(2)}) collective-permute-start(bf16[4,4096]{1,0:T(4,128)(2,1)S(1)} %get-tuple-element.37), channel_id=1, source_target_pairs={{0,8},{4,12},{8,0},{12,4},{1,9},{5,13},{9,1},{13,5},{2,10},{6,14},... | collective-permute-start | bytes 98312 | tf_op jit(solution)/shard_map/ppermute | solution.py:60
  11.3 4.1 %collective-permute-start.3 = (bf16[4,3584]{1,0:T(4,128)(2,1)S(1)}, bf16[4,3584]{1,0:T(4,128)(2,1)S(1)}, u32[]{:S(2)}, u32[]{:S(2)}) collective-permute-start(bf16[4,3584]{1,0:T(4,128)(2,1)S(1)} %get-tuple-element.34), channel_id=1, source_target_pairs={{0,16},{16,0},{1,17},{17,1},{2,18},{18,2},{3,19},{19,3},{4,20},{20... | collective-permute-start | bytes 86024 | tf_op jit(solution)/shard_map/ppermute | solution.py:60
  13.8 4.2 %collective-permute-start.4 = (bf16[4,6144]{1,0:T(4,128)(2,1)S(1)}, bf16[4,6144]{1,0:T(4,128)(2,1)S(1)}, u32[]{:S(2)}, u32[]{:S(2)}) collective-permute-start(bf16[4,6144]{1,0:T(4,128)(2,1)S(1)} %get-tuple-element.35), channel_id=1, source_target_pairs={{0,16},{16,0},{1,17},{17,1},{2,18},{18,2},{3,19},{19,3},{4,20},{20... | collective-permute-start | bytes 147464 | tf_op jit(solution)/shard_map/ppermute | solution.py:60
  15.5 4.5 %collective-permute-start.6 = (f32[16,128]{1,0:T(8,128)S(1)}, f32[16,128]{1,0:T(8,128)S(1)}, u32[]{:S(2)}, u32[]{:S(2)}) collective-permute-start(f32[16,128]{1,0:T(8,128)S(1)} %get-tuple-element.40.refs_0_), channel_id=1, source_target_pairs={{0,3},{1,2},{2,1},{3,0},{4,7},{5,6},{6,5},{7,4},{8,11},{9,10},{10,... | collective-permute-start | bytes 24584 | tf_op jit(solution)/shard_map/ppermute | solution.py:60
  15.5 4.5 %collective-permute-start.7 = (f32[16,128]{1,0:T(8,128)S(1)}, f32[16,128]{1,0:T(8,128)S(1)}, u32[]{:S(2)}, u32[]{:S(2)}) collective-permute-start(f32[16,128]{1,0:T(8,128)S(1)} %get-tuple-element.40.refs_0_), channel_id=1, source_target_pairs={{0,2},{1,3},{2,0},{3,1},{4,6},{5,7},{6,4},{7,5},{8,10},{9,11},{10,... | collective-permute-start | bytes 24584 | tf_op jit(solution)/shard_map/ppermute | solution.py:60
  17.1 2.9 %collective-permute-start.8 = (f32[16,128]{1,0:T(8,128)S(1)}, f32[16,128]{1,0:T(8,128)S(1)}, u32[]{:S(2)}, u32[]{:S(2)}) collective-permute-start(f32[16,128]{1,0:T(8,128)S(1)} %get-tuple-element.40.refs_0_), channel_id=1, source_target_pairs={{0,1},{1,0},{2,3},{3,2},{4,5},{5,4},{6,7},{7,6},{8,9},{9,8},{10,11... | collective-permute-start | bytes 24584 | tf_op jit(solution)/shard_map/ppermute | solution.py:60

commit v21 on v20

--- a/solution.py
+++ b/solution.py
@@ -9,7 +9,7 @@
 
 CAP = 4
 LANES = 128
-AFTER_WAIT = (10**9, 10**7)
+AFTER_WAIT = (3 * 10**8, 3 * 10**6)
 WIDE = 1024
 PAD = 8
 VMEM = pl.BlockSpec(memory_space=pltpu.VMEM)
@@ -60,13 +60,12 @@
     return lax.ppermute(value, axis, [(i, give(i, step, size)) for i in range(size)])
 
 
-def front_kernel(count, groups, pieces, *refs):
+def front_kernel(count, pieces, *refs):
     ids_hbm, gates_hbm, grad_hbm, hidden_hbm, weight_hbm = refs[:5]
     ids_ref, match_ref, weight_ref, hidden_ref = refs[5:9]
     sends = refs[9 : 9 + count]
     products = dict(zip(apart(count), refs[9 + count :]))
-    early = refs[-4 - groups : -5]
-    gates_ref, grad_ref, saved_ref, total_ref, sems = refs[-5:]
+    spread_ref, gates_ref, grad_ref, saved_ref, total_ref, sems = refs[-6:]
     units, width = weight_ref.shape
     top, tokens = ids_ref.shape
     pairs = [(ids_hbm, ids_ref), (gates_hbm, gates_ref), (hidden_hbm.at[0, 0], saved_ref)]
@@ -127,16 +126,9 @@
         picked = dot(match, grad_ref[:, part], ((1,), (0,)))
         for r in range(count):
             sends[r][:, part] = picked[r * PAD : r * PAD + CAP].astype(jnp.bfloat16)
-        total_ref[:PAD, part] = picked[:PAD]
-    share = width // groups
-    group = lax.axis_index("dp")
-    for r, early_ref in enumerate(early, 1):
-        begin = pl.multiple_of(target(group, r, groups) * share, share)
-        weighted = slot_gate[:CAP] * total_ref[:CAP, pl.ds(begin, share)]
-        early_ref[:, :share] = weighted.astype(jnp.bfloat16)
-        for k in range(count):
-            part = slice(share + k * units, share + (k + 1) * units)
-            early_ref[:, part] = spread[k * PAD : k * PAD + CAP].astype(jnp.bfloat16)
+    for k in range(count):
+        hidden_of = spread[k * PAD : k * PAD + CAP].astype(jnp.bfloat16)
+        spread_ref[:, k * units : (k + 1) * units] = hidden_of
     block = units // pieces
     for p in range(pieces):
         for copy in copies[5 + 2 * p : 7 + 2 * p]:
@@ -168,6 +160,22 @@
     return ((saved == block * CAP + place) & (place < CAP)).astype(jnp.bfloat16)
 
 
+def early_kernel(groups, spread_ref, *refs):
+    received, early, row_ref = refs[: -groups], refs[-groups:-1], refs[-1]
+    width = row_ref.shape[1]
+    share = width // groups
+    me = lax.axis_index("dp")
+    for n, ref in enumerate(received):
+        row = ref[:, : width + LANES].astype(jnp.float32)
+        row_ref[:CAP, :] = row[:, width : width + 1] * row[:, :width]
+        for r, early_ref in enumerate(early, 1):
+            begin = pl.multiple_of(target(me, r, groups) * share, share)
+            part = row_ref[:CAP, pl.ds(begin, share)].astype(jnp.bfloat16)
+            early_ref[:, n * share : (n + 1) * share] = part
+    for early_ref in early:
+        early_ref[:, len(received) * share :] = spread_ref[...]
+
+
 def slot_kernel(count, groups, hidden_ref, *refs):
     received = refs[:count]
     rows_ref, gate_ref, own_ref = refs[count : count + 3]
@@ -187,22 +195,19 @@
     me = lax.axis_index("dp")
     for r, late_ref in enumerate(lates, 1):
         begin = pl.multiple_of(target(me, r, groups) * share, share)
-        for k in range(1, count):
+        for n, k in enumerate(apart(count)[1:]):
             late = spread_ref[k * PAD : k * PAD + CAP, pl.ds(begin, share)]
-            late_ref[:, (k - 1) * share : k * share] = late.astype(jnp.bfloat16)
+            late_ref[:, n * share : (n + 1) * share] = late.astype(jnp.bfloat16)
     weighted = gate[:, :1] * wide_ref[:slots, pl.ds(pl.multiple_of(me * share, share), share)]
     own_ref[:, :share] = weighted.astype(jnp.bfloat16)
     own_ref[:, share:] = hidden_ref[...]
 
 
-def back_kernel(count, groups, *refs):
+def back_kernel(count, *refs):
     sent, refs = refs[:count], refs[count:]
     received, refs = dict(enumerate(refs[: count - 1], 1)), refs[count - 1 :]
     received.update(zip(apart(count), refs))
-    refs = refs[len(apart(count)) :]
-    early, refs = refs[: groups - 1], refs[groups - 1 :]
-    out_ref, hiddens = refs[0], refs[1:groups]
-    back_ref, units_ref = refs[groups:]
+    out_ref, back_ref = refs[-2:]
     width = received[0].shape[1]
     for r in range(count):
         ref = received[reply(r, count)]
@@ -210,38 +215,45 @@
         mine = sent[r][:, :width].astype(jnp.float32)
         back = jnp.sum(mine * theirs, axis=1, keepdims=True)
         back_ref[r * CAP : (r + 1) * CAP, :] = jnp.broadcast_to(back, (CAP, LANES))
-    slots, units = count * CAP, units_ref.shape[1]
-    out_ref[...] = back_ref[:slots, :]
-    for early_ref, hidden_ref in zip(early, hiddens):
-        share = early_ref.shape[1] - count * units
-        for k in range(count):
-            part = early_ref[:, share + k * units : share + (k + 1) * units]
-            units_ref[k * CAP : (k + 1) * CAP, :] = part.astype(jnp.float32)
-        hidden_ref[...] = units_ref[:slots, :].astype(jnp.bfloat16)
+    out_ref[...] = back_ref[: count * CAP, :]
 
 
 def upstream_part(rows_ref, weight_ref, begin, end):
     return dot(rows_ref[:, begin:end], weight_ref[:, begin:end], ((1,), (1,)))
 
 
-def upstream_kernel(split, rows_ref, weight_ref, out_ref):
+def upstream_kernel(count, split, rows_ref, weight_ref, *refs):
+    others = (len(refs) - 3) // 3
+    early, out_ref, refs = refs[:others], refs[others], refs[others + 1 :]
+    wides, hiddens, (units_ref, row_ref) = refs[:others], refs[others : 2 * others], refs[2 * others :]
+    units, share = units_ref.shape[1], row_ref.shape[1]
+    first = [0, 1, count - 1]
+    for early_ref, wide_ref, hidden_ref in zip(early, wides, hiddens):
+        for n, k in enumerate(first):
+            part = early_ref[:, n * share : (n + 1) * share]
+            wide_ref[k * CAP : (k + 1) * CAP, :] = part.astype(jnp.float32)
+        begin = len(first) * share
+        for k in range(count):
+            part = early_ref[:, begin + k * units : begin + (k + 1) * units]
+            units_ref[k * CAP : (k + 1) * CAP, :] = part.astype(jnp.float32)
+        hidden_ref[...] = units_ref[: count * CAP, :].astype(jnp.bfloat16)
     out_ref[...] = upstream_part(rows_ref, weight_ref, 0, split)
 
 
 def down_kernel(count, groups, pieces, split, part_ref, rows_ref, gate_ref, weight_ref, match_ref, *refs):
     others = groups - 1
-    own_ref, early, refs = refs[0], refs[1:groups], refs[groups:]
+    own_ref, wides, refs = refs[0], refs[1:groups], refs[groups:]
     lates, hiddens, refs = refs[:others], refs[others : 2 * others], refs[2 * others :]
-    hidden_hbm, down_hbm, match_out, hidden_out, down_out, wide_ref, sems = refs
+    hidden_hbm, down_hbm, match_out, hidden_out, down_out, all_ref, sems = refs
     units, share = down_out.shape
     block = units // pieces
     rows, hidden = [own_ref[:, :share]], [own_ref[:, share:]]
-    for early_ref, late_ref, hidden_ref in zip(early, lates, hiddens):
-        wide_ref[:CAP, :] = early_ref[:, :share].astype(jnp.float32)
-        for k in range(1, count):
-            late = late_ref[:, (k - 1) * share : k * share].astype(jnp.float32)
-            wide_ref[k * CAP : (k + 1) * CAP, :] = late
-        rows.append(wide_ref[: count * CAP, :].astype(jnp.bfloat16))
+    for wide_ref, late_ref, hidden_ref in zip(wides, lates, hiddens):
+        all_ref[...] = wide_ref[...]
+        for n, k in enumerate(apart(count)[1:]):
+            late = late_ref[:, n * share : (n + 1) * share].astype(jnp.float32)
+            all_ref[k * CAP : (k + 1) * CAP, :] = late
+        rows.append(all_ref[: count * CAP, :].astype(jnp.bfloat16))
         hidden.append(hidden_ref[...])
     rows, hidden = jnp.concatenate(rows, axis=0), jnp.concatenate(hidden, axis=0)
     copies = []
@@ -292,7 +304,7 @@
     pieces = units // LANES
 
     ids, match, weight, hidden, *rest = pl.pallas_call(
-        functools.partial(front_kernel, count, groups, pieces),
+        functools.partial(front_kernel, count, pieces),
         out_shape=[
             jax.ShapeDtypeStruct((top, tokens), jnp.int32),
             jax.ShapeDtypeStruct((count * PAD, tokens), jnp.float32),
@@ -304,9 +316,9 @@
             for r in range(count)
         ]
         + [jax.ShapeDtypeStruct((CAP, width), jnp.bfloat16)] * len(apart(count))
-        + [jax.ShapeDtypeStruct((CAP, share + count * units), jnp.bfloat16)] * (groups - 1),
+        + [jax.ShapeDtypeStruct((CAP, count * units), jnp.bfloat16)],
         in_specs=[HBM] * 5,
-        out_specs=[VMEM] * (3 + count + len(apart(count)) + groups),
+        out_specs=[VMEM] * (5 + count + len(apart(count))),
         scratch_shapes=[
             pltpu.VMEM((top, tokens), jnp.bfloat16),
             pltpu.VMEM((tokens, width), jnp.bfloat16),
@@ -319,11 +331,23 @@
         name="front",
     )(*in_hbm(expert_ids.T, gate_values.T, grad_out, saved_hidden, down_weight))
     sends, rest = rest[:count], rest[count:]
-    products, early = rest[: len(apart(count))], rest[len(apart(count)) :]
+    products, spread = rest[:-1], rest[-1]
 
     received = [sends[0]] + [send(sends[r], "expert", r) for r in range(1, count)]
     theirs = [products[0]]
     theirs += [send(x, "expert", r) for r, x in zip(apart(count)[1:], products[1:])]
+    first, middle = [0, 1, count - 1], apart(count)[1:]
+    early = pl.pallas_call(
+        functools.partial(early_kernel, groups),
+        out_shape=[jax.ShapeDtypeStruct((CAP, len(first) * share + count * units), jnp.bfloat16)]
+        * (groups - 1),
+        in_specs=[VMEM] * (1 + len(first)),
+        out_specs=[VMEM] * (groups - 1),
+        scratch_shapes=[pltpu.VMEM((PAD, width), jnp.float32)],
+        compiler_params=PARAMS,
+        cost_estimate=cost(len(first) * CAP * width, 4 * len(first) * CAP * width),
+        name="early",
+    )(spread, *[received[r] for r in first])
     early = [send(x, "dp", r) for r, x in enumerate(early, 1)]
 
     rows, gate, own, *lates = pl.pallas_call(
@@ -333,7 +357,7 @@
             jax.ShapeDtypeStruct((slots, LANES), jnp.float32),
             jax.ShapeDtypeStruct((slots, share + units), jnp.bfloat16),
         ]
-        + [jax.ShapeDtypeStruct((CAP, (count - 1) * share), jnp.bfloat16)] * (groups - 1),
+        + [jax.ShapeDtypeStruct((CAP, len(middle) * share), jnp.bfloat16)] * (groups - 1),
         in_specs=[VMEM] * (1 + count),
         out_specs=[VMEM] * (2 + groups),
         scratch_shapes=[
@@ -345,34 +369,37 @@
         name="slots",
     )(hidden, *received)
 
-    back, *hiddens = pl.pallas_call(
-        functools.partial(back_kernel, count, groups),
-        out_shape=[jax.ShapeDtypeStruct((slots, LANES), jnp.float32)]
-        + [jax.ShapeDtypeStruct((slots, units), jnp.bfloat16)] * (groups - 1),
-        in_specs=[VMEM] * (2 * count - 2 + len(apart(count)) + groups),
-        out_specs=[VMEM] * groups,
-        scratch_shapes=[
-            pltpu.VMEM((slots + PAD, LANES), jnp.float32),
-            pltpu.VMEM((slots + PAD, units), jnp.float32),
-        ],
+    back = pl.pallas_call(
+        functools.partial(back_kernel, count),
+        out_shape=jax.ShapeDtypeStruct((slots, LANES), jnp.float32),
+        in_specs=[VMEM] * (2 * count - 1 + len(apart(count))),
+        out_specs=VMEM,
+        scratch_shapes=[pltpu.VMEM((slots + PAD, LANES), jnp.float32)],
         compiler_params=PARAMS,
         cost_estimate=cost(*AFTER_WAIT),
         name="backs",
-    )(*sends, *received[1:], *theirs, *early)
+    )(*sends, *received[1:], *theirs)
 
     lates = [send(x, "dp", r) for r, x in enumerate(lates, 1)]
-    backs = [back] + [send(back, "tensor", r) for r in range(1, tensors)]
-
-    split = width * 3 // 8
-    upstream = pl.pallas_call(
-        functools.partial(upstream_kernel, split),
-        out_shape=jax.ShapeDtypeStruct((slots, units), jnp.float32),
-        in_specs=[VMEM] * 2,
-        out_specs=VMEM,
+    backs = [back] + [send(back, "tensor", r) for r in reversed(range(1, tensors))]
+
+    split = width // 8
+    upstream, *rest = pl.pallas_call(
+        functools.partial(upstream_kernel, count, split),
+        out_shape=[jax.ShapeDtypeStruct((slots, units), jnp.float32)]
+        + [jax.ShapeDtypeStruct((slots + PAD, share), jnp.float32)] * (groups - 1)
+        + [jax.ShapeDtypeStruct((slots, units), jnp.bfloat16)] * (groups - 1),
+        in_specs=[VMEM] * (1 + groups),
+        out_specs=[VMEM] * (2 * groups - 1),
+        scratch_shapes=[
+            pltpu.VMEM((slots + PAD, units), jnp.float32),
+            pltpu.VMEM((PAD, share), jnp.float32),
+        ],
         compiler_params=PARAMS,
         cost_estimate=cost(2 * slots * units * split, 2 * units * split),
         name="upstream",
-    )(rows, weight)
+    )(rows, weight, *early)
+    wides, hiddens = rest[: groups - 1], rest[groups - 1 :]
 
     hidden_grad, down_grad, match = pl.pallas_call(
         functools.partial(down_kernel, count, groups, pieces, split),
@@ -392,7 +419,7 @@
         compiler_params=PARAMS,
         cost_estimate=cost(2 * slots * units * share, 4 * units * share),
         name="down",
-    )(upstream, rows, gate, weight, match, own, *early, *lates, *hiddens)
+    )(upstream, rows, gate, weight, match, own, *wides, *lates, *hiddens)
 
     gate_grad = pl.pallas_call(
         functools.partial(gate_kernel, count),

time: 20.8 us -> 21.8 us (1.048)
  waiting for transfers between devices: 1.05 us -> 2.85 us
  starting transfers between devices: 12.9 us -> 12.1 us
    ppermute x9, waiting for transfers between devices: 1.05 us -> 2.85 us  [send(): lax.ppermute(value, axis, [(i, give(i, step, size)) for i in range(size)])]
    ppermute x9, starting transfers between devices: 12.9 us -> 12.1 us  [send(): lax.ppermute(value, axis, [(i, give(i, step, size)) for i in range(size)])]
    pallas_call x3 -> x4, Pallas kernels: 3.16 us -> 3.09 us  [the longest x1 2.57 us: on_device(): pl.pallas_call(functools.partial(front_kernel, count, pieces), out_shape=...]
  transfers between devices with their start and end apart: 9 -> 9, of which waited for: 2 -> 3; matrix products, arithmetic and copies ran while one was open for 0% -> 0% of each run, Pallas kernels for 13% -> 13%
where the time goes in v21:
time: 21.8 us; the launch traced here: 21.6 us
  starting transfers between devices  12.1 us (56%)
  Pallas kernels  5.97 us (27%)
  waiting for transfers between devices  2.85 us (13%)
  between operations  0.69 us (3%)
    ppermute x9, starting transfers between devices, send(): lax.ppermute(value, axis, [(i, give(i, step, size)) for i in range(size)])  12.1 us
    ppermute x9, waiting for transfers between devices, send(): lax.ppermute(value, axis, [(i, give(i, step, size)) for i in range(size)])  2.85 us
    pallas_call x1, Pallas kernels, on_device(): pl.pallas_call(functools.partial(front_kernel, count, pieces), out_shape=...  2.57 us
    pallas_call x1, Pallas kernels, on_device(): pl.pallas_call(functools.partial(down_kernel, count, groups, pieces, spli...  2.15 us
    pallas_call x1, Pallas kernels, on_device(): pl.pallas_call(functools.partial(gate_kernel, count), out_shape=jax.Shape...  0.61 us
  transfers between devices with their start and end apart: 9, of which 3 were waited for; matrix products, arithmetic and copies ran while one was open for 0% of the time, Pallas kernels for 13%

profile of v21, /device:TPU:0, one launch (start us, length us, event | category | flops | bytes accessed | tf_op | source)
XLA Modules:
  0.0 21.6 jit_solution(456693980691199650)
XLA Ops:
  0.6 2.6 %front.1 = (s32[8,128]{1,0:T(8,128)S(1)}, f32[32,128]{1,0:T(8,128)S(1)}, bf16[384,4096]{1,0:T(8,128)(2,1)S(1)}, bf16[16,384]{1,0:T(8,128)(2,1)S(1)}, bf16[4,4224...) custom-call(s32[8,128]{1,0:T(8,128)} %bitcast.4, ...), custom_call_target="tpu_custom_call" | custom-call | flops 134217728 | bytes 4194304 | tf_op jit(solution)/shard_map/front/pallas_call | solution.py:306
  3.2 5.1 %collective-permute-start = (bf16[4,8320]{1,0:T(4,128)(2,1)S(1)}, bf16[4,8320]{1,0:T(4,128)(2,1)S(1)}, u32[]{:S(2)}, u32[]{:S(2)}) collective-permute-start(bf16[4,8320]{1,0:T(4,128)(2,1)S(1)} %get-tuple-element.27.refs_1_), channel_id=1, source_target_pairs={{0,12},{4,8},{8,4},{12,0},{1,13},{5,9},{9,5},{13,1},{2,14},{6,10},... | collective-permute-start | bytes 199688 | tf_op jit(solution)/shard_map/ppermute | solution.py:60
  8.3 0.0 collective-permute-start.2
  8.3 0.6 %collective-permute-start.1 = (bf16[4,4224]{1,0:T(4,128)(2,1)S(1)}, bf16[4,4224]{1,0:T(4,128)(2,1)S(1)}, u32[]{:S(2)}, u32[]{:S(2)}) collective-permute-start(bf16[4,4224]{1,0:T(4,128)(2,1)S(1)} %get-tuple-element.28.refs_2_), channel_id=1, source_target_pairs={{0,8},{4,12},{8,0},{12,4},{1,9},{5,13},{9,1},{13,5},{2,10},{6,14},... | collective-permute-start | bytes 101384 | tf_op jit(solution)/shard_map/ppermute | solution.py:60
  9.0 2.3 %collective-permute-start.5 = (bf16[4,4096]{1,0:T(4,128)(2,1)S(1)}, bf16[4,4096]{1,0:T(4,128)(2,1)S(1)}, u32[]{:S(2)}, u32[]{:S(2)}) collective-permute-start(bf16[4,4096]{1,0:T(4,128)(2,1)S(1)} %get-tuple-element.42), channel_id=1, source_target_pairs={{0,8},{4,12},{8,0},{12,4},{1,9},{5,13},{9,1},{13,5},{2,10},{6,14},... | collective-permute-start | bytes 98312 | tf_op jit(solution)/shard_map/ppermute | solution.py:60
  11.3 0.0 collective-permute-done.refs_1_.refs_4_
  11.3 1.8 %collective-permute-done.2.refs_3_.refs_2_.refs_6_ = bf16[4,8320]{1,0:T(4,128)(2,1)S(1)} collective-permute-done((bf16[4,8320]{1,0:T(4,128)(2,1)S(1)}, bf16[4,8320]{1,0:T(4,128)(2,1)S(1)}, u32[]{:S(2)}, u32[]{:S(2)}) %collective-permute-start.2) | collective-permute-done | bytes 66592 | tf_op jit(solution)/shard_map/ppermute | solution.py:60
  13.0 0.1 early.1
  13.2 1.7 %collective-permute-start.3 = (bf16[4,7680]{1,0:T(4,128)(2,1)S(1)}, bf16[4,7680]{1,0:T(4,128)(2,1)S(1)}, u32[]{:S(2)}, u32[]{:S(2)}) collective-permute-start(bf16[4,7680]{1,0:T(4,128)(2,1)S(1)} %early.1), channel_id=1, source_target_pairs={{0,16},{16,0},{1,17},{17,1},{2,18},{18,2},{3,19},{19,3},{4,20},{20... | collective-permute-start | bytes 184328 | tf_op jit(solution)/shard_map/ppermute | solution.py:60
  14.9 0.0 collective-permute-done.1.refs_2_.refs_5_
  14.9 0.1 slots.1
  15.0 0.5 %collective-permute-start.4 = (bf16[4,2048]{1,0:T(4,128)(2,1)S(1)}, bf16[4,2048]{1,0:T(4,128)(2,1)S(1)}, u32[]{:S(2)}, u32[]{:S(2)}) collective-permute-start(bf16[4,2048]{1,0:T(4,128)(2,1)S(1)} %get-tuple-element.38), channel_id=1, source_target_pairs={{0,16},{16,0},{1,17},{17,1},{2,18},{18,2},{3,19},{19,3},{4,20},{20... | collective-permute-start | bytes 49160 | tf_op jit(solution)/shard_map/ppermute | solution.py:60
  15.4 0.0 collective-permute-done.5.refs_8_
  15.4 0.2 backs.1.refs_0_
  15.6 0.3 %collective-permute-start.8 = (f32[16,128]{1,0:T(8,128)S(1)}, f32[16,128]{1,0:T(8,128)S(1)}, u32[]{:S(2)}, u32[]{:S(2)}) collective-permute-start(f32[16,128]{1,0:T(8,128)S(1)} %backs.1.refs_0_), channel_id=1, source_target_pairs={{0,3},{1,2},{2,1},{3,0},{4,7},{5,6},{6,5},{7,4},{8,11},{9,10},{10,... | collective-permute-start | bytes 24584 | tf_op jit(solution)/shard_map/ppermute | solution.py:60
  15.9 1.4 %collective-permute-start.7 = (f32[16,128]{1,0:T(8,128)S(1)}, f32[16,128]{1,0:T(8,128)S(1)}, u32[]{:S(2)}, u32[]{:S(2)}) collective-permute-start(f32[16,128]{1,0:T(8,128)S(1)} %backs.1.refs_0_), channel_id=1, source_target_pairs={{0,2},{1,3},{2,0},{3,1},{4,6},{5,7},{6,4},{7,5},{8,10},{9,11},{10,... | collective-permute-start | bytes 24584 | tf_op jit(solution)/shard_map/ppermute | solution.py:60
  17.3 0.2 collective-permute-start.6
  17.5 0.1 collective-permute-done.3.refs_0_
  17.6 0.2 %upstream.1 = (f32[16,384]{1,0:T(8,128)S(1)}, f32[24,2048]{1,0:T(8,128)S(1)}, bf16[16,384]{1,0:T(8,128)(2,1)S(1)}) custom-call(bf16[16,4096]{1,0:T(8,128)(2,1)S(1)} %get-tuple-element.30.rows_ref, bf16[384,4096]{1,0:T(8,128)(2,1)S(1)} %get-tuple-element.31.weight_ref, bf16[4,7680]{1,0:T(4,128)(2,1)S(1)} %collective-permute-done.3.refs_0_), custom_call_target="tpu_custom_call" | custom-call | flops 6291456 | bytes 393216 | tf_op jit(solution)/shard_map/upstream/pallas_call | solution.py:387
  17.9 0.9 %collective-permute-done.4.refs_2_ = bf16[4,2048]{1,0:T(4,128)(2,1)S(1)} collective-permute-done((bf16[4,2048]{1,0:T(4,128)(2,1)S(1)}, bf16[4,2048]{1,0:T(4,128)(2,1)S(1)}, u32[]{:S(2)}, u32[]{:S(2)}) %collective-permute-start.4) | collective-permute-done | bytes 16416 | tf_op jit(solution)/shard_map/ppermute | solution.py:60
  18.8 2.2 %down.1 = (bf16[1,1,16,384]{3,2,1,0:T(8,128)(2,1)}, f32[1,384,2048]{2,1,0:T(8,128)}, f32[32,128]{1,0:T(8,128)S(1)}) custom-call(f32[16,384]{1,0:T(8,128)S(1)} %get-tuple-element.33.part_ref, bf16[16,4096]{1,0:T(8,128)(2,1)S(1)} %get-tuple-element.30.rows_ref, f32[16,128]{1,0:T(8,128)S(1)} %get-tuple-element.34.gate_ref, ...), custom_call_target="tpu_custom_call" | custom-call | flops 25165824 | bytes 3145728 | tf_op jit(solution)/shard_map/down/pallas_call | solution.py:404
  20.9 0.0 collective-permute-done.8.refs_3_
  21.0 0.0 collective-permute-done.7.refs_2_
  21.0 0.0 collective-permute-done.6.refs_1_
  21.0 0.6 %gates.1 = f32[8,128]{1,0:T(8,128)} custom-call(s32[8,128]{1,0:T(8,128)S(1)} %get-tuple-element.24.ids_ref, f32[32,128]{1,0:T(8,128)S(1)} %get-tuple-element.40.match_ref, f32[16,128]{1,0:T(8,128)S(1)} %backs.1.refs_0_, f32[16,128]{1,0:T(8,128)S(1)} %collective-permute-done.6.refs_1_, f32[16,128]{1,0:T(8,128)S(1)} %collective-permute-done.7.refs_2_, ...), custom_call_target="tpu_custom_call" | custom-call | flops 2048 | bytes 8192 | tf_op jit(solution)/shard_map/gates/pallas_call | solution.py:424
Async XLA Ops:
  3.2 8.0 %collective-permute-start = (bf16[4,8320]{1,0:T(4,128)(2,1)S(1)}, bf16[4,8320]{1,0:T(4,128)(2,1)S(1)}, u32[]{:S(2)}, u32[]{:S(2)}) collective-permute-start(bf16[4,8320]{1,0:T(4,128)(2,1)S(1)} %get-tuple-element.27.refs_1_), channel_id=1, source_target_pairs={{0,12},{4,8},{8,4},{12,0},{1,13},{5,9},{9,5},{13,1},{2,14},{6,10},... | collective-permute-start | bytes 199688 | tf_op jit(solution)/shard_map/ppermute | solution.py:60
  8.3 4.7 %collective-permute-start.2 = (bf16[4,8320]{1,0:T(4,128)(2,1)S(1)}, bf16[4,8320]{1,0:T(4,128)(2,1)S(1)}, u32[]{:S(2)}, u32[]{:S(2)}) collective-permute-start(bf16[4,8320]{1,0:T(4,128)(2,1)S(1)} %get-tuple-element.29.refs_3_), channel_id=1, source_target_pairs={{0,4},{4,0},{8,12},{12,8},{1,5},{5,1},{9,13},{13,9},{2,6},{6,2},{1... | collective-permute-start | bytes 199688 | tf_op jit(solution)/shard_map/ppermute | solution.py:60
  8.3 6.5 %collective-permute-start.1 = (bf16[4,4224]{1,0:T(4,128)(2,1)S(1)}, bf16[4,4224]{1,0:T(4,128)(2,1)S(1)}, u32[]{:S(2)}, u32[]{:S(2)}) collective-permute-start(bf16[4,4224]{1,0:T(4,128)(2,1)S(1)} %get-tuple-element.28.refs_2_), channel_id=1, source_target_pairs={{0,8},{4,12},{8,0},{12,4},{1,9},{5,13},{9,1},{13,5},{2,10},{6,14},... | collective-permute-start | bytes 101384 | tf_op jit(solution)/shard_map/ppermute | solution.py:60
  9.0 6.5 %collective-permute-start.5 = (bf16[4,4096]{1,0:T(4,128)(2,1)S(1)}, bf16[4,4096]{1,0:T(4,128)(2,1)S(1)}, u32[]{:S(2)}, u32[]{:S(2)}) collective-permute-start(bf16[4,4096]{1,0:T(4,128)(2,1)S(1)} %get-tuple-element.42), channel_id=1, source_target_pairs={{0,8},{4,12},{8,0},{12,4},{1,9},{5,13},{9,1},{13,5},{2,10},{6,14},... | collective-permute-start | bytes 98312 | tf_op jit(solution)/shard_map/ppermute | solution.py:60
  13.2 4.5 %collective-permute-start.3 = (bf16[4,7680]{1,0:T(4,128)(2,1)S(1)}, bf16[4,7680]{1,0:T(4,128)(2,1)S(1)}, u32[]{:S(2)}, u32[]{:S(2)}) collective-permute-start(bf16[4,7680]{1,0:T(4,128)(2,1)S(1)} %early.1), channel_id=1, source_target_pairs={{0,16},{16,0},{1,17},{17,1},{2,18},{18,2},{3,19},{19,3},{4,20},{20... | collective-permute-start | bytes 184328 | tf_op jit(solution)/shard_map/ppermute | solution.py:60
  15.0 3.8 %collective-permute-start.4 = (bf16[4,2048]{1,0:T(4,128)(2,1)S(1)}, bf16[4,2048]{1,0:T(4,128)(2,1)S(1)}, u32[]{:S(2)}, u32[]{:S(2)}) collective-permute-start(bf16[4,2048]{1,0:T(4,128)(2,1)S(1)} %get-tuple-element.38), channel_id=1, source_target_pairs={{0,16},{16,0},{1,17},{17,1},{2,18},{18,2},{3,19},{19,3},{4,20},{20... | collective-permute-start | bytes 49160 | tf_op jit(solution)/shard_map/ppermute | solution.py:60
  15.6 5.3 %collective-permute-start.8 = (f32[16,128]{1,0:T(8,128)S(1)}, f32[16,128]{1,0:T(8,128)S(1)}, u32[]{:S(2)}, u32[]{:S(2)}) collective-permute-start(f32[16,128]{1,0:T(8,128)S(1)} %backs.1.refs_0_), channel_id=1, source_target_pairs={{0,3},{1,2},{2,1},{3,0},{4,7},{5,6},{6,5},{7,4},{8,11},{9,10},{10,... | collective-permute-start | bytes 24584 | tf_op jit(solution)/shard_map/ppermute | solution.py:60
  15.9 5.1 %collective-permute-start.7 = (f32[16,128]{1,0:T(8,128)S(1)}, f32[16,128]{1,0:T(8,128)S(1)}, u32[]{:S(2)}, u32[]{:S(2)}) collective-permute-start(f32[16,128]{1,0:T(8,128)S(1)} %backs.1.refs_0_), channel_id=1, source_target_pairs={{0,2},{1,3},{2,0},{3,1},{4,6},{5,7},{6,4},{7,5},{8,10},{9,11},{10,... | collective-permute-start | bytes 24584 | tf_op jit(solution)/shard_map/ppermute | solution.py:60
  17.3 3.6 %collective-permute-start.6 = (f32[16,128]{1,0:T(8,128)S(1)}, f32[16,128]{1,0:T(8,128)S(1)}, u32[]{:S(2)}, u32[]{:S(2)}) collective-permute-start(f32[16,128]{1,0:T(8,128)S(1)} %backs.1.refs_0_), channel_id=1, source_target_pairs={{0,1},{1,0},{2,3},{3,2},{4,5},{5,4},{6,7},{7,6},{8,9},{9,8},{10,11... | collective-permute-start | bytes 24584 | tf_op jit(solution)/shard_map/ppermute | solution.py:60

commit v22 on v20

--- a/solution.py
+++ b/solution.py
@@ -168,29 +168,35 @@
     return ((saved == block * CAP + place) & (place < CAP)).astype(jnp.bfloat16)
 
 
+def late_kernel(count, groups, *refs):
+    received, lates, weighted_ref = refs[: count - 1], refs[count - 1 : -1], refs[-1]
+    width = weighted_ref.shape[1]
+    share = width // groups
+    me = lax.axis_index("dp")
+    for k in range(1, count):
+        row = received[k - 1][:, : width + LANES].astype(jnp.float32)
+        part = slice(k * PAD, k * PAD + CAP)
+        weighted_ref[part, :] = row[:, width : width + 1] * row[:, :width]
+        for r, late_ref in enumerate(lates, 1):
+            begin = pl.multiple_of(target(me, r, groups) * share, share)
+            late = weighted_ref[part, pl.ds(begin, share)].astype(jnp.bfloat16)
+            late_ref[:, (k - 1) * share : k * share] = late
+
+
 def slot_kernel(count, groups, hidden_ref, *refs):
     received = refs[:count]
-    rows_ref, gate_ref, own_ref = refs[count : count + 3]
-    lates = refs[count + 3 : count + 2 + groups]
-    wide_ref, spread_ref = refs[count + 2 + groups :]
+    rows_ref, gate_ref, own_ref, wide_ref = refs[count:]
     width = rows_ref.shape[1]
     share = width // groups
     slots = count * CAP
     for r in range(count):
         row = received[r][:, : width + LANES].astype(jnp.float32)
         wide_ref[r * CAP : (r + 1) * CAP, :] = row
-        spread_ref[r * PAD : r * PAD + CAP, :] = row[:, width : width + 1] * row[:, :width]
-    rows = wide_ref[:slots, :width]
     gate = wide_ref[:slots, width:]
     gate_ref[...] = gate
-    rows_ref[...] = rows.astype(jnp.bfloat16)
-    me = lax.axis_index("dp")
-    for r, late_ref in enumerate(lates, 1):
-        begin = pl.multiple_of(target(me, r, groups) * share, share)
-        for k in range(1, count):
-            late = spread_ref[k * PAD : k * PAD + CAP, pl.ds(begin, share)]
-            late_ref[:, (k - 1) * share : k * share] = late.astype(jnp.bfloat16)
-    weighted = gate[:, :1] * wide_ref[:slots, pl.ds(pl.multiple_of(me * share, share), share)]
+    rows_ref[...] = wide_ref[:slots, :width].astype(jnp.bfloat16)
+    begin = pl.multiple_of(lax.axis_index("dp") * share, share)
+    weighted = gate[:, :1] * wide_ref[:slots, pl.ds(begin, share)]
     own_ref[:, :share] = weighted.astype(jnp.bfloat16)
     own_ref[:, share:] = hidden_ref[...]
 
@@ -250,10 +256,11 @@
         copies.append(pltpu.make_async_copy(values, destination, sems.at[len(copies)]))
         copies[-1].start()
 
-    for p in range(pieces):
-        part = slice(p * block, (p + 1) * block)
+    cuts = [0, block // 2, *range(block, units + 1, block)]
+    for start, end in zip(cuts, cuts[1:]):
+        part = slice(start, end)
         down_out[part, :] = dot(hidden[:, part], rows, ((0,), (0,)))
-        part = pl.ds(p * block, block)
+        part = pl.ds(start, end - start)
         write(down_out.at[part], down_hbm.at[0, part])
     upstream = part_ref[...] + upstream_part(rows_ref, weight_ref, split, weight_ref.shape[1])
     scaled = (gate_ref[:, :1] * upstream).astype(jnp.bfloat16)
@@ -326,20 +333,27 @@
     theirs += [send(x, "expert", r) for r, x in zip(apart(count)[1:], products[1:])]
     early = [send(x, "dp", r) for r, x in enumerate(early, 1)]
 
-    rows, gate, own, *lates = pl.pallas_call(
+    lates = pl.pallas_call(
+        functools.partial(late_kernel, count, groups),
+        out_shape=[jax.ShapeDtypeStruct((CAP, (count - 1) * share), jnp.bfloat16)] * (groups - 1),
+        in_specs=[VMEM] * (count - 1),
+        out_specs=[VMEM] * (groups - 1),
+        scratch_shapes=[pltpu.VMEM((count * PAD, width), jnp.float32)],
+        compiler_params=PARAMS,
+        cost_estimate=cost(2 * slots * width, 4 * slots * width),
+        name="late",
+    )(*received[1:])
+
+    rows, gate, own = pl.pallas_call(
         functools.partial(slot_kernel, count, groups),
         out_shape=[
             jax.ShapeDtypeStruct((slots, width), jnp.bfloat16),
             jax.ShapeDtypeStruct((slots, LANES), jnp.float32),
             jax.ShapeDtypeStruct((slots, share + units), jnp.bfloat16),
-        ]
-        + [jax.ShapeDtypeStruct((CAP, (count - 1) * share), jnp.bfloat16)] * (groups - 1),
+        ],
         in_specs=[VMEM] * (1 + count),
-        out_specs=[VMEM] * (2 + groups),
-        scratch_shapes=[
-            pltpu.VMEM((slots + PAD, width + LANES), jnp.float32),
-            pltpu.VMEM((count * PAD, width), jnp.float32),
-        ],
+        out_specs=[VMEM] * 3,
+        scratch_shapes=[pltpu.VMEM((slots + PAD, width + LANES), jnp.float32)],
         compiler_params=PARAMS,
         cost_estimate=cost(4 * slots * width, 8 * slots * width),
         name="slots",
@@ -387,7 +401,7 @@
             pltpu.VMEM((slots, units), jnp.bfloat16),
             pltpu.VMEM((units, share), jnp.float32),
             pltpu.VMEM((slots + PAD, share), jnp.float32),
-            pltpu.SemaphoreType.DMA((pieces + 1,)),
+            pltpu.SemaphoreType.DMA((pieces + 2,)),
         ],
         compiler_params=PARAMS,
         cost_estimate=cost(2 * slots * units * share, 4 * units * share),

time: 20.8 us -> 20.8 us (level)
  transfers between devices with their start and end apart: 9 -> 9, of which waited for: 2 -> 1; matrix products, arithmetic and copies ran while one was open for 0% -> 0% of each run, Pallas kernels for 13% -> 13%
where the time goes in v22:
time: 20.8 us; the launch traced here: 20.6 us
  starting transfers between devices  12.9 us (62%)
  Pallas kernels  5.97 us (29%)
  waiting for transfers between devices  0.95 us (5%)
  between operations  0.69 us (3%)
    ppermute x9, starting transfers between devices, send(): lax.ppermute(value, axis, [(i, give(i, step, size)) for i in range(size)])  12.9 us
    pallas_call x1, Pallas kernels, on_device(): pl.pallas_call(functools.partial(front_kernel, count, groups, pieces), ou...  2.58 us
    pallas_call x1, Pallas kernels, on_device(): pl.pallas_call(functools.partial(down_kernel, count, groups, pieces, spli...  1.98 us
    ppermute x9, waiting for transfers between devices, send(): lax.ppermute(value, axis, [(i, give(i, step, size)) for i in range(size)])  0.95 us
    pallas_call x1, Pallas kernels, on_device(): pl.pallas_call(functools.partial(gate_kernel, count), out_shape=jax.Shape...  0.61 us
    pallas_call x1, Pallas kernels, on_device(): pl.pallas_call(functools.partial(upstream_kernel, split), out_shape=jax.S...  0.42 us
  transfers between devices with their start and end apart: 9, of which 1 were waited for; matrix products, arithmetic and copies ran while one was open for 0% of the time, Pallas kernels for 13%

profile of v22, /device:TPU:0, one launch (start us, length us, event | category | flops | bytes accessed | tf_op | source)
XLA Modules:
  0.0 20.6 jit_solution(15024032168227460285)
XLA Ops:
  0.6 2.6 %front.1 = (s32[8,128]{1,0:T(8,128)S(1)}, f32[32,128]{1,0:T(8,128)S(1)}, bf16[384,4096]{1,0:T(8,128)(2,1)S(1)}, bf16[16,384]{1,0:T(8,128)(2,1)S(1)}, bf16[4,4224...) custom-call(s32[8,128]{1,0:T(8,128)} %bitcast.4, ...), custom_call_target="tpu_custom_call" | custom-call | flops 134217728 | bytes 4194304 | tf_op jit(solution)/shard_map/front/pallas_call | solution.py:301
  3.2 5.1 %collective-permute-start = (bf16[4,8320]{1,0:T(4,128)(2,1)S(1)}, bf16[4,8320]{1,0:T(4,128)(2,1)S(1)}, u32[]{:S(2)}, u32[]{:S(2)}) collective-permute-start(bf16[4,8320]{1,0:T(4,128)(2,1)S(1)} %get-tuple-element.25.refs_1_), channel_id=1, source_target_pairs={{0,12},{4,8},{8,4},{12,0},{1,13},{5,9},{9,5},{13,1},{2,14},{6,10},... | collective-permute-start | bytes 199688 | tf_op jit(solution)/shard_map/ppermute | solution.py:60
  8.3 0.0 collective-permute-start.2
  8.3 0.6 %collective-permute-start.1 = (bf16[4,4224]{1,0:T(4,128)(2,1)S(1)}, bf16[4,4224]{1,0:T(4,128)(2,1)S(1)}, u32[]{:S(2)}, u32[]{:S(2)}) collective-permute-start(bf16[4,4224]{1,0:T(4,128)(2,1)S(1)} %get-tuple-element.26.refs_2_), channel_id=1, source_target_pairs={{0,8},{4,12},{8,0},{12,4},{1,9},{5,13},{9,1},{13,5},{2,10},{6,14},... | collective-permute-start | bytes 101384 | tf_op jit(solution)/shard_map/ppermute | solution.py:60
  9.0 2.3 %collective-permute-start.5 = (bf16[4,4096]{1,0:T(4,128)(2,1)S(1)}, bf16[4,4096]{1,0:T(4,128)(2,1)S(1)}, u32[]{:S(2)}, u32[]{:S(2)}) collective-permute-start(bf16[4,4096]{1,0:T(4,128)(2,1)S(1)} %get-tuple-element.35), channel_id=1, source_target_pairs={{0,8},{4,12},{8,0},{12,4},{1,9},{5,13},{9,1},{13,5},{2,10},{6,14},... | collective-permute-start | bytes 98312 | tf_op jit(solution)/shard_map/ppermute | solution.py:60
  11.3 1.5 %collective-permute-start.3 = (bf16[4,3584]{1,0:T(4,128)(2,1)S(1)}, bf16[4,3584]{1,0:T(4,128)(2,1)S(1)}, u32[]{:S(2)}, u32[]{:S(2)}) collective-permute-start(bf16[4,3584]{1,0:T(4,128)(2,1)S(1)} %get-tuple-element.33), channel_id=1, source_target_pairs={{0,16},{16,0},{1,17},{17,1},{2,18},{18,2},{3,19},{19,3},{4,20},{20... | collective-permute-start | bytes 86024 | tf_op jit(solution)/shard_map/ppermute | solution.py:60
  12.7 0.9 %collective-permute-done.1.refs_2_.refs_1_.refs_5_ = bf16[4,4224]{1,0:T(4,128)(2,1)S(1)} collective-permute-done((bf16[4,4224]{1,0:T(4,128)(2,1)S(1)}, bf16[4,4224]{1,0:T(4,128)(2,1)S(1)}, u32[]{:S(2)}, u32[]{:S(2)}) %collective-permute-start.1) | collective-permute-done | bytes 33824 | tf_op jit(solution)/shard_map/ppermute | solution.py:60
  13.6 0.0 collective-permute-done.refs_1_.refs_0_.refs_4_
  13.6 0.0 collective-permute-done.2.refs_3_.refs_2_.refs_6_
  13.6 0.1 late.1
  13.8 1.6 %collective-permute-start.4 = (bf16[4,6144]{1,0:T(4,128)(2,1)S(1)}, bf16[4,6144]{1,0:T(4,128)(2,1)S(1)}, u32[]{:S(2)}, u32[]{:S(2)}) collective-permute-start(bf16[4,6144]{1,0:T(4,128)(2,1)S(1)} %late.1), channel_id=1, source_target_pairs={{0,16},{16,0},{1,17},{17,1},{2,18},{18,2},{3,19},{19,3},{4,20},{20... | collective-permute-start | bytes 147464 | tf_op jit(solution)/shard_map/ppermute | solution.py:60
  15.3 0.0 collective-permute-done.3.refs_9_.refs_1_
  15.3 0.0 collective-permute-done.5.refs_8_
  15.3 0.2 backs.1
  15.5 0.0 collective-permute-start.6
  15.5 1.6 %collective-permute-start.7 = (f32[16,128]{1,0:T(8,128)S(1)}, f32[16,128]{1,0:T(8,128)S(1)}, u32[]{:S(2)}, u32[]{:S(2)}) collective-permute-start(f32[16,128]{1,0:T(8,128)S(1)} %get-tuple-element.38.refs_0_), channel_id=1, source_target_pairs={{0,2},{1,3},{2,0},{3,1},{4,6},{5,7},{6,4},{7,5},{8,10},{9,11},{10,... | collective-permute-start | bytes 24584 | tf_op jit(solution)/shard_map/ppermute | solution.py:60
  17.1 0.3 %collective-permute-start.8 = (f32[16,128]{1,0:T(8,128)S(1)}, f32[16,128]{1,0:T(8,128)S(1)}, u32[]{:S(2)}, u32[]{:S(2)}) collective-permute-start(f32[16,128]{1,0:T(8,128)S(1)} %get-tuple-element.38.refs_0_), channel_id=1, source_target_pairs={{0,1},{1,0},{2,3},{3,2},{4,5},{5,4},{6,7},{7,6},{8,9},{9,8},{10,11... | collective-permute-start | bytes 24584 | tf_op jit(solution)/shard_map/ppermute | solution.py:60
  17.4 0.1 slots.1
  17.5 0.4 %upstream.1.part_ref = f32[16,384]{1,0:T(8,128)S(1)} custom-call(bf16[16,4096]{1,0:T(8,128)(2,1)S(1)} %get-tuple-element.28.rows_ref, bf16[384,4096]{1,0:T(8,128)(2,1)S(1)} %get-tuple-element.29.weight_ref), custom_call_target="tpu_custom_call" | custom-call | flops 18874368 | bytes 1179648 | tf_op jit(solution)/shard_map/upstream/pallas_call | solution.py:381
  17.9 0.0 collective-permute-done.4.refs_2_
  17.9 2.0 %down.1 = (bf16[1,1,16,384]{3,2,1,0:T(8,128)(2,1)}, f32[1,384,2048]{2,1,0:T(8,128)}, f32[32,128]{1,0:T(8,128)S(1)}) custom-call(f32[16,384]{1,0:T(8,128)S(1)} %upstream.1.part_ref, bf16[16,4096]{1,0:T(8,128)(2,1)S(1)} %get-tuple-element.28.rows_ref, f32[16,128]{1,0:T(8,128)S(1)} %get-tuple-element.30.gate_ref, ...), custom_call_target="tpu_custom_call" | custom-call | flops 25165824 | bytes 3145728 | tf_op jit(solution)/shard_map/down/pallas_call | solution.py:391
  19.9 0.0 collective-permute-done.6.refs_1_
  19.9 0.0 collective-permute-done.7.refs_2_
  19.9 0.0 collective-permute-done.8.refs_3_
  19.9 0.6 %gates.1 = f32[8,128]{1,0:T(8,128)} custom-call(s32[8,128]{1,0:T(8,128)S(1)} %get-tuple-element.22.ids_ref, f32[32,128]{1,0:T(8,128)S(1)} %get-tuple-element.37.match_ref, f32[16,128]{1,0:T(8,128)S(1)} %get-tuple-element.38.refs_0_, f32[16,128]{1,0:T(8,128)S(1)} %collective-permute-done.6.refs_1_, f32[16,128]{1,0:T(8,128)S(1)} %collective-permute-done.7.refs_2_, ...), custom_call_target="tpu_custom_call" | custom-call | flops 2048 | bytes 8192 | tf_op jit(solution)/shard_map/gates/pallas_call | solution.py:411
Async XLA Ops:
  3.2 10.4 %collective-permute-start = (bf16[4,8320]{1,0:T(4,128)(2,1)S(1)}, bf16[4,8320]{1,0:T(4,128)(2,1)S(1)}, u32[]{:S(2)}, u32[]{:S(2)}) collective-permute-start(bf16[4,8320]{1,0:T(4,128)(2,1)S(1)} %get-tuple-element.25.refs_1_), channel_id=1, source_target_pairs={{0,12},{4,8},{8,4},{12,0},{1,13},{5,9},{9,5},{13,1},{2,14},{6,10},... | collective-permute-start | bytes 199688 | tf_op jit(solution)/shard_map/ppermute | solution.py:60
  8.3 5.3 %collective-permute-start.2 = (bf16[4,8320]{1,0:T(4,128)(2,1)S(1)}, bf16[4,8320]{1,0:T(4,128)(2,1)S(1)}, u32[]{:S(2)}, u32[]{:S(2)}) collective-permute-start(bf16[4,8320]{1,0:T(4,128)(2,1)S(1)} %get-tuple-element.27.refs_3_), channel_id=1, source_target_pairs={{0,4},{4,0},{8,12},{12,8},{1,5},{5,1},{9,13},{13,9},{2,6},{6,2},{1... | collective-permute-start | bytes 199688 | tf_op jit(solution)/shard_map/ppermute | solution.py:60
  8.3 5.3 %collective-permute-start.1 = (bf16[4,4224]{1,0:T(4,128)(2,1)S(1)}, bf16[4,4224]{1,0:T(4,128)(2,1)S(1)}, u32[]{:S(2)}, u32[]{:S(2)}) collective-permute-start(bf16[4,4224]{1,0:T(4,128)(2,1)S(1)} %get-tuple-element.26.refs_2_), channel_id=1, source_target_pairs={{0,8},{4,12},{8,0},{12,4},{1,9},{5,13},{9,1},{13,5},{2,10},{6,14},... | collective-permute-start | bytes 101384 | tf_op jit(solution)/shard_map/ppermute | solution.py:60
  9.0 6.4 %collective-permute-start.5 = (bf16[4,4096]{1,0:T(4,128)(2,1)S(1)}, bf16[4,4096]{1,0:T(4,128)(2,1)S(1)}, u32[]{:S(2)}, u32[]{:S(2)}) collective-permute-start(bf16[4,4096]{1,0:T(4,128)(2,1)S(1)} %get-tuple-element.35), channel_id=1, source_target_pairs={{0,8},{4,12},{8,0},{12,4},{1,9},{5,13},{9,1},{13,5},{2,10},{6,14},... | collective-permute-start | bytes 98312 | tf_op jit(solution)/shard_map/ppermute | solution.py:60
  11.3 4.1 %collective-permute-start.3 = (bf16[4,3584]{1,0:T(4,128)(2,1)S(1)}, bf16[4,3584]{1,0:T(4,128)(2,1)S(1)}, u32[]{:S(2)}, u32[]{:S(2)}) collective-permute-start(bf16[4,3584]{1,0:T(4,128)(2,1)S(1)} %get-tuple-element.33), channel_id=1, source_target_pairs={{0,16},{16,0},{1,17},{17,1},{2,18},{18,2},{3,19},{19,3},{4,20},{20... | collective-permute-start | bytes 86024 | tf_op jit(solution)/shard_map/ppermute | solution.py:60
  13.8 4.2 %collective-permute-start.4 = (bf16[4,6144]{1,0:T(4,128)(2,1)S(1)}, bf16[4,6144]{1,0:T(4,128)(2,1)S(1)}, u32[]{:S(2)}, u32[]{:S(2)}) collective-permute-start(bf16[4,6144]{1,0:T(4,128)(2,1)S(1)} %late.1), channel_id=1, source_target_pairs={{0,16},{16,0},{1,17},{17,1},{2,18},{18,2},{3,19},{19,3},{4,20},{20... | collective-permute-start | bytes 147464 | tf_op jit(solution)/shard_map/ppermute | solution.py:60
  15.5 4.4 %collective-permute-start.6 = (f32[16,128]{1,0:T(8,128)S(1)}, f32[16,128]{1,0:T(8,128)S(1)}, u32[]{:S(2)}, u32[]{:S(2)}) collective-permute-start(f32[16,128]{1,0:T(8,128)S(1)} %get-tuple-element.38.refs_0_), channel_id=1, source_target_pairs={{0,3},{1,2},{2,1},{3,0},{4,7},{5,6},{6,5},{7,4},{8,11},{9,10},{10,... | collective-permute-start | bytes 24584 | tf_op jit(solution)/shard_map/ppermute | solution.py:60
  15.5 4.4 %collective-permute-start.7 = (f32[16,128]{1,0:T(8,128)S(1)}, f32[16,128]{1,0:T(8,128)S(1)}, u32[]{:S(2)}, u32[]{:S(2)}) collective-permute-start(f32[16,128]{1,0:T(8,128)S(1)} %get-tuple-element.38.refs_0_), channel_id=1, source_target_pairs={{0,2},{1,3},{2,0},{3,1},{4,6},{5,7},{6,4},{7,5},{8,10},{9,11},{10,... | collective-permute-start | bytes 24584 | tf_op jit(solution)/shard_map/ppermute | solution.py:60
  17.1 2.9 %collective-permute-start.8 = (f32[16,128]{1,0:T(8,128)S(1)}, f32[16,128]{1,0:T(8,128)S(1)}, u32[]{:S(2)}, u32[]{:S(2)}) collective-permute-start(f32[16,128]{1,0:T(8,128)S(1)} %get-tuple-element.38.refs_0_), channel_id=1, source_target_pairs={{0,1},{1,0},{2,3},{3,2},{4,5},{5,4},{6,7},{7,6},{8,9},{9,8},{10,11... | collective-permute-start | bytes 24584 | tf_op jit(solution)/shard_map/ppermute | solution.py:60

commit v23 on v22

--- a/solution.py
+++ b/solution.py
@@ -62,11 +62,11 @@
 
 def front_kernel(count, groups, pieces, *refs):
     ids_hbm, gates_hbm, grad_hbm, hidden_hbm, weight_hbm = refs[:5]
-    ids_ref, match_ref, weight_ref, hidden_ref = refs[5:9]
+    hits_ref, match_ref, weight_ref, hidden_ref = refs[5:9]
     sends = refs[9 : 9 + count]
     products = dict(zip(apart(count), refs[9 + count :]))
-    early = refs[-4 - groups : -5]
-    gates_ref, grad_ref, saved_ref, total_ref, sems = refs[-5:]
+    early = refs[-5 - groups : -6]
+    ids_ref, gates_ref, grad_ref, saved_ref, total_ref, sems = refs[-6:]
     units, width = weight_ref.shape
     top, tokens = ids_ref.shape
     pairs = [(ids_hbm, ids_ref), (gates_hbm, gates_ref), (hidden_hbm.at[0, 0], saved_ref)]
@@ -99,6 +99,8 @@
         hit = ids[k : k + 1, :] == expert
         member = jnp.where(hit, 1.0, member)
         gate = jnp.where(hit, gates[k : k + 1, :], gate)
+    for r in range(count):
+        hits_ref[r] = (ids == target(me, r, count)).astype(jnp.float32)
     before = dot(member.astype(jnp.bfloat16), order, ((1,), (0,)))
     taken = (member > 0) & (before == place.astype(jnp.float32)) & (place < CAP)
     match = taken.astype(jnp.float32)
@@ -271,22 +273,6 @@
         copy.wait()
 
 
-def gate_kernel(count, ids_ref, match_ref, *refs):
-    backs, out_ref = refs[:-1], refs[-1]
-    me = lax.axis_index("expert")
-    ids = ids_ref[...]
-    back = backs[0][...]
-    for ref in backs[1:]:
-        back = back + ref[...]
-    total = jnp.zeros(out_ref.shape, jnp.float32)
-    for r in range(count):
-        value = back[r * CAP : (r + 1) * CAP, :]
-        match = match_ref[r * PAD : r * PAD + CAP, :]
-        chosen = jnp.sum(jnp.where(match > 0, value, 0.0), axis=0, keepdims=True)
-        total = total + jnp.where(ids == target(me, r, count), chosen, 0.0)
-    out_ref[...] = total
-
-
 def on_device(grad_out, expert_ids, gate_values, saved_hidden, down_weight):
     count = lax.axis_size("expert")
     groups = lax.axis_size("dp")
@@ -298,10 +284,10 @@
     share = width // groups
     pieces = units // LANES
 
-    ids, match, weight, hidden, *rest = pl.pallas_call(
+    hits, match, weight, hidden, *rest = pl.pallas_call(
         functools.partial(front_kernel, count, groups, pieces),
         out_shape=[
-            jax.ShapeDtypeStruct((top, tokens), jnp.int32),
+            jax.ShapeDtypeStruct((count, top, tokens), jnp.float32),
             jax.ShapeDtypeStruct((count * PAD, tokens), jnp.float32),
             jax.ShapeDtypeStruct((units, width), jnp.bfloat16),
             jax.ShapeDtypeStruct((slots, units), jnp.bfloat16),
@@ -315,6 +301,7 @@
         in_specs=[HBM] * 5,
         out_specs=[VMEM] * (3 + count + len(apart(count)) + groups),
         scratch_shapes=[
+            pltpu.VMEM((top, tokens), jnp.int32),
             pltpu.VMEM((top, tokens), jnp.bfloat16),
             pltpu.VMEM((tokens, width), jnp.bfloat16),
             pltpu.VMEM((slots, units), jnp.bfloat16),
@@ -408,15 +395,11 @@
         name="down",
     )(upstream, rows, gate, weight, match, own, *early, *lates, *hiddens)
 
-    gate_grad = pl.pallas_call(
-        functools.partial(gate_kernel, count),
-        out_shape=jax.ShapeDtypeStruct(ids.shape, jnp.float32),
-        in_specs=[VMEM] * (2 + tensors),
-        out_specs=VMEM,
-        compiler_params=PARAMS,
-        cost_estimate=cost(slots * tokens, 4 * slots * tokens),
-        name="gates",
-    )(ids, match, *backs)
+    match, backs = lax.optimization_barrier((match, backs))
+    back = sum(backs[1:], backs[0]).reshape(count, CAP, tokens)
+    taken = match.reshape(count, PAD, tokens)[:, :CAP]
+    chosen = jnp.sum(jnp.where(taken > 0, back, 0.0), axis=1)
+    gate_grad = jnp.sum(jnp.where(hits > 0, chosen[:, None, :], 0.0), axis=0)
     return (gate_grad.T, hidden_grad, down_grad)
 
 

time: 20.8 us -> 20.8 us (level)
  other arithmetic: 0 us -> 0.63 us
  Pallas kernels: 5.97 us -> 5.35 us
    reduce_sum x0 -> x2, other arithmetic: none -> 0.62 us  [the longest x1 0.6 us: on_device(): gate_grad = jnp.sum(jnp.where(hits > 0, chosen[:, None, :], 0.0), axis=0)]
    pallas_call x1 -> x0, Pallas kernels: 0.61 us -> none  [on_device(): pl.pallas_call(functools.partial(gate_kernel, count), out_shape=jax.Shape...]
where the time goes in v23:
time: 20.8 us; the launch traced here: 20.6 us
  starting transfers between devices  12.9 us (62%)
  Pallas kernels  5.35 us (26%)
  waiting for transfers between devices  0.95 us (5%)
  between operations  0.7 us (3%)
  other arithmetic  0.63 us (3%)
    ppermute x9, starting transfers between devices, send(): lax.ppermute(value, axis, [(i, give(i, step, size)) for i in range(size)])  12.9 us
    pallas_call x1, Pallas kernels, on_device(): pl.pallas_call(functools.partial(front_kernel, count, groups, pieces), ou...  2.58 us
    pallas_call x1, Pallas kernels, on_device(): pl.pallas_call(functools.partial(down_kernel, count, groups, pieces, spli...  1.97 us
    ppermute x9, waiting for transfers between devices, send(): lax.ppermute(value, axis, [(i, give(i, step, size)) for i in range(size)])  0.95 us
    reduce_sum x1, other arithmetic, on_device(): gate_grad = jnp.sum(jnp.where(hits > 0, chosen[:, None, :], 0.0), axis=0)  0.6 us
    pallas_call x1, Pallas kernels, on_device(): pl.pallas_call(functools.partial(upstream_kernel, split), out_shape=jax.S...  0.42 us
  transfers between devices with their start and end apart: 9, of which 1 were waited for; matrix products, arithmetic and copies ran while one was open for 0% of the time, Pallas kernels for 13%

profile of v23, /device:TPU:0, one launch (start us, length us, event | category | flops | bytes accessed | tf_op | source)
XLA Modules:
  0.0 20.6 jit_solution(7766642881293912291)
XLA Ops:
  0.6 2.6 %front.1 = (f32[4,8,128]{2,1,0:T(8,128)S(1)}, f32[32,128]{1,0:T(8,128)S(1)}, bf16[384,4096]{1,0:T(8,128)(2,1)S(1)}, bf16[16,384]{1,0:T(8,128)(2,1)S(1)}, bf16[4,...) custom-call(s32[8,128]{1,0:T(8,128)} %bitcast.8, ...), custom_call_target="tpu_custom_call" | custom-call | flops 134217728 | bytes 4194304 | tf_op jit(solution)/shard_map/front/pallas_call | solution.py:287
  3.2 5.1 %collective-permute-start = (bf16[4,8320]{1,0:T(4,128)(2,1)S(1)}, bf16[4,8320]{1,0:T(4,128)(2,1)S(1)}, u32[]{:S(2)}, u32[]{:S(2)}) collective-permute-start(bf16[4,8320]{1,0:T(4,128)(2,1)S(1)} %get-tuple-element.30.refs_1_), channel_id=1, source_target_pairs={{0,12},{4,8},{8,4},{12,0},{1,13},{5,9},{9,5},{13,1},{2,14},{6,10},... | collective-permute-start | bytes 199688 | tf_op jit(solution)/shard_map/ppermute | solution.py:60
  8.3 0.0 collective-permute-start.2
  8.3 0.6 %collective-permute-start.1 = (bf16[4,4224]{1,0:T(4,128)(2,1)S(1)}, bf16[4,4224]{1,0:T(4,128)(2,1)S(1)}, u32[]{:S(2)}, u32[]{:S(2)}) collective-permute-start(bf16[4,4224]{1,0:T(4,128)(2,1)S(1)} %get-tuple-element.31.refs_2_), channel_id=1, source_target_pairs={{0,8},{4,12},{8,0},{12,4},{1,9},{5,13},{9,1},{13,5},{2,10},{6,14},... | collective-permute-start | bytes 101384 | tf_op jit(solution)/shard_map/ppermute | solution.py:60
  9.0 2.3 %collective-permute-start.5 = (bf16[4,4096]{1,0:T(4,128)(2,1)S(1)}, bf16[4,4096]{1,0:T(4,128)(2,1)S(1)}, u32[]{:S(2)}, u32[]{:S(2)}) collective-permute-start(bf16[4,4096]{1,0:T(4,128)(2,1)S(1)} %get-tuple-element.40), channel_id=1, source_target_pairs={{0,8},{4,12},{8,0},{12,4},{1,9},{5,13},{9,1},{13,5},{2,10},{6,14},... | collective-permute-start | bytes 98312 | tf_op jit(solution)/shard_map/ppermute | solution.py:60
  11.3 1.5 %collective-permute-start.3 = (bf16[4,3584]{1,0:T(4,128)(2,1)S(1)}, bf16[4,3584]{1,0:T(4,128)(2,1)S(1)}, u32[]{:S(2)}, u32[]{:S(2)}) collective-permute-start(bf16[4,3584]{1,0:T(4,128)(2,1)S(1)} %get-tuple-element.38), channel_id=1, source_target_pairs={{0,16},{16,0},{1,17},{17,1},{2,18},{18,2},{3,19},{19,3},{4,20},{20... | collective-permute-start | bytes 86024 | tf_op jit(solution)/shard_map/ppermute | solution.py:60
  12.8 0.9 %collective-permute-done.1.refs_2_.refs_1_.refs_5_ = bf16[4,4224]{1,0:T(4,128)(2,1)S(1)} collective-permute-done((bf16[4,4224]{1,0:T(4,128)(2,1)S(1)}, bf16[4,4224]{1,0:T(4,128)(2,1)S(1)}, u32[]{:S(2)}, u32[]{:S(2)}) %collective-permute-start.1) | collective-permute-done | bytes 33824 | tf_op jit(solution)/shard_map/ppermute | solution.py:60
  13.6 0.0 collective-permute-done.refs_1_.refs_0_.refs_4_
  13.6 0.0 collective-permute-done.2.refs_3_.refs_2_.refs_6_
  13.6 0.1 late.1
  13.8 1.6 %collective-permute-start.4 = (bf16[4,6144]{1,0:T(4,128)(2,1)S(1)}, bf16[4,6144]{1,0:T(4,128)(2,1)S(1)}, u32[]{:S(2)}, u32[]{:S(2)}) collective-permute-start(bf16[4,6144]{1,0:T(4,128)(2,1)S(1)} %late.1), channel_id=1, source_target_pairs={{0,16},{16,0},{1,17},{17,1},{2,18},{18,2},{3,19},{19,3},{4,20},{20... | collective-permute-start | bytes 147464 | tf_op jit(solution)/shard_map/ppermute | solution.py:60
  15.3 0.0 collective-permute-done.3.refs_9_.refs_1_
  15.3 0.0 collective-permute-done.5.refs_8_
  15.3 0.2 backs.1
  15.5 0.0 collective-permute-start.6
  15.5 1.6 %collective-permute-start.7 = (f32[16,128]{1,0:T(8,128)S(1)}, f32[16,128]{1,0:T(8,128)S(1)}, u32[]{:S(2)}, u32[]{:S(2)}) collective-permute-start(f32[16,128]{1,0:T(8,128)S(1)} %get-tuple-element.45), channel_id=1, source_target_pairs={{0,2},{1,3},{2,0},{3,1},{4,6},{5,7},{6,4},{7,5},{8,10},{9,11},{10,... | collective-permute-start | bytes 24584 | tf_op jit(solution)/shard_map/ppermute | solution.py:60
  17.1 0.3 %collective-permute-start.8 = (f32[16,128]{1,0:T(8,128)S(1)}, f32[16,128]{1,0:T(8,128)S(1)}, u32[]{:S(2)}, u32[]{:S(2)}) collective-permute-start(f32[16,128]{1,0:T(8,128)S(1)} %get-tuple-element.45), channel_id=1, source_target_pairs={{0,1},{1,0},{2,3},{3,2},{4,5},{5,4},{6,7},{7,6},{8,9},{9,8},{10,11... | collective-permute-start | bytes 24584 | tf_op jit(solution)/shard_map/ppermute | solution.py:60
  17.4 0.1 slots.1
  17.5 0.4 %upstream.1.part_ref = f32[16,384]{1,0:T(8,128)S(1)} custom-call(bf16[16,4096]{1,0:T(8,128)(2,1)S(1)} %get-tuple-element.33.rows_ref, bf16[384,4096]{1,0:T(8,128)(2,1)S(1)} %get-tuple-element.34.weight_ref), custom_call_target="tpu_custom_call" | custom-call | flops 18874368 | bytes 1179648 | tf_op jit(solution)/shard_map/upstream/pallas_call | solution.py:368
  17.9 0.0 collective-permute-done.4.refs_2_
  17.9 2.0 %down.1 = (bf16[1,1,16,384]{3,2,1,0:T(8,128)(2,1)}, f32[1,384,2048]{2,1,0:T(8,128)}, f32[32,128]{1,0:T(8,128)S(1)}) custom-call(f32[16,384]{1,0:T(8,128)S(1)} %upstream.1.part_ref, bf16[16,4096]{1,0:T(8,128)(2,1)S(1)} %get-tuple-element.33.rows_ref, f32[16,128]{1,0:T(8,128)S(1)} %get-tuple-element.35.gate_ref, ...), custom_call_target="tpu_custom_call" | custom-call | flops 25165824 | bytes 3145728 | tf_op jit(solution)/shard_map/down/pallas_call | solution.py:378
  19.9 0.0 collective-permute-done.6
  19.9 0.0 collective-permute-done.7
  19.9 0.0 collective-permute-done.8
  20.0 0.6 %select_reduce_fusion = f32[8,128]{1,0:T(8,128)} fusion(f32[4,8,128]{2,1,0:T(8,128)S(1)} %get-tuple-element.27, f32[4,128]{1,0:T(4,128)S(1)} %select_reduce_fusion.1), kind=kLoop, calls=%fused_computation | loop fusion | flops 11264 | bytes 22528 | tf_op jit(solution)/shard_map/reduce_sum | solution.py:402
  (2 shorter events, 0.0 us)
Async XLA Ops:
  3.2 10.4 %collective-permute-start = (bf16[4,8320]{1,0:T(4,128)(2,1)S(1)}, bf16[4,8320]{1,0:T(4,128)(2,1)S(1)}, u32[]{:S(2)}, u32[]{:S(2)}) collective-permute-start(bf16[4,8320]{1,0:T(4,128)(2,1)S(1)} %get-tuple-element.30.refs_1_), channel_id=1, source_target_pairs={{0,12},{4,8},{8,4},{12,0},{1,13},{5,9},{9,5},{13,1},{2,14},{6,10},... | collective-permute-start | bytes 199688 | tf_op jit(solution)/shard_map/ppermute | solution.py:60
  8.3 5.3 %collective-permute-start.2 = (bf16[4,8320]{1,0:T(4,128)(2,1)S(1)}, bf16[4,8320]{1,0:T(4,128)(2,1)S(1)}, u32[]{:S(2)}, u32[]{:S(2)}) collective-permute-start(bf16[4,8320]{1,0:T(4,128)(2,1)S(1)} %get-tuple-element.32.refs_3_), channel_id=1, source_target_pairs={{0,4},{4,0},{8,12},{12,8},{1,5},{5,1},{9,13},{13,9},{2,6},{6,2},{1... | collective-permute-start | bytes 199688 | tf_op jit(solution)/shard_map/ppermute | solution.py:60
  8.3 5.3 %collective-permute-start.1 = (bf16[4,4224]{1,0:T(4,128)(2,1)S(1)}, bf16[4,4224]{1,0:T(4,128)(2,1)S(1)}, u32[]{:S(2)}, u32[]{:S(2)}) collective-permute-start(bf16[4,4224]{1,0:T(4,128)(2,1)S(1)} %get-tuple-element.31.refs_2_), channel_id=1, source_target_pairs={{0,8},{4,12},{8,0},{12,4},{1,9},{5,13},{9,1},{13,5},{2,10},{6,14},... | collective-permute-start | bytes 101384 | tf_op jit(solution)/shard_map/ppermute | solution.py:60
  9.0 6.4 %collective-permute-start.5 = (bf16[4,4096]{1,0:T(4,128)(2,1)S(1)}, bf16[4,4096]{1,0:T(4,128)(2,1)S(1)}, u32[]{:S(2)}, u32[]{:S(2)}) collective-permute-start(bf16[4,4096]{1,0:T(4,128)(2,1)S(1)} %get-tuple-element.40), channel_id=1, source_target_pairs={{0,8},{4,12},{8,0},{12,4},{1,9},{5,13},{9,1},{13,5},{2,10},{6,14},... | collective-permute-start | bytes 98312 | tf_op jit(solution)/shard_map/ppermute | solution.py:60
  11.3 4.1 %collective-permute-start.3 = (bf16[4,3584]{1,0:T(4,128)(2,1)S(1)}, bf16[4,3584]{1,0:T(4,128)(2,1)S(1)}, u32[]{:S(2)}, u32[]{:S(2)}) collective-permute-start(bf16[4,3584]{1,0:T(4,128)(2,1)S(1)} %get-tuple-element.38), channel_id=1, source_target_pairs={{0,16},{16,0},{1,17},{17,1},{2,18},{18,2},{3,19},{19,3},{4,20},{20... | collective-permute-start | bytes 86024 | tf_op jit(solution)/shard_map/ppermute | solution.py:60
  13.8 4.2 %collective-permute-start.4 = (bf16[4,6144]{1,0:T(4,128)(2,1)S(1)}, bf16[4,6144]{1,0:T(4,128)(2,1)S(1)}, u32[]{:S(2)}, u32[]{:S(2)}) collective-permute-start(bf16[4,6144]{1,0:T(4,128)(2,1)S(1)} %late.1), channel_id=1, source_target_pairs={{0,16},{16,0},{1,17},{17,1},{2,18},{18,2},{3,19},{19,3},{4,20},{20... | collective-permute-start | bytes 147464 | tf_op jit(solution)/shard_map/ppermute | solution.py:60
  15.5 4.4 %collective-permute-start.6 = (f32[16,128]{1,0:T(8,128)S(1)}, f32[16,128]{1,0:T(8,128)S(1)}, u32[]{:S(2)}, u32[]{:S(2)}) collective-permute-start(f32[16,128]{1,0:T(8,128)S(1)} %get-tuple-element.45), channel_id=1, source_target_pairs={{0,3},{1,2},{2,1},{3,0},{4,7},{5,6},{6,5},{7,4},{8,11},{9,10},{10,... | collective-permute-start | bytes 24584 | tf_op jit(solution)/shard_map/ppermute | solution.py:60
  15.5 4.4 %collective-permute-start.7 = (f32[16,128]{1,0:T(8,128)S(1)}, f32[16,128]{1,0:T(8,128)S(1)}, u32[]{:S(2)}, u32[]{:S(2)}) collective-permute-start(f32[16,128]{1,0:T(8,128)S(1)} %get-tuple-element.45), channel_id=1, source_target_pairs={{0,2},{1,3},{2,0},{3,1},{4,6},{5,7},{6,4},{7,5},{8,10},{9,11},{10,... | collective-permute-start | bytes 24584 | tf_op jit(solution)/shard_map/ppermute | solution.py:60
  17.1 2.8 %collective-permute-start.8 = (f32[16,128]{1,0:T(8,128)S(1)}, f32[16,128]{1,0:T(8,128)S(1)}, u32[]{:S(2)}, u32[]{:S(2)}) collective-permute-start(f32[16,128]{1,0:T(8,128)S(1)} %get-tuple-element.45), channel_id=1, source_target_pairs={{0,1},{1,0},{2,3},{3,2},{4,5},{5,4},{6,7},{7,6},{8,9},{9,8},{10,11... | collective-permute-start | bytes 24584 | tf_op jit(solution)/shard_map/ppermute | solution.py:60

commit v24 on v23

--- a/solution.py
+++ b/solution.py
@@ -70,13 +70,10 @@
     units, width = weight_ref.shape
     top, tokens = ids_ref.shape
     pairs = [(ids_hbm, ids_ref), (gates_hbm, gates_ref), (hidden_hbm.at[0, 0], saved_ref)]
-    half = tokens // 2
-    for p in range(2):
-        part = pl.ds(p * half, half)
-        pairs.append((grad_hbm.at[part], grad_ref.at[part]))
-    half = units // (2 * pieces)
-    for p in range(2 * pieces):
-        part = pl.ds(p * half, half)
+    pairs.append((grad_hbm, grad_ref))
+    block = units // pieces
+    for p in range(pieces):
+        part = pl.ds(p * block, block)
         pairs.append((weight_hbm.at[0, part], weight_ref.at[part]))
     copies = [pltpu.make_async_copy(*pair, sems.at[n]) for n, pair in enumerate(pairs)]
     for copy in copies:
@@ -117,8 +114,7 @@
     chosen = (here % PAD < CAP) & (there == target(me, here // PAD, count) * CAP + here % PAD)
     hidden = dot(chosen.astype(jnp.bfloat16), saved, ((1,), (0,))).astype(jnp.bfloat16)
 
-    for copy in copies[3:5]:
-        copy.wait()
+    copies[3].wait()
     for r in range(count):
         part = slice(r * PAD, r * PAD + CAP)
         gate = jnp.broadcast_to(slot_gate[part], (CAP, LANES)).astype(jnp.bfloat16)
@@ -139,10 +135,8 @@
         for k in range(count):
             part = slice(share + k * units, share + (k + 1) * units)
             early_ref[:, part] = spread[k * PAD : k * PAD + CAP].astype(jnp.bfloat16)
-    block = units // pieces
     for p in range(pieces):
-        for copy in copies[5 + 2 * p : 7 + 2 * p]:
-            copy.wait()
+        copies[4 + p].wait()
         rows = slice(p * block, (p + 1) * block)
         for begin in range(0, width, wide):
             part = slice(begin, begin + wide)
@@ -306,7 +300,7 @@
             pltpu.VMEM((tokens, width), jnp.bfloat16),
             pltpu.VMEM((slots, units), jnp.bfloat16),
             pltpu.VMEM((count * PAD, width), jnp.float32),
-            pltpu.SemaphoreType.DMA((5 + 2 * pieces,)),
+            pltpu.SemaphoreType.DMA((4 + pieces,)),
         ],
         compiler_params=PARAMS,
         cost_estimate=cost(2 * count * PAD * (tokens + units) * width, 2 * (tokens + units) * width),

time: 20.8 us -> 20.8 us (level)
  no operation moved by 1% of the time
where the time goes in v24:
time: 20.8 us; the launch traced here: 20.6 us
  starting transfers between devices  12.9 us (62%)
  Pallas kernels  5.34 us (26%)
  waiting for transfers between devices  0.95 us (5%)
  between operations  0.7 us (3%)
  other arithmetic  0.63 us (3%)
    ppermute x9, starting transfers between devices, send(): lax.ppermute(value, axis, [(i, give(i, step, size)) for i in range(size)])  12.9 us
    pallas_call x1, Pallas kernels, on_device(): pl.pallas_call(functools.partial(front_kernel, count, groups, pieces), ou...  2.57 us
    pallas_call x1, Pallas kernels, on_device(): pl.pallas_call(functools.partial(down_kernel, count, groups, pieces, spli...  1.97 us
    ppermute x9, waiting for transfers between devices, send(): lax.ppermute(value, axis, [(i, give(i, step, size)) for i in range(size)])  0.95 us
    reduce_sum x1, other arithmetic, on_device(): gate_grad = jnp.sum(jnp.where(hits > 0, chosen[:, None, :], 0.0), axis=0)  0.6 us
    pallas_call x1, Pallas kernels, on_device(): pl.pallas_call(functools.partial(upstream_kernel, split), out_shape=jax.S...  0.42 us
  transfers between devices with their start and end apart: 9, of which 1 were waited for; matrix products, arithmetic and copies ran while one was open for 0% of the time, Pallas kernels for 13%

profile of v24, /device:TPU:0, one launch (start us, length us, event | category | flops | bytes accessed | tf_op | source)
XLA Modules:
  0.0 20.6 jit_solution(10498819084784750342)
XLA Ops:
  0.6 2.6 %front.1 = (f32[4,8,128]{2,1,0:T(8,128)S(1)}, f32[32,128]{1,0:T(8,128)S(1)}, bf16[384,4096]{1,0:T(8,128)(2,1)S(1)}, bf16[16,384]{1,0:T(8,128)(2,1)S(1)}, bf16[4,...) custom-call(s32[8,128]{1,0:T(8,128)} %bitcast.8, ...), custom_call_target="tpu_custom_call" | custom-call | flops 134217728 | bytes 4194304 | tf_op jit(solution)/shard_map/front/pallas_call | solution.py:281
  3.2 5.1 %collective-permute-start = (bf16[4,8320]{1,0:T(4,128)(2,1)S(1)}, bf16[4,8320]{1,0:T(4,128)(2,1)S(1)}, u32[]{:S(2)}, u32[]{:S(2)}) collective-permute-start(bf16[4,8320]{1,0:T(4,128)(2,1)S(1)} %get-tuple-element.30.refs_1_), channel_id=1, source_target_pairs={{0,12},{4,8},{8,4},{12,0},{1,13},{5,9},{9,5},{13,1},{2,14},{6,10},... | collective-permute-start | bytes 199688 | tf_op jit(solution)/shard_map/ppermute | solution.py:60
  8.3 0.0 collective-permute-start.2
  8.3 0.6 %collective-permute-start.1 = (bf16[4,4224]{1,0:T(4,128)(2,1)S(1)}, bf16[4,4224]{1,0:T(4,128)(2,1)S(1)}, u32[]{:S(2)}, u32[]{:S(2)}) collective-permute-start(bf16[4,4224]{1,0:T(4,128)(2,1)S(1)} %get-tuple-element.31.refs_2_), channel_id=1, source_target_pairs={{0,8},{4,12},{8,0},{12,4},{1,9},{5,13},{9,1},{13,5},{2,10},{6,14},... | collective-permute-start | bytes 101384 | tf_op jit(solution)/shard_map/ppermute | solution.py:60
  9.0 2.3 %collective-permute-start.5 = (bf16[4,4096]{1,0:T(4,128)(2,1)S(1)}, bf16[4,4096]{1,0:T(4,128)(2,1)S(1)}, u32[]{:S(2)}, u32[]{:S(2)}) collective-permute-start(bf16[4,4096]{1,0:T(4,128)(2,1)S(1)} %get-tuple-element.40), channel_id=1, source_target_pairs={{0,8},{4,12},{8,0},{12,4},{1,9},{5,13},{9,1},{13,5},{2,10},{6,14},... | collective-permute-start | bytes 98312 | tf_op jit(solution)/shard_map/ppermute | solution.py:60
  11.2 1.5 %collective-permute-start.3 = (bf16[4,3584]{1,0:T(4,128)(2,1)S(1)}, bf16[4,3584]{1,0:T(4,128)(2,1)S(1)}, u32[]{:S(2)}, u32[]{:S(2)}) collective-permute-start(bf16[4,3584]{1,0:T(4,128)(2,1)S(1)} %get-tuple-element.38), channel_id=1, source_target_pairs={{0,16},{16,0},{1,17},{17,1},{2,18},{18,2},{3,19},{19,3},{4,20},{20... | collective-permute-start | bytes 86024 | tf_op jit(solution)/shard_map/ppermute | solution.py:60
  12.7 0.9 %collective-permute-done.1.refs_2_.refs_1_.refs_5_ = bf16[4,4224]{1,0:T(4,128)(2,1)S(1)} collective-permute-done((bf16[4,4224]{1,0:T(4,128)(2,1)S(1)}, bf16[4,4224]{1,0:T(4,128)(2,1)S(1)}, u32[]{:S(2)}, u32[]{:S(2)}) %collective-permute-start.1) | collective-permute-done | bytes 33824 | tf_op jit(solution)/shard_map/ppermute | solution.py:60
  13.6 0.0 collective-permute-done.refs_1_.refs_0_.refs_4_
  13.6 0.0 collective-permute-done.2.refs_3_.refs_2_.refs_6_
  13.6 0.1 late.1
  13.8 1.6 %collective-permute-start.4 = (bf16[4,6144]{1,0:T(4,128)(2,1)S(1)}, bf16[4,6144]{1,0:T(4,128)(2,1)S(1)}, u32[]{:S(2)}, u32[]{:S(2)}) collective-permute-start(bf16[4,6144]{1,0:T(4,128)(2,1)S(1)} %late.1), channel_id=1, source_target_pairs={{0,16},{16,0},{1,17},{17,1},{2,18},{18,2},{3,19},{19,3},{4,20},{20... | collective-permute-start | bytes 147464 | tf_op jit(solution)/shard_map/ppermute | solution.py:60
  15.3 0.0 collective-permute-done.3.refs_9_.refs_1_
  15.3 0.0 collective-permute-done.5.refs_8_
  15.3 0.2 backs.1
  15.5 0.0 collective-permute-start.6
  15.5 1.6 %collective-permute-start.7 = (f32[16,128]{1,0:T(8,128)S(1)}, f32[16,128]{1,0:T(8,128)S(1)}, u32[]{:S(2)}, u32[]{:S(2)}) collective-permute-start(f32[16,128]{1,0:T(8,128)S(1)} %get-tuple-element.45), channel_id=1, source_target_pairs={{0,2},{1,3},{2,0},{3,1},{4,6},{5,7},{6,4},{7,5},{8,10},{9,11},{10,... | collective-permute-start | bytes 24584 | tf_op jit(solution)/shard_map/ppermute | solution.py:60
  17.1 0.3 %collective-permute-start.8 = (f32[16,128]{1,0:T(8,128)S(1)}, f32[16,128]{1,0:T(8,128)S(1)}, u32[]{:S(2)}, u32[]{:S(2)}) collective-permute-start(f32[16,128]{1,0:T(8,128)S(1)} %get-tuple-element.45), channel_id=1, source_target_pairs={{0,1},{1,0},{2,3},{3,2},{4,5},{5,4},{6,7},{7,6},{8,9},{9,8},{10,11... | collective-permute-start | bytes 24584 | tf_op jit(solution)/shard_map/ppermute | solution.py:60
  17.4 0.1 slots.1
  17.4 0.4 %upstream.1.part_ref = f32[16,384]{1,0:T(8,128)S(1)} custom-call(bf16[16,4096]{1,0:T(8,128)(2,1)S(1)} %get-tuple-element.33.rows_ref, bf16[384,4096]{1,0:T(8,128)(2,1)S(1)} %get-tuple-element.34.weight_ref), custom_call_target="tpu_custom_call" | custom-call | flops 18874368 | bytes 1179648 | tf_op jit(solution)/shard_map/upstream/pallas_call | solution.py:362
  17.9 0.0 collective-permute-done.4.refs_2_
  17.9 2.0 %down.1 = (bf16[1,1,16,384]{3,2,1,0:T(8,128)(2,1)}, f32[1,384,2048]{2,1,0:T(8,128)}, f32[32,128]{1,0:T(8,128)S(1)}) custom-call(f32[16,384]{1,0:T(8,128)S(1)} %upstream.1.part_ref, bf16[16,4096]{1,0:T(8,128)(2,1)S(1)} %get-tuple-element.33.rows_ref, f32[16,128]{1,0:T(8,128)S(1)} %get-tuple-element.35.gate_ref, ...), custom_call_target="tpu_custom_call" | custom-call | flops 25165824 | bytes 3145728 | tf_op jit(solution)/shard_map/down/pallas_call | solution.py:372
  19.9 0.0 collective-permute-done.6
  19.9 0.0 collective-permute-done.7
  19.9 0.0 collective-permute-done.8
  20.0 0.6 %select_reduce_fusion = f32[8,128]{1,0:T(8,128)} fusion(f32[4,8,128]{2,1,0:T(8,128)S(1)} %get-tuple-element.27, f32[4,128]{1,0:T(4,128)S(1)} %select_reduce_fusion.1), kind=kLoop, calls=%fused_computation | loop fusion | flops 11264 | bytes 22528 | tf_op jit(solution)/shard_map/reduce_sum | solution.py:396
  (2 shorter events, 0.0 us)
Async XLA Ops:
  3.2 10.4 %collective-permute-start = (bf16[4,8320]{1,0:T(4,128)(2,1)S(1)}, bf16[4,8320]{1,0:T(4,128)(2,1)S(1)}, u32[]{:S(2)}, u32[]{:S(2)}) collective-permute-start(bf16[4,8320]{1,0:T(4,128)(2,1)S(1)} %get-tuple-element.30.refs_1_), channel_id=1, source_target_pairs={{0,12},{4,8},{8,4},{12,0},{1,13},{5,9},{9,5},{13,1},{2,14},{6,10},... | collective-permute-start | bytes 199688 | tf_op jit(solution)/shard_map/ppermute | solution.py:60
  8.3 5.3 %collective-permute-start.2 = (bf16[4,8320]{1,0:T(4,128)(2,1)S(1)}, bf16[4,8320]{1,0:T(4,128)(2,1)S(1)}, u32[]{:S(2)}, u32[]{:S(2)}) collective-permute-start(bf16[4,8320]{1,0:T(4,128)(2,1)S(1)} %get-tuple-element.32.refs_3_), channel_id=1, source_target_pairs={{0,4},{4,0},{8,12},{12,8},{1,5},{5,1},{9,13},{13,9},{2,6},{6,2},{1... | collective-permute-start | bytes 199688 | tf_op jit(solution)/shard_map/ppermute | solution.py:60
  8.3 5.3 %collective-permute-start.1 = (bf16[4,4224]{1,0:T(4,128)(2,1)S(1)}, bf16[4,4224]{1,0:T(4,128)(2,1)S(1)}, u32[]{:S(2)}, u32[]{:S(2)}) collective-permute-start(bf16[4,4224]{1,0:T(4,128)(2,1)S(1)} %get-tuple-element.31.refs_2_), channel_id=1, source_target_pairs={{0,8},{4,12},{8,0},{12,4},{1,9},{5,13},{9,1},{13,5},{2,10},{6,14},... | collective-permute-start | bytes 101384 | tf_op jit(solution)/shard_map/ppermute | solution.py:60
  9.0 6.4 %collective-permute-start.5 = (bf16[4,4096]{1,0:T(4,128)(2,1)S(1)}, bf16[4,4096]{1,0:T(4,128)(2,1)S(1)}, u32[]{:S(2)}, u32[]{:S(2)}) collective-permute-start(bf16[4,4096]{1,0:T(4,128)(2,1)S(1)} %get-tuple-element.40), channel_id=1, source_target_pairs={{0,8},{4,12},{8,0},{12,4},{1,9},{5,13},{9,1},{13,5},{2,10},{6,14},... | collective-permute-start | bytes 98312 | tf_op jit(solution)/shard_map/ppermute | solution.py:60
  11.2 4.1 %collective-permute-start.3 = (bf16[4,3584]{1,0:T(4,128)(2,1)S(1)}, bf16[4,3584]{1,0:T(4,128)(2,1)S(1)}, u32[]{:S(2)}, u32[]{:S(2)}) collective-permute-start(bf16[4,3584]{1,0:T(4,128)(2,1)S(1)} %get-tuple-element.38), channel_id=1, source_target_pairs={{0,16},{16,0},{1,17},{17,1},{2,18},{18,2},{3,19},{19,3},{4,20},{20... | collective-permute-start | bytes 86024 | tf_op jit(solution)/shard_map/ppermute | solution.py:60
  13.8 4.2 %collective-permute-start.4 = (bf16[4,6144]{1,0:T(4,128)(2,1)S(1)}, bf16[4,6144]{1,0:T(4,128)(2,1)S(1)}, u32[]{:S(2)}, u32[]{:S(2)}) collective-permute-start(bf16[4,6144]{1,0:T(4,128)(2,1)S(1)} %late.1), channel_id=1, source_target_pairs={{0,16},{16,0},{1,17},{17,1},{2,18},{18,2},{3,19},{19,3},{4,20},{20... | collective-permute-start | bytes 147464 | tf_op jit(solution)/shard_map/ppermute | solution.py:60
  15.5 4.4 %collective-permute-start.6 = (f32[16,128]{1,0:T(8,128)S(1)}, f32[16,128]{1,0:T(8,128)S(1)}, u32[]{:S(2)}, u32[]{:S(2)}) collective-permute-start(f32[16,128]{1,0:T(8,128)S(1)} %get-tuple-element.45), channel_id=1, source_target_pairs={{0,3},{1,2},{2,1},{3,0},{4,7},{5,6},{6,5},{7,4},{8,11},{9,10},{10,... | collective-permute-start | bytes 24584 | tf_op jit(solution)/shard_map/ppermute | solution.py:60
  15.5 4.4 %collective-permute-start.7 = (f32[16,128]{1,0:T(8,128)S(1)}, f32[16,128]{1,0:T(8,128)S(1)}, u32[]{:S(2)}, u32[]{:S(2)}) collective-permute-start(f32[16,128]{1,0:T(8,128)S(1)} %get-tuple-element.45), channel_id=1, source_target_pairs={{0,2},{1,3},{2,0},{3,1},{4,6},{5,7},{6,4},{7,5},{8,10},{9,11},{10,... | collective-permute-start | bytes 24584 | tf_op jit(solution)/shard_map/ppermute | solution.py:60
  17.1 2.8 %collective-permute-start.8 = (f32[16,128]{1,0:T(8,128)S(1)}, f32[16,128]{1,0:T(8,128)S(1)}, u32[]{:S(2)}, u32[]{:S(2)}) collective-permute-start(f32[16,128]{1,0:T(8,128)S(1)} %get-tuple-element.45), channel_id=1, source_target_pairs={{0,1},{1,0},{2,3},{3,2},{4,5},{5,4},{6,7},{7,6},{8,9},{9,8},{10,11... | collective-permute-start | bytes 24584 | tf_op jit(solution)/shard_map/ppermute | solution.py:60

commit v25 on v24

--- a/solution.py
+++ b/solution.py
@@ -165,18 +165,16 @@
 
 
 def late_kernel(count, groups, *refs):
-    received, lates, weighted_ref = refs[: count - 1], refs[count - 1 : -1], refs[-1]
-    width = weighted_ref.shape[1]
-    share = width // groups
+    received, lates = refs[: count - 1], refs[count - 1 :]
+    share = lates[0].shape[1] // (count - 1)
+    width = share * groups
     me = lax.axis_index("dp")
     for k in range(1, count):
-        row = received[k - 1][:, : width + LANES].astype(jnp.float32)
-        part = slice(k * PAD, k * PAD + CAP)
-        weighted_ref[part, :] = row[:, width : width + 1] * row[:, :width]
+        gate = received[k - 1][:, width : width + LANES].astype(jnp.float32)
         for r, late_ref in enumerate(lates, 1):
             begin = pl.multiple_of(target(me, r, groups) * share, share)
-            late = weighted_ref[part, pl.ds(begin, share)].astype(jnp.bfloat16)
-            late_ref[:, (k - 1) * share : k * share] = late
+            row = received[k - 1][:, pl.ds(begin, share)].astype(jnp.float32)
+            late_ref[:, (k - 1) * share : k * share] = (gate[:, :1] * row).astype(jnp.bfloat16)
 
 
 def slot_kernel(count, groups, hidden_ref, *refs):
@@ -319,7 +317,6 @@
         out_shape=[jax.ShapeDtypeStruct((CAP, (count - 1) * share), jnp.bfloat16)] * (groups - 1),
         in_specs=[VMEM] * (count - 1),
         out_specs=[VMEM] * (groups - 1),
-        scratch_shapes=[pltpu.VMEM((count * PAD, width), jnp.float32)],
         compiler_params=PARAMS,
         cost_estimate=cost(2 * slots * width, 4 * slots * width),
         name="late",

time: 20.8 us -> 20.7 us (level)
  no operation moved by 1% of the time
where the time goes in v25:
time: 20.7 us; the launch traced here: 20.5 us
  starting transfers between devices  12.9 us (62%)
  Pallas kernels  5.31 us (26%)
  waiting for transfers between devices  0.95 us (5%)
  between operations  0.7 us (3%)
  other arithmetic  0.63 us (3%)
    ppermute x9, starting transfers between devices, send(): lax.ppermute(value, axis, [(i, give(i, step, size)) for i in range(size)])  12.9 us
    pallas_call x1, Pallas kernels, on_device(): pl.pallas_call(functools.partial(front_kernel, count, groups, pieces), ou...  2.57 us
    pallas_call x1, Pallas kernels, on_device(): pl.pallas_call(functools.partial(down_kernel, count, groups, pieces, spli...  1.97 us
    ppermute x9, waiting for transfers between devices, send(): lax.ppermute(value, axis, [(i, give(i, step, size)) for i in range(size)])  0.95 us
    reduce_sum x1, other arithmetic, on_device(): gate_grad = jnp.sum(jnp.where(hits > 0, chosen[:, None, :], 0.0), axis=0)  0.6 us
    pallas_call x1, Pallas kernels, on_device(): pl.pallas_call(functools.partial(upstream_kernel, split), out_shape=jax.S...  0.42 us
  transfers between devices with their start and end apart: 9, of which 1 were waited for; matrix products, arithmetic and copies ran while one was open for 0% of the time, Pallas kernels for 13%

profile of v25, /device:TPU:0, one launch (start us, length us, event | category | flops | bytes accessed | tf_op | source)
XLA Modules:
  0.0 20.5 jit_solution(14437751505930761909)
XLA Ops:
  0.6 2.6 %front.1 = (f32[4,8,128]{2,1,0:T(8,128)S(1)}, f32[32,128]{1,0:T(8,128)S(1)}, bf16[384,4096]{1,0:T(8,128)(2,1)S(1)}, bf16[16,384]{1,0:T(8,128)(2,1)S(1)}, bf16[4,...) custom-call(s32[8,128]{1,0:T(8,128)} %bitcast.8, ...), custom_call_target="tpu_custom_call" | custom-call | flops 134217728 | bytes 4194304 | tf_op jit(solution)/shard_map/front/pallas_call | solution.py:279
  3.2 5.1 %collective-permute-start = (bf16[4,8320]{1,0:T(4,128)(2,1)S(1)}, bf16[4,8320]{1,0:T(4,128)(2,1)S(1)}, u32[]{:S(2)}, u32[]{:S(2)}) collective-permute-start(bf16[4,8320]{1,0:T(4,128)(2,1)S(1)} %get-tuple-element.30.refs_1_), channel_id=1, source_target_pairs={{0,12},{4,8},{8,4},{12,0},{1,13},{5,9},{9,5},{13,1},{2,14},{6,10},... | collective-permute-start | bytes 199688 | tf_op jit(solution)/shard_map/ppermute | solution.py:60
  8.3 0.0 collective-permute-start.2
  8.3 0.6 %collective-permute-start.1 = (bf16[4,4224]{1,0:T(4,128)(2,1)S(1)}, bf16[4,4224]{1,0:T(4,128)(2,1)S(1)}, u32[]{:S(2)}, u32[]{:S(2)}) collective-permute-start(bf16[4,4224]{1,0:T(4,128)(2,1)S(1)} %get-tuple-element.31.refs_2_), channel_id=1, source_target_pairs={{0,8},{4,12},{8,0},{12,4},{1,9},{5,13},{9,1},{13,5},{2,10},{6,14},... | collective-permute-start | bytes 101384 | tf_op jit(solution)/shard_map/ppermute | solution.py:60
  9.0 2.3 %collective-permute-start.5 = (bf16[4,4096]{1,0:T(4,128)(2,1)S(1)}, bf16[4,4096]{1,0:T(4,128)(2,1)S(1)}, u32[]{:S(2)}, u32[]{:S(2)}) collective-permute-start(bf16[4,4096]{1,0:T(4,128)(2,1)S(1)} %get-tuple-element.40), channel_id=1, source_target_pairs={{0,8},{4,12},{8,0},{12,4},{1,9},{5,13},{9,1},{13,5},{2,10},{6,14},... | collective-permute-start | bytes 98312 | tf_op jit(solution)/shard_map/ppermute | solution.py:60
  11.2 1.5 %collective-permute-start.3 = (bf16[4,3584]{1,0:T(4,128)(2,1)S(1)}, bf16[4,3584]{1,0:T(4,128)(2,1)S(1)}, u32[]{:S(2)}, u32[]{:S(2)}) collective-permute-start(bf16[4,3584]{1,0:T(4,128)(2,1)S(1)} %get-tuple-element.38), channel_id=1, source_target_pairs={{0,16},{16,0},{1,17},{17,1},{2,18},{18,2},{3,19},{19,3},{4,20},{20... | collective-permute-start | bytes 86024 | tf_op jit(solution)/shard_map/ppermute | solution.py:60
  12.7 0.9 %collective-permute-done.1.refs_2_.refs_1_.refs_5_ = bf16[4,4224]{1,0:T(4,128)(2,1)S(1)} collective-permute-done((bf16[4,4224]{1,0:T(4,128)(2,1)S(1)}, bf16[4,4224]{1,0:T(4,128)(2,1)S(1)}, u32[]{:S(2)}, u32[]{:S(2)}) %collective-permute-start.1) | collective-permute-done | bytes 33824 | tf_op jit(solution)/shard_map/ppermute | solution.py:60
  13.6 0.0 collective-permute-done.refs_1_.refs_0_.refs_4_
  13.6 0.0 collective-permute-done.2.refs_3_.refs_2_.refs_6_
  13.6 0.1 late.1
  13.7 1.6 %collective-permute-start.4 = (bf16[4,6144]{1,0:T(4,128)(2,1)S(1)}, bf16[4,6144]{1,0:T(4,128)(2,1)S(1)}, u32[]{:S(2)}, u32[]{:S(2)}) collective-permute-start(bf16[4,6144]{1,0:T(4,128)(2,1)S(1)} %late.1), channel_id=1, source_target_pairs={{0,16},{16,0},{1,17},{17,1},{2,18},{18,2},{3,19},{19,3},{4,20},{20... | collective-permute-start | bytes 147464 | tf_op jit(solution)/shard_map/ppermute | solution.py:60
  15.3 0.0 collective-permute-done.3.refs_9_.refs_1_
  15.3 0.0 collective-permute-done.5.refs_8_
  15.3 0.2 backs.1
  15.5 0.0 collective-permute-start.6
  15.5 1.6 %collective-permute-start.7 = (f32[16,128]{1,0:T(8,128)S(1)}, f32[16,128]{1,0:T(8,128)S(1)}, u32[]{:S(2)}, u32[]{:S(2)}) collective-permute-start(f32[16,128]{1,0:T(8,128)S(1)} %get-tuple-element.45), channel_id=1, source_target_pairs={{0,2},{1,3},{2,0},{3,1},{4,6},{5,7},{6,4},{7,5},{8,10},{9,11},{10,... | collective-permute-start | bytes 24584 | tf_op jit(solution)/shard_map/ppermute | solution.py:60
  17.1 0.3 %collective-permute-start.8 = (f32[16,128]{1,0:T(8,128)S(1)}, f32[16,128]{1,0:T(8,128)S(1)}, u32[]{:S(2)}, u32[]{:S(2)}) collective-permute-start(f32[16,128]{1,0:T(8,128)S(1)} %get-tuple-element.45), channel_id=1, source_target_pairs={{0,1},{1,0},{2,3},{3,2},{4,5},{5,4},{6,7},{7,6},{8,9},{9,8},{10,11... | collective-permute-start | bytes 24584 | tf_op jit(solution)/shard_map/ppermute | solution.py:60
  17.3 0.1 slots.1
  17.4 0.4 %upstream.1.part_ref = f32[16,384]{1,0:T(8,128)S(1)} custom-call(bf16[16,4096]{1,0:T(8,128)(2,1)S(1)} %get-tuple-element.33.rows_ref, bf16[384,4096]{1,0:T(8,128)(2,1)S(1)} %get-tuple-element.34.weight_ref), custom_call_target="tpu_custom_call" | custom-call | flops 18874368 | bytes 1179648 | tf_op jit(solution)/shard_map/upstream/pallas_call | solution.py:359
  17.8 0.0 collective-permute-done.4.refs_2_
  17.9 2.0 %down.1 = (bf16[1,1,16,384]{3,2,1,0:T(8,128)(2,1)}, f32[1,384,2048]{2,1,0:T(8,128)}, f32[32,128]{1,0:T(8,128)S(1)}) custom-call(f32[16,384]{1,0:T(8,128)S(1)} %upstream.1.part_ref, bf16[16,4096]{1,0:T(8,128)(2,1)S(1)} %get-tuple-element.33.rows_ref, f32[16,128]{1,0:T(8,128)S(1)} %get-tuple-element.35.gate_ref, ...), custom_call_target="tpu_custom_call" | custom-call | flops 25165824 | bytes 3145728 | tf_op jit(solution)/shard_map/down/pallas_call | solution.py:369
  19.9 0.0 collective-permute-done.6
  19.9 0.0 collective-permute-done.7
  19.9 0.0 collective-permute-done.8
  19.9 0.6 %select_reduce_fusion = f32[8,128]{1,0:T(8,128)} fusion(f32[4,8,128]{2,1,0:T(8,128)S(1)} %get-tuple-element.27, f32[4,128]{1,0:T(4,128)S(1)} %select_reduce_fusion.1), kind=kLoop, calls=%fused_computation | loop fusion | flops 11264 | bytes 22528 | tf_op jit(solution)/shard_map/reduce_sum | solution.py:393
  (2 shorter events, 0.0 us)
Async XLA Ops:
  3.2 10.4 %collective-permute-start = (bf16[4,8320]{1,0:T(4,128)(2,1)S(1)}, bf16[4,8320]{1,0:T(4,128)(2,1)S(1)}, u32[]{:S(2)}, u32[]{:S(2)}) collective-permute-start(bf16[4,8320]{1,0:T(4,128)(2,1)S(1)} %get-tuple-element.30.refs_1_), channel_id=1, source_target_pairs={{0,12},{4,8},{8,4},{12,0},{1,13},{5,9},{9,5},{13,1},{2,14},{6,10},... | collective-permute-start | bytes 199688 | tf_op jit(solution)/shard_map/ppermute | solution.py:60
  8.3 5.3 %collective-permute-start.2 = (bf16[4,8320]{1,0:T(4,128)(2,1)S(1)}, bf16[4,8320]{1,0:T(4,128)(2,1)S(1)}, u32[]{:S(2)}, u32[]{:S(2)}) collective-permute-start(bf16[4,8320]{1,0:T(4,128)(2,1)S(1)} %get-tuple-element.32.refs_3_), channel_id=1, source_target_pairs={{0,4},{4,0},{8,12},{12,8},{1,5},{5,1},{9,13},{13,9},{2,6},{6,2},{1... | collective-permute-start | bytes 199688 | tf_op jit(solution)/shard_map/ppermute | solution.py:60
  8.3 5.3 %collective-permute-start.1 = (bf16[4,4224]{1,0:T(4,128)(2,1)S(1)}, bf16[4,4224]{1,0:T(4,128)(2,1)S(1)}, u32[]{:S(2)}, u32[]{:S(2)}) collective-permute-start(bf16[4,4224]{1,0:T(4,128)(2,1)S(1)} %get-tuple-element.31.refs_2_), channel_id=1, source_target_pairs={{0,8},{4,12},{8,0},{12,4},{1,9},{5,13},{9,1},{13,5},{2,10},{6,14},... | collective-permute-start | bytes 101384 | tf_op jit(solution)/shard_map/ppermute | solution.py:60
  9.0 6.3 %collective-permute-start.5 = (bf16[4,4096]{1,0:T(4,128)(2,1)S(1)}, bf16[4,4096]{1,0:T(4,128)(2,1)S(1)}, u32[]{:S(2)}, u32[]{:S(2)}) collective-permute-start(bf16[4,4096]{1,0:T(4,128)(2,1)S(1)} %get-tuple-element.40), channel_id=1, source_target_pairs={{0,8},{4,12},{8,0},{12,4},{1,9},{5,13},{9,1},{13,5},{2,10},{6,14},... | collective-permute-start | bytes 98312 | tf_op jit(solution)/shard_map/ppermute | solution.py:60
  11.2 4.0 %collective-permute-start.3 = (bf16[4,3584]{1,0:T(4,128)(2,1)S(1)}, bf16[4,3584]{1,0:T(4,128)(2,1)S(1)}, u32[]{:S(2)}, u32[]{:S(2)}) collective-permute-start(bf16[4,3584]{1,0:T(4,128)(2,1)S(1)} %get-tuple-element.38), channel_id=1, source_target_pairs={{0,16},{16,0},{1,17},{17,1},{2,18},{18,2},{3,19},{19,3},{4,20},{20... | collective-permute-start | bytes 86024 | tf_op jit(solution)/shard_map/ppermute | solution.py:60
  13.7 4.2 %collective-permute-start.4 = (bf16[4,6144]{1,0:T(4,128)(2,1)S(1)}, bf16[4,6144]{1,0:T(4,128)(2,1)S(1)}, u32[]{:S(2)}, u32[]{:S(2)}) collective-permute-start(bf16[4,6144]{1,0:T(4,128)(2,1)S(1)} %late.1), channel_id=1, source_target_pairs={{0,16},{16,0},{1,17},{17,1},{2,18},{18,2},{3,19},{19,3},{4,20},{20... | collective-permute-start | bytes 147464 | tf_op jit(solution)/shard_map/ppermute | solution.py:60
  15.5 4.4 %collective-permute-start.6 = (f32[16,128]{1,0:T(8,128)S(1)}, f32[16,128]{1,0:T(8,128)S(1)}, u32[]{:S(2)}, u32[]{:S(2)}) collective-permute-start(f32[16,128]{1,0:T(8,128)S(1)} %get-tuple-element.45), channel_id=1, source_target_pairs={{0,3},{1,2},{2,1},{3,0},{4,7},{5,6},{6,5},{7,4},{8,11},{9,10},{10,... | collective-permute-start | bytes 24584 | tf_op jit(solution)/shard_map/ppermute | solution.py:60
  15.5 4.4 %collective-permute-start.7 = (f32[16,128]{1,0:T(8,128)S(1)}, f32[16,128]{1,0:T(8,128)S(1)}, u32[]{:S(2)}, u32[]{:S(2)}) collective-permute-start(f32[16,128]{1,0:T(8,128)S(1)} %get-tuple-element.45), channel_id=1, source_target_pairs={{0,2},{1,3},{2,0},{3,1},{4,6},{5,7},{6,4},{7,5},{8,10},{9,11},{10,... | collective-permute-start | bytes 24584 | tf_op jit(solution)/shard_map/ppermute | solution.py:60
  17.1 2.8 %collective-permute-start.8 = (f32[16,128]{1,0:T(8,128)S(1)}, f32[16,128]{1,0:T(8,128)S(1)}, u32[]{:S(2)}, u32[]{:S(2)}) collective-permute-start(f32[16,128]{1,0:T(8,128)S(1)} %get-tuple-element.45), channel_id=1, source_target_pairs={{0,1},{1,0},{2,3},{3,2},{4,5},{5,4},{6,7},{7,6},{8,9},{9,8},{10,11... | collective-permute-start | bytes 24584 | tf_op jit(solution)/shard_map/ppermute | solution.py:60
